TPU v7x, 128 devices: a whole 4x4x4 slice. The times are simulated.
128 devices in a mesh: rows: 4 (over z), lat: 32 (over x, y, core).
Axes of the slice: x: 4, y: 4, z: 4, core: 2. Of those that a mesh axis runs over, the one named last changes fastest.
Arguments:
- mlp_inputs: bfloat16 [512, 8192], P(None, 'rows'), may hold values from -6 to 6
- enc_weight: bfloat16 [8192, 16384], P('rows', 'lat'), may hold values from -0.0625 to 0.0625
- enc_bias: float32 [16384], P('lat'), may hold values from -3 to 3
- active: int32 [512, 16384], P(None, 'lat'), may hold values from 0 to 1, as said below
- dec_weight: bfloat16 [3, 16384, 8192], P(None, 'lat', 'rows'), may hold values from -0.625 to 0.625
- target: bfloat16 [3, 512, 8192], P(None, 'lat', 'rows'), may hold values from -6 to 6
Outputs:
- enc_grad: bfloat16 [8192, 16384], P('rows', 'lat')
- bias_grad: float32 [16384], P('lat')
- dec_grad: bfloat16 [3, 16384, 8192], P(None, 'lat', 'rows')
Inputs may be any that keep to these rules, and one draw needn't show every extreme that they name: active[r, f] is 1 where latent f fires on row r.
All inputs are finite; a program needn't handle non-finite values.
Results may differ from a plain program's by a relative error of at most 0.0062.
Values may be sent and summed in bfloat16 or wider, within the bound.
No kernel may reach another device: no remote copies, remote signals or barrier semaphores. Data moves between devices by JAX's collectives and lax.ppermute only.
A program may use at most 128 MiB of HBM per device.

v0:
```python
import math

import jax
import jax.numpy as jnp
from jax import lax
from jax.sharding import PartitionSpec as P

TARGETS = 3


def add_rows(latent_grad, contribution):
    return latent_grad + contribution


def per_device(mlp_inputs, enc_weight, enc_bias, active, dec_weight, target):
    all_rows = mlp_inputs.shape[0]
    own_rows = all_rows // lax.axis_size("rows")
    sub_rows = all_rows // lax.axis_size("lat")
    row_start = lax.axis_index("rows") * own_rows
    error_scale = 1.0 / math.sqrt(all_rows)
    pre_own = (
        lax.psum_scatter(
            jnp.dot(mlp_inputs, enc_weight, preferred_element_type=jnp.float32),
            "rows",
            scatter_dimension=0,
            tiled=True,
        )
        + enc_bias
    )
    mask_own = lax.dynamic_slice_in_dim(active, row_start, own_rows, 0)
    lat_own = jnp.where(mask_own > 0, pre_own, jnp.zeros_like(pre_own)).astype(jnp.bfloat16)
    latents = lax.all_gather(lat_own, "rows", axis=0, tiled=True)
    latent_grad = jnp.zeros((all_rows, enc_weight.shape[1]), jnp.float32)
    dec_parts = []
    for target_id in range(TARGETS):

        def dec_term(first_row, row_count, target_id=target_id):
            return jnp.dot(latents, dec_weight[target_id], preferred_element_type=jnp.float32)

        rebuilt = lax.psum_scatter(
            dec_term(jnp.int32(0), sub_rows * lax.axis_size("lat")),
            "lat",
            scatter_dimension=0,
            tiled=True,
        )
        scaled_error = ((rebuilt - target[target_id]) * error_scale).astype(jnp.bfloat16)

        def fold_error(totals, shard_piece, first_row, target_id=target_id):
            contribution = jnp.einsum(
                "rd,fd->rf", shard_piece, dec_weight[target_id], preferred_element_type=jnp.float32
            )
            dec_total = jnp.einsum(
                "rf,rd->fd", latents, shard_piece, preferred_element_type=jnp.float32
            )
            return (add_rows(totals[0], contribution), dec_total)

        dec_start = jnp.zeros(dec_weight.shape[1:], jnp.float32)
        latent_grad, dec_total = fold_error(
            (latent_grad, dec_start),
            lax.all_gather(scaled_error, "lat", axis=0, tiled=True),
            jnp.int32(0),
        )
        dec_parts.append(dec_total.astype(jnp.bfloat16))
    dec_grad = jnp.stack(dec_parts)
    grad_own = lax.psum_scatter(latent_grad, "rows", scatter_dimension=0, tiled=True)
    mask_rows = lax.dynamic_slice_in_dim(active, row_start, own_rows, 0)
    masked_own = jnp.where(mask_rows > 0, grad_own, jnp.zeros_like(grad_own)).astype(jnp.bfloat16)
    pre_grad = lax.all_gather(masked_own, "rows", axis=0, tiled=True)
    enc_grad = jnp.einsum(
        "rd,rf->df", mlp_inputs, pre_grad, preferred_element_type=jnp.float32
    ).astype(jnp.bfloat16)
    bias_grad = jnp.sum(pre_grad.astype(jnp.float32), axis=0)
    return (enc_grad, bias_grad, dec_grad)


def solution(mesh):
    in_specs = (
        P(None, "rows"),
        P("rows", "lat"),
        P("lat"),
        P(None, "lat"),
        P(None, "lat", "rows"),
        P(None, "lat", "rows"),
    )
    out_specs = (P("rows", "lat"), P("lat"), P(None, "lat", "rows"))
    return jax.shard_map(
        per_device, mesh=mesh, in_specs=in_specs, out_specs=out_specs, check_vma=False
    )
```

profile of v0, /device:TPU:0, one launch (start us, length us, event | category | flops | bytes accessed | tf_op | source)
XLA Modules:
  0.0 502.5 jit_solution(106179655086136195)
XLA Ops:
  7.2 0.0 copy-start
  7.2 0.0 copy-start.2
  7.2 0.0 reduce-scatter.6.cloned.1.call-start
  7.2 1.5 copy-done
  8.8 3.8 fusion.34
  12.6 0.0 reduce-scatter.6.cloned.1.call-update
  12.6 0.0 reduce-scatter.12.cloned.1.call-start
  12.6 26.3 %reduce-scatter.6.cloned.1.call-done = f32[128,512]{1,0:T(8,128)} async-done(((f32[512,512]{1,0:T(8,128)}), f32[128,512]{1,0:T(8,128)}) %reduce-scatter.6.cloned.1.call-update) | async-done | bytes 262160 | tf_op jit(solution)/shard_map/reduce_scatter | solution.py:22
  39.0 0.0 copy-done.2
  39.0 1.1 select_convert_fusion.1
  40.1 12.8 %all_gather.15 = bf16[512,512]{1,0:T(8,128)(2,1)S(1)} all-gather(bf16[128,512]{1,0:T(8,128)(2,1)S(1)} %get-tuple-element.6), channel_id=1, replica_groups=mesh['rows'=4,'lat'=32] {'rows'}, dimensions={0}, use_global_device_ids=true | all-gather | bytes 655360 | tf_op jit(solution)/shard_map/all_gather | solution.py:32
  52.9 4.8 fusion.6
  57.6 0.0 reduce-scatter.12.cloned.1.call-update
  57.7 0.0 reduce-scatter.10.cloned.1.call-start
  57.7 4.8 fusion.10
  62.6 0.0 reduce-scatter.10.cloned.1.call-update
  62.6 0.0 reduce-scatter.8.cloned.1.call-start
  62.6 4.9 fusion.14
  67.5 0.0 reduce-scatter.8.cloned.1.call-update
  67.5 0.0 all-gather.6.cloned.1.call-start
  67.6 71.6 %reduce-scatter.12.cloned.1.call-done = f32[16,2048]{1,0:T(8,128)} async-done(((f32[512,2048]{1,0:T(8,128)}), f32[16,2048]{1,0:T(8,128)}) %reduce-scatter.12.cloned.1.call-update) | async-done | bytes 131088 | tf_op jit(solution)/shard_map/reduce_scatter | solution.py:40
  139.2 84.9 %reduce-scatter.10.cloned.1.call-done = f32[16,2048]{1,0:T(8,128)} async-done(((f32[512,2048]{1,0:T(8,128)}), f32[16,2048]{1,0:T(8,128)}) %reduce-scatter.10.cloned.1.call-update) | async-done | bytes 131088 | tf_op jit(solution)/shard_map/reduce_scatter | solution.py:40
  224.0 85.7 %reduce-scatter.8.cloned.1.call-done = f32[16,2048]{1,0:T(8,128)} async-done(((f32[512,2048]{1,0:T(8,128)}), f32[16,2048]{1,0:T(8,128)}) %reduce-scatter.8.cloned.1.call-update) | async-done | bytes 131088 | tf_op jit(solution)/shard_map/reduce_scatter | solution.py:40
  309.8 1.7 fusion.33
  311.5 0.0 all-gather.6.cloned.1.call-update
  311.5 0.0 all-gather.8.cloned.1.call-start
  311.6 0.5 all-gather.8.cloned.1.call-update
  312.1 0.0 all-gather.4.cloned.1.call-start
  312.2 0.7 all-gather.4.cloned.1.call-update
  312.9 0.0 reduce-scatter.14.cloned.1.call-start
  312.9 42.6 %all-gather.6.cloned.1.call-done = bf16[512,2048]{1,0:T(8,128)(2,1)} async-done(((bf16[16,2048]{1,0:T(8,128)(2,1)}), bf16[512,2048]{1,0:T(8,128)(2,1)}) %all-gather.6.cloned.1.call-update) | async-done | bytes 2097168 | tf_op jit(solution)/shard_map/all_gather | solution.py:60
  355.5 4.5 fusion.8
  360.0 41.2 %all-gather.8.cloned.1.call-done = bf16[512,2048]{1,0:T(8,128)(2,1)} async-done(((bf16[16,2048]{1,0:T(8,128)(2,1)}), bf16[512,2048]{1,0:T(8,128)(2,1)}) %all-gather.8.cloned.1.call-update) | async-done | bytes 2097168 | tf_op jit(solution)/shard_map/all_gather | solution.py:60
  401.2 4.5 fusion.4
  405.7 40.8 %all-gather.4.cloned.1.call-done = bf16[512,2048]{1,0:T(8,128)(2,1)} async-done(((bf16[16,2048]{1,0:T(8,128)(2,1)}), bf16[512,2048]{1,0:T(8,128)(2,1)}) %all-gather.4.cloned.1.call-update) | async-done | bytes 2097168 | tf_op jit(solution)/shard_map/all_gather | solution.py:60
  446.5 5.1 %fusion.25 = f32[512,512]{1,0:T(8,128)} fusion(f32[512,512]{1,0:T(8,128)} %fusion.4, f32[512,512]{1,0:T(8,128)} %fusion.8, bf16[512,2048]{1,0:T(8,128)(2,1)} %all-gather.4.cloned.1.call-done, bf16[3,512,2048]{2,1,0:T(8,128)(2,1)} %param.10), kind=kOutput, calls=%fused_computation.28 | convolution fusion | flops 1074266112 | bytes 7340032 | tf_op jit(solution)/shard_map/rd,fd->rf/dot_general | solution.py:49
  451.5 0.0 reduce-scatter.14.cloned.1.call-update
  451.6 3.0 fusion.2
  454.6 1.3 fusion.1
  455.9 0.3 copy-done.3
  456.2 1.3 fusion.3
  457.5 3.2 pad_maximum_fusion
  460.6 14.0 %reduce-scatter.14.cloned.1.call-done = f32[128,512]{1,0:T(8,128)} async-done(((f32[512,512]{1,0:T(8,128)}), f32[128,512]{1,0:T(8,128)}) %reduce-scatter.14.cloned.1.call-update) | async-done | bytes 262160 | tf_op jit(solution)/shard_map/reduce_scatter | solution.py:65
  474.7 1.0 select_convert_fusion
  475.7 12.8 %all_gather.19 = bf16[512,512]{1,0:T(8,128)(2,1)S(1)} all-gather(bf16[128,512]{1,0:T(8,128)(2,1)S(1)} %select_convert_fusion), channel_id=1, replica_groups=mesh['rows'=4,'lat'=32] {'rows'}, dimensions={0}, use_global_device_ids=true | all-gather | bytes 655360 | tf_op jit(solution)/shard_map/all_gather | solution.py:68
  488.4 0.7 convert_reduce_fusion
  489.1 2.6 fusion
  491.7 3.9 copy.9
  (5 shorter events, 0.0 us)
Async XLA Ops:
  7.2 1.6 copy-start
  7.2 31.8 %copy-start.2 = (f32[512]{0:T(512)S(1)}, f32[512]{0:T(512)}, u32[]{:S(2)}) copy-start(f32[512]{0:T(512)} %param.8) | copy-start | bytes 6148
  7.2 31.8 %reduce-scatter.6.cloned.1.call-start = ((), (), s32[]{:S(2)}) async-start(), calls=%async_computation.5 | async-start | bytes 1310720 | tf_op jit(solution)/shard_map/reduce_scatter | solution.py:22
  12.6 126.6 %reduce-scatter.12.cloned.1.call-start = ((), (), s32[]{:S(2)}) async-start(), calls=%async_computation.10 | async-start | bytes 4325376 | tf_op jit(solution)/shard_map/reduce_scatter | solution.py:40
  57.7 166.4 %reduce-scatter.10.cloned.1.call-start = ((), (), s32[]{:S(2)}) async-start(), calls=%async_computation.8 | async-start | bytes 4325376 | tf_op jit(solution)/shard_map/reduce_scatter | solution.py:40
  62.6 247.2 %reduce-scatter.8.cloned.1.call-start = ((), (), s32[]{:S(2)}) async-start(), calls=%async_computation.6 | async-start | bytes 4325376 | tf_op jit(solution)/shard_map/reduce_scatter | solution.py:40
  67.5 242.3 %copy-start.1 = (bf16[3,16,2048]{2,1,0:T(8,128)(2,1)S(1)}, bf16[3,16,2048]{2,1,0:T(8,128)(2,1)}, u32[]{:S(2)}) copy-start(bf16[3,16,2048]{2,1,0:T(8,128)(2,1)} %param.11) | copy-start | bytes 589828
  67.5 288.0 %all-gather.6.cloned.1.call-start = ((), (), s32[]{:S(2)}) async-start(), calls=%async_computation.9 | async-start | bytes 2162688 | tf_op jit(solution)/shard_map/all_gather | solution.py:60
  311.5 89.7 %all-gather.8.cloned.1.call-start = ((), (), s32[]{:S(2)}) async-start(), calls=%async_computation.11 | async-start | bytes 2162688 | tf_op jit(solution)/shard_map/all_gather | solution.py:60
  312.1 134.4 %all-gather.4.cloned.1.call-start = ((), (), s32[]{:S(2)}) async-start(), calls=%async_computation.7 | async-start | bytes 2162688 | tf_op jit(solution)/shard_map/all_gather | solution.py:60
  312.9 161.8 %reduce-scatter.14.cloned.1.call-start = ((), (), s32[]{:S(2)}) async-start(), calls=%async_computation.12 | async-start | bytes 1310720 | tf_op jit(solution)/shard_map/reduce_scatter | solution.py:65
  451.6 3.0 copy-start.4
  454.6 1.6 copy-start.3
Sparse Core Ops, SparseCore 0:
  12.7 26.2 reduce-scatter.5
  57.8 81.3 reduce-scatter.11
  142.8 81.1 reduce-scatter.9
  228.5 81.1 reduce-scatter.7
  312.5 43.0 all-gather.5
  358.2 42.9 all-gather.7
  403.5 42.9 all-gather.3
  451.7 22.9 reduce-scatter.13
where the time goes:
time: 503 us; the launch traced here: 502 us
  waiting for transfers between devices  408 us (81%)
  matrix products  40.5 us (8%)
  blocking collectives  25.6 us (5%)
  between operations  14.2 us (3%)
  other arithmetic  7.65 us (2%)
  local copies, waits for them, and re-layouts  5.74 us (1%)
    reduce_scatter x3, waiting for transfers between devices, per_device(): lax.psum_scatter(dec_term(jnp.int32(0), sub_rows * lax.axis_size('lat')),...  242 us
    all_gather x3, waiting for transfers between devices, per_device(): lax.all_gather(scaled_error, 'lat', axis=0, tiled=True)  125 us
    reduce_scatter x1, waiting for transfers between devices, per_device(): lax.psum_scatter(jnp.dot(mlp_inputs, enc_weight, preferred_element_type=j...  26.3 us
    dot_general x3, matrix products, dec_term(): jnp.dot(latents, dec_weight[target_id], preferred_element_type=jnp.float32)  14.5 us
    reduce_scatter x1, waiting for transfers between devices, per_device(): lax.psum_scatter(latent_grad, 'rows', scatter_dimension=0, tiled=True)  14 us
    dot_general x3, matrix products, fold_error(): jnp.einsum('rd,fd->rf', shard_piece, dec_weight[target_id], preferred_ele...  14 us
    all_gather x1, blocking collectives, per_device(): latents = lax.all_gather(lat_own, 'rows', axis=0, tiled=True)  12.8 us
    all_gather x1, blocking collectives, per_device(): pre_grad = lax.all_gather(masked_own, 'rows', axis=0, tiled=True)  12.8 us
  transfers between devices with their start and end apart: 8, of which 8 were waited for; matrix products, arithmetic and copies ran while one was open for 5% of the time, Pallas kernels for 0%

commit v1 on v0

v1 whole, which is shorter than its diff:
```python
import math

import jax
import jax.numpy as jnp
from jax import lax
from jax.sharding import Mesh, PartitionSpec as P

TARGETS = 3
BF = jnp.bfloat16
F32 = jnp.float32


def shift(value, axis, step):
    size = lax.axis_size(axis)
    return lax.ppermute(value, axis, [(i, (i + step) % size) for i in range(size)])


def pick(value, index, axis):
    return lax.dynamic_index_in_dim(value, index, axis, keepdims=False)


def scatter_sum(blocks, axis, dim):
    size = lax.axis_size(axis)
    me = lax.axis_index(axis)
    got = [
        shift(pick(blocks, lax.rem(me + k, size), dim).astype(BF), axis, k)
        for k in (2, 1, 3)
    ]
    total = pick(blocks, me, dim).astype(F32)
    for piece in got:
        total = total + piece.astype(F32)
    return total


def gather(value, axis, dim):
    size = lax.axis_size(axis)
    me = lax.axis_index(axis)
    got = [value] + [shift(value, axis, k) for k in range(1, size)]
    order = [pick(jnp.stack([got[(p - j) % size] for p in range(size)]), me, 0) for j in range(size)]
    return jnp.stack(order, axis=dim)


def per_device(mlp_inputs, enc_weight, enc_bias, active, dec_weight, target):
    rows = mlp_inputs.shape[0]
    zs, xs, ys = lax.axis_size("z"), lax.axis_size("x"), lax.axis_size("y")
    z, x, y, c = (lax.axis_index(a) for a in "zxyc")
    own = rows // zs
    lat_n = enc_weight.shape[1]
    half = dec_weight.shape[2] // 2
    scale = 1.0 / math.sqrt(rows)

    sent = lax.dynamic_slice_in_dim(dec_weight, (1 - c) * half, half, 2)
    dec_sib = shift(sent, "c", 1)
    dec_own = lax.dynamic_slice_in_dim(dec_weight, c * half, half, 2)
    dec = jnp.concatenate([dec_own, dec_sib], axis=1)
    tgt_sent = lax.dynamic_slice_in_dim(target, (1 - c) * half, half, 2)
    tgt_own = lax.dynamic_slice_in_dim(target, c * half, half, 2)
    tgt_sib = shift(tgt_sent, "c", 1)
    tgt = jnp.where(
        c == 0,
        jnp.concatenate([tgt_own, tgt_sib], axis=1),
        jnp.concatenate([tgt_sib, tgt_own], axis=1),
    )

    def z_sum(value):
        got = lax.all_to_all(value.astype(BF).reshape(zs, own, lat_n), "z", 0, 0)
        return jnp.sum(got.astype(F32), axis=0)

    def z_gather(value):
        got = lax.all_to_all(jnp.broadcast_to(value[None], (zs,) + value.shape), "z", 0, 0)
        return got.reshape(rows, lat_n)

    mask = lax.dynamic_slice_in_dim(active, z * own, own, 0) > 0
    pre = z_sum(jnp.dot(mlp_inputs, enc_weight, preferred_element_type=F32)) + enc_bias
    lat_own = z_gather(jnp.where(mask, pre, 0.0).astype(BF))
    latents = jnp.concatenate([lat_own, shift(lat_own, "c", 1)], axis=1)

    parts = [jnp.dot(latents, dec[t], preferred_element_type=F32).astype(BF) for t in range(TARGETS)]
    rebuilt = jnp.stack(parts).reshape(TARGETS, xs, ys, rows // (xs * ys), half)
    q = half // 2
    sum_a = scatter_sum(rebuilt[..., :q], "x", 1)
    sum_b = scatter_sum(rebuilt[..., q:], "y", 2)
    sum_a = scatter_sum(sum_a, "y", 1)
    sum_b = scatter_sum(sum_b, "x", 1)
    err_a = ((sum_a - tgt[..., :q].astype(F32)) * scale).astype(BF)
    err_b = ((sum_b - tgt[..., q:].astype(F32)) * scale).astype(BF)
    err_a = gather(err_a, "y", 1)
    err_b = gather(err_b, "x", 1)
    err_a = gather(err_a, "x", 1).reshape(TARGETS, rows, q)
    err_b = gather(err_b, "y", 2).reshape(TARGETS, rows, q)
    err = jnp.concatenate([err_a, err_b], axis=2)

    lat_grad = jnp.zeros((rows, 2 * lat_n), F32)
    for t in range(TARGETS):
        lat_grad = lat_grad + jnp.einsum("rd,fd->rf", err[t], dec[t], preferred_element_type=F32)
    lat_grad = lat_grad[:, :lat_n] + shift(lat_grad[:, lat_n:].astype(BF), "c", 1).astype(F32)
    grad_own = jnp.where(mask, z_sum(lat_grad), 0.0).astype(BF)
    pre_grad = z_gather(grad_own)
    enc_grad = jnp.einsum("rd,rf->df", mlp_inputs, pre_grad, preferred_element_type=F32).astype(BF)
    bias_grad = jnp.sum(pre_grad.astype(F32), axis=0)

    dec_parts = []
    for t in range(TARGETS):
        total = jnp.einsum("rf,rd->fd", latents, err[t], preferred_element_type=F32).astype(BF)
        mine, other = total[:lat_n], shift(total[lat_n:], "c", 1)
        dec_parts.append(
            jnp.where(
                c == 0,
                jnp.concatenate([mine, other], axis=1),
                jnp.concatenate([other, mine], axis=1),
            )
        )
    return enc_grad, bias_grad, jnp.stack(dec_parts)


def solution(mesh):
    grid = Mesh(mesh.devices.reshape(4, 4, 4, 2), ("z", "x", "y", "c"))
    lat = ("x", "y", "c")
    in_specs = (
        P(None, "z"),
        P("z", lat),
        P(lat),
        P(None, lat),
        P(None, lat, "z"),
        P(None, lat, "z"),
    )
    out_specs = (P("z", lat), P(lat), P(None, lat, "z"))
    return jax.shard_map(
        per_device, mesh=grid, in_specs=in_specs, out_specs=out_specs, check_vma=False
    )
```

time: 503 us -> 223 us (0.44)
  waiting for transfers between devices: 408 us -> 66.3 us
  starting transfers between devices: 0.32 us -> 57.7 us
  local copies, waits for them, and re-layouts: 5.74 us -> 33.8 us
  other arithmetic: 7.65 us -> 24.1 us
  matrix products: 40.5 us -> 26.5 us
  blocking collectives: 25.6 us -> 11.7 us
  between operations: 14.2 us -> 1.1 us
    reduce_scatter x5 -> x0, waiting for transfers between devices: 283 us -> none  [the longest x3 242 us: per_device(): lax.psum_scatter(dec_term(jnp.int32(0), sub_rows * lax.axis_size('lat')),...]
    all_gather x3 -> x0, waiting for transfers between devices: 125 us -> none  [per_device(): lax.all_gather(scaled_error, 'lat', axis=0, tiled=True)]
    ppermute x0 -> x31, waiting for transfers between devices: none -> 49.3 us  [shift(): lax.ppermute(value, axis, [(i, (i + step) % size) for i in range(size)])]
    ppermute x0 -> x31, starting transfers between devices: none -> 44 us  [shift(): lax.ppermute(value, axis, [(i, (i + step) % size) for i in range(size)])]
    all_gather x2 -> x0, blocking collectives: 25.6 us -> none  [the longest x1 12.8 us: per_device(): latents = lax.all_gather(lat_own, 'rows', axis=0, tiled=True)]
    all_to_all x0 -> x3, waiting for transfers between devices: none -> 17 us  [the longest x2 17 us: z_sum(): got = lax.all_to_all(value.astype(BF).reshape(zs, own, lat_n), 'z', 0, 0)]
    dot_general x11, matrix products: 40.5 us -> 26.5 us  [the longest x3 7.99 us: per_device(): jnp.dot(latents, dec[t], preferred_element_type=F32).astype(BF)]
    all_to_all x0 -> x3, starting transfers between devices: none -> 13.7 us  [the longest x2 9.55 us: z_sum(): got = lax.all_to_all(value.astype(BF).reshape(zs, own, lat_n), 'z', 0, 0)]
  transfers between devices with their start and end apart: 8 -> 34, of which waited for: 8 -> 16; matrix products, arithmetic and copies ran while one was open for 5% -> 20% of each run, Pallas kernels for 0% -> 0%
where the time goes in v1:
time: 223 us; the launch traced here: 221 us
  waiting for transfers between devices  66.3 us (30%)
  starting transfers between devices  57.7 us (26%)
  local copies, waits for them, and re-layouts  33.8 us (15%)
  matrix products  26.5 us (12%)
  other arithmetic  24.1 us (11%)
  blocking collectives  11.7 us (5%)
    ppermute x31, waiting for transfers between devices, shift(): lax.ppermute(value, axis, [(i, (i + step) % size) for i in range(size)])  49.3 us
    ppermute x31, starting transfers between devices, shift(): lax.ppermute(value, axis, [(i, (i + step) % size) for i in range(size)])  44 us
    all_to_all x2, waiting for transfers between devices, z_sum(): got = lax.all_to_all(value.astype(BF).reshape(zs, own, lat_n), 'z', 0, 0)  17 us
    unnamed x30, local copies, waits for them, and re-layouts  15.6 us
    all_to_all x1, blocking collectives, z_gather(): lax.all_to_all(jnp.broadcast_to(value[None], (zs,) + value.shape), 'z', 0...  11.7 us
    all_to_all x2, starting transfers between devices, z_sum(): got = lax.all_to_all(value.astype(BF).reshape(zs, own, lat_n), 'z', 0, 0)  9.55 us
    dot_general x3, matrix products, per_device(): jnp.dot(latents, dec[t], preferred_element_type=F32).astype(BF)  7.99 us
    dot_general x3, matrix products, per_device(): jnp.einsum('rd,fd->rf', err[t], dec[t], preferred_element_type=F32)  7.59 us
  transfers between devices with their start and end apart: 34, of which 16 were waited for; matrix products, arithmetic and copies ran while one was open for 20% of the time, Pallas kernels for 0%

profile of v1, /device:TPU:0, one launch (start us, length us, event | category | flops | bytes accessed | tf_op | source)
XLA Modules:
  0.0 221.3 jit_solution(2288476416412036909)
XLA Ops:
  0.7 7.1 %constant_dynamic-slice_fusion.3 = (bf16[3,512,1024]{2,1,0:T(8,128)(2,1)}, bf16[3,512,1024]{2,1,0:T(8,128)(2,1)}) fusion(bf16[3,512,2048]{2,1,0:T(8,128)(2,1)} %param.10, s32[]{:T(128)S(6)} %select_n.118, s32[]{:T(128)S(6)} %select_n.119), kind=kLoop, calls=%fused_computation.220 | loop fusion | bytes 12582920 | tf_op jit(solution)/shard_map/dynamic_slice | solution.py:54
  7.8 2.0 convolution_convert_fusion.7
  9.8 5.4 %all-to-all-start = ((bf16[4,128,512]{2,1,0:T(8,128)(2,1)}), bf16[4,128,512]{2,1,0:T(8,128)(2,1)S(1)}, u32[]{:S(2)}, u32[]{:S(2)}) async-start(bf16[4,128,512]{2,1,0:T(8,128)(2,1)} %bitcast), calls=%async_computation | async-start | bytes 1048576 | tf_op jit(solution)/shard_map/all_to_all | solution.py:66
  15.2 10.1 %all-to-all-done = bf16[4,128,512]{2,1,0:T(8,128)(2,1)S(1)} async-done(((bf16[4,128,512]{2,1,0:T(8,128)(2,1)}), bf16[4,128,512]{2,1,0:T(8,128)(2,1)S(1)}, u32[]{:S(2)}, u32[]{:S(2)}) %all-to-all-start) | async-done | bytes 524320 | tf_op jit(solution)/shard_map/all_to_all | solution.py:66
  25.4 1.6 select_convert_fusion.1
  27.1 11.7 %all_to_all.20 = bf16[4,128,512]{2,1,0:T(8,128)(2,1)S(1)} all-to-all(bf16[4,128,512]{2,1,0:T(8,128)(2,1)S(1)} %broadcast_in_dim.10), channel_id=1, replica_groups=mesh['z'=4,'x'=4,'y'=4,'c'=2] {'z'}, dimensions={0} | all-to-all | bytes 1048576 | tf_op jit(solution)/shard_map/all_to_all | solution.py:70
  38.8 1.9 collective-permute-done
  40.7 3.0 %convolution_convert_fusion.4 = bf16[512,1024]{1,0:T(8,128)(2,1)S(1)} fusion(bf16[3,512,1024]{2,1,0:T(8,128)(2,1)} %collective-permute-done.1, bf16[3,512,1024]{2,1,0:T(8,128)(2,1)} %get-tuple-element.14, bf16[512,512]{1,0:T(8,128)(2,1)S(1)} %collective-permute-done, bf16[512,512]{1,0:T(8,128)(2,1)S(1)} %bitcast.175), kind=kOutput, calls=%fused_computation.59 | convolution fusion | flops 1080557568 | bytes 8388608 | tf_op jit(solution)/shard_map/dot_general | solution.py:78
  43.8 2.5 %convolution_convert_fusion.5 = bf16[512,1024]{1,0:T(8,128)(2,1)S(1)} fusion(bf16[512,512]{1,0:T(8,128)(2,1)S(1)} %collective-permute-done, bf16[512,512]{1,0:T(8,128)(2,1)S(1)} %bitcast.176, bf16[3,512,1024]{2,1,0:T(8,128)(2,1)S(1)} %copy-done.1, bf16[3,512,1024]{2,1,0:T(8,128)(2,1)} %collective-permute-done.1), kind=kOutput, calls=%fused_computation.60 | convolution fusion | flops 1080557568 | bytes 8388608 | tf_op jit(solution)/shard_map/dot_general | solution.py:78
  46.3 2.5 %convolution_convert_fusion.6 = bf16[512,1024]{1,0:T(8,128)(2,1)S(1)} fusion(bf16[512,512]{1,0:T(8,128)(2,1)S(1)} %collective-permute-done, bf16[512,512]{1,0:T(8,128)(2,1)S(1)} %bitcast.177, bf16[3,512,1024]{2,1,0:T(8,128)(2,1)S(1)} %copy-done.1, bf16[3,512,1024]{2,1,0:T(8,128)(2,1)} %collective-permute-done.1), kind=kOutput, calls=%fused_computation.61 | convolution fusion | flops 1080557568 | bytes 8388608 | tf_op jit(solution)/shard_map/dot_general | solution.py:78
  52.7 3.0 %collective-permute-start.17 = (bf16[3,4,32,512]{3,2,0,1:T(8,128)(2,1)}, bf16[3,4,32,512]{3,2,0,1:T(8,128)(2,1)S(1)}, u32[]{:S(2)}, u32[]{:S(2)}) collective-permute-start(bf16[3,4,32,512]{3,2,0,1:T(8,128)(2,1)} %get-tuple-element.29), channel_id=1, source_target_pairs={{0,6},{2,0},{4,2},{6,4},{1,7},{3,1},{5,3},{7,5},{8,14},{10,8},{12,... | collective-permute-start | bytes 1179656 | tf_op jit(solution)/shard_map/ppermute | solution.py:15
  55.7 2.2 collective-permute-start.15
  59.9 2.8 %collective-permute-start.4 = (bf16[3,4,32,512]{3,2,0,1:T(8,128)(2,1)S(1)}, bf16[3,4,32,512]{3,2,0,1:T(8,128)(2,1)S(1)}, u32[]{:S(2)}, u32[]{:S(2)}) collective-permute-start(bf16[3,4,32,512]{3,2,0,1:T(8,128)(2,1)S(1)} %get-tuple-element.36), channel_id=1, source_target_pairs={{0,24},{8,0},{16,8},{24,16},{1,25},{9,1},{17,9},{25,17},{2,26},{10... | collective-permute-start | bytes 1179656 | tf_op jit(solution)/shard_map/ppermute | solution.py:15
  62.8 10.3 %collective-permute-done.17 = bf16[3,4,32,512]{3,2,0,1:T(8,128)(2,1)S(1)} collective-permute-done((bf16[3,4,32,512]{3,2,0,1:T(8,128)(2,1)}, bf16[3,4,32,512]{3,2,0,1:T(8,128)(2,1)S(1)}, u32[]{:S(2)}, u32[]{:S(2)}) %collective-permute-start.17) | collective-permute-done | bytes 393248 | tf_op jit(solution)/shard_map/ppermute | solution.py:15
  74.6 1.9 collective-permute-done.16
  76.5 3.0 %collective-permute-start.2 = (bf16[3,4,32,512]{3,2,0,1:T(8,128)(2,1)S(1)}, bf16[3,4,32,512]{3,2,0,1:T(8,128)(2,1)S(1)}, u32[]{:S(2)}, u32[]{:S(2)}) collective-permute-start(bf16[3,4,32,512]{3,2,0,1:T(8,128)(2,1)S(1)} %get-tuple-element.35), channel_id=1, source_target_pairs={{0,16},{8,24},{16,0},{24,8},{1,17},{9,25},{17,1},{25,9},{2,18},{10... | collective-permute-start | bytes 1179656 | tf_op jit(solution)/shard_map/ppermute | solution.py:15
  83.2 4.3 %collective-permute-done.3 = bf16[3,4,32,512]{3,2,0,1:T(8,128)(2,1)S(1)} collective-permute-done((bf16[3,4,32,512]{3,2,0,1:T(8,128)(2,1)S(1)}, bf16[3,4,32,512]{3,2,0,1:T(8,128)(2,1)S(1)}, u32[]{:S(2)}, u32[]{:S(2)}) %collective-permute-start.3) | collective-permute-done | bytes 393248 | tf_op jit(solution)/shard_map/ppermute | solution.py:15
  87.4 7.5 %collective-permute-start.18 = (bf16[3,32,512]{2,1,0:T(8,128)(2,1)S(1)}, bf16[3,32,512]{2,1,0:T(8,128)(2,1)S(1)}, u32[]{:S(2)}, u32[]{:S(2)}) collective-permute-start(bf16[3,32,512]{2,1,0:T(8,128)(2,1)S(1)} %get-tuple-element.38), channel_id=1, source_target_pairs={{0,16},{8,24},{16,0},{24,8},{1,17},{9,25},{17,1},{25,9},{2,18},{10... | collective-permute-start | bytes 294920 | tf_op jit(solution)/shard_map/ppermute | solution.py:15
  97.1 3.7 %collective-permute-start.7 = (bf16[3,32,512]{2,1,0:T(8,128)(2,1)S(1)}, bf16[3,32,512]{2,1,0:T(8,128)(2,1)S(1)}, u32[]{:S(2)}, u32[]{:S(2)}) collective-permute-start(bf16[3,32,512]{2,1,0:T(8,128)(2,1)S(1)} %get-tuple-element.42), channel_id=1, source_target_pairs={{0,6},{2,0},{4,2},{6,4},{1,7},{3,1},{5,3},{7,5},{8,14},{10,8},{12,... | collective-permute-start | bytes 294920 | tf_op jit(solution)/shard_map/ppermute | solution.py:15
  103.4 4.8 %collective-permute-done.6 = bf16[3,32,512]{2,1,0:T(8,128)(2,1)S(1)} collective-permute-done((bf16[3,32,512]{2,1,0:T(8,128)(2,1)S(1)}, bf16[3,32,512]{2,1,0:T(8,128)(2,1)S(1)}, u32[]{:S(2)}, u32[]{:S(2)}) %collective-permute-start.6) | collective-permute-done | bytes 98336 | tf_op jit(solution)/shard_map/ppermute | solution.py:15
  108.4 3.4 %collective-permute-start.10 = (bf16[3,32,512]{2,1,0:T(8,128)(2,1)S(1)}, bf16[3,32,512]{2,1,0:T(8,128)(2,1)S(1)}, u32[]{:S(2)}, u32[]{:S(2)}) collective-permute-start(bf16[3,32,512]{2,1,0:T(8,128)(2,1)S(1)} %get-tuple-element.57), channel_id=1, source_target_pairs={{0,4},{2,6},{4,0},{6,2},{1,5},{3,7},{5,1},{7,3},{8,12},{10,14},{12... | collective-permute-start | bytes 294920 | tf_op jit(solution)/shard_map/ppermute | solution.py:15
  112.3 1.9 collective-permute-done.9
  118.0 2.5 %collective-permute-start.14 = (bf16[3,4,32,512]{3,2,1,0:T(8,128)(2,1)S(1)}, bf16[3,4,32,512]{3,2,1,0:T(8,128)(2,1)S(1)}, u32[]{:S(2)}, u32[]{:S(2)}) collective-permute-start(bf16[3,4,32,512]{3,2,1,0:T(8,128)(2,1)S(1)} %get-tuple-element.51), channel_id=1, source_target_pairs={{0,24},{8,0},{16,8},{24,16},{1,25},{9,1},{17,9},{25,17},{2,26},{10... | collective-permute-start | bytes 1179656 | tf_op jit(solution)/shard_map/ppermute | solution.py:15
  120.5 2.7 %collective-permute-start.22 = (bf16[3,32,512]{2,1,0:T(8,128)(2,1)S(1)}, bf16[3,32,512]{2,1,0:T(8,128)(2,1)S(1)}, u32[]{:S(2)}, u32[]{:S(2)}) collective-permute-start(bf16[3,32,512]{2,1,0:T(8,128)(2,1)S(1)} %get-tuple-element.56), channel_id=1, source_target_pairs={{0,16},{8,24},{16,0},{24,8},{1,17},{9,25},{17,1},{25,9},{2,18},{10... | collective-permute-start | bytes 294920 | tf_op jit(solution)/shard_map/ppermute | solution.py:15
  123.8 8.5 %collective-permute-done.22 = bf16[3,32,512]{2,1,0:T(8,128)(2,1)S(1)} collective-permute-done((bf16[3,32,512]{2,1,0:T(8,128)(2,1)S(1)}, bf16[3,32,512]{2,1,0:T(8,128)(2,1)S(1)}, u32[]{:S(2)}, u32[]{:S(2)}) %collective-permute-start.22) | collective-permute-done | bytes 98336 | tf_op jit(solution)/shard_map/ppermute | solution.py:15
  132.3 3.8 %collective-permute-done.23 = bf16[3,32,512]{2,1,0:T(8,128)(2,1)S(1)} collective-permute-done((bf16[3,32,512]{2,1,0:T(8,128)(2,1)S(1)}, bf16[3,32,512]{2,1,0:T(8,128)(2,1)S(1)}, u32[]{:S(2)}, u32[]{:S(2)}) %collective-permute-start.23) | collective-permute-done | bytes 98336 | tf_op jit(solution)/shard_map/ppermute | solution.py:15
  136.8 3.4 %collective-permute-start.25 = (bf16[3,4,32,512]{3,2,1,0:T(8,128)(2,1)S(1)}, bf16[3,4,32,512]{3,2,1,0:T(8,128)(2,1)S(1)}, u32[]{:S(2)}, u32[]{:S(2)}) collective-permute-start(bf16[3,4,32,512]{3,2,1,0:T(8,128)(2,1)S(1)} %get-tuple-element.45), channel_id=1, source_target_pairs={{0,4},{2,6},{4,0},{6,2},{1,5},{3,7},{5,1},{7,3},{8,12},{10,14},{12... | collective-permute-start | bytes 1179656 | tf_op jit(solution)/shard_map/ppermute | solution.py:15
  141.1 1.6 fusion.47
  142.9 3.9 %collective-permute-done.24 = bf16[3,4,32,512]{3,2,1,0:T(8,128)(2,1)S(1)} collective-permute-done((bf16[3,4,32,512]{3,2,1,0:T(8,128)(2,1)S(1)}, bf16[3,4,32,512]{3,2,1,0:T(8,128)(2,1)S(1)}, u32[]{:S(2)}, u32[]{:S(2)}) %collective-permute-start.24) | collective-permute-done | bytes 393248 | tf_op jit(solution)/shard_map/ppermute | solution.py:15
  146.8 4.2 %collective-permute-done.25 = bf16[3,4,32,512]{3,2,1,0:T(8,128)(2,1)S(1)} collective-permute-done((bf16[3,4,32,512]{3,2,1,0:T(8,128)(2,1)S(1)}, bf16[3,4,32,512]{3,2,1,0:T(8,128)(2,1)S(1)}, u32[]{:S(2)}, u32[]{:S(2)}) %collective-permute-start.25) | collective-permute-done | bytes 393248 | tf_op jit(solution)/shard_map/ppermute | solution.py:15
  151.6 1.6 fusion.31
  153.4 1.7 copy-done.2
  155.1 2.5 %fusion.101 = f32[512,1024]{1,0:T(8,128)S(1)} fusion(bf16[3,512,512]{2,1,0:T(8,128)(2,1)S(1)} %bitcast.158, bf16[3,512,512]{2,1,0:T(8,128)(2,1)S(1)} %bitcast.164, bf16[3,512,1024]{2,1,0:T(8,128)(2,1)S(1)} %copy-done.2, bf16[3,512,1024]{2,1,0:T(8,128)(2,1)} %collective-permute-done.1), kind=kOutput, calls=%fused_computation.223 | convolution fusion | flops 1080033280 | bytes 11534336 | tf_op jit(solution)/shard_map/rd,fd->rf/dot_general | solution.py:95
  157.6 2.5 %fusion.104 = f32[512,1024]{1,0:T(8,128)S(1)} fusion(bf16[3,512,512]{2,1,0:T(8,128)(2,1)S(1)} %bitcast.159, bf16[3,512,512]{2,1,0:T(8,128)(2,1)S(1)} %bitcast.165, bf16[3,512,1024]{2,1,0:T(8,128)(2,1)S(1)} %copy-done.2, bf16[3,512,1024]{2,1,0:T(8,128)(2,1)} %collective-permute-done.1), kind=kOutput, calls=%fused_computation.224 | convolution fusion | flops 1080033280 | bytes 11534336 | tf_op jit(solution)/shard_map/rd,fd->rf/dot_general | solution.py:95
  160.1 2.6 %add_add_fusion = f32[512,1024]{1,0:T(8,128)S(1)} fusion(f32[512,1024]{1,0:T(8,128)S(1)} %fusion.101, f32[512,1024]{1,0:T(8,128)S(1)} %fusion.104, bf16[3,512,512]{2,1,0:T(8,128)(2,1)S(1)} %bitcast.166, bf16[3,512,512]{2,1,0:T(8,128)(2,1)S(1)} %bitcast.160, bf16[3,512,1024]{2,1,0:T(8,128)(2,1)} %collective-permute-done.1, ...), kind=kOutput, calls=%fused_computation.21 | convolution fusion | flops 1081081856 | bytes 15728640 | tf_op jit(solution)/shard_map/rd,fd->rf/dot_general | solution.py:95
  168.8 2.6 %convolution_convert_fusion.3 = bf16[1024,1024]{0,1:T(8,128)(2,1)} fusion(bf16[3,512,512]{2,1,0:T(8,128)(2,1)S(1)} %bitcast.163, bf16[3,512,512]{2,1,0:T(8,128)(2,1)S(1)} %bitcast.169, bf16[512,512]{1,0:T(8,128)(2,1)S(1)} %copy-done.13, bf16[512,512]{1,0:T(8,128)(2,1)S(1)} %bitcast.180), kind=kOutput, calls=%fused_computation.24 | convolution fusion | flops 1078984704 | bytes 6291456 | tf_op jit(solution)/shard_map/rf,rd->fd/dot_general | solution.py:104
  172.5 4.2 %all-to-all-start.2 = ((bf16[4,128,512]{2,1,0:T(8,128)(2,1)}), bf16[4,128,512]{2,1,0:T(8,128)(2,1)}, u32[]{:S(2)}, u32[]{:S(2)}) async-start(bf16[4,128,512]{2,1,0:T(8,128)(2,1)} %bitcast.170), calls=%async_computation.2 | async-start | bytes 1048576 | tf_op jit(solution)/shard_map/all_to_all | solution.py:66
  176.7 3.1 %slice_bitcast_fusion.2 = (bf16[1,512,1024]{1,2,0:T(8,128)(2,1)}, bf16[512,1024]{0,1:T(8,128)(2,1)}) fusion(bf16[1024,1024]{0,1:T(8,128)(2,1)} %convolution_convert_fusion.3), kind=kLoop, calls=%fused_computation.69 | loop fusion | bytes 4194304 | tf_op jit(solution)/shard_map/concatenate | solution.py:109
  180.2 6.9 %all-to-all-done.2 = bf16[4,128,512]{2,1,0:T(8,128)(2,1)} async-done(((bf16[4,128,512]{2,1,0:T(8,128)(2,1)}), bf16[4,128,512]{2,1,0:T(8,128)(2,1)}, u32[]{:S(2)}, u32[]{:S(2)}) %all-to-all-start.2) | async-done | bytes 524320 | tf_op jit(solution)/shard_map/all_to_all | solution.py:66
  189.1 4.2 %all-to-all-start.3 = ((bf16[4,128,512]{2,1,0:T(8,128)(2,1)}), bf16[4,128,512]{2,1,0:T(8,128)(2,1)}, u32[]{:S(2)}, u32[]{:S(2)}) async-start(bf16[4,128,512]{2,1,0:T(8,128)(2,1)} %broadcast_in_dim.20), calls=%async_computation.3 | async-start | bytes 1048576 | tf_op jit(solution)/shard_map/all_to_all | solution.py:70
  193.3 2.2 %maximum_select_fusion.2 = bf16[1,512,2048]{1,2,0:T(8,128)(2,1)S(1)} fusion(bf16[1,512,1024]{1,2,0:T(8,128)(2,1)} %bitcast.72, bf16[1,512,1024]{1,2,0:T(8,128)(2,1)S(1)} %get-tuple-element.22, pred[]{:T(512)S(6)} %eq.2), kind=kLoop, calls=%fused_computation.20 | loop fusion | flops 9437184 | bytes 4194305 | tf_op jit(solution)/shard_map/jit(_where)/select_n | solution.py:107
  195.6 2.3 %maximum_select_fusion.1 = bf16[1,512,2048]{1,2,0:T(8,128)(2,1)S(1)} fusion(bf16[1,512,1024]{1,2,0:T(8,128)(2,1)} %bitcast.70, bf16[1,512,1024]{1,2,0:T(8,128)(2,1)S(1)} %copy-done.4, pred[]{:T(512)S(6)} %eq.2), kind=kLoop, calls=%fused_computation.19 | loop fusion | flops 9437184 | bytes 4194305 | tf_op jit(solution)/shard_map/jit(_where)/select_n | solution.py:107
  197.9 2.2 maximum_select_fusion
  200.1 3.1 %pad_maximum_fusion = bf16[3,512,2048]{1,2,0:T(8,128)(2,1)} fusion(bf16[1,512,2048]{1,2,0:T(8,128)(2,1)S(1)} %maximum_select_fusion.2, bf16[1,512,2048]{1,2,0:T(8,128)(2,1)S(1)} %maximum_select_fusion.1, bf16[1,512,2048]{1,2,0:T(8,128)(2,1)S(1)} %maximum_select_fusion), kind=kLoop, calls=%fused_computation.4 | loop fusion | flops 6291456 | bytes 12582912 | tf_op jit(solution)/shard_map/stack | solution.py:113
  203.2 8.8 %copy.23 = bf16[3,512,2048]{2,1,0:T(8,128)(2,1)} copy(bf16[3,512,2048]{1,2,0:T(8,128)(2,1)} %pad_maximum_fusion) | data formatting | bytes 12582912
  211.9 3.7 %fusion = bf16[2048,512]{0,1:T(8,128)(2,1)} fusion(bf16[512,512]{1,0:T(8,128)(2,1)} %bitcast.65, bf16[512,2048]{1,0:T(8,128)(2,1)S(1)} %copy-done), kind=kOutput, calls=%fused_computation.11 | convolution fusion | flops 1074790400 | bytes 4718592 | tf_op jit(solution)/shard_map/rd,rf->df/dot_general | solution.py:99
  215.6 3.9 %copy.22 = bf16[2048,512]{1,0:T(8,128)(2,1)} copy(bf16[2048,512]{0,1:T(8,128)(2,1)} %fusion) | data formatting | bytes 4194304
  219.5 1.7 convert_reduce_fusion
  (98 shorter events, 32.9 us)
Async XLA Ops:
  0.6 7.1 %copy-start = (bf16[512,2048]{1,0:T(8,128)(2,1)S(1)}, bf16[512,2048]{1,0:T(8,128)(2,1)}, u32[]{:S(2)}) copy-start(bf16[512,2048]{1,0:T(8,128)(2,1)} %param.6) | copy-start | bytes 6291460
  0.7 7.1 %copy-start.11 = (bf16[2048,512]{1,0:T(8,128)(2,1)S(1)}, bf16[2048,512]{1,0:T(8,128)(2,1)}, u32[]{:S(2)}) copy-start(bf16[2048,512]{1,0:T(8,128)(2,1)} %param.7) | copy-start | bytes 6291460
  7.8 17.7 %copy-start.10 = (f32[512]{0:T(512)S(1)}, f32[512]{0:T(512)}, u32[]{:S(2)}) copy-start(f32[512]{0:T(512)} %param.8) | copy-start | bytes 6148
  7.8 33.0 %collective-permute-start.1 = (bf16[3,512,1024]{2,1,0:T(8,128)(2,1)}, bf16[3,512,1024]{2,1,0:T(8,128)(2,1)}, u32[]{:S(2)}, u32[]{:S(2)}) collective-permute-start(bf16[3,512,1024]{2,1,0:T(8,128)(2,1)} %get-tuple-element.15), channel_id=1, source_target_pairs={{0,1},{1,0},{2,3},{3,2},{4,5},{5,4},{6,7},{7,6},{8,9},{9,8},{10,11... | collective-permute-start | bytes 9437192 | tf_op jit(solution)/shard_map/ppermute | solution.py:15
  9.8 15.5 %all-to-all-start = ((bf16[4,128,512]{2,1,0:T(8,128)(2,1)}), bf16[4,128,512]{2,1,0:T(8,128)(2,1)S(1)}, u32[]{:S(2)}, u32[]{:S(2)}) async-start(bf16[4,128,512]{2,1,0:T(8,128)(2,1)} %bitcast), calls=%async_computation | async-start | bytes 1048576 | tf_op jit(solution)/shard_map/all_to_all | solution.py:66
  38.8 124.3 %copy-start.6 = (bf16[4,128,512]{2,1,0:T(8,128)(2,1)}, bf16[4,128,512]{2,1,0:T(8,128)(2,1)S(1)}, u32[]{:S(2)}) copy-start(bf16[4,128,512]{2,1,0:T(8,128)(2,1)S(1)} %all_to_all.20) | copy-start | bytes 1572868
  38.8 1.9 collective-permute-start
  40.7 5.5 %copy-start.12 = (bf16[512,512]{1,0:T(8,128)(2,1)}, bf16[512,512]{1,0:T(8,128)(2,1)S(1)}, u32[]{:S(2)}) copy-start(bf16[512,512]{1,0:T(8,128)(2,1)S(1)} %collective-permute-done) | copy-start | bytes 1572868
  40.7 3.0 %copy-start.1 = (bf16[3,512,1024]{2,1,0:T(8,128)(2,1)S(1)}, bf16[3,512,1024]{2,1,0:T(8,128)(2,1)}, u32[]{:S(2)}) copy-start(bf16[3,512,1024]{2,1,0:T(8,128)(2,1)} %get-tuple-element.14) | copy-start | bytes 9437188
  50.5 1.2 copy-start.3
  50.5 7.4 %copy-start.9 = (bf16[3,16,2048]{2,1,0:T(8,128)(2,1)S(1)}, bf16[3,16,2048]{2,1,0:T(8,128)(2,1)}, u32[]{:S(2)}) copy-start(bf16[3,16,2048]{2,1,0:T(8,128)(2,1)} %param.11) | copy-start | bytes 589828
  52.7 20.4 %collective-permute-start.17 = (bf16[3,4,32,512]{3,2,0,1:T(8,128)(2,1)}, bf16[3,4,32,512]{3,2,0,1:T(8,128)(2,1)S(1)}, u32[]{:S(2)}, u32[]{:S(2)}) collective-permute-start(bf16[3,4,32,512]{3,2,0,1:T(8,128)(2,1)} %get-tuple-element.29), channel_id=1, source_target_pairs={{0,6},{2,0},{4,2},{6,4},{1,7},{3,1},{5,3},{7,5},{8,14},{10,8},{12,... | collective-permute-start | bytes 1179656 | tf_op jit(solution)/shard_map/ppermute | solution.py:15
  55.7 20.8 %collective-permute-start.16 = (bf16[3,4,32,512]{3,2,0,1:T(8,128)(2,1)}, bf16[3,4,32,512]{3,2,0,1:T(8,128)(2,1)}, u32[]{:S(2)}, u32[]{:S(2)}) collective-permute-start(bf16[3,4,32,512]{3,2,0,1:T(8,128)(2,1)} %get-tuple-element.30), channel_id=1, source_target_pairs={{0,2},{2,4},{4,6},{6,0},{1,3},{3,5},{5,7},{7,1},{8,10},{10,12},{12... | collective-permute-start | bytes 1179656 | tf_op jit(solution)/shard_map/ppermute | solution.py:15
  55.7 23.9 %collective-permute-start.15 = (bf16[3,4,32,512]{3,2,0,1:T(8,128)(2,1)S(1)}, bf16[3,4,32,512]{3,2,0,1:T(8,128)(2,1)}, u32[]{:S(2)}, u32[]{:S(2)}) collective-permute-start(bf16[3,4,32,512]{3,2,0,1:T(8,128)(2,1)S(1)} %get-tuple-element.28), channel_id=1, source_target_pairs={{0,4},{2,6},{4,0},{6,2},{1,5},{3,7},{5,1},{7,3},{8,12},{10,14},{12... | collective-permute-start | bytes 1179656 | tf_op jit(solution)/shard_map/ppermute | solution.py:15
  58.6 42.2 %collective-permute-start.8 = (bf16[3,16,1024]{2,1,0:T(8,128)(2,1)}, bf16[3,16,1024]{2,1,0:T(8,128)(2,1)}, u32[]{:S(2)}, u32[]{:S(2)}) collective-permute-start(bf16[3,16,1024]{2,1,0:T(8,128)(2,1)} %get-tuple-element.59), channel_id=1, source_target_pairs={{0,1},{1,0},{2,3},{3,2},{4,5},{5,4},{6,7},{7,6},{8,9},{9,8},{10,11... | collective-permute-start | bytes 294920 | tf_op jit(solution)/shard_map/ppermute | solution.py:15
  59.9 22.3 %collective-permute-start.4 = (bf16[3,4,32,512]{3,2,0,1:T(8,128)(2,1)S(1)}, bf16[3,4,32,512]{3,2,0,1:T(8,128)(2,1)S(1)}, u32[]{:S(2)}, u32[]{:S(2)}) collective-permute-start(bf16[3,4,32,512]{3,2,0,1:T(8,128)(2,1)S(1)} %get-tuple-element.36), channel_id=1, source_target_pairs={{0,24},{8,0},{16,8},{24,16},{1,25},{9,1},{17,9},{25,17},{2,26},{10... | collective-permute-start | bytes 1179656 | tf_op jit(solution)/shard_map/ppermute | solution.py:15
  73.1 14.3 %collective-permute-start.3 = (bf16[3,4,32,512]{3,2,0,1:T(8,128)(2,1)S(1)}, bf16[3,4,32,512]{3,2,0,1:T(8,128)(2,1)S(1)}, u32[]{:S(2)}, u32[]{:S(2)}) collective-permute-start(bf16[3,4,32,512]{3,2,0,1:T(8,128)(2,1)S(1)} %get-tuple-element.37), channel_id=1, source_target_pairs={{0,8},{8,16},{16,24},{24,0},{1,9},{9,17},{17,25},{25,1},{2,10},{10... | collective-permute-start | bytes 1179656 | tf_op jit(solution)/shard_map/ppermute | solution.py:15
  76.5 19.3 %collective-permute-start.2 = (bf16[3,4,32,512]{3,2,0,1:T(8,128)(2,1)S(1)}, bf16[3,4,32,512]{3,2,0,1:T(8,128)(2,1)S(1)}, u32[]{:S(2)}, u32[]{:S(2)}) collective-permute-start(bf16[3,4,32,512]{3,2,0,1:T(8,128)(2,1)S(1)} %get-tuple-element.35), channel_id=1, source_target_pairs={{0,16},{8,24},{16,0},{24,8},{1,17},{9,25},{17,1},{25,9},{2,18},{10... | collective-permute-start | bytes 1179656 | tf_op jit(solution)/shard_map/ppermute | solution.py:15
  81.1 19.7 %collective-permute-start.20 = (bf16[3,32,512]{2,1,0:T(8,128)(2,1)S(1)}, bf16[3,32,512]{2,1,0:T(8,128)(2,1)S(1)}, u32[]{:S(2)}, u32[]{:S(2)}) collective-permute-start(bf16[3,32,512]{2,1,0:T(8,128)(2,1)S(1)} %get-tuple-element.39), channel_id=1, source_target_pairs={{0,24},{8,0},{16,8},{24,16},{1,25},{9,1},{17,9},{25,17},{2,26},{10... | collective-permute-start | bytes 294920 | tf_op jit(solution)/shard_map/ppermute | solution.py:15
  82.3 21.1 %collective-permute-start.19 = (bf16[3,32,512]{2,1,0:T(8,128)(2,1)S(1)}, bf16[3,32,512]{2,1,0:T(8,128)(2,1)S(1)}, u32[]{:S(2)}, u32[]{:S(2)}) collective-permute-start(bf16[3,32,512]{2,1,0:T(8,128)(2,1)S(1)} %get-tuple-element.40), channel_id=1, source_target_pairs={{0,8},{8,16},{16,24},{24,0},{1,9},{9,17},{17,25},{25,1},{2,10},{10... | collective-permute-start | bytes 294920 | tf_op jit(solution)/shard_map/ppermute | solution.py:15
  87.4 15.9 %collective-permute-start.18 = (bf16[3,32,512]{2,1,0:T(8,128)(2,1)S(1)}, bf16[3,32,512]{2,1,0:T(8,128)(2,1)S(1)}, u32[]{:S(2)}, u32[]{:S(2)}) collective-permute-start(bf16[3,32,512]{2,1,0:T(8,128)(2,1)S(1)} %get-tuple-element.38), channel_id=1, source_target_pairs={{0,16},{8,24},{16,0},{24,8},{1,17},{9,25},{17,1},{25,9},{2,18},{10... | collective-permute-start | bytes 294920 | tf_op jit(solution)/shard_map/ppermute | solution.py:15
  97.1 6.3 %collective-permute-start.7 = (bf16[3,32,512]{2,1,0:T(8,128)(2,1)S(1)}, bf16[3,32,512]{2,1,0:T(8,128)(2,1)S(1)}, u32[]{:S(2)}, u32[]{:S(2)}) collective-permute-start(bf16[3,32,512]{2,1,0:T(8,128)(2,1)S(1)} %get-tuple-element.42), channel_id=1, source_target_pairs={{0,6},{2,0},{4,2},{6,4},{1,7},{3,1},{5,3},{7,5},{8,14},{10,8},{12,... | collective-permute-start | bytes 294920 | tf_op jit(solution)/shard_map/ppermute | solution.py:15
  100.8 7.4 %collective-permute-start.6 = (bf16[3,32,512]{2,1,0:T(8,128)(2,1)S(1)}, bf16[3,32,512]{2,1,0:T(8,128)(2,1)S(1)}, u32[]{:S(2)}, u32[]{:S(2)}) collective-permute-start(bf16[3,32,512]{2,1,0:T(8,128)(2,1)S(1)} %get-tuple-element.43), channel_id=1, source_target_pairs={{0,2},{2,4},{4,6},{6,0},{1,3},{3,5},{5,7},{7,1},{8,10},{10,12},{12... | collective-permute-start | bytes 294920 | tf_op jit(solution)/shard_map/ppermute | solution.py:15
  100.8 7.4 %collective-permute-start.5 = (bf16[3,32,512]{2,1,0:T(8,128)(2,1)S(1)}, bf16[3,32,512]{2,1,0:T(8,128)(2,1)S(1)}, u32[]{:S(2)}, u32[]{:S(2)}) collective-permute-start(bf16[3,32,512]{2,1,0:T(8,128)(2,1)S(1)} %get-tuple-element.41), channel_id=1, source_target_pairs={{0,4},{2,6},{4,0},{6,2},{1,5},{3,7},{5,1},{7,3},{8,12},{10,14},{12... | collective-permute-start | bytes 294920 | tf_op jit(solution)/shard_map/ppermute | solution.py:15
  108.4 5.9 %collective-permute-start.9 = (bf16[3,32,512]{2,1,0:T(8,128)(2,1)S(1)}, bf16[3,32,512]{2,1,0:T(8,128)(2,1)S(1)}, u32[]{:S(2)}, u32[]{:S(2)}) collective-permute-start(bf16[3,32,512]{2,1,0:T(8,128)(2,1)S(1)} %get-tuple-element.57), channel_id=1, source_target_pairs={{0,2},{2,4},{4,6},{6,0},{1,3},{3,5},{5,7},{7,1},{8,10},{10,12},{12... | collective-permute-start | bytes 294920 | tf_op jit(solution)/shard_map/ppermute | solution.py:15
  108.4 7.0 %collective-permute-start.10 = (bf16[3,32,512]{2,1,0:T(8,128)(2,1)S(1)}, bf16[3,32,512]{2,1,0:T(8,128)(2,1)S(1)}, u32[]{:S(2)}, u32[]{:S(2)}) collective-permute-start(bf16[3,32,512]{2,1,0:T(8,128)(2,1)S(1)} %get-tuple-element.57), channel_id=1, source_target_pairs={{0,4},{2,6},{4,0},{6,2},{1,5},{3,7},{5,1},{7,3},{8,12},{10,14},{12... | collective-permute-start | bytes 294920 | tf_op jit(solution)/shard_map/ppermute | solution.py:15
  111.8 4.6 %collective-permute-start.11 = (bf16[3,32,512]{2,1,0:T(8,128)(2,1)S(1)}, bf16[3,32,512]{2,1,0:T(8,128)(2,1)S(1)}, u32[]{:S(2)}, u32[]{:S(2)}) collective-permute-start(bf16[3,32,512]{2,1,0:T(8,128)(2,1)S(1)} %get-tuple-element.57), channel_id=1, source_target_pairs={{0,6},{2,0},{4,2},{6,4},{1,7},{3,1},{5,3},{7,5},{8,14},{10,8},{12,... | collective-permute-start | bytes 294920 | tf_op jit(solution)/shard_map/ppermute | solution.py:15
  112.3 10.9 %collective-permute-start.21 = (bf16[3,32,512]{2,1,0:T(8,128)(2,1)S(1)}, bf16[3,32,512]{2,1,0:T(8,128)(2,1)S(1)}, u32[]{:S(2)}, u32[]{:S(2)}) collective-permute-start(bf16[3,32,512]{2,1,0:T(8,128)(2,1)S(1)} %get-tuple-element.56), channel_id=1, source_target_pairs={{0,8},{8,16},{16,24},{24,0},{1,9},{9,17},{17,25},{25,1},{2,10},{10... | collective-permute-start | bytes 294920 | tf_op jit(solution)/shard_map/ppermute | solution.py:15
  116.9 23.3 %collective-permute-start.12 = (bf16[3,4,32,512]{3,2,1,0:T(8,128)(2,1)S(1)}, bf16[3,4,32,512]{3,2,1,0:T(8,128)(2,1)S(1)}, u32[]{:S(2)}, u32[]{:S(2)}) collective-permute-start(bf16[3,4,32,512]{3,2,1,0:T(8,128)(2,1)S(1)} %get-tuple-element.51), channel_id=1, source_target_pairs={{0,8},{8,16},{16,24},{24,0},{1,9},{9,17},{17,25},{25,1},{2,10},{10... | collective-permute-start | bytes 1179656 | tf_op jit(solution)/shard_map/ppermute | solution.py:15
  117.0 24.0 %collective-permute-start.13 = (bf16[3,4,32,512]{3,2,1,0:T(8,128)(2,1)S(1)}, bf16[3,4,32,512]{3,2,1,0:T(8,128)(2,1)S(1)}, u32[]{:S(2)}, u32[]{:S(2)}) collective-permute-start(bf16[3,4,32,512]{3,2,1,0:T(8,128)(2,1)S(1)} %get-tuple-element.51), channel_id=1, source_target_pairs={{0,16},{8,24},{16,0},{24,8},{1,17},{9,25},{17,1},{25,9},{2,18},{10... | collective-permute-start | bytes 1179656 | tf_op jit(solution)/shard_map/ppermute | solution.py:15
  118.0 23.1 %collective-permute-start.14 = (bf16[3,4,32,512]{3,2,1,0:T(8,128)(2,1)S(1)}, bf16[3,4,32,512]{3,2,1,0:T(8,128)(2,1)S(1)}, u32[]{:S(2)}, u32[]{:S(2)}) collective-permute-start(bf16[3,4,32,512]{3,2,1,0:T(8,128)(2,1)S(1)} %get-tuple-element.51), channel_id=1, source_target_pairs={{0,24},{8,0},{16,8},{24,16},{1,25},{9,1},{17,9},{25,17},{2,26},{10... | collective-permute-start | bytes 1179656 | tf_op jit(solution)/shard_map/ppermute | solution.py:15
  120.5 11.8 %collective-permute-start.22 = (bf16[3,32,512]{2,1,0:T(8,128)(2,1)S(1)}, bf16[3,32,512]{2,1,0:T(8,128)(2,1)S(1)}, u32[]{:S(2)}, u32[]{:S(2)}) collective-permute-start(bf16[3,32,512]{2,1,0:T(8,128)(2,1)S(1)} %get-tuple-element.56), channel_id=1, source_target_pairs={{0,16},{8,24},{16,0},{24,8},{1,17},{9,25},{17,1},{25,9},{2,18},{10... | collective-permute-start | bytes 294920 | tf_op jit(solution)/shard_map/ppermute | solution.py:15
  123.2 12.9 %collective-permute-start.23 = (bf16[3,32,512]{2,1,0:T(8,128)(2,1)S(1)}, bf16[3,32,512]{2,1,0:T(8,128)(2,1)S(1)}, u32[]{:S(2)}, u32[]{:S(2)}) collective-permute-start(bf16[3,32,512]{2,1,0:T(8,128)(2,1)S(1)} %get-tuple-element.56), channel_id=1, source_target_pairs={{0,24},{8,0},{16,8},{24,16},{1,25},{9,1},{17,9},{25,17},{2,26},{10... | collective-permute-start | bytes 294920 | tf_op jit(solution)/shard_map/ppermute | solution.py:15
  136.6 10.3 %collective-permute-start.24 = (bf16[3,4,32,512]{3,2,1,0:T(8,128)(2,1)S(1)}, bf16[3,4,32,512]{3,2,1,0:T(8,128)(2,1)S(1)}, u32[]{:S(2)}, u32[]{:S(2)}) collective-permute-start(bf16[3,4,32,512]{3,2,1,0:T(8,128)(2,1)S(1)} %get-tuple-element.45), channel_id=1, source_target_pairs={{0,2},{2,4},{4,6},{6,0},{1,3},{3,5},{5,7},{7,1},{8,10},{10,12},{12... | collective-permute-start | bytes 1179656 | tf_op jit(solution)/shard_map/ppermute | solution.py:15
  136.8 14.3 %collective-permute-start.25 = (bf16[3,4,32,512]{3,2,1,0:T(8,128)(2,1)S(1)}, bf16[3,4,32,512]{3,2,1,0:T(8,128)(2,1)S(1)}, u32[]{:S(2)}, u32[]{:S(2)}) collective-permute-start(bf16[3,4,32,512]{3,2,1,0:T(8,128)(2,1)S(1)} %get-tuple-element.45), channel_id=1, source_target_pairs={{0,4},{2,6},{4,0},{6,2},{1,5},{3,7},{5,1},{7,3},{8,12},{10,14},{12... | collective-permute-start | bytes 1179656 | tf_op jit(solution)/shard_map/ppermute | solution.py:15
  140.2 11.3 %collective-permute-start.26 = (bf16[3,4,32,512]{3,2,1,0:T(8,128)(2,1)S(1)}, bf16[3,4,32,512]{3,2,1,0:T(8,128)(2,1)S(1)}, u32[]{:S(2)}, u32[]{:S(2)}) collective-permute-start(bf16[3,4,32,512]{3,2,1,0:T(8,128)(2,1)S(1)} %get-tuple-element.45), channel_id=1, source_target_pairs={{0,6},{2,0},{4,2},{6,4},{1,7},{3,1},{5,3},{7,5},{8,14},{10,8},{12,... | collective-permute-start | bytes 1179656 | tf_op jit(solution)/shard_map/ppermute | solution.py:15
  153.2 1.9 copy-start.2
  160.1 3.0 %copy-start.13 = (bf16[512,512]{1,0:T(8,128)(2,1)S(1)}, bf16[512,512]{1,0:T(8,128)(2,1)}, u32[]{:S(2)}) copy-start(bf16[512,512]{1,0:T(8,128)(2,1)} %copy-done.12) | copy-start | bytes 1572868
  162.8 8.7 %collective-permute-start.27 = (bf16[512,512]{1,0:T(8,128)(2,1)S(1)}, bf16[512,512]{1,0:T(8,128)(2,1)S(1)}, u32[]{:S(2)}, u32[]{:S(2)}) collective-permute-start(bf16[512,512]{1,0:T(8,128)(2,1)S(1)} %slice.156), channel_id=1, source_target_pairs={{0,1},{1,0},{2,3},{3,2},{4,5},{5,4},{6,7},{7,6},{8,9},{9,8},{10,11... | collective-permute-start | bytes 1572872 | tf_op jit(solution)/shard_map/ppermute | solution.py:15
  164.4 1.6 copy-start.7
  165.6 27.7 %collective-permute-start.30 = (bf16[512,1024]{0,1:T(8,128)(2,1)}, bf16[512,1024]{0,1:T(8,128)(2,1)}, u32[]{:S(2)}, u32[]{:S(2)}) collective-permute-start(bf16[512,1024]{0,1:T(8,128)(2,1)} %get-tuple-element.23), channel_id=1, source_target_pairs={{0,1},{1,0},{2,3},{3,2},{4,5},{5,4},{6,7},{7,6},{8,9},{9,8},{10,11... | collective-permute-start | bytes 3145736 | tf_op jit(solution)/shard_map/ppermute | solution.py:15
  168.8 26.7 %collective-permute-start.29 = (bf16[512,1024]{0,1:T(8,128)(2,1)}, bf16[512,1024]{0,1:T(8,128)(2,1)}, u32[]{:S(2)}, u32[]{:S(2)}) collective-permute-start(bf16[512,1024]{0,1:T(8,128)(2,1)} %get-tuple-element.21), channel_id=1, source_target_pairs={{0,1},{1,0},{2,3},{3,2},{4,5},{5,4},{6,7},{7,6},{8,9},{9,8},{10,11... | collective-permute-start | bytes 3145736 | tf_op jit(solution)/shard_map/ppermute | solution.py:15
  172.5 14.6 %all-to-all-start.2 = ((bf16[4,128,512]{2,1,0:T(8,128)(2,1)}), bf16[4,128,512]{2,1,0:T(8,128)(2,1)}, u32[]{:S(2)}, u32[]{:S(2)}) async-start(bf16[4,128,512]{2,1,0:T(8,128)(2,1)} %bitcast.170), calls=%async_computation.2 | async-start | bytes 1048576 | tf_op jit(solution)/shard_map/all_to_all | solution.py:66
  176.7 11.6 %copy-start.8 = (pred[128,512]{1,0:T(8,128)(4,1)S(1)}, pred[128,512]{1,0:T(8,128)(4,1)}, u32[]{:S(2)}) copy-start(pred[128,512]{1,0:T(8,128)(4,1)} %get-tuple-element.13) | copy-start | bytes 196612
  179.7 18.1 %collective-permute-start.28 = (bf16[512,1024]{0,1:T(8,128)(2,1)}, bf16[512,1024]{0,1:T(8,128)(2,1)}, u32[]{:S(2)}, u32[]{:S(2)}) collective-permute-start(bf16[512,1024]{0,1:T(8,128)(2,1)} %get-tuple-element.19), channel_id=1, source_target_pairs={{0,1},{1,0},{2,3},{3,2},{4,5},{5,4},{6,7},{7,6},{8,9},{9,8},{10,11... | collective-permute-start | bytes 3145736 | tf_op jit(solution)/shard_map/ppermute | solution.py:15
  189.1 22.8 %all-to-all-start.3 = ((bf16[4,128,512]{2,1,0:T(8,128)(2,1)}), bf16[4,128,512]{2,1,0:T(8,128)(2,1)}, u32[]{:S(2)}, u32[]{:S(2)}) async-start(bf16[4,128,512]{2,1,0:T(8,128)(2,1)} %broadcast_in_dim.20), calls=%async_computation.3 | async-start | bytes 1048576 | tf_op jit(solution)/shard_map/all_to_all | solution.py:70
  193.3 2.2 %copy-start.4 = (bf16[1,512,1024]{1,2,0:T(8,128)(2,1)S(1)}, bf16[1,512,1024]{1,2,0:T(8,128)(2,1)}, u32[]{:S(2)}) copy-start(bf16[1,512,1024]{1,2,0:T(8,128)(2,1)} %get-tuple-element.20) | copy-start | bytes 3145732
  195.6 2.3 %copy-start.5 = (bf16[1,512,1024]{1,2,0:T(8,128)(2,1)S(1)}, bf16[1,512,1024]{1,2,0:T(8,128)(2,1)}, u32[]{:S(2)}) copy-start(bf16[1,512,1024]{1,2,0:T(8,128)(2,1)} %get-tuple-element.18) | copy-start | bytes 3145732

commit v2 on v1

v2 whole, which is shorter than its diff:
```python
import functools
import math

import jax
import jax.numpy as jnp
from jax import lax
from jax.experimental import pallas as pl
from jax.experimental.pallas import tpu as pltpu
from jax.sharding import Mesh, PartitionSpec as P

BF = jnp.bfloat16
F32 = jnp.float32
VMEM_LIMIT = 16 * 1024 * 1024
SIDE = 4


def dot(a, b, ca, cb):
    return lax.dot_general(a, b, (((ca,), (cb,)), ((), ())), preferred_element_type=F32)


def call(body, name, grid, ins, outs, shapes, args, flops, moved, scratch=(), core=None):
    spec = dict(grid=grid, in_specs=ins, out_specs=outs, scratch_shapes=list(scratch))
    if core is not None:
        spec = dict(grid_spec=pltpu.PrefetchScalarGridSpec(num_scalar_prefetch=1, **spec))
        args = (core,) + tuple(args)
    return pl.pallas_call(
        body,
        out_shape=shapes,
        compiler_params=pltpu.CompilerParams(
            dimension_semantics=("arbitrary",) * len(grid), vmem_limit_bytes=VMEM_LIMIT
        ),
        cost_estimate=pl.CostEstimate(
            flops=int(flops), bytes_accessed=int(moved), transcendentals=0
        ),
        name=name,
        **spec,
    )(*args)


def pre_kernel(x_ref, w_ref, a_ref, b_ref, acc):
    k = pl.program_id(0)
    part = jnp.dot(x_ref[...], w_ref[...], preferred_element_type=F32)

    @pl.when(k == 0)
    def _():
        acc[...] = part

    @pl.when(k > 0)
    def _():
        acc[...] += part

    @pl.when(k == pl.num_programs(0) - 1)
    def _():
        n = a_ref.shape[0]
        a_ref[...] = acc[:n, :].astype(BF)
        b_ref[...] = acc[n:, :].astype(BF)


def pre_call(x, w):
    rows, depth = x.shape
    lats = w.shape[1]
    step = 512
    part = pl.BlockSpec((rows // 2, lats), lambda k: (0, 0))
    return call(
        pre_kernel,
        "pre",
        (depth // step,),
        [
            pl.BlockSpec((rows, step), lambda k: (0, k)),
            pl.BlockSpec((step, lats), lambda k: (k, 0)),
        ],
        [part, part],
        [jax.ShapeDtypeStruct((rows // 2, lats), BF)] * 2,
        (x, w),
        2 * rows * depth * lats,
        2 * (rows + lats) * depth,
        [pltpu.VMEM((rows, lats), F32)],
    )


def pick_kernel(p_ref, dec_ref, after_ref, out_ref):
    out_ref[...] = dec_ref[...]


def pick_call(place, dec, after):
    targets, lats, wide = dec.shape
    half = wide // 2
    return call(
        pick_kernel,
        "pick_half",
        (targets,),
        [
            pl.BlockSpec((1, lats, half), lambda t, p: (t, 0, 1 - p[2])),
            pl.BlockSpec(memory_space=pl.ANY),
        ],
        pl.BlockSpec((1, lats, half), lambda t, p: (t, 0, 0)),
        jax.ShapeDtypeStruct((targets, lats, half), BF),
        (dec, after),
        0,
        4 * targets * lats * half,
        core=place,
    )


def rebuild_a_kernel(p_ref, lat_ref, sib_ref, dec_ref, got_ref, out_ref):
    total = jnp.dot(lat_ref[...], dec_ref[0], preferred_element_type=F32)
    total += jnp.dot(sib_ref[...], got_ref[0], preferred_element_type=F32)
    out_ref[:, 0] = total.astype(BF).reshape(SIDE, SIDE, out_ref.shape[3], out_ref.shape[4])


def rebuild_b_kernel(p_ref, lat_ref, sib_ref, dec_ref, got_ref, *refs):
    outs, held = refs[:SIDE], refs[SIDE]
    total = jnp.dot(lat_ref[...], dec_ref[0], preferred_element_type=F32)
    total += jnp.dot(sib_ref[...], got_ref[0], preferred_element_type=F32)
    held[...] = total.astype(BF).reshape(held.shape)
    for k in range(SIDE):
        y = lax.rem(p_ref[1] + k, SIDE)
        for x in range(SIDE):
            outs[k][x, 0] = held[x * SIDE + y]


def rebuild_call(second, place, lat, sib, dec, got):
    rows, lats = lat.shape
    targets, _, half = got.shape
    q = half // 2
    piece = rows // (SIDE * SIDE)
    whole = pl.BlockSpec((rows, lats), lambda t, p: (0, 0))
    if second:
        outs = [pl.BlockSpec((SIDE, 1, piece, q), lambda t, p: (0, t, 0, 0))] * SIDE
        shapes = [jax.ShapeDtypeStruct((SIDE, targets, piece, q), BF)] * SIDE
        scratch = [pltpu.VMEM((SIDE * SIDE, piece, q), BF)]
    else:
        outs = pl.BlockSpec((SIDE, 1, SIDE, piece, q), lambda t, p: (0, t, 0, 0, 0))
        shapes = jax.ShapeDtypeStruct((SIDE, targets, SIDE, piece, q), BF)
        scratch = []
    return call(
        rebuild_b_kernel if second else rebuild_a_kernel,
        "rebuild_b" if second else "rebuild_a",
        (targets,),
        [
            whole,
            whole,
            pl.BlockSpec((1, lats, q), lambda t, p: (t, 0, 2 * p[2] + second)),
            pl.BlockSpec((1, lats, q), lambda t, p: (t, 0, second)),
        ],
        outs,
        shapes,
        (lat, sib, dec, got),
        4 * rows * lats * q * targets,
        6e6,
        scratch,
        core=place,
    )


def sum_a_kernel(parts_ref, out_ref):
    total = parts_ref[0, 0].astype(F32)
    for p in range(1, SIDE):
        total += parts_ref[p, 0].astype(F32)
    out_ref[:, 0] = total.astype(BF)


def sum_a_call(parts):
    _, targets, _, piece, q = parts.shape
    return call(
        sum_a_kernel,
        "sum_a",
        (targets,),
        [pl.BlockSpec((SIDE, 1, SIDE, piece, q), lambda t: (0, t, 0, 0, 0))],
        pl.BlockSpec((SIDE, 1, piece, q), lambda t: (0, t, 0, 0)),
        jax.ShapeDtypeStruct((SIDE, targets, piece, q), BF),
        (parts,),
        parts.size,
        2.5 * parts.size,
    )


def sum_b_kernel(p_ref, *refs):
    parts, outs, held = refs[:SIDE], refs[SIDE : 2 * SIDE], refs[2 * SIDE]
    total = parts[0][:, 0].astype(F32)
    for part in parts[1:]:
        total += part[:, 0].astype(F32)
    held[...] = total.astype(BF)
    for k in range(SIDE):
        outs[k][0] = held[lax.rem(p_ref[0] + k, SIDE)]


def sum_b_call(place, parts):
    _, targets, piece, q = parts[0].shape
    return call(
        sum_b_kernel,
        "sum_b",
        (targets,),
        [pl.BlockSpec((SIDE, 1, piece, q), lambda t, p: (0, t, 0, 0))] * SIDE,
        [pl.BlockSpec((1, piece, q), lambda t, p: (t, 0, 0))] * SIDE,
        [jax.ShapeDtypeStruct((targets, piece, q), BF)] * SIDE,
        tuple(parts),
        4 * parts[0].size,
        10 * parts[0].size,
        [pltpu.VMEM((SIDE, piece, q), BF)],
        core=place,
    )


def error_kernel(scale, target_ref, a_ref, *refs):
    parts, (a_out, b_out) = refs[:SIDE], refs[SIDE:]
    q = b_out.shape[2]
    total = a_ref[0, 0].astype(F32)
    for p in range(1, SIDE):
        total += a_ref[p, 0].astype(F32)
    err = ((total - target_ref[0, :, :q].astype(F32)) * scale).astype(BF)
    for p in range(SIDE):
        a_out[p, 0] = err
    total = parts[0][0].astype(F32)
    for part in parts[1:]:
        total += part[0].astype(F32)
    b_out[0] = ((total - target_ref[0, :, q:].astype(F32)) * scale).astype(BF)


def error_call(scale, target, a, parts):
    _, targets, piece, q = a.shape
    four = pl.BlockSpec((SIDE, 1, piece, q), lambda t: (0, t, 0, 0))
    one = pl.BlockSpec((1, piece, q), lambda t: (t, 0, 0))
    return call(
        functools.partial(error_kernel, scale),
        "error",
        (targets,),
        [pl.BlockSpec((1, piece, 2 * q), lambda t: (t, 0, 0)), four] + [one] * SIDE,
        [four, one],
        [
            jax.ShapeDtypeStruct((SIDE, targets, piece, q), BF),
            jax.ShapeDtypeStruct((targets, piece, q), BF),
        ],
        (target, a, *parts),
        8 * targets * piece * q,
        2e6,
    )


def join_kernel(p_ref, *refs):
    parts, out_ref = refs[:SIDE], refs[SIDE]
    for k in range(SIDE):
        x = lax.rem(p_ref[0] + SIDE - k, SIDE)
        for y in range(SIDE):
            out_ref[y, x, 0] = parts[k][0]


def join_call(place, parts):
    targets, piece, q = parts[0].shape
    return call(
        join_kernel,
        "join",
        (targets,),
        [pl.BlockSpec((1, piece, q), lambda t, p: (t, 0, 0))] * SIDE,
        pl.BlockSpec((SIDE, SIDE, 1, piece, q), lambda t, p: (0, 0, t, 0, 0)),
        jax.ShapeDtypeStruct((SIDE, SIDE, targets, piece, q), BF),
        tuple(parts),
        0,
        2e6,
        core=place,
    )


def back_dot(err, dec_ref, out_ref, acc):
    t = pl.program_id(0)
    part = dot(err, dec_ref[0], 1, 1)

    @pl.when(t == 0)
    def _():
        acc[...] = part

    @pl.when(t > 0)
    def _():
        acc[...] += part

    @pl.when(t == pl.num_programs(0) - 1)
    def _():
        out_ref[...] = acc[...].astype(out_ref.dtype)


def back_sib_kernel(p_ref, dec_ref, after_ref, b_ref, *refs):
    parts, (err_ref, out_ref, acc) = refs[:SIDE], refs[SIDE:]
    piece, q = b_ref.shape[3:]
    strip = SIDE * piece
    for k in range(SIDE):
        x = lax.rem(p_ref[0] + SIDE - k, SIDE)
        at = pl.ds(pl.multiple_of(x * strip, strip), strip)
        err_ref[0, at, :q] = parts[k][:, 0].reshape(strip, q)
    for x in range(SIDE):
        for y in range(SIDE):
            at = (x * SIDE + y) * piece
            err_ref[0, at : at + piece, q:] = b_ref[y, x, 0]
    back_dot(err_ref[0], dec_ref, out_ref, acc)


def back_sib_call(place, a_parts, b, dec, after):
    _, _, targets, piece, q = b.shape
    lats, half = dec.shape[1:]
    rows = SIDE * SIDE * piece
    return call(
        back_sib_kernel,
        "back_sib",
        (targets,),
        [
            pl.BlockSpec((1, lats, half), lambda t, p: (t, 0, 0)),
            pl.BlockSpec(memory_space=pl.ANY),
            pl.BlockSpec((SIDE, SIDE, 1, piece, q), lambda t, p: (0, 0, t, 0, 0)),
        ]
        + [pl.BlockSpec((SIDE, 1, piece, q), lambda t, p: (0, t, 0, 0))] * SIDE,
        [
            pl.BlockSpec((1, rows, half), lambda t, p: (t, 0, 0)),
            pl.BlockSpec((rows, lats), lambda t, p: (0, 0)),
        ],
        [
            jax.ShapeDtypeStruct((targets, rows, half), BF),
            jax.ShapeDtypeStruct((rows, lats), BF),
        ],
        (dec, after, b, *a_parts),
        2 * rows * lats * half * targets,
        10e6,
        [pltpu.VMEM((rows, lats), F32)],
        core=place,
    )


def back_own_kernel(p_ref, err_ref, dec_ref, out_ref, acc):
    back_dot(err_ref[0], dec_ref, out_ref, acc)


def back_own_call(place, err, dec):
    targets, rows, half = err.shape
    lats = dec.shape[1]
    return call(
        back_own_kernel,
        "back_own",
        (targets,),
        [
            pl.BlockSpec((1, rows, half), lambda t, p: (t, 0, 0)),
            pl.BlockSpec((1, lats, half), lambda t, p: (t, 0, p[2])),
        ],
        pl.BlockSpec((rows, lats), lambda t, p: (0, 0)),
        jax.ShapeDtypeStruct((rows, lats), F32),
        (err, dec),
        2 * rows * lats * half * targets,
        7e6,
        [pltpu.VMEM((rows, lats), F32)],
        core=place,
    )


def turn_kernel(x_ref, lat_ref, sib_ref, after_ref, x_out, lat_out, sib_out):
    x_out[...] = x_ref[...].T

    @pl.when(pl.program_id(0) == 0)
    def _():
        lat_out[...] = lat_ref[...].T
        sib_out[...] = sib_ref[...].T


def turn_call(x, lat, sib, after):
    rows, depth = x.shape
    lats = lat.shape[1]
    step = 512
    whole = pl.BlockSpec((rows, lats), lambda i: (0, 0))
    turned = pl.BlockSpec((lats, rows), lambda i: (0, 0))
    return call(
        turn_kernel,
        "turn",
        (depth // step,),
        [
            pl.BlockSpec((rows, step), lambda i: (0, i)),
            whole,
            whole,
            pl.BlockSpec(memory_space=pl.ANY),
        ],
        [pl.BlockSpec((step, rows), lambda i: (i, 0)), turned, turned],
        [jax.ShapeDtypeStruct((depth, rows), BF)] + [jax.ShapeDtypeStruct((lats, rows), BF)] * 2,
        (x, lat, sib, after),
        0,
        6e6,
    )


def dec_sib_kernel(lat_ref, err_ref, after_ref, out_ref):
    out_ref[0] = dot(lat_ref[...], err_ref[0], 1, 0).astype(BF)


def dec_sib_call(lat, err, after):
    targets, rows, half = err.shape
    lats = lat.shape[0]
    return call(
        dec_sib_kernel,
        "dec_sib",
        (targets,),
        [
            pl.BlockSpec((lats, rows), lambda t: (0, 0)),
            pl.BlockSpec((1, rows, half), lambda t: (t, 0, 0)),
            pl.BlockSpec(memory_space=pl.ANY),
        ],
        pl.BlockSpec((1, lats, half), lambda t: (t, 0, 0)),
        jax.ShapeDtypeStruct((targets, lats, half), BF),
        (lat, err, after),
        2 * rows * lats * half * targets,
        7e6,
    )


def dec_kernel(p_ref, lat_ref, err_ref, got_ref, out_ref):
    j = pl.program_id(1)

    @pl.when(j == 0)
    def _():
        out_ref[0] = dot(lat_ref[...], err_ref[0], 1, 0).astype(BF)

    @pl.when(j == 1)
    def _():
        out_ref[...] = got_ref[...]


def dec_call(place, lat, err, got):
    targets, rows, half = err.shape
    lats = lat.shape[0]
    return call(
        dec_kernel,
        "dec_grad",
        (targets, 2),
        [
            pl.BlockSpec((lats, rows), lambda t, j, p: (0, 0)),
            pl.BlockSpec((1, rows, half), lambda t, j, p: (t, 0, 0)),
            pl.BlockSpec((1, lats, half), lambda t, j, p: (t, 0, 0)),
        ],
        pl.BlockSpec((1, lats, half), lambda t, j, p: (t, 0, (j + p[2]) % 2)),
        jax.ShapeDtypeStruct((targets, lats, 2 * half), BF),
        (lat, err, got),
        2 * rows * lats * half * targets,
        13e6,
        core=place,
    )


def enc_kernel(x_ref, active_ref, after_ref, *refs):
    parts, (enc_ref, bias_ref, grad) = refs[:4], refs[4:]

    @pl.when(pl.program_id(0) == 0)
    def _():
        n = parts[0].shape[0]
        sums = jnp.zeros(bias_ref.shape, F32)
        for i in range(2):
            total = parts[2 * i][...].astype(F32) + parts[2 * i + 1][...].astype(F32)
            on = active_ref[i * n : (i + 1) * n, :] > 0
            kept = jnp.where(on, total, 0.0).astype(BF)
            grad[i * n : (i + 1) * n, :] = kept
            sums += jnp.sum(kept.astype(F32), axis=0, keepdims=True)
        bias_ref[...] = sums

    enc_ref[...] = dot(x_ref[...], grad[...], 1, 0).astype(BF)


def enc_call(x, active, after, parts):
    depth, rows = x.shape
    lats = active.shape[1]
    step = 512
    part = pl.BlockSpec((rows // 2, lats), lambda i: (0, 0))
    return call(
        enc_kernel,
        "enc_grad",
        (depth // step,),
        [
            pl.BlockSpec((step, rows), lambda i: (i, 0)),
            pl.BlockSpec((rows, lats), lambda i: (0, 0)),
            pl.BlockSpec(memory_space=pl.ANY),
            part,
            part,
            part,
            part,
        ],
        [
            pl.BlockSpec((step, lats), lambda i: (i, 0)),
            pl.BlockSpec((1, lats), lambda i: (0, 0)),
        ],
        [jax.ShapeDtypeStruct((depth, lats), BF), jax.ShapeDtypeStruct((1, lats), F32)],
        (x, active, after, *parts),
        2 * rows * depth * lats,
        7e6,
        [pltpu.VMEM((rows, lats), BF)],
    )


def swap(value):
    return lax.ppermute(value, "c", [(0, 1), (1, 0)])


EVEN = [(0, 1), (1, 0), (2, 3), (3, 2)]
ODD = [(1, 2), (2, 1), (3, 0), (0, 3)]


def z_pairs(a, b):
    a_got = lax.ppermute(a, "z", EVEN)
    b_got = lax.ppermute(b, "z", ODD)
    a = (a.astype(F32) + a_got.astype(F32)).astype(BF)
    b = (b.astype(F32) + b_got.astype(F32)).astype(BF)
    return a, lax.ppermute(a, "z", ODD), b, lax.ppermute(b, "z", EVEN)


def shift(value, axis, step):
    size = lax.axis_size(axis)
    return lax.ppermute(value, axis, [(i, (i + step) % size) for i in range(size)])


def per_device(mlp_inputs, enc_weight, enc_bias, active, dec_weight, target):
    rows = mlp_inputs.shape[0]
    core = lax.axis_index("c")
    place = jnp.stack([lax.axis_index(a) for a in "xyc"]).astype(jnp.int32)
    half = dec_weight.shape[2] // 2
    scale = 1.0 / math.sqrt(rows)
    mid = rows // 2

    pre_a, pre_b = pre_call(mlp_inputs, enc_weight)
    dec_got = swap(pick_call(place, dec_weight, pre_a))
    tgt_own = lax.dynamic_slice_in_dim(target, core * half, half, 2)
    tgt_got = swap(lax.dynamic_slice_in_dim(target, (1 - core) * half, half, 2))
    tgt = jnp.where(
        core == 0,
        jnp.concatenate([tgt_own, tgt_got], axis=1),
        jnp.concatenate([tgt_got, tgt_own], axis=1),
    )

    a, a_got, b, b_got = z_pairs(pre_a, pre_b)
    pre = jnp.concatenate(
        [a.astype(F32) + a_got.astype(F32), b.astype(F32) + b_got.astype(F32)], axis=0
    )
    lat = jnp.where(active > 0, pre + enc_bias, 0.0).astype(BF)
    lat_sib = swap(lat)

    far = (2, 1, 3)
    a_sum = rebuild_call(0, place, lat, lat_sib, dec_weight, dec_got)
    a_sum = lax.all_to_all(a_sum, "x", 0, 0)
    b_sum = rebuild_call(1, place, lat, lat_sib, dec_weight, dec_got)
    b_sum = [b_sum[0]] + [shift(b_sum[k], "y", k) for k in far]
    a_sum = lax.all_to_all(sum_a_call(a_sum), "y", 0, 0)
    b_sum = sum_b_call(place, b_sum)
    b_sum = [b_sum[0]] + [shift(b_sum[k], "x", k) for k in far]
    a_err, b_err = error_call(scale, tgt, a_sum, b_sum)
    x_turned, lat_turned, sib_turned = turn_call(mlp_inputs, lat, lat_sib, b_err)
    a_err = lax.all_to_all(a_err, "y", 0, 0)
    b_err = join_call(place, [b_err] + [shift(b_err, "x", k) for k in (1, 2, 3)])
    b_err = lax.all_to_all(b_err, "y", 0, 0)
    a_err = [a_err] + [shift(a_err, "x", k) for k in (1, 2, 3)]

    err, grad_got = back_sib_call(place, a_err, b_err, dec_got, x_turned)
    grad_got = swap(grad_got)
    grad_own = back_own_call(place, err, dec_weight)
    grad = (grad_own + grad_got.astype(F32)).astype(BF)
    dec_part = swap(dec_sib_call(sib_turned, err, grad))
    sums = z_pairs(grad[:mid], grad[mid:])
    dec_grad = dec_call(place, lat_turned, err, dec_part)
    enc_grad, bias_grad = enc_call(x_turned, active, dec_grad, sums)
    return enc_grad, bias_grad.reshape(-1), dec_grad


def solution(mesh):
    grid = Mesh(mesh.devices.reshape(4, 4, 4, 2), ("z", "x", "y", "c"))
    lat = ("x", "y", "c")
    in_specs = (
        P(None, "z"),
        P("z", lat),
        P(lat),
        P(None, lat),
        P(None, lat, "z"),
        P(None, lat, "z"),
    )
    out_specs = (P("z", lat), P(lat), P(None, lat, "z"))
    return jax.shard_map(
        per_device, mesh=grid, in_specs=in_specs, out_specs=out_specs, check_vma=False
    )
```

time: 223 us -> 171 us (0.77)
  Pallas kernels: 0 us -> 38.6 us
  matrix products: 26.5 us -> 0 us
  other arithmetic: 24.1 us -> 0.97 us
  waiting for transfers between devices: 66.3 us -> 46.8 us
  blocking collectives: 11.7 us -> 0 us
  starting transfers between devices: 57.7 us -> 50.7 us
  local copies, waits for them, and re-layouts: 33.8 us -> 31.4 us
    pallas_call x0 -> x14, Pallas kernels: none -> 38.6 us  [call(): pl.pallas_call(body, out_shape=shapes, compiler_params=pltpu.CompilerPara...]
    ppermute x31 -> x12, waiting for transfers between devices: 49.3 us -> 14.5 us  [shift(): lax.ppermute(value, axis, [(i, (i + step) % size) for i in range(size)])]
    dot_general x11 -> x0, matrix products: 26.5 us -> none  [the longest x3 7.99 us: per_device(): jnp.dot(latents, dec[t], preferred_element_type=F32).astype(BF)]
    ppermute x0 -> x13, waiting for transfers between devices: none -> 26.1 us  [the longest x2 14.3 us: z_pairs(): b_got = lax.ppermute(b, 'z', ODD)]
    ppermute x31 -> x12, starting transfers between devices: 44 us -> 23 us  [shift(): lax.ppermute(value, axis, [(i, (i + step) % size) for i in range(size)])]
    unnamed x30 -> x74, local copies, waits for them, and re-layouts: 15.6 us -> 31.4 us
    all_to_all x1 -> x0, blocking collectives: 11.7 us -> none  [z_gather(): lax.all_to_all(jnp.broadcast_to(value[None], (zs,) + value.shape), 'z', 0...]
    all_to_all x3 -> x4, waiting for transfers between devices: 17 us -> 6.2 us  [the longest x1 6.2 us: per_device(): a_sum = lax.all_to_all(a_sum, 'x', 0, 0)]
  transfers between devices with their start and end apart: 34 -> 29, of which waited for: 16 -> 18; matrix products, arithmetic and copies ran while one was open for 20% -> 0% of each run, Pallas kernels for 0% -> 12%
where the time goes in v2:
time: 171 us; the launch traced here: 170 us
  starting transfers between devices  50.7 us (30%)
  waiting for transfers between devices  46.8 us (27%)
  Pallas kernels  38.6 us (23%)
  local copies, waits for them, and re-layouts  31.4 us (18%)
    pallas_call x14, Pallas kernels, call(): pl.pallas_call(body, out_shape=shapes, compiler_params=pltpu.CompilerPara...  38.6 us
    unnamed x74, local copies, waits for them, and re-layouts  31.4 us
    ppermute x12, starting transfers between devices, shift(): lax.ppermute(value, axis, [(i, (i + step) % size) for i in range(size)])  23 us
    ppermute x12, waiting for transfers between devices, shift(): lax.ppermute(value, axis, [(i, (i + step) % size) for i in range(size)])  14.5 us
    ppermute x2, waiting for transfers between devices, z_pairs(): b_got = lax.ppermute(b, 'z', ODD)  14.3 us
    ppermute x4, waiting for transfers between devices, z_pairs(): return (a, lax.ppermute(a, 'z', ODD), b, lax.ppermute(b, 'z', EVEN))  8.08 us
    ppermute x2, starting transfers between devices, z_pairs(): b_got = lax.ppermute(b, 'z', ODD)  6.27 us
    all_to_all x1, waiting for transfers between devices, per_device(): a_sum = lax.all_to_all(a_sum, 'x', 0, 0)  6.2 us
  transfers between devices with their start and end apart: 29, of which 18 were waited for; matrix products, arithmetic and copies ran while one was open for 0% of the time, Pallas kernels for 12%

profile of v2, /device:TPU:0, one launch (start us, length us, event | category | flops | bytes accessed | tf_op | source)
XLA Modules:
  0.0 169.6 jit_solution(7182385454598311841)
XLA Ops:
  0.6 1.6 copy-done.6
  2.2 1.6 copy-done.20
  3.8 2.4 %pre.1 = (bf16[256,512]{1,0:T(8,128)(2,1)S(1)}, bf16[256,512]{1,0:T(8,128)(2,1)S(1)}) custom-call(bf16[512,2048]{1,0:T(8,128)(2,1)S(1)} %copy-done.6, bf16[2048,512]{1,0:T(8,128)(2,1)S(1)} %copy-done.20), custom_call_target="tpu_custom_call" | custom-call | flops 1073741824 | bytes 4194304 | tf_op jit(solution)/shard_map/pre/pallas_call | solution.py:26
  6.3 2.8 %copy-done = bf16[3,512,2048]{2,1,0:T(8,128)(2,1)S(1)} copy-done((bf16[3,512,2048]{2,1,0:T(8,128)(2,1)S(1)}, bf16[3,512,2048]{2,1,0:T(8,128)(2,1)}, u32[]{:S(2)}) %copy-start) | copy-done | bytes 6291480
  10.2 4.2 %collective-permute-start.2 = (bf16[256,512]{1,0:T(8,128)(2,1)S(1)}, bf16[256,512]{1,0:T(8,128)(2,1)S(1)}, u32[]{:S(2)}, u32[]{:S(2)}) collective-permute-start(bf16[256,512]{1,0:T(8,128)(2,1)S(1)} %get-tuple-element.23), channel_id=1, source_target_pairs={{32,64},{64,32},{96,0},{0,96},{33,65},{65,33},{97,1},{1,97},{34,66... | collective-permute-start | bytes 786440 | tf_op jit(solution)/shard_map/ppermute | solution.py:499
  14.4 6.9 %collective-permute-done.2 = bf16[256,512]{1,0:T(8,128)(2,1)S(1)} collective-permute-done((bf16[256,512]{1,0:T(8,128)(2,1)S(1)}, bf16[256,512]{1,0:T(8,128)(2,1)S(1)}, u32[]{:S(2)}, u32[]{:S(2)}) %collective-permute-start.2) | collective-permute-done | bytes 262176 | tf_op jit(solution)/shard_map/ppermute | solution.py:499
  21.5 1.3 collective-permute-done
  22.9 1.7 %collective-permute-start.1 = (bf16[256,512]{1,0:T(8,128)(2,1)S(1)}, bf16[256,512]{1,0:T(8,128)(2,1)S(1)}, u32[]{:S(2)}, u32[]{:S(2)}) collective-permute-start(bf16[256,512]{1,0:T(8,128)(2,1)S(1)} %add_convert_fusion.4), channel_id=1, source_target_pairs={{32,64},{64,32},{96,0},{0,96},{33,65},{65,33},{97,1},{1,97},{34,66... | collective-permute-start | bytes 786440 | tf_op jit(solution)/shard_map/ppermute | solution.py:502
  24.6 4.9 %collective-permute-done.3 = bf16[256,512]{1,0:T(8,128)(2,1)S(1)} collective-permute-done((bf16[256,512]{1,0:T(8,128)(2,1)S(1)}, bf16[256,512]{1,0:T(8,128)(2,1)S(1)}, u32[]{:S(2)}, u32[]{:S(2)}) %collective-permute-start.3) | collective-permute-done | bytes 262176 | tf_op jit(solution)/shard_map/ppermute | solution.py:502
  29.6 2.1 %collective-permute-done.1 = bf16[256,512]{1,0:T(8,128)(2,1)S(1)} collective-permute-done((bf16[256,512]{1,0:T(8,128)(2,1)S(1)}, bf16[256,512]{1,0:T(8,128)(2,1)S(1)}, u32[]{:S(2)}, u32[]{:S(2)}) %collective-permute-start.1) | collective-permute-done | bytes 262176 | tf_op jit(solution)/shard_map/ppermute | solution.py:502
  32.1 1.9 %collective-permute-done.4.sib_ref = bf16[512,512]{1,0:T(8,128)(2,1)S(1)} collective-permute-done((bf16[512,512]{1,0:T(8,128)(2,1)S(1)}, bf16[512,512]{1,0:T(8,128)(2,1)S(1)}, u32[]{:S(2)}, u32[]{:S(2)}) %collective-permute-start.4) | collective-permute-done | bytes 524320 | tf_op jit(solution)/shard_map/ppermute | solution.py:490
  34.0 3.0 %rebuild_a.1 = bf16[4,3,4,32,512]{4,3,2,1,0:T(8,128)(2,1)S(1)} custom-call(s32[3]{0:T(128)S(1)} %pad_add_fusion.p_ref, bf16[512,512]{1,0:T(8,128)(2,1)S(1)} %fusion.1.lat_ref, bf16[512,512]{1,0:T(8,128)(2,1)S(1)} %collective-permute-done.4.sib_ref, bf16[3,512,2048]{2,1,0:T(8,128)(2,1)S(1)} %copy-done.1, ...), custom_call_target="tpu_custom_call" | custom-call | flops 1610612736 | bytes 6000000 | tf_op jit(solution)/shard_map/rebuild_a/pallas_call | solution.py:26
  39.8 4.4 %all-to-all-start = ((bf16[4,3,4,32,512]{4,3,2,1,0:T(8,128)(2,1)}), bf16[4,3,4,32,512]{4,3,2,1,0:T(8,128)(2,1)}, u32[]{:S(2)}, u32[]{:S(2)}) async-start(bf16[4,3,4,32,512]{4,3,2,1,0:T(8,128)(2,1)} %copy-done.14), calls=%async_computation | async-start | bytes 3145728 | tf_op jit(solution)/shard_map/all_to_all | solution.py:537
  44.2 2.8 %copy-done.2 = bf16[3,512,2048]{2,1,0:T(8,128)(2,1)S(1)} copy-done((bf16[3,512,2048]{2,1,0:T(8,128)(2,1)S(1)}, bf16[3,512,2048]{2,1,0:T(8,128)(2,1)}, u32[]{:S(2)}) %copy-start.2) | copy-done | bytes 6291480
  49.1 3.8 %rebuild_b.1 = (bf16[4,3,32,512]{3,2,1,0:T(8,128)(2,1)S(1)}, bf16[4,3,32,512]{3,2,1,0:T(8,128)(2,1)}, bf16[4,3,32,512]{3,2,1,0:T(8,128)(2,1)}, bf16[4,3,32,512]{3,2,1,0:T(8,128)(2,1)}) custom-call(s32[3]{0:T(128)S(1)} %pad_add_fusion.p_ref, bf16[512,512]{1,0:T(8,128)(2,1)S(1)} %copy-done.12, bf16[512,512]{1,0:T(8,128)(2,1)S(1)} %copy-done.16, ...), custom_call_target="tpu_custom_call" | custom-call | flops 1610612736 | bytes 6000000 | tf_op jit(solution)/shard_map/rebuild_b/pallas_call | solution.py:26
  52.9 3.2 %collective-permute-start.7 = (bf16[4,3,32,512]{3,2,1,0:T(8,128)(2,1)}, bf16[4,3,32,512]{3,2,1,0:T(8,128)(2,1)S(1)}, u32[]{:S(2)}, u32[]{:S(2)}) collective-permute-start(bf16[4,3,32,512]{3,2,1,0:T(8,128)(2,1)} %get-tuple-element.25), channel_id=1, source_target_pairs={{0,4},{2,6},{4,0},{6,2},{1,5},{3,7},{5,1},{7,3},{8,12},{10,14},{12... | collective-permute-start | bytes 1179656 | tf_op jit(solution)/shard_map/ppermute | solution.py:507
  56.8 2.6 %collective-permute-start.9 = (bf16[4,3,32,512]{3,2,1,0:T(8,128)(2,1)}, bf16[4,3,32,512]{3,2,1,0:T(8,128)(2,1)S(1)}, u32[]{:S(2)}, u32[]{:S(2)}) collective-permute-start(bf16[4,3,32,512]{3,2,1,0:T(8,128)(2,1)} %get-tuple-element.27), channel_id=1, source_target_pairs={{0,6},{2,0},{4,2},{6,4},{1,7},{3,1},{5,3},{7,5},{8,14},{10,8},{12,... | collective-permute-start | bytes 1179656 | tf_op jit(solution)/shard_map/ppermute | solution.py:507
  59.4 6.2 %all-to-all-done.parts_ref = bf16[4,3,4,32,512]{4,3,2,1,0:T(8,128)(2,1)} async-done(((bf16[4,3,4,32,512]{4,3,2,1,0:T(8,128)(2,1)}), bf16[4,3,4,32,512]{4,3,2,1,0:T(8,128)(2,1)}, u32[]{:S(2)}, u32[]{:S(2)}) %all-to-all-start) | async-done | bytes 1572896 | tf_op jit(solution)/shard_map/all_to_all | solution.py:537
  65.5 3.0 %sum_a.1 = bf16[4,3,32,512]{3,2,1,0:T(8,128)(2,1)} custom-call(bf16[4,3,4,32,512]{4,3,2,1,0:T(8,128)(2,1)} %all-to-all-done.parts_ref), custom_call_target="tpu_custom_call" | custom-call | flops 786432 | bytes 1966080 | tf_op jit(solution)/shard_map/sum_a/pallas_call | solution.py:26
  68.6 4.5 %all-to-all-start.1 = ((bf16[4,3,32,512]{3,2,1,0:T(8,128)(2,1)}), bf16[4,3,32,512]{3,2,1,0:T(8,128)(2,1)S(1)}, u32[]{:S(2)}, u32[]{:S(2)}) async-start(bf16[4,3,32,512]{3,2,1,0:T(8,128)(2,1)} %sum_a.1), calls=%async_computation.1 | async-start | bytes 786432 | tf_op jit(solution)/shard_map/all_to_all | solution.py:540
  73.1 1.2 collective-permute-done.8.refs_2_
  75.6 4.4 %collective-permute-start.10 = (bf16[3,32,512]{2,1,0:T(8,128)(2,1)S(1)}, bf16[3,32,512]{2,1,0:T(8,128)(2,1)S(1)}, u32[]{:S(2)}, u32[]{:S(2)}) collective-permute-start(bf16[3,32,512]{2,1,0:T(8,128)(2,1)S(1)} %get-tuple-element.29), channel_id=1, source_target_pairs={{0,16},{8,24},{16,0},{24,8},{1,17},{9,25},{17,1},{25,9},{2,18},{10... | collective-permute-start | bytes 294920 | tf_op jit(solution)/shard_map/ppermute | solution.py:507
  80.6 2.7 %collective-permute-start.12 = (bf16[3,32,512]{2,1,0:T(8,128)(2,1)S(1)}, bf16[3,32,512]{2,1,0:T(8,128)(2,1)S(1)}, u32[]{:S(2)}, u32[]{:S(2)}) collective-permute-start(bf16[3,32,512]{2,1,0:T(8,128)(2,1)S(1)} %get-tuple-element.31), channel_id=1, source_target_pairs={{0,24},{8,0},{16,8},{24,16},{1,25},{9,1},{17,9},{25,17},{2,26},{10... | collective-permute-start | bytes 294920 | tf_op jit(solution)/shard_map/ppermute | solution.py:507
  83.7 2.2 %collective-permute-done.11.refs_2_ = bf16[3,32,512]{2,1,0:T(8,128)(2,1)S(1)} collective-permute-done((bf16[3,32,512]{2,1,0:T(8,128)(2,1)S(1)}, bf16[3,32,512]{2,1,0:T(8,128)(2,1)S(1)}, u32[]{:S(2)}, u32[]{:S(2)}) %collective-permute-start.11) | collective-permute-done | bytes 98336 | tf_op jit(solution)/shard_map/ppermute | solution.py:507
  85.9 1.5 error.1
  87.3 3.5 %all-to-all-start.3 = ((bf16[4,3,32,512]{3,2,1,0:T(8,128)(2,1)}), bf16[4,3,32,512]{3,2,1,0:T(8,128)(2,1)S(1)}, u32[]{:S(2)}, u32[]{:S(2)}) async-start(bf16[4,3,32,512]{3,2,1,0:T(8,128)(2,1)} %get-tuple-element.35), calls=%async_computation.3 | async-start | bytes 786432 | tf_op jit(solution)/shard_map/all_to_all | solution.py:545
  91.1 4.4 %collective-permute-start.14 = (bf16[3,32,512]{2,1,0:T(8,128)(2,1)S(1)}, bf16[3,32,512]{2,1,0:T(8,128)(2,1)S(1)}, u32[]{:S(2)}, u32[]{:S(2)}) collective-permute-start(bf16[3,32,512]{2,1,0:T(8,128)(2,1)S(1)} %get-tuple-element.32.after_ref.refs_0_), channel_id=1, source_target_pairs={{0,16},{8,24},{16,0},{24,8},{1,17},{9,25},{17,1},{25,9},{2,18},{10... | collective-permute-start | bytes 294920 | tf_op jit(solution)/shard_map/ppermute | solution.py:507
  95.6 1.4 collective-permute-done.13.refs_1_
  97.0 2.2 %collective-permute-done.14.refs_2_ = bf16[3,32,512]{2,1,0:T(8,128)(2,1)S(1)} collective-permute-done((bf16[3,32,512]{2,1,0:T(8,128)(2,1)S(1)}, bf16[3,32,512]{2,1,0:T(8,128)(2,1)S(1)}, u32[]{:S(2)}, u32[]{:S(2)}) %collective-permute-start.14) | collective-permute-done | bytes 98336 | tf_op jit(solution)/shard_map/ppermute | solution.py:507
  100.2 2.2 %join.1 = bf16[4,4,3,32,512]{4,3,2,1,0:T(8,128)(2,1)} custom-call(s32[3]{0:T(128)S(1)} %pad_add_fusion.p_ref, bf16[3,32,512]{2,1,0:T(8,128)(2,1)S(1)} %get-tuple-element.32.after_ref.refs_0_, bf16[3,32,512]{2,1,0:T(8,128)(2,1)S(1)} %collective-permute-done.13.refs_1_, bf16[3,32,512]{2,1,0:T(8,128)(2,1)S(1)} %collective-permute-done.14.refs_2_, ...), custom_call_target="tpu_custom_call" | custom-call | bytes 2000000 | tf_op jit(solution)/shard_map/join/pallas_call | solution.py:26
  102.4 4.7 %all-to-all-start.2 = ((bf16[4,4,3,32,512]{4,3,2,1,0:T(8,128)(2,1)}), bf16[4,4,3,32,512]{4,3,2,1,0:T(8,128)(2,1)}, u32[]{:S(2)}, u32[]{:S(2)}) async-start(bf16[4,4,3,32,512]{4,3,2,1,0:T(8,128)(2,1)} %join.1), calls=%async_computation.2 | async-start | bytes 3145728 | tf_op jit(solution)/shard_map/all_to_all | solution.py:547
  107.1 2.7 %collective-permute-start.17 = (bf16[4,3,32,512]{3,2,1,0:T(8,128)(2,1)S(1)}, bf16[4,3,32,512]{3,2,1,0:T(8,128)(2,1)S(1)}, u32[]{:S(2)}, u32[]{:S(2)}) collective-permute-start(bf16[4,3,32,512]{3,2,1,0:T(8,128)(2,1)S(1)} %all-to-all-done.3.refs_0_), channel_id=1, source_target_pairs={{0,16},{8,24},{16,0},{24,8},{1,17},{9,25},{17,1},{25,9},{2,18},{10... | collective-permute-start | bytes 1179656 | tf_op jit(solution)/shard_map/ppermute | solution.py:507
  109.8 1.5 collective-permute-start.18
  111.2 1.6 copy-done.7
  113.7 1.3 turn.1
  115.0 1.3 copy-done.8
  117.9 5.8 %collective-permute-done.16.refs_1_ = bf16[4,3,32,512]{3,2,1,0:T(8,128)(2,1)S(1)} collective-permute-done((bf16[4,3,32,512]{3,2,1,0:T(8,128)(2,1)S(1)}, bf16[4,3,32,512]{3,2,1,0:T(8,128)(2,1)S(1)}, u32[]{:S(2)}, u32[]{:S(2)}) %collective-permute-start.16) | collective-permute-done | bytes 393248 | tf_op jit(solution)/shard_map/ppermute | solution.py:507
  126.1 1.9 %copy-done.4 = bf16[3,512,1024]{2,1,0:T(8,128)(2,1)S(1)} copy-done((bf16[3,512,1024]{2,1,0:T(8,128)(2,1)S(1)}, bf16[3,512,1024]{2,1,0:T(8,128)(2,1)}, u32[]{:S(2)}) %copy-start.4) | copy-done | bytes 3145752
  128.0 1.6 copy-done.9
  132.6 4.6 %back_sib.1 = (bf16[3,512,1024]{2,1,0:T(8,128)(2,1)S(1)}, bf16[512,512]{1,0:T(8,128)(2,1)S(1)}) custom-call(s32[3]{0:T(128)S(1)} %pad_add_fusion.p_ref, bf16[3,512,1024]{2,1,0:T(8,128)(2,1)S(1)} %copy-done.4, bf16[2048,512]{1,0:T(8,128)(2,1)S(1)} %copy-done.9, bf16[4,4,3,32,512]{4,3,2,1,0:T(8,128)(2,1)} %all-to-all-done.2.b_ref, ...), custom_call_target="tpu_custom_call" | custom-call | flops 1610612736 | bytes 10000000 | tf_op jit(solution)/shard_map/back_sib/pallas_call | solution.py:26
  137.5 3.4 %back_own.1 = f32[512,512]{1,0:T(8,128)S(1)} custom-call(s32[3]{0:T(128)S(1)} %pad_add_fusion.p_ref, bf16[3,512,1024]{2,1,0:T(8,128)(2,1)S(1)} %get-tuple-element.36.err_ref, bf16[3,512,2048]{2,1,0:T(8,128)(2,1)S(1)} %bitcast.5), custom_call_target="tpu_custom_call" | custom-call | flops 1610612736 | bytes 7000000 | tf_op jit(solution)/shard_map/back_own/pallas_call | solution.py:26
  141.9 2.2 %dec_sib.1 = bf16[3,512,1024]{2,1,0:T(8,128)(2,1)S(1)} custom-call(bf16[512,512]{1,0:T(8,128)(2,1)S(1)} %copy-done.22, bf16[3,512,1024]{2,1,0:T(8,128)(2,1)S(1)} %get-tuple-element.36.err_ref, bf16[512,512]{1,0:T(8,128)(2,1)S(1)} %add_convert_fusion.after_ref), custom_call_target="tpu_custom_call" | custom-call | flops 1610612736 | bytes 7000000 | tf_op jit(solution)/shard_map/dec_sib/pallas_call | solution.py:26
  144.7 2.1 %collective-permute-start.23 = (bf16[256,512]{1,0:T(8,128)(2,1)S(1)}, bf16[256,512]{1,0:T(8,128)(2,1)S(1)}, u32[]{:S(2)}, u32[]{:S(2)}) collective-permute-start(bf16[256,512]{1,0:T(8,128)(2,1)S(1)} %get-tuple-element.43), channel_id=1, source_target_pairs={{32,64},{64,32},{96,0},{0,96},{33,65},{65,33},{97,1},{1,97},{34,66... | collective-permute-start | bytes 786440 | tf_op jit(solution)/shard_map/ppermute | solution.py:499
  146.8 7.5 %collective-permute-done.23 = bf16[256,512]{1,0:T(8,128)(2,1)S(1)} collective-permute-done((bf16[256,512]{1,0:T(8,128)(2,1)S(1)}, bf16[256,512]{1,0:T(8,128)(2,1)S(1)}, u32[]{:S(2)}, u32[]{:S(2)}) %collective-permute-start.23) | collective-permute-done | bytes 262176 | tf_op jit(solution)/shard_map/ppermute | solution.py:499
  154.9 1.6 collective-permute-start.22
  156.5 6.0 %dec_grad.1.after_ref = bf16[3,512,2048]{2,1,0:T(8,128)(2,1)} custom-call(s32[3]{0:T(128)S(1)} %pad_add_fusion.p_ref, bf16[512,512]{1,0:T(8,128)(2,1)S(1)} %copy-done.24, bf16[3,512,1024]{2,1,0:T(8,128)(2,1)S(1)} %get-tuple-element.36.err_ref, bf16[3,512,1024]{2,1,0:T(8,128)(2,1)S(1)} %collective-permute-done.20.got_ref), custom_call_target="tpu_custom_call" | custom-call | flops 1610612736 | bytes 13000000 | tf_op jit(solution)/shard_map/dec_grad/pallas_call | solution.py:26
  163.6 2.8 %copy-done.5 = bf16[3,512,2048]{2,1,0:T(8,128)(2,1)S(1)} copy-done((bf16[3,512,2048]{2,1,0:T(8,128)(2,1)S(1)}, bf16[3,512,2048]{2,1,0:T(8,128)(2,1)}, u32[]{:S(2)}) %copy-start.5) | copy-done | bytes 6291480
  166.4 3.2 %enc_grad.1 = (bf16[2048,512]{1,0:T(8,128)(2,1)}, f32[1,512]{1,0:T(1,128)}) custom-call(bf16[2048,512]{1,0:T(8,128)(2,1)S(1)} %copy-done.10, s32[512,512]{1,0:T(8,128)S(1)} %copy-done.19, bf16[3,512,2048]{2,1,0:T(8,128)(2,1)S(1)} %copy-done.5, bf16[256,512]{1,0:T(8,128)(2,1)S(1)} %get-tuple-element.42.refs_0_, ...), custom_call_target="tpu_custom_call" | custom-call | flops 1073741824 | bytes 7000000 | tf_op jit(solution)/shard_map/enc_grad/pallas_call | solution.py:26
  (110 shorter events, 22.5 us)
Async XLA Ops:
  0.6 1.6 copy-start.6
  6.3 2.8 %copy-start = (bf16[3,512,2048]{2,1,0:T(8,128)(2,1)S(1)}, bf16[3,512,2048]{2,1,0:T(8,128)(2,1)}, u32[]{:S(2)}) copy-start(bf16[3,512,2048]{2,1,0:T(8,128)(2,1)} %dec_ref.7) | copy-start | bytes 18874372
  9.1 22.7 %copy-start.18 = (s32[512,512]{1,0:T(8,128)S(1)}, s32[512,512]{1,0:T(8,128)}, u32[]{:S(2)}) copy-start(s32[512,512]{1,0:T(8,128)} %active_ref.1) | copy-start | bytes 3145732
  10.1 21.6 %copy-start.34 = (f32[512]{0:T(512)S(1)}, f32[512]{0:T(512)}, u32[]{:S(2)}) copy-start(f32[512]{0:T(512)} %param.8) | copy-start | bytes 6148
  10.1 23.9 %collective-permute-start.6 = (bf16[3,512,1024]{2,1,0:T(8,128)(2,1)S(1)}, bf16[3,512,1024]{2,1,0:T(8,128)(2,1)S(1)}, u32[]{:S(2)}, u32[]{:S(2)}) collective-permute-start(bf16[3,512,1024]{2,1,0:T(8,128)(2,1)S(1)} %pick_half.1), channel_id=1, source_target_pairs={{0,1},{1,0},{2,3},{3,2},{4,5},{5,4},{6,7},{7,6},{8,9},{9,8},{10,11... | collective-permute-start | bytes 9437192 | tf_op jit(solution)/shard_map/ppermute | solution.py:490
  10.2 11.1 %collective-permute-start.2 = (bf16[256,512]{1,0:T(8,128)(2,1)S(1)}, bf16[256,512]{1,0:T(8,128)(2,1)S(1)}, u32[]{:S(2)}, u32[]{:S(2)}) collective-permute-start(bf16[256,512]{1,0:T(8,128)(2,1)S(1)} %get-tuple-element.23), channel_id=1, source_target_pairs={{32,64},{64,32},{96,0},{0,96},{33,65},{65,33},{97,1},{1,97},{34,66... | collective-permute-start | bytes 786440 | tf_op jit(solution)/shard_map/ppermute | solution.py:499
  14.4 8.4 %collective-permute-start = (bf16[256,512]{1,0:T(8,128)(2,1)S(1)}, bf16[256,512]{1,0:T(8,128)(2,1)S(1)}, u32[]{:S(2)}, u32[]{:S(2)}) collective-permute-start(bf16[256,512]{1,0:T(8,128)(2,1)S(1)} %get-tuple-element.22.after_ref), channel_id=1, source_target_pairs={{0,32},{32,0},{64,96},{96,64},{1,33},{33,1},{65,97},{97,65},{2,34}... | collective-permute-start | bytes 786440 | tf_op jit(solution)/shard_map/ppermute | solution.py:498
  21.3 12.7 %copy-start.1 = (bf16[3,512,2048]{2,1,0:T(8,128)(2,1)S(1)}, bf16[3,512,2048]{2,1,0:T(8,128)(2,1)}, u32[]{:S(2)}) copy-start(bf16[3,512,2048]{2,1,0:T(8,128)(2,1)} %dec_ref.7) | copy-start | bytes 18874372
  21.4 8.1 %collective-permute-start.3 = (bf16[256,512]{1,0:T(8,128)(2,1)S(1)}, bf16[256,512]{1,0:T(8,128)(2,1)S(1)}, u32[]{:S(2)}, u32[]{:S(2)}) collective-permute-start(bf16[256,512]{1,0:T(8,128)(2,1)S(1)} %add_convert_fusion.3), channel_id=1, source_target_pairs={{0,32},{32,0},{64,96},{96,64},{1,33},{33,1},{65,97},{97,65},{2,34}... | collective-permute-start | bytes 786440 | tf_op jit(solution)/shard_map/ppermute | solution.py:502
  22.9 8.8 %collective-permute-start.1 = (bf16[256,512]{1,0:T(8,128)(2,1)S(1)}, bf16[256,512]{1,0:T(8,128)(2,1)S(1)}, u32[]{:S(2)}, u32[]{:S(2)}) collective-permute-start(bf16[256,512]{1,0:T(8,128)(2,1)S(1)} %add_convert_fusion.4), channel_id=1, source_target_pairs={{32,64},{64,32},{96,0},{0,96},{33,65},{65,33},{97,1},{1,97},{34,66... | collective-permute-start | bytes 786440 | tf_op jit(solution)/shard_map/ppermute | solution.py:502
  32.0 2.0 %collective-permute-start.4 = (bf16[512,512]{1,0:T(8,128)(2,1)S(1)}, bf16[512,512]{1,0:T(8,128)(2,1)S(1)}, u32[]{:S(2)}, u32[]{:S(2)}) collective-permute-start(bf16[512,512]{1,0:T(8,128)(2,1)S(1)} %fusion.1.lat_ref), channel_id=1, source_target_pairs={{0,1},{1,0},{2,3},{3,2},{4,5},{5,4},{6,7},{7,6},{8,9},{9,8},{10,11... | collective-permute-start | bytes 1572872 | tf_op jit(solution)/shard_map/ppermute | solution.py:490
  34.0 10.2 %copy-start.3 = (bf16[3,512,1024]{2,1,0:T(8,128)(2,1)}, bf16[3,512,1024]{2,1,0:T(8,128)(2,1)S(1)}, u32[]{:S(2)}) copy-start(bf16[3,512,1024]{2,1,0:T(8,128)(2,1)S(1)} %collective-permute-done.6.got_ref.dec_ref) | copy-start | bytes 9437188
  39.8 25.7 %all-to-all-start = ((bf16[4,3,4,32,512]{4,3,2,1,0:T(8,128)(2,1)}), bf16[4,3,4,32,512]{4,3,2,1,0:T(8,128)(2,1)}, u32[]{:S(2)}, u32[]{:S(2)}) async-start(bf16[4,3,4,32,512]{4,3,2,1,0:T(8,128)(2,1)} %copy-done.14), calls=%async_computation | async-start | bytes 3145728 | tf_op jit(solution)/shard_map/all_to_all | solution.py:537
  44.2 2.8 %copy-start.2 = (bf16[3,512,2048]{2,1,0:T(8,128)(2,1)S(1)}, bf16[3,512,2048]{2,1,0:T(8,128)(2,1)}, u32[]{:S(2)}) copy-start(bf16[3,512,2048]{2,1,0:T(8,128)(2,1)} %dec_ref.7) | copy-start | bytes 18874372
  52.9 20.1 %copy-start.33 = (bf16[3,16,2048]{2,1,0:T(8,128)(2,1)S(1)}, bf16[3,16,2048]{2,1,0:T(8,128)(2,1)}, u32[]{:S(2)}) copy-start(bf16[3,16,2048]{2,1,0:T(8,128)(2,1)} %param.11) | copy-start | bytes 589828
  52.9 20.2 %collective-permute-start.7 = (bf16[4,3,32,512]{3,2,1,0:T(8,128)(2,1)}, bf16[4,3,32,512]{3,2,1,0:T(8,128)(2,1)S(1)}, u32[]{:S(2)}, u32[]{:S(2)}) collective-permute-start(bf16[4,3,32,512]{3,2,1,0:T(8,128)(2,1)} %get-tuple-element.25), channel_id=1, source_target_pairs={{0,4},{2,6},{4,0},{6,2},{1,5},{3,7},{5,1},{7,3},{8,12},{10,14},{12... | collective-permute-start | bytes 1179656 | tf_op jit(solution)/shard_map/ppermute | solution.py:507
  56.1 18.3 %collective-permute-start.8 = (bf16[4,3,32,512]{3,2,1,0:T(8,128)(2,1)}, bf16[4,3,32,512]{3,2,1,0:T(8,128)(2,1)S(1)}, u32[]{:S(2)}, u32[]{:S(2)}) collective-permute-start(bf16[4,3,32,512]{3,2,1,0:T(8,128)(2,1)} %get-tuple-element.26), channel_id=1, source_target_pairs={{0,2},{2,4},{4,6},{6,0},{1,3},{3,5},{5,7},{7,1},{8,10},{10,12},{12... | collective-permute-start | bytes 1179656 | tf_op jit(solution)/shard_map/ppermute | solution.py:507
  56.8 17.8 %collective-permute-start.9 = (bf16[4,3,32,512]{3,2,1,0:T(8,128)(2,1)}, bf16[4,3,32,512]{3,2,1,0:T(8,128)(2,1)S(1)}, u32[]{:S(2)}, u32[]{:S(2)}) collective-permute-start(bf16[4,3,32,512]{3,2,1,0:T(8,128)(2,1)} %get-tuple-element.27), channel_id=1, source_target_pairs={{0,6},{2,0},{4,2},{6,4},{1,7},{3,1},{5,3},{7,5},{8,14},{10,8},{12,... | collective-permute-start | bytes 1179656 | tf_op jit(solution)/shard_map/ppermute | solution.py:507
  68.6 17.3 %all-to-all-start.1 = ((bf16[4,3,32,512]{3,2,1,0:T(8,128)(2,1)}), bf16[4,3,32,512]{3,2,1,0:T(8,128)(2,1)S(1)}, u32[]{:S(2)}, u32[]{:S(2)}) async-start(bf16[4,3,32,512]{3,2,1,0:T(8,128)(2,1)} %sum_a.1), calls=%async_computation.1 | async-start | bytes 786432 | tf_op jit(solution)/shard_map/all_to_all | solution.py:540
  73.0 10.2 %collective-permute-start.5 = (bf16[3,16,1024]{2,1,0:T(8,128)(2,1)S(1)}, bf16[3,16,1024]{2,1,0:T(8,128)(2,1)S(1)}, u32[]{:S(2)}, u32[]{:S(2)}) collective-permute-start(bf16[3,16,1024]{2,1,0:T(8,128)(2,1)S(1)} %get-tuple-element.46), channel_id=1, source_target_pairs={{0,1},{1,0},{2,3},{3,2},{4,5},{5,4},{6,7},{7,6},{8,9},{9,8},{10,11... | collective-permute-start | bytes 294920 | tf_op jit(solution)/shard_map/ppermute | solution.py:490
  75.6 8.0 %collective-permute-start.10 = (bf16[3,32,512]{2,1,0:T(8,128)(2,1)S(1)}, bf16[3,32,512]{2,1,0:T(8,128)(2,1)S(1)}, u32[]{:S(2)}, u32[]{:S(2)}) collective-permute-start(bf16[3,32,512]{2,1,0:T(8,128)(2,1)S(1)} %get-tuple-element.29), channel_id=1, source_target_pairs={{0,16},{8,24},{16,0},{24,8},{1,17},{9,25},{17,1},{25,9},{2,18},{10... | collective-permute-start | bytes 294920 | tf_op jit(solution)/shard_map/ppermute | solution.py:507
  80.0 5.8 %collective-permute-start.11 = (bf16[3,32,512]{2,1,0:T(8,128)(2,1)S(1)}, bf16[3,32,512]{2,1,0:T(8,128)(2,1)S(1)}, u32[]{:S(2)}, u32[]{:S(2)}) collective-permute-start(bf16[3,32,512]{2,1,0:T(8,128)(2,1)S(1)} %get-tuple-element.30), channel_id=1, source_target_pairs={{0,8},{8,16},{16,24},{24,0},{1,9},{9,17},{17,25},{25,1},{2,10},{10... | collective-permute-start | bytes 294920 | tf_op jit(solution)/shard_map/ppermute | solution.py:507
  80.6 5.3 %collective-permute-start.12 = (bf16[3,32,512]{2,1,0:T(8,128)(2,1)S(1)}, bf16[3,32,512]{2,1,0:T(8,128)(2,1)S(1)}, u32[]{:S(2)}, u32[]{:S(2)}) collective-permute-start(bf16[3,32,512]{2,1,0:T(8,128)(2,1)S(1)} %get-tuple-element.31), channel_id=1, source_target_pairs={{0,24},{8,0},{16,8},{24,16},{1,25},{9,1},{17,9},{25,17},{2,26},{10... | collective-permute-start | bytes 294920 | tf_op jit(solution)/shard_map/ppermute | solution.py:507
  87.3 15.1 %copy-start.31 = (bf16[3,32,512]{2,1,0:T(8,128)(2,1)}, bf16[3,32,512]{2,1,0:T(8,128)(2,1)S(1)}, u32[]{:S(2)}) copy-start(bf16[3,32,512]{2,1,0:T(8,128)(2,1)S(1)} %get-tuple-element.32.after_ref.refs_0_) | copy-start | bytes 294916
  87.3 15.1 %all-to-all-start.3 = ((bf16[4,3,32,512]{3,2,1,0:T(8,128)(2,1)}), bf16[4,3,32,512]{3,2,1,0:T(8,128)(2,1)S(1)}, u32[]{:S(2)}, u32[]{:S(2)}) async-start(bf16[4,3,32,512]{3,2,1,0:T(8,128)(2,1)} %get-tuple-element.35), calls=%async_computation.3 | async-start | bytes 786432 | tf_op jit(solution)/shard_map/all_to_all | solution.py:545
  90.8 20.4 %copy-start.13 = (bf16[512,512]{1,0:T(8,128)(2,1)S(1)}, bf16[512,512]{1,0:T(8,128)(2,1)}, u32[]{:S(2)}) copy-start(bf16[512,512]{1,0:T(8,128)(2,1)} %copy-done.11) | copy-start | bytes 1572868
  90.8 20.4 %copy-start.17 = (bf16[512,512]{1,0:T(8,128)(2,1)S(1)}, bf16[512,512]{1,0:T(8,128)(2,1)}, u32[]{:S(2)}) copy-start(bf16[512,512]{1,0:T(8,128)(2,1)} %copy-done.15) | copy-start | bytes 1572868
  90.8 6.2 %collective-permute-start.13 = (bf16[3,32,512]{2,1,0:T(8,128)(2,1)S(1)}, bf16[3,32,512]{2,1,0:T(8,128)(2,1)S(1)}, u32[]{:S(2)}, u32[]{:S(2)}) collective-permute-start(bf16[3,32,512]{2,1,0:T(8,128)(2,1)S(1)} %get-tuple-element.32.after_ref.refs_0_), channel_id=1, source_target_pairs={{0,8},{8,16},{16,24},{24,0},{1,9},{9,17},{17,25},{25,1},{2,10},{10... | collective-permute-start | bytes 294920 | tf_op jit(solution)/shard_map/ppermute | solution.py:507
  91.1 8.1 %collective-permute-start.14 = (bf16[3,32,512]{2,1,0:T(8,128)(2,1)S(1)}, bf16[3,32,512]{2,1,0:T(8,128)(2,1)S(1)}, u32[]{:S(2)}, u32[]{:S(2)}) collective-permute-start(bf16[3,32,512]{2,1,0:T(8,128)(2,1)S(1)} %get-tuple-element.32.after_ref.refs_0_), channel_id=1, source_target_pairs={{0,16},{8,24},{16,0},{24,8},{1,17},{9,25},{17,1},{25,9},{2,18},{10... | collective-permute-start | bytes 294920 | tf_op jit(solution)/shard_map/ppermute | solution.py:507
  95.6 4.6 %collective-permute-start.15 = (bf16[3,32,512]{2,1,0:T(8,128)(2,1)S(1)}, bf16[3,32,512]{2,1,0:T(8,128)(2,1)S(1)}, u32[]{:S(2)}, u32[]{:S(2)}) collective-permute-start(bf16[3,32,512]{2,1,0:T(8,128)(2,1)S(1)} %get-tuple-element.32.after_ref.refs_0_), channel_id=1, source_target_pairs={{0,24},{8,0},{16,8},{24,16},{1,25},{9,1},{17,9},{25,17},{2,26},{10... | collective-permute-start | bytes 294920 | tf_op jit(solution)/shard_map/ppermute | solution.py:507
  102.4 23.7 %all-to-all-start.2 = ((bf16[4,4,3,32,512]{4,3,2,1,0:T(8,128)(2,1)}), bf16[4,4,3,32,512]{4,3,2,1,0:T(8,128)(2,1)}, u32[]{:S(2)}, u32[]{:S(2)}) async-start(bf16[4,4,3,32,512]{4,3,2,1,0:T(8,128)(2,1)} %join.1), calls=%async_computation.2 | async-start | bytes 3145728 | tf_op jit(solution)/shard_map/all_to_all | solution.py:547
  107.1 16.7 %collective-permute-start.16 = (bf16[4,3,32,512]{3,2,1,0:T(8,128)(2,1)S(1)}, bf16[4,3,32,512]{3,2,1,0:T(8,128)(2,1)S(1)}, u32[]{:S(2)}, u32[]{:S(2)}) collective-permute-start(bf16[4,3,32,512]{3,2,1,0:T(8,128)(2,1)S(1)} %all-to-all-done.3.refs_0_), channel_id=1, source_target_pairs={{0,8},{8,16},{16,24},{24,0},{1,9},{9,17},{17,25},{25,1},{2,10},{10... | collective-permute-start | bytes 1179656 | tf_op jit(solution)/shard_map/ppermute | solution.py:507
  107.1 17.5 %collective-permute-start.17 = (bf16[4,3,32,512]{3,2,1,0:T(8,128)(2,1)S(1)}, bf16[4,3,32,512]{3,2,1,0:T(8,128)(2,1)S(1)}, u32[]{:S(2)}, u32[]{:S(2)}) collective-permute-start(bf16[4,3,32,512]{3,2,1,0:T(8,128)(2,1)S(1)} %all-to-all-done.3.refs_0_), channel_id=1, source_target_pairs={{0,16},{8,24},{16,0},{24,8},{1,17},{9,25},{17,1},{25,9},{2,18},{10... | collective-permute-start | bytes 1179656 | tf_op jit(solution)/shard_map/ppermute | solution.py:507
  109.8 15.6 %collective-permute-start.18 = (bf16[4,3,32,512]{3,2,1,0:T(8,128)(2,1)S(1)}, bf16[4,3,32,512]{3,2,1,0:T(8,128)(2,1)S(1)}, u32[]{:S(2)}, u32[]{:S(2)}) collective-permute-start(bf16[4,3,32,512]{3,2,1,0:T(8,128)(2,1)S(1)} %all-to-all-done.3.refs_0_), channel_id=1, source_target_pairs={{0,24},{8,0},{16,8},{24,16},{1,25},{9,1},{17,9},{25,17},{2,26},{10... | collective-permute-start | bytes 1179656 | tf_op jit(solution)/shard_map/ppermute | solution.py:507
  111.2 1.6 copy-start.7
  113.7 23.8 %slice-start = ((s8[6291456]{0:T(1024)(128)(4,1)}), s8[2097152]{0:T(1024)(128)(4,1)S(1)}, s32[]{:S(2)}) async-start(s8[6291456]{0:T(1024)(128)(4,1)} %bitcast.4), calls=%async_computation.4 | async-start | bytes 4194304
  126.1 1.9 %copy-start.4 = (bf16[3,512,1024]{2,1,0:T(8,128)(2,1)S(1)}, bf16[3,512,1024]{2,1,0:T(8,128)(2,1)}, u32[]{:S(2)}) copy-start(bf16[3,512,1024]{2,1,0:T(8,128)(2,1)} %copy-done.3) | copy-start | bytes 9437188
  132.6 4.9 %slice-start.1 = ((s8[6291456]{0:T(1024)(128)(4,1)}), s8[4194304]{0:T(1024)(128)(4,1)S(1)}, s32[]{:S(2)}) async-start(s8[6291456]{0:T(1024)(128)(4,1)} %bitcast.4), calls=%async_computation.5 | async-start | bytes 8388608
  137.2 3.7 %collective-permute-start.19 = (bf16[512,512]{1,0:T(8,128)(2,1)S(1)}, bf16[512,512]{1,0:T(8,128)(2,1)S(1)}, u32[]{:S(2)}, u32[]{:S(2)}) collective-permute-start(bf16[512,512]{1,0:T(8,128)(2,1)S(1)} %get-tuple-element.38), channel_id=1, source_target_pairs={{0,1},{1,0},{2,3},{3,2},{4,5},{5,4},{6,7},{7,6},{8,9},{9,8},{10,11... | collective-permute-start | bytes 1572872 | tf_op jit(solution)/shard_map/ppermute | solution.py:490
  144.1 12.4 %copy-start.24 = (bf16[512,512]{1,0:T(8,128)(2,1)S(1)}, bf16[512,512]{1,0:T(8,128)(2,1)}, u32[]{:S(2)}) copy-start(bf16[512,512]{1,0:T(8,128)(2,1)} %copy-done.23) | copy-start | bytes 1572868
  144.1 12.3 %collective-permute-start.20 = (bf16[3,512,1024]{2,1,0:T(8,128)(2,1)S(1)}, bf16[3,512,1024]{2,1,0:T(8,128)(2,1)S(1)}, u32[]{:S(2)}, u32[]{:S(2)}) collective-permute-start(bf16[3,512,1024]{2,1,0:T(8,128)(2,1)S(1)} %dec_sib.1), channel_id=1, source_target_pairs={{0,1},{1,0},{2,3},{3,2},{4,5},{5,4},{6,7},{7,6},{8,9},{9,8},{10,11... | collective-permute-start | bytes 9437192 | tf_op jit(solution)/shard_map/ppermute | solution.py:490
  144.7 9.5 %collective-permute-start.23 = (bf16[256,512]{1,0:T(8,128)(2,1)S(1)}, bf16[256,512]{1,0:T(8,128)(2,1)S(1)}, u32[]{:S(2)}, u32[]{:S(2)}) collective-permute-start(bf16[256,512]{1,0:T(8,128)(2,1)S(1)} %get-tuple-element.43), channel_id=1, source_target_pairs={{32,64},{64,32},{96,0},{0,96},{33,65},{65,33},{97,1},{1,97},{34,66... | collective-permute-start | bytes 786440 | tf_op jit(solution)/shard_map/ppermute | solution.py:499
  146.8 8.0 %collective-permute-start.21 = (bf16[256,512]{1,0:T(8,128)(2,1)S(1)}, bf16[256,512]{1,0:T(8,128)(2,1)S(1)}, u32[]{:S(2)}, u32[]{:S(2)}) collective-permute-start(bf16[256,512]{1,0:T(8,128)(2,1)S(1)} %get-tuple-element.44), channel_id=1, source_target_pairs={{0,32},{32,0},{64,96},{96,64},{1,33},{33,1},{65,97},{97,65},{2,34}... | collective-permute-start | bytes 786440 | tf_op jit(solution)/shard_map/ppermute | solution.py:498
  154.9 8.4 %collective-permute-start.22 = (bf16[256,512]{1,0:T(8,128)(2,1)S(1)}, bf16[256,512]{1,0:T(8,128)(2,1)S(1)}, u32[]{:S(2)}, u32[]{:S(2)}) collective-permute-start(bf16[256,512]{1,0:T(8,128)(2,1)S(1)} %get-tuple-element.42.refs_0_), channel_id=1, source_target_pairs={{32,64},{64,32},{96,0},{0,96},{33,65},{65,33},{97,1},{1,97},{34,66... | collective-permute-start | bytes 786440 | tf_op jit(solution)/shard_map/ppermute | solution.py:502
  156.4 7.1 %collective-permute-start.24 = (bf16[256,512]{1,0:T(8,128)(2,1)S(1)}, bf16[256,512]{1,0:T(8,128)(2,1)S(1)}, u32[]{:S(2)}, u32[]{:S(2)}) collective-permute-start(bf16[256,512]{1,0:T(8,128)(2,1)S(1)} %get-tuple-element.41.refs_2_), channel_id=1, source_target_pairs={{0,32},{32,0},{64,96},{96,64},{1,33},{33,1},{65,97},{97,65},{2,34}... | collective-permute-start | bytes 786440 | tf_op jit(solution)/shard_map/ppermute | solution.py:502
  156.5 7.1 %copy-start.10 = (bf16[2048,512]{1,0:T(8,128)(2,1)S(1)}, bf16[2048,512]{1,0:T(8,128)(2,1)}, u32[]{:S(2)}) copy-start(bf16[2048,512]{1,0:T(8,128)(2,1)} %copy-done.8) | copy-start | bytes 6291460
  156.5 7.1 %copy-start.19 = (s32[512,512]{1,0:T(8,128)S(1)}, s32[512,512]{1,0:T(8,128)}, u32[]{:S(2)}) copy-start(s32[512,512]{1,0:T(8,128)} %active_ref.1) | copy-start | bytes 3145732
  163.6 2.8 %copy-start.5 = (bf16[3,512,2048]{2,1,0:T(8,128)(2,1)S(1)}, bf16[3,512,2048]{2,1,0:T(8,128)(2,1)}, u32[]{:S(2)}) copy-start(bf16[3,512,2048]{2,1,0:T(8,128)(2,1)} %dec_grad.1.after_ref) | copy-start | bytes 18874372
  (18 other events, 18.2 us)

commit v3 on v2

v3 whole, which is shorter than its diff:
```python
import functools
import math

import jax
import jax.numpy as jnp
from jax import lax
from jax.experimental import pallas as pl
from jax.experimental.pallas import tpu as pltpu
from jax.sharding import Mesh, PartitionSpec as P

BF = jnp.bfloat16
F32 = jnp.float32
VMEM_LIMIT = 16 * 1024 * 1024
PRE_LIMIT = 60 * 1024 * 1024
SIDE = 4


def dot(a, b, ca, cb):
    return lax.dot_general(a, b, (((ca,), (cb,)), ((), ())), preferred_element_type=F32)


def call(body, name, grid, ins, outs, shapes, args, flops, moved, scratch=(), core=None, limit=VMEM_LIMIT):
    spec = dict(grid=grid, in_specs=ins, out_specs=outs, scratch_shapes=list(scratch))
    if core is not None:
        spec = dict(grid_spec=pltpu.PrefetchScalarGridSpec(num_scalar_prefetch=1, **spec))
        args = (core,) + tuple(args)
    return pl.pallas_call(
        body,
        out_shape=shapes,
        compiler_params=pltpu.CompilerParams(
            dimension_semantics=("arbitrary",) * len(grid), vmem_limit_bytes=limit
        ),
        cost_estimate=pl.CostEstimate(
            flops=int(flops), bytes_accessed=int(moved), transcendentals=0
        ),
        name=name,
        **spec,
    )(*args)


def pre_kernel(p_ref, x_ref, w_ref, dec_ref, tgt_ref, part_ref, dec_out, own_ref, sent_ref, acc):
    k = pl.program_id(0)
    dec_out[...] = dec_ref[...]
    part = jnp.dot(x_ref[...], w_ref[...], preferred_element_type=F32)

    @pl.when(k == 0)
    def _():
        acc[...] = part
        half = own_ref.shape[2]
        for ref, side in ((own_ref, p_ref[2]), (sent_ref, 1 - p_ref[2])):
            ref[...] = tgt_ref[:, :, pl.ds(pl.multiple_of(side * half, half), half)]

    @pl.when(k > 0)
    def _():
        acc[...] += part

    @pl.when(k == pl.num_programs(0) - 1)
    def _():
        part_ref[...] = acc[...].astype(BF)


def pre_call(place, x, w, dec, target):
    rows, depth = x.shape
    lats = w.shape[1]
    targets, few, wide = target.shape
    half = wide // 2
    step = 512
    steps = depth // step
    goal = pl.BlockSpec((targets, few, half), lambda k, p: (0, 0, 0))
    return call(
        pre_kernel,
        "pre",
        (steps,),
        [
            pl.BlockSpec((rows, step), lambda k, p: (0, k)),
            pl.BlockSpec((step, lats), lambda k, p: (k, 0)),
            pl.BlockSpec((targets, lats // steps, half), lambda k, p: (0, k, 1 - p[2])),
            pl.BlockSpec((targets, few, wide), lambda k, p: (0, 0, 0)),
        ],
        [
            pl.BlockSpec((rows, lats), lambda k, p: (0, 0)),
            pl.BlockSpec((targets, lats // steps, half), lambda k, p: (0, k, 0)),
            goal,
            goal,
        ],
        [
            jax.ShapeDtypeStruct((rows, lats), BF),
            jax.ShapeDtypeStruct((targets, lats, half), BF),
        ]
        + [jax.ShapeDtypeStruct((targets, few, half), BF)] * 2,
        (x, w, dec, target),
        2 * rows * depth * lats,
        2 * (rows + lats) * depth,
        [pltpu.VMEM((rows, lats), F32)],
        core=place,
        limit=PRE_LIMIT,
    )


def place_of(p_ref, far, near):
    return jnp.where(p_ref[2] == 0, far * SIDE + near, near * SIDE + far)


def rebuild_kernel(p_ref, lat_ref, sib_ref, dec_ref, got_ref, *refs):
    outs, held = refs[:SIDE], refs[SIDE]
    total = jnp.dot(lat_ref[...], dec_ref[0], preferred_element_type=F32)
    total += jnp.dot(sib_ref[...], got_ref[0], preferred_element_type=F32)
    held[...] = total.reshape(held.shape)
    for k in range(SIDE):
        to = lax.rem(p_ref[3] + k, SIDE)
        for i in range(SIDE):
            outs[k][i, 0] = held[place_of(p_ref, to, i)].astype(outs[k].dtype)


def rebuild_call(place, lat, sib, dec, got):
    rows, lats = lat.shape
    targets, _, half = got.shape
    piece = rows // (SIDE * SIDE)
    whole = pl.BlockSpec((rows, lats), lambda t, p: (0, 0))
    return call(
        rebuild_kernel,
        "rebuild",
        (targets,),
        [
            whole,
            whole,
            pl.BlockSpec((1, lats, half), lambda t, p: (t, 0, p[2])),
            pl.BlockSpec((1, lats, half), lambda t, p: (t, 0, 0)),
        ],
        [pl.BlockSpec((SIDE, 1, piece, half), lambda t, p: (0, t, 0, 0))] * SIDE,
        [
            jax.ShapeDtypeStruct((SIDE, targets, piece, half), F32 if k == 0 else BF)
            for k in range(SIDE)
        ],
        (lat, sib, dec, got),
        4 * rows * lats * half * targets,
        11e6,
        [pltpu.VMEM((SIDE * SIDE, piece, half), F32)],
        core=place,
    )


def sum_kernel(p_ref, *refs):
    parts, outs, held = refs[:SIDE], refs[SIDE : 2 * SIDE], refs[2 * SIDE]
    total = parts[0][:, 0]
    for part in parts[1:]:
        total += part[:, 0].astype(F32)
    held[...] = total
    for k in range(SIDE):
        outs[k][0] = held[lax.rem(p_ref[4] + k, SIDE)].astype(outs[k].dtype)


def sum_call(place, parts):
    _, targets, piece, half = parts[0].shape
    return call(
        sum_kernel,
        "sum_first",
        (targets,),
        [pl.BlockSpec((SIDE, 1, piece, half), lambda t, p: (0, t, 0, 0))] * SIDE,
        [pl.BlockSpec((1, piece, half), lambda t, p: (t, 0, 0))] * SIDE,
        [jax.ShapeDtypeStruct((targets, piece, half), F32 if k == 0 else BF) for k in range(SIDE)],
        tuple(parts),
        4 * parts[0].size,
        12 * parts[0].size,
        [pltpu.VMEM((SIDE, piece, half), F32)],
        core=place,
    )


def error_kernel(scale, p_ref, own_ref, got_ref, *refs):
    parts, out, goal = refs[:SIDE], refs[SIDE], refs[SIDE + 1]
    few = own_ref.shape[1]
    for ref, side in ((own_ref, p_ref[2]), (got_ref, 1 - p_ref[2])):
        goal[pl.ds(pl.multiple_of(side * few, few), few), :] = ref[0].astype(F32)
    total = parts[0][0]
    for part in parts[1:]:
        total += part[0].astype(F32)
    out[0] = ((total - goal[...]) * scale).astype(BF)


def error_call(scale, place, own, got, parts):
    targets, piece, half = parts[0].shape
    one = pl.BlockSpec((1, piece, half), lambda t, p: (t, 0, 0))
    goal = pl.BlockSpec((1,) + own.shape[1:], lambda t, p: (t, 0, 0))
    return call(
        functools.partial(error_kernel, scale),
        "error",
        (targets,),
        [goal, goal] + [one] * SIDE,
        one,
        jax.ShapeDtypeStruct((targets, piece, half), BF),
        (own, got, *parts),
        8 * targets * piece * half,
        2e6,
        [pltpu.VMEM((piece, half), F32)],
        core=place,
    )


def join_kernel(p_ref, *refs):
    parts, out_ref = refs[:SIDE], refs[SIDE]
    for k in range(SIDE):
        out_ref[lax.rem(p_ref[4] + SIDE - k, SIDE), 0] = parts[k][0]


def join_call(place, parts):
    targets, piece, half = parts[0].shape
    return call(
        join_kernel,
        "join",
        (targets,),
        [pl.BlockSpec((1, piece, half), lambda t, p: (t, 0, 0))] * SIDE,
        pl.BlockSpec((SIDE, 1, piece, half), lambda t, p: (0, t, 0, 0)),
        jax.ShapeDtypeStruct((SIDE, targets, piece, half), BF),
        tuple(parts),
        0,
        8 * parts[0].size,
        core=place,
    )


def back_dot(err, dec_ref, out_ref, acc):
    t = pl.program_id(0)
    part = dot(err, dec_ref[0], 1, 1)

    @pl.when(t == 0)
    def _():
        acc[...] = part

    @pl.when(t > 0)
    def _():
        acc[...] += part

    @pl.when(t == pl.num_programs(0) - 1)
    def _():
        out_ref[...] = acc[...].astype(out_ref.dtype)


def back_sib_kernel(p_ref, dec_ref, after_ref, *refs):
    parts, (err_ref, out_ref, acc) = refs[:SIDE], refs[SIDE:]
    piece = parts[0].shape[2]
    for k in range(SIDE):
        far = lax.rem(p_ref[3] + SIDE - k, SIDE)
        for i in range(SIDE):
            at = pl.ds(pl.multiple_of(place_of(p_ref, far, i) * piece, piece), piece)
            err_ref[0, at, :] = parts[k][i, 0]
    back_dot(err_ref[0], dec_ref, out_ref, acc)


def back_sib_call(place, parts, dec, after):
    _, targets, piece, half = parts[0].shape
    lats = dec.shape[1]
    rows = SIDE * SIDE * piece
    return call(
        back_sib_kernel,
        "back_sib",
        (targets,),
        [
            pl.BlockSpec((1, lats, half), lambda t, p: (t, 0, 0)),
            pl.BlockSpec(memory_space=pl.ANY),
        ]
        + [pl.BlockSpec((SIDE, 1, piece, half), lambda t, p: (0, t, 0, 0))] * SIDE,
        [
            pl.BlockSpec((1, rows, half), lambda t, p: (t, 0, 0)),
            pl.BlockSpec((rows, lats), lambda t, p: (0, 0)),
        ],
        [
            jax.ShapeDtypeStruct((targets, rows, half), BF),
            jax.ShapeDtypeStruct((rows, lats), BF),
        ],
        (dec, after, *parts),
        2 * rows * lats * half * targets,
        10e6,
        [pltpu.VMEM((rows, lats), F32)],
        core=place,
    )


def back_own_kernel(p_ref, err_ref, dec_ref, out_ref, acc):
    back_dot(err_ref[0], dec_ref, out_ref, acc)


def back_own_call(place, err, dec):
    targets, rows, half = err.shape
    lats = dec.shape[1]
    return call(
        back_own_kernel,
        "back_own",
        (targets,),
        [
            pl.BlockSpec((1, rows, half), lambda t, p: (t, 0, 0)),
            pl.BlockSpec((1, lats, half), lambda t, p: (t, 0, p[2])),
        ],
        pl.BlockSpec((rows, lats), lambda t, p: (0, 0)),
        jax.ShapeDtypeStruct((rows, lats), F32),
        (err, dec),
        2 * rows * lats * half * targets,
        7e6,
        [pltpu.VMEM((rows, lats), F32)],
        core=place,
    )


def turn_kernel(x_ref, lat_ref, sib_ref, after_ref, x_out, lat_out, sib_out, done_ref):
    done_ref[...] = jnp.zeros(done_ref.shape, F32)
    x_out[...] = x_ref[...].T

    @pl.when(pl.program_id(0) == 0)
    def _():
        lat_out[...] = lat_ref[...].T
        sib_out[...] = sib_ref[...].T


def turn_call(x, lat, sib, after):
    rows, depth = x.shape
    lats = lat.shape[1]
    step = 512
    whole = pl.BlockSpec((rows, lats), lambda i: (0, 0))
    turned = pl.BlockSpec((lats, rows), lambda i: (0, 0))
    return call(
        turn_kernel,
        "turn",
        (depth // step,),
        [
            pl.BlockSpec((rows, step), lambda i: (0, i)),
            whole,
            whole,
            pl.BlockSpec(memory_space=pl.ANY),
        ],
        [
            pl.BlockSpec((step, rows), lambda i: (i, 0)),
            turned,
            turned,
            pl.BlockSpec((8, 128), lambda i: (0, 0)),
        ],
        [jax.ShapeDtypeStruct((depth, rows), BF)]
        + [jax.ShapeDtypeStruct((lats, rows), BF)] * 2
        + [jax.ShapeDtypeStruct((8, 128), F32)],
        (x, lat, sib, after),
        0,
        6e6,
    )


def dec_sib_kernel(lat_ref, err_ref, after_ref, out_ref):
    out_ref[0] = dot(lat_ref[...], err_ref[0], 1, 0).astype(BF)


def dec_sib_call(lat, err, after):
    targets, rows, half = err.shape
    lats = lat.shape[0]
    return call(
        dec_sib_kernel,
        "dec_sib",
        (targets,),
        [
            pl.BlockSpec((lats, rows), lambda t: (0, 0)),
            pl.BlockSpec((1, rows, half), lambda t: (t, 0, 0)),
            pl.BlockSpec(memory_space=pl.ANY),
        ],
        pl.BlockSpec((1, lats, half), lambda t: (t, 0, 0)),
        jax.ShapeDtypeStruct((targets, lats, half), BF),
        (lat, err, after),
        2 * rows * lats * half * targets,
        7e6,
    )


def dec_kernel(p_ref, lat_ref, err_ref, got_ref, out_ref, done_ref):
    j = pl.program_id(1)
    done_ref[...] = jnp.zeros(done_ref.shape, F32)

    @pl.when(j == 0)
    def _():
        out_ref[0] = dot(lat_ref[...], err_ref[0], 1, 0).astype(BF)

    @pl.when(j == 1)
    def _():
        out_ref[...] = got_ref[...]


def dec_call(place, lat, err, got):
    targets, rows, half = err.shape
    lats = lat.shape[0]
    return call(
        dec_kernel,
        "dec_grad",
        (targets, 2),
        [
            pl.BlockSpec((lats, rows), lambda t, j, p: (0, 0)),
            pl.BlockSpec((1, rows, half), lambda t, j, p: (t, 0, 0)),
            pl.BlockSpec((1, lats, half), lambda t, j, p: (t, 0, 0)),
        ],
        [
            pl.BlockSpec((1, lats, half), lambda t, j, p: (t, 0, (j + p[2]) % 2)),
            pl.BlockSpec((8, 128), lambda t, j, p: (0, 0)),
        ],
        [
            jax.ShapeDtypeStruct((targets, lats, 2 * half), BF),
            jax.ShapeDtypeStruct((8, 128), F32),
        ],
        (lat, err, got),
        2 * rows * lats * half * targets,
        13e6,
        core=place,
    )


def enc_kernel(x_ref, active_ref, after_ref, sum_ref, got_ref, enc_ref, bias_ref, grad):
    @pl.when(pl.program_id(0) == 0)
    def _():
        total = sum_ref[...] + got_ref[...].astype(F32)
        kept = jnp.where(active_ref[...] > 0, total, 0.0).astype(BF)
        grad[...] = kept
        bias_ref[...] = jnp.sum(kept.astype(F32), axis=0, keepdims=True)

    enc_ref[...] = dot(x_ref[...], grad[...], 1, 0).astype(BF)


def enc_call(x, active, after, sums, got):
    depth, rows = x.shape
    lats = active.shape[1]
    step = 512
    whole = pl.BlockSpec((rows, lats), lambda i: (0, 0))
    return call(
        enc_kernel,
        "enc_grad",
        (depth // step,),
        [
            pl.BlockSpec((step, rows), lambda i: (i, 0)),
            whole,
            pl.BlockSpec(memory_space=pl.ANY),
            whole,
            whole,
        ],
        [
            pl.BlockSpec((step, lats), lambda i: (i, 0)),
            pl.BlockSpec((1, lats), lambda i: (0, 0)),
        ],
        [jax.ShapeDtypeStruct((depth, lats), BF), jax.ShapeDtypeStruct((1, lats), F32)],
        (x, active, after, sums, got),
        2 * rows * depth * lats,
        7e6,
        [pltpu.VMEM((rows, lats), BF)],
    )


def swap(value):
    return lax.ppermute(value, "c", [(0, 1), (1, 0)])


EVEN = (1, 0, 3, 2)
ODD = (3, 2, 1, 0)


def pair(value, tables):
    moves = [(z * 2 + c, tables[c][z] * 2 + c) for z in range(SIDE) for c in range(2)]
    return lax.ppermute(value, ("z", "c"), moves)


def z_sum(part):
    first = part.astype(F32) + pair(part.astype(BF), (EVEN, ODD)).astype(F32)
    return first, pair(first.astype(BF), (ODD, EVEN))


def shift(value, second, step):
    moves = []
    for x in range(SIDE):
        for y in range(SIDE):
            for c in range(2):
                along_x = (c == 0) != second
                to = ((x + step) % SIDE, y) if along_x else (x, (y + step) % SIDE)
                moves.append(((x * SIDE + y) * 2 + c, (to[0] * SIDE + to[1]) * 2 + c))
    return lax.ppermute(value, ("x", "y", "c"), moves)


def scatter(parts, second):
    return [parts[0]] + [shift(parts[k], second, k) for k in (1, 2, 3)]


def spread(value, second):
    return [value] + [shift(value, second, k) for k in (1, 2, 3)]


def per_device(mlp_inputs, enc_weight, enc_bias, active, dec_weight, target):
    rows = mlp_inputs.shape[0]
    x, y, c = (lax.axis_index(a) for a in "xyc")
    first, second = jnp.where(c == 0, x, y), jnp.where(c == 0, y, x)
    place = jnp.stack([x, y, c, first, second]).astype(jnp.int32)
    scale = 1.0 / math.sqrt(rows)

    part, dec_sent, tgt_own, tgt_sent = pre_call(
        place, mlp_inputs, enc_weight, dec_weight, target
    )
    dec_got = swap(dec_sent)
    tgt_got = swap(tgt_sent)
    near, far = z_sum(part)
    lat = jnp.where(active > 0, near + far.astype(F32) + enc_bias, 0.0).astype(BF)
    lat_sib = swap(lat)

    parts = scatter(rebuild_call(place, lat, lat_sib, dec_weight, dec_got), False)
    parts = scatter(sum_call(place, parts), True)
    err = error_call(scale, place, tgt_own, tgt_got, parts)
    parts = spread(join_call(place, spread(err, True)), False)
    x_turned, lat_turned, sib_turned, done = turn_call(mlp_inputs, lat, lat_sib, parts[1])

    err, grad_got = back_sib_call(place, parts, dec_got, done)
    grad_got = swap(grad_got)
    near, far = z_sum(back_own_call(place, err, dec_weight) + grad_got.astype(F32))
    dec_part = swap(dec_sib_call(sib_turned, err, near))
    dec_grad, done = dec_call(place, lat_turned, err, dec_part)
    enc_grad, bias_grad = enc_call(x_turned, active, done, near, far)
    return enc_grad, bias_grad.reshape(-1), dec_grad


def solution(mesh):
    grid = Mesh(mesh.devices.reshape(4, 4, 4, 2), ("z", "x", "y", "c"))
    lat = ("x", "y", "c")
    in_specs = (
        P(None, "z"),
        P("z", lat),
        P(lat),
        P(None, lat),
        P(None, lat, "z"),
        P(None, lat, "z"),
    )
    out_specs = (P("z", lat), P(lat), P(None, lat, "z"))
    return jax.shard_map(
        per_device, mesh=grid, in_specs=in_specs, out_specs=out_specs, check_vma=False
    )
```

time: 171 us -> 149 us (0.87)
  local copies, waits for them, and re-layouts: 31.4 us -> 3.44 us
  waiting for transfers between devices: 46.8 us -> 72.8 us
  starting transfers between devices: 50.7 us -> 32.1 us
  Pallas kernels: 38.6 us -> 34.9 us
  other arithmetic: 0.97 us -> 3.04 us
    unnamed x74 -> x18, local copies, waits for them, and re-layouts: 31.4 us -> 2.82 us
    ppermute x20 -> x16, waiting for transfers between devices: 38.7 us -> 67.2 us  [the longest x12 43.5 us: shift(): return lax.ppermute(value, ('x', 'y', 'c'), moves)]
    all_to_all x4 -> x0, starting transfers between devices: 17 us -> none  [the longest x1 4.68 us: per_device(): b_err = lax.all_to_all(b_err, 'y', 0, 0)]
    all_to_all x4 -> x0, waiting for transfers between devices: 6.2 us -> none  [the longest x1 6.2 us: per_device(): a_sum = lax.all_to_all(a_sum, 'x', 0, 0)]
    pallas_call x14 -> x11, Pallas kernels: 38.6 us -> 34.9 us  [call(): pl.pallas_call(body, out_shape=shapes, compiler_params=pltpu.CompilerPara...]
    ppermute x5, waiting for transfers between devices: 1.91 us -> 5.54 us  [swap(): return lax.ppermute(value, 'c', [(0, 1), (1, 0)])]
    convert_element_type x5 -> x4, other arithmetic: 0.72 us -> 3.04 us  [the longest x2 1.46 us: z_sum(): return (first, pair(first.astype(BF), (ODD, EVEN)))]
    ppermute x20 -> x16, starting transfers between devices: 32.7 us -> 30.9 us  [the longest x12 21.6 us: shift(): return lax.ppermute(value, ('x', 'y', 'c'), moves)]
  transfers between devices with their start and end apart: 29 -> 21, of which waited for: 18 -> 15; matrix products, arithmetic and copies ran while one was open for 0% -> 2% of each run, Pallas kernels for 12% -> 7%
where the time goes in v3:
time: 149 us; the launch traced here: 147 us
  waiting for transfers between devices  72.8 us (49%)
  Pallas kernels  34.9 us (23%)
  starting transfers between devices  32.1 us (22%)
  local copies, waits for them, and re-layouts  3.44 us (2%)
  other arithmetic  3.04 us (2%)
    ppermute x12, waiting for transfers between devices, shift(): return lax.ppermute(value, ('x', 'y', 'c'), moves)  43.5 us
    pallas_call x11, Pallas kernels, call(): pl.pallas_call(body, out_shape=shapes, compiler_params=pltpu.CompilerPara...  34.9 us
    ppermute x4, waiting for transfers between devices, pair(): return lax.ppermute(value, ('z', 'c'), moves)  23.7 us
    ppermute x12, starting transfers between devices, shift(): return lax.ppermute(value, ('x', 'y', 'c'), moves)  21.6 us
    ppermute x4, starting transfers between devices, pair(): return lax.ppermute(value, ('z', 'c'), moves)  9.31 us
    ppermute x5, waiting for transfers between devices, swap(): return lax.ppermute(value, 'c', [(0, 1), (1, 0)])  5.54 us
  transfers between devices with their start and end apart: 21, of which 15 were waited for; matrix products, arithmetic and copies ran while one was open for 2% of the time, Pallas kernels for 7%

profile of v3, /device:TPU:0, one launch (start us, length us, event | category | flops | bytes accessed | tf_op | source)
XLA Modules:
  0.0 147.0 jit_solution(10164786964289554194)
XLA Ops:
  0.6 0.6 stack.23.p_ref
  1.3 7.3 %pre.1 = (bf16[512,512]{1,0:T(8,128)(2,1)}, bf16[3,512,1024]{2,1,0:T(8,128)(2,1)}, bf16[3,16,1024]{2,1,0:T(8,128)(2,1)}, bf16[3,16,1024]{2,1,0:T(8,128)(2,1)}) custom-call(s32[5]{0:T(128)} %stack.23.p_ref, bf16[512,2048]{1,0:T(8,128)(2,1)} %x_ref.3, bf16[2048,512]{1,0:T(8,128)(2,1)} %w_ref.1, bf16[3,512,2048]{2,1,0:T(8,128)(2,1)} %dec_ref.5, ...), custom_call_target="tpu_custom_call" | custom-call | flops 1073741824 | bytes 4194304 | tf_op jit(solution)/shard_map/pre/pallas_call | solution.py:27
  8.6 2.1 %collective-permute-start = (bf16[512,512]{1,0:T(8,128)(2,1)}, bf16[512,512]{1,0:T(8,128)(2,1)S(1)}, u32[]{:S(2)}, u32[]{:S(2)}) collective-permute-start(bf16[512,512]{1,0:T(8,128)(2,1)} %get-tuple-element.25), channel_id=1, source_target_pairs={{0,32},{1,97},{32,0},{33,65},{64,96},{65,33},{96,64},{97,1},{2,34}... | collective-permute-start | bytes 1572872 | tf_op jit(solution)/shard_map/ppermute | solution.py:458
  10.7 7.4 %collective-permute-done = bf16[512,512]{1,0:T(8,128)(2,1)S(1)} collective-permute-done((bf16[512,512]{1,0:T(8,128)(2,1)}, bf16[512,512]{1,0:T(8,128)(2,1)S(1)}, u32[]{:S(2)}, u32[]{:S(2)}) %collective-permute-start) | collective-permute-done | bytes 524320 | tf_op jit(solution)/shard_map/ppermute | solution.py:458
  18.1 1.2 fusion
  19.3 4.2 %collective-permute-start.1 = (bf16[512,512]{1,0:T(8,128)(2,1)S(1)}, bf16[512,512]{1,0:T(8,128)(2,1)S(1)}, u32[]{:S(2)}, u32[]{:S(2)}) collective-permute-start(bf16[512,512]{1,0:T(8,128)(2,1)S(1)} %fusion), channel_id=1, source_target_pairs={{0,96},{1,33},{32,64},{33,1},{64,32},{65,97},{96,0},{97,65},{2,98}... | collective-permute-start | bytes 1572872 | tf_op jit(solution)/shard_map/ppermute | solution.py:458
  23.5 7.2 %collective-permute-done.1 = bf16[512,512]{1,0:T(8,128)(2,1)S(1)} collective-permute-done((bf16[512,512]{1,0:T(8,128)(2,1)S(1)}, bf16[512,512]{1,0:T(8,128)(2,1)S(1)}, u32[]{:S(2)}, u32[]{:S(2)}) %collective-permute-start.1) | collective-permute-done | bytes 524320 | tf_op jit(solution)/shard_map/ppermute | solution.py:458
  30.7 1.4 select_convert_fusion.lat_ref
  32.1 1.9 %collective-permute-done.2.sib_ref = bf16[512,512]{1,0:T(8,128)(2,1)S(1)} collective-permute-done((bf16[512,512]{1,0:T(8,128)(2,1)S(1)}, bf16[512,512]{1,0:T(8,128)(2,1)S(1)}, u32[]{:S(2)}, u32[]{:S(2)}) %collective-permute-start.2) | collective-permute-done | bytes 524320 | tf_op jit(solution)/shard_map/ppermute | solution.py:449
  34.1 2.8 %copy-done = bf16[3,512,2048]{2,1,0:T(8,128)(2,1)S(1)} copy-done((bf16[3,512,2048]{2,1,0:T(8,128)(2,1)S(1)}, bf16[3,512,2048]{2,1,0:T(8,128)(2,1)}, u32[]{:S(2)}) %copy-start) | copy-done | bytes 6291480
  36.8 5.2 %rebuild.1 = (f32[4,3,32,1024]{3,2,1,0:T(8,128)S(1)}, bf16[4,3,32,1024]{3,2,1,0:T(8,128)(2,1)S(1)}, bf16[4,3,32,1024]{3,2,1,0:T(8,128)(2,1)S(1)}, bf16[4,3,32,1024]{3,2,1,0:T(8,128)(2,1)S(1)}) custom-call(s32[5]{0:T(128)S(1)} %copy-done.4, bf16[512,512]{1,0:T(8,128)(2,1)S(1)} %select_convert_fusion.lat_ref, ...), custom_call_target="tpu_custom_call" | custom-call | flops 3221225472 | bytes 11000000 | tf_op jit(solution)/shard_map/rebuild/pallas_call | solution.py:27
  42.1 1.6 %collective-permute-start.5 = (bf16[4,3,32,1024]{3,2,1,0:T(8,128)(2,1)S(1)}, bf16[4,3,32,1024]{3,2,1,0:T(8,128)(2,1)S(1)}, u32[]{:S(2)}, u32[]{:S(2)}) collective-permute-start(bf16[4,3,32,1024]{3,2,1,0:T(8,128)(2,1)S(1)} %get-tuple-element.30), channel_id=1, source_target_pairs={{0,8},{1,3},{2,10},{3,5},{4,12},{5,7},{6,14},{7,1},{8,16},{9,11},{... | collective-permute-start | bytes 2359304 | tf_op jit(solution)/shard_map/ppermute | solution.py:474
  43.6 2.7 %collective-permute-start.6 = (bf16[4,3,32,1024]{3,2,1,0:T(8,128)(2,1)S(1)}, bf16[4,3,32,1024]{3,2,1,0:T(8,128)(2,1)S(1)}, u32[]{:S(2)}, u32[]{:S(2)}) collective-permute-start(bf16[4,3,32,1024]{3,2,1,0:T(8,128)(2,1)S(1)} %get-tuple-element.31), channel_id=1, source_target_pairs={{0,16},{1,5},{2,18},{3,7},{4,20},{5,1},{6,22},{7,3},{8,24},{9,13},... | collective-permute-start | bytes 2359304 | tf_op jit(solution)/shard_map/ppermute | solution.py:474
  46.4 1.4 collective-permute-start.7
  47.8 7.5 %collective-permute-done.5.refs_1_ = bf16[4,3,32,1024]{3,2,1,0:T(8,128)(2,1)S(1)} collective-permute-done((bf16[4,3,32,1024]{3,2,1,0:T(8,128)(2,1)S(1)}, bf16[4,3,32,1024]{3,2,1,0:T(8,128)(2,1)S(1)}, u32[]{:S(2)}, u32[]{:S(2)}) %collective-permute-start.5) | collective-permute-done | bytes 786464 | tf_op jit(solution)/shard_map/ppermute | solution.py:474
  55.4 9.4 %collective-permute-done.6.refs_2_ = bf16[4,3,32,1024]{3,2,1,0:T(8,128)(2,1)S(1)} collective-permute-done((bf16[4,3,32,1024]{3,2,1,0:T(8,128)(2,1)S(1)}, bf16[4,3,32,1024]{3,2,1,0:T(8,128)(2,1)S(1)}, u32[]{:S(2)}, u32[]{:S(2)}) %collective-permute-start.6) | collective-permute-done | bytes 786464 | tf_op jit(solution)/shard_map/ppermute | solution.py:474
  64.8 1.5 sum_first.1
  66.2 1.6 %collective-permute-start.8 = (bf16[3,32,1024]{2,1,0:T(8,128)(2,1)S(1)}, bf16[3,32,1024]{2,1,0:T(8,128)(2,1)S(1)}, u32[]{:S(2)}, u32[]{:S(2)}) collective-permute-start(bf16[3,32,1024]{2,1,0:T(8,128)(2,1)S(1)} %get-tuple-element.34), channel_id=1, source_target_pairs={{0,2},{1,9},{2,4},{3,11},{4,6},{5,13},{6,0},{7,15},{8,10},{9,17},{... | collective-permute-start | bytes 589832 | tf_op jit(solution)/shard_map/ppermute | solution.py:474
  67.9 2.9 %collective-permute-start.9 = (bf16[3,32,1024]{2,1,0:T(8,128)(2,1)S(1)}, bf16[3,32,1024]{2,1,0:T(8,128)(2,1)S(1)}, u32[]{:S(2)}, u32[]{:S(2)}) collective-permute-start(bf16[3,32,1024]{2,1,0:T(8,128)(2,1)S(1)} %get-tuple-element.35), channel_id=1, source_target_pairs={{0,4},{1,17},{2,6},{3,19},{4,0},{5,21},{6,2},{7,23},{8,12},{9,25},... | collective-permute-start | bytes 589832 | tf_op jit(solution)/shard_map/ppermute | solution.py:474
  70.8 1.3 collective-permute-start.10
  72.1 1.3 collective-permute-done.3.got_ref
  73.4 3.1 %collective-permute-done.9.refs_2_ = bf16[3,32,1024]{2,1,0:T(8,128)(2,1)S(1)} collective-permute-done((bf16[3,32,1024]{2,1,0:T(8,128)(2,1)S(1)}, bf16[3,32,1024]{2,1,0:T(8,128)(2,1)S(1)}, u32[]{:S(2)}, u32[]{:S(2)}) %collective-permute-start.9) | collective-permute-done | bytes 196640 | tf_op jit(solution)/shard_map/ppermute | solution.py:474
  76.5 0.7 error.1.refs_0_
  77.3 2.5 %collective-permute-start.13 = (bf16[3,32,1024]{2,1,0:T(8,128)(2,1)S(1)}, bf16[3,32,1024]{2,1,0:T(8,128)(2,1)S(1)}, u32[]{:S(2)}, u32[]{:S(2)}) collective-permute-start(bf16[3,32,1024]{2,1,0:T(8,128)(2,1)S(1)} %error.1.refs_0_), channel_id=1, source_target_pairs={{0,6},{1,25},{2,0},{3,27},{4,2},{5,29},{6,4},{7,31},{8,14},{9,1},{... | collective-permute-start | bytes 589832 | tf_op jit(solution)/shard_map/ppermute | solution.py:474
  79.8 1.2 collective-permute-start.12
  81.1 0.6 collective-permute-start.11
  81.6 3.5 %collective-permute-done.13.refs_3_ = bf16[3,32,1024]{2,1,0:T(8,128)(2,1)S(1)} collective-permute-done((bf16[3,32,1024]{2,1,0:T(8,128)(2,1)S(1)}, bf16[3,32,1024]{2,1,0:T(8,128)(2,1)S(1)}, u32[]{:S(2)}, u32[]{:S(2)}) %collective-permute-start.13) | collective-permute-done | bytes 196640 | tf_op jit(solution)/shard_map/ppermute | solution.py:474
  85.1 1.9 %collective-permute-done.12.refs_2_ = bf16[3,32,1024]{2,1,0:T(8,128)(2,1)S(1)} collective-permute-done((bf16[3,32,1024]{2,1,0:T(8,128)(2,1)S(1)}, bf16[3,32,1024]{2,1,0:T(8,128)(2,1)S(1)}, u32[]{:S(2)}, u32[]{:S(2)}) %collective-permute-start.12) | collective-permute-done | bytes 196640 | tf_op jit(solution)/shard_map/ppermute | solution.py:474
  87.1 2.0 %collective-permute-done.11.refs_1_ = bf16[3,32,1024]{2,1,0:T(8,128)(2,1)S(1)} collective-permute-done((bf16[3,32,1024]{2,1,0:T(8,128)(2,1)S(1)}, bf16[3,32,1024]{2,1,0:T(8,128)(2,1)S(1)}, u32[]{:S(2)}, u32[]{:S(2)}) %collective-permute-start.11) | collective-permute-done | bytes 196640 | tf_op jit(solution)/shard_map/ppermute | solution.py:474
  89.1 0.7 join.1.refs_0_
  89.9 3.0 %collective-permute-start.14 = (bf16[4,3,32,1024]{3,2,1,0:T(8,128)(2,1)S(1)}, bf16[4,3,32,1024]{3,2,1,0:T(8,128)(2,1)S(1)}, u32[]{:S(2)}, u32[]{:S(2)}) collective-permute-start(bf16[4,3,32,1024]{3,2,1,0:T(8,128)(2,1)S(1)} %join.1.refs_0_), channel_id=1, source_target_pairs={{0,8},{1,3},{2,10},{3,5},{4,12},{5,7},{6,14},{7,1},{8,16},{9,11},{... | collective-permute-start | bytes 2359304 | tf_op jit(solution)/shard_map/ppermute | solution.py:474
  92.9 0.3 collective-permute-start.16
  93.2 2.3 %collective-permute-start.15 = (bf16[4,3,32,1024]{3,2,1,0:T(8,128)(2,1)S(1)}, bf16[4,3,32,1024]{3,2,1,0:T(8,128)(2,1)S(1)}, u32[]{:S(2)}, u32[]{:S(2)}) collective-permute-start(bf16[4,3,32,1024]{3,2,1,0:T(8,128)(2,1)S(1)} %join.1.refs_0_), channel_id=1, source_target_pairs={{0,16},{1,5},{2,18},{3,7},{4,20},{5,1},{6,22},{7,3},{8,24},{9,13},... | collective-permute-start | bytes 2359304 | tf_op jit(solution)/shard_map/ppermute | solution.py:474
  95.5 7.6 %collective-permute-done.14.after_ref.refs_1_ = bf16[4,3,32,1024]{3,2,1,0:T(8,128)(2,1)S(1)} collective-permute-done((bf16[4,3,32,1024]{3,2,1,0:T(8,128)(2,1)S(1)}, bf16[4,3,32,1024]{3,2,1,0:T(8,128)(2,1)S(1)}, u32[]{:S(2)}, u32[]{:S(2)}) %collective-permute-start.14) | collective-permute-done | bytes 786464 | tf_op jit(solution)/shard_map/ppermute | solution.py:474
  103.1 1.3 turn.1
  104.4 0.5 collective-permute-done.16.refs_3_
  104.9 7.9 %collective-permute-done.15.refs_2_ = bf16[4,3,32,1024]{3,2,1,0:T(8,128)(2,1)S(1)} collective-permute-done((bf16[4,3,32,1024]{3,2,1,0:T(8,128)(2,1)S(1)}, bf16[4,3,32,1024]{3,2,1,0:T(8,128)(2,1)S(1)}, u32[]{:S(2)}, u32[]{:S(2)}) %collective-permute-start.15) | collective-permute-done | bytes 786464 | tf_op jit(solution)/shard_map/ppermute | solution.py:474
  112.8 3.4 %back_sib.1 = (bf16[3,512,1024]{2,1,0:T(8,128)(2,1)S(1)}, bf16[512,512]{1,0:T(8,128)(2,1)S(1)}) custom-call(s32[5]{0:T(128)S(1)} %copy-done.4, bf16[3,512,1024]{2,1,0:T(8,128)(2,1)S(1)} %collective-permute-done.4.got_ref.dec_ref, f32[8,128]{1,0:T(8,128)S(1)} %get-tuple-element.39.after_ref, bf16[4,3,32,1024]{3,2,1,0:T(8,128)(2,1)S(1)} %join.1.refs_0_, ...), custom_call_target="tpu_custom_call" | custom-call | flops 1610612736 | bytes 10000000 | tf_op jit(solution)/shard_map/back_sib/pallas_call | solution.py:27
  116.3 3.4 %back_own.1 = f32[512,512]{1,0:T(8,128)S(1)} custom-call(s32[5]{0:T(128)S(1)} %copy-done.4, bf16[3,512,1024]{2,1,0:T(8,128)(2,1)S(1)} %get-tuple-element.40.err_ref, bf16[3,512,2048]{2,1,0:T(8,128)(2,1)S(1)} %bitcast.7), custom_call_target="tpu_custom_call" | custom-call | flops 1610612736 | bytes 7000000 | tf_op jit(solution)/shard_map/back_own/pallas_call | solution.py:27
  119.7 0.2 fusion.1
  120.0 9.2 %collective-permute-done.18 = bf16[512,512]{1,0:T(8,128)(2,1)S(1)} collective-permute-done((bf16[512,512]{1,0:T(8,128)(2,1)S(1)}, bf16[512,512]{1,0:T(8,128)(2,1)S(1)}, u32[]{:S(2)}, u32[]{:S(2)}) %collective-permute-start.18) | collective-permute-done | bytes 524320 | tf_op jit(solution)/shard_map/ppermute | solution.py:458
  129.2 0.3 fusion.2
  129.5 2.2 %dec_sib.1 = bf16[3,512,1024]{2,1,0:T(8,128)(2,1)S(1)} custom-call(bf16[512,512]{1,0:T(8,128)(2,1)S(1)} %get-tuple-element.41.lat_ref, bf16[3,512,1024]{2,1,0:T(8,128)(2,1)S(1)} %get-tuple-element.40.err_ref, f32[512,512]{1,0:T(8,128)S(1)} %get-tuple-element.48.after_ref.sum_ref), custom_call_target="tpu_custom_call" | custom-call | flops 1610612736 | bytes 7000000 | tf_op jit(solution)/shard_map/dec_sib/pallas_call | solution.py:27
  131.7 0.9 collective-permute-start.19
  132.6 3.0 %collective-permute-start.20 = (bf16[512,512]{1,0:T(8,128)(2,1)S(1)}, bf16[512,512]{1,0:T(8,128)(2,1)S(1)}, u32[]{:S(2)}, u32[]{:S(2)}) collective-permute-start(bf16[512,512]{1,0:T(8,128)(2,1)S(1)} %get-tuple-element.47), channel_id=1, source_target_pairs={{0,96},{1,33},{32,64},{33,1},{64,32},{65,97},{96,0},{97,65},{2,98}... | collective-permute-start | bytes 1572872 | tf_op jit(solution)/shard_map/ppermute | solution.py:458
  135.5 2.3 %collective-permute-done.19.got_ref = bf16[3,512,1024]{2,1,0:T(8,128)(2,1)S(1)} collective-permute-done((bf16[3,512,1024]{2,1,0:T(8,128)(2,1)S(1)}, bf16[3,512,1024]{2,1,0:T(8,128)(2,1)S(1)}, u32[]{:S(2)}, u32[]{:S(2)}) %collective-permute-start.19) | collective-permute-done | bytes 3145760 | tf_op jit(solution)/shard_map/ppermute | solution.py:449
  137.8 6.0 %dec_grad.1 = (bf16[3,512,2048]{2,1,0:T(8,128)(2,1)}, f32[8,128]{1,0:T(8,128)S(1)}) custom-call(s32[5]{0:T(128)S(1)} %copy-done.4, bf16[512,512]{1,0:T(8,128)(2,1)S(1)} %get-tuple-element.38.lat_ref, bf16[3,512,1024]{2,1,0:T(8,128)(2,1)S(1)} %get-tuple-element.40.err_ref, bf16[3,512,1024]{2,1,0:T(8,128)(2,1)S(1)} %collective-permute-done.19.got_ref), custom_call_target="tpu_custom_call" | custom-call | flops 1610612736 | bytes 13000000 | tf_op jit(solution)/shard_map/dec_grad/pallas_call | solution.py:27
  143.8 3.2 %enc_grad.1 = (bf16[2048,512]{1,0:T(8,128)(2,1)}, f32[1,512]{1,0:T(1,128)}) custom-call(bf16[2048,512]{1,0:T(8,128)(2,1)S(1)} %get-tuple-element.37.x_ref, s32[512,512]{1,0:T(8,128)S(1)} %copy-done.2, f32[8,128]{1,0:T(8,128)S(1)} %get-tuple-element.43.after_ref, f32[512,512]{1,0:T(8,128)S(1)} %get-tuple-element.48.after_ref.sum_ref, ...), custom_call_target="tpu_custom_call" | custom-call | flops 1073741824 | bytes 7000000 | tf_op jit(solution)/shard_map/enc_grad/pallas_call | solution.py:27
  (29 shorter events, 0.4 us)
Async XLA Ops:
  1.3 29.4 %copy-start.2 = (s32[512,512]{1,0:T(8,128)S(1)}, s32[512,512]{1,0:T(8,128)}, u32[]{:S(2)}) copy-start(s32[512,512]{1,0:T(8,128)} %active_ref.1) | copy-start | bytes 3145732
  1.3 29.4 %copy-start.5 = (f32[512]{0:T(512)S(1)}, f32[512]{0:T(512)}, u32[]{:S(2)}) copy-start(f32[512]{0:T(512)} %param.8) | copy-start | bytes 6148
  8.5 25.5 %copy-start.4 = (s32[5]{0:T(128)S(1)}, s32[5]{0:T(128)}, u32[]{:S(2)}) copy-start(s32[5]{0:T(128)} %stack.23.p_ref) | copy-start | bytes 64
  8.5 25.5 %collective-permute-start.4 = (bf16[3,512,1024]{2,1,0:T(8,128)(2,1)}, bf16[3,512,1024]{2,1,0:T(8,128)(2,1)S(1)}, u32[]{:S(2)}, u32[]{:S(2)}) collective-permute-start(bf16[3,512,1024]{2,1,0:T(8,128)(2,1)} %get-tuple-element.28), channel_id=1, source_target_pairs={{0,1},{1,0},{2,3},{3,2},{4,5},{5,4},{6,7},{7,6},{8,9},{9,8},{10,11... | collective-permute-start | bytes 9437192 | tf_op jit(solution)/shard_map/ppermute | solution.py:449
  8.6 9.5 %collective-permute-start = (bf16[512,512]{1,0:T(8,128)(2,1)}, bf16[512,512]{1,0:T(8,128)(2,1)S(1)}, u32[]{:S(2)}, u32[]{:S(2)}) collective-permute-start(bf16[512,512]{1,0:T(8,128)(2,1)} %get-tuple-element.25), channel_id=1, source_target_pairs={{0,32},{1,97},{32,0},{33,65},{64,96},{65,33},{96,64},{97,1},{2,34}... | collective-permute-start | bytes 1572872 | tf_op jit(solution)/shard_map/ppermute | solution.py:458
  19.3 11.4 %collective-permute-start.1 = (bf16[512,512]{1,0:T(8,128)(2,1)S(1)}, bf16[512,512]{1,0:T(8,128)(2,1)S(1)}, u32[]{:S(2)}, u32[]{:S(2)}) collective-permute-start(bf16[512,512]{1,0:T(8,128)(2,1)S(1)} %fusion), channel_id=1, source_target_pairs={{0,96},{1,33},{32,64},{33,1},{64,32},{65,97},{96,0},{97,65},{2,98}... | collective-permute-start | bytes 1572872 | tf_op jit(solution)/shard_map/ppermute | solution.py:458
  32.1 2.0 %collective-permute-start.2 = (bf16[512,512]{1,0:T(8,128)(2,1)S(1)}, bf16[512,512]{1,0:T(8,128)(2,1)S(1)}, u32[]{:S(2)}, u32[]{:S(2)}) collective-permute-start(bf16[512,512]{1,0:T(8,128)(2,1)S(1)} %select_convert_fusion.lat_ref), channel_id=1, source_target_pairs={{0,1},{1,0},{2,3},{3,2},{4,5},{5,4},{6,7},{7,6},{8,9},{9,8},{10,11... | collective-permute-start | bytes 1572872 | tf_op jit(solution)/shard_map/ppermute | solution.py:449
  34.0 2.8 %copy-start = (bf16[3,512,2048]{2,1,0:T(8,128)(2,1)S(1)}, bf16[3,512,2048]{2,1,0:T(8,128)(2,1)}, u32[]{:S(2)}) copy-start(bf16[3,512,2048]{2,1,0:T(8,128)(2,1)} %dec_ref.5) | copy-start | bytes 18874372
  42.1 30.1 %copy-start.6 = (bf16[3,16,1024]{2,1,0:T(8,128)(2,1)S(1)}, bf16[3,16,1024]{2,1,0:T(8,128)(2,1)}, u32[]{:S(2)}) copy-start(bf16[3,16,1024]{2,1,0:T(8,128)(2,1)} %get-tuple-element.27) | copy-start | bytes 294916
  42.1 34.5 %copy-start.3 = (bf16[3,16,1024]{2,1,0:T(8,128)(2,1)S(1)}, bf16[3,16,1024]{2,1,0:T(8,128)(2,1)}, u32[]{:S(2)}) copy-start(bf16[3,16,1024]{2,1,0:T(8,128)(2,1)} %get-tuple-element.26.own_ref) | copy-start | bytes 294916
  42.1 13.3 %collective-permute-start.5 = (bf16[4,3,32,1024]{3,2,1,0:T(8,128)(2,1)S(1)}, bf16[4,3,32,1024]{3,2,1,0:T(8,128)(2,1)S(1)}, u32[]{:S(2)}, u32[]{:S(2)}) collective-permute-start(bf16[4,3,32,1024]{3,2,1,0:T(8,128)(2,1)S(1)} %get-tuple-element.30), channel_id=1, source_target_pairs={{0,8},{1,3},{2,10},{3,5},{4,12},{5,7},{6,14},{7,1},{8,16},{9,11},{... | collective-permute-start | bytes 2359304 | tf_op jit(solution)/shard_map/ppermute | solution.py:474
  43.6 21.1 %collective-permute-start.6 = (bf16[4,3,32,1024]{3,2,1,0:T(8,128)(2,1)S(1)}, bf16[4,3,32,1024]{3,2,1,0:T(8,128)(2,1)S(1)}, u32[]{:S(2)}, u32[]{:S(2)}) collective-permute-start(bf16[4,3,32,1024]{3,2,1,0:T(8,128)(2,1)S(1)} %get-tuple-element.31), channel_id=1, source_target_pairs={{0,16},{1,5},{2,18},{3,7},{4,20},{5,1},{6,22},{7,3},{8,24},{9,13},... | collective-permute-start | bytes 2359304 | tf_op jit(solution)/shard_map/ppermute | solution.py:474
  46.4 18.4 %collective-permute-start.7 = (bf16[4,3,32,1024]{3,2,1,0:T(8,128)(2,1)S(1)}, bf16[4,3,32,1024]{3,2,1,0:T(8,128)(2,1)S(1)}, u32[]{:S(2)}, u32[]{:S(2)}) collective-permute-start(bf16[4,3,32,1024]{3,2,1,0:T(8,128)(2,1)S(1)} %get-tuple-element.32), channel_id=1, source_target_pairs={{0,24},{1,7},{2,26},{3,1},{4,28},{5,3},{6,30},{7,5},{8,0},{9,15},{... | collective-permute-start | bytes 2359304 | tf_op jit(solution)/shard_map/ppermute | solution.py:474
  64.8 38.4 %copy-start.1 = (bf16[512,2048]{1,0:T(8,128)(2,1)S(1)}, bf16[512,2048]{1,0:T(8,128)(2,1)}, u32[]{:S(2)}) copy-start(bf16[512,2048]{1,0:T(8,128)(2,1)} %x_ref.3) | copy-start | bytes 6291460
  66.2 7.2 %collective-permute-start.8 = (bf16[3,32,1024]{2,1,0:T(8,128)(2,1)S(1)}, bf16[3,32,1024]{2,1,0:T(8,128)(2,1)S(1)}, u32[]{:S(2)}, u32[]{:S(2)}) collective-permute-start(bf16[3,32,1024]{2,1,0:T(8,128)(2,1)S(1)} %get-tuple-element.34), channel_id=1, source_target_pairs={{0,2},{1,9},{2,4},{3,11},{4,6},{5,13},{6,0},{7,15},{8,10},{9,17},{... | collective-permute-start | bytes 589832 | tf_op jit(solution)/shard_map/ppermute | solution.py:474
  67.9 8.7 %collective-permute-start.9 = (bf16[3,32,1024]{2,1,0:T(8,128)(2,1)S(1)}, bf16[3,32,1024]{2,1,0:T(8,128)(2,1)S(1)}, u32[]{:S(2)}, u32[]{:S(2)}) collective-permute-start(bf16[3,32,1024]{2,1,0:T(8,128)(2,1)S(1)} %get-tuple-element.35), channel_id=1, source_target_pairs={{0,4},{1,17},{2,6},{3,19},{4,0},{5,21},{6,2},{7,23},{8,12},{9,25},... | collective-permute-start | bytes 589832 | tf_op jit(solution)/shard_map/ppermute | solution.py:474
  70.8 5.8 %collective-permute-start.10 = (bf16[3,32,1024]{2,1,0:T(8,128)(2,1)S(1)}, bf16[3,32,1024]{2,1,0:T(8,128)(2,1)S(1)}, u32[]{:S(2)}, u32[]{:S(2)}) collective-permute-start(bf16[3,32,1024]{2,1,0:T(8,128)(2,1)S(1)} %get-tuple-element.36), channel_id=1, source_target_pairs={{0,6},{1,25},{2,0},{3,27},{4,2},{5,29},{6,4},{7,31},{8,14},{9,1},{... | collective-permute-start | bytes 589832 | tf_op jit(solution)/shard_map/ppermute | solution.py:474
  72.1 1.3 collective-permute-start.3
  76.5 39.8 %slice-start = ((s8[6291456]{0:T(1024)(128)(4,1)}), s8[4194304]{0:T(1024)(128)(4,1)S(1)}, s32[]{:S(2)}) async-start(s8[6291456]{0:T(1024)(128)(4,1)} %bitcast.6), calls=%async_computation | async-start | bytes 8388608
  77.3 7.9 %collective-permute-start.13 = (bf16[3,32,1024]{2,1,0:T(8,128)(2,1)S(1)}, bf16[3,32,1024]{2,1,0:T(8,128)(2,1)S(1)}, u32[]{:S(2)}, u32[]{:S(2)}) collective-permute-start(bf16[3,32,1024]{2,1,0:T(8,128)(2,1)S(1)} %error.1.refs_0_), channel_id=1, source_target_pairs={{0,6},{1,25},{2,0},{3,27},{4,2},{5,29},{6,4},{7,31},{8,14},{9,1},{... | collective-permute-start | bytes 589832 | tf_op jit(solution)/shard_map/ppermute | solution.py:474
  79.8 7.3 %collective-permute-start.12 = (bf16[3,32,1024]{2,1,0:T(8,128)(2,1)S(1)}, bf16[3,32,1024]{2,1,0:T(8,128)(2,1)S(1)}, u32[]{:S(2)}, u32[]{:S(2)}) collective-permute-start(bf16[3,32,1024]{2,1,0:T(8,128)(2,1)S(1)} %error.1.refs_0_), channel_id=1, source_target_pairs={{0,4},{1,17},{2,6},{3,19},{4,0},{5,21},{6,2},{7,23},{8,12},{9,25},... | collective-permute-start | bytes 589832 | tf_op jit(solution)/shard_map/ppermute | solution.py:474
  81.1 8.1 %collective-permute-start.11 = (bf16[3,32,1024]{2,1,0:T(8,128)(2,1)S(1)}, bf16[3,32,1024]{2,1,0:T(8,128)(2,1)S(1)}, u32[]{:S(2)}, u32[]{:S(2)}) collective-permute-start(bf16[3,32,1024]{2,1,0:T(8,128)(2,1)S(1)} %error.1.refs_0_), channel_id=1, source_target_pairs={{0,2},{1,9},{2,4},{3,11},{4,6},{5,13},{6,0},{7,15},{8,10},{9,17},{... | collective-permute-start | bytes 589832 | tf_op jit(solution)/shard_map/ppermute | solution.py:474
  89.8 26.5 %slice-start.1 = ((s8[6291456]{0:T(1024)(128)(4,1)}), s8[2097152]{0:T(1024)(128)(4,1)S(1)}, s32[]{:S(2)}) async-start(s8[6291456]{0:T(1024)(128)(4,1)} %bitcast.6), calls=%async_computation.1 | async-start | bytes 4194304
  89.9 13.3 %collective-permute-start.14 = (bf16[4,3,32,1024]{3,2,1,0:T(8,128)(2,1)S(1)}, bf16[4,3,32,1024]{3,2,1,0:T(8,128)(2,1)S(1)}, u32[]{:S(2)}, u32[]{:S(2)}) collective-permute-start(bf16[4,3,32,1024]{3,2,1,0:T(8,128)(2,1)S(1)} %join.1.refs_0_), channel_id=1, source_target_pairs={{0,8},{1,3},{2,10},{3,5},{4,12},{5,7},{6,14},{7,1},{8,16},{9,11},{... | collective-permute-start | bytes 2359304 | tf_op jit(solution)/shard_map/ppermute | solution.py:474
  92.9 12.0 %collective-permute-start.16 = (bf16[4,3,32,1024]{3,2,1,0:T(8,128)(2,1)S(1)}, bf16[4,3,32,1024]{3,2,1,0:T(8,128)(2,1)S(1)}, u32[]{:S(2)}, u32[]{:S(2)}) collective-permute-start(bf16[4,3,32,1024]{3,2,1,0:T(8,128)(2,1)S(1)} %join.1.refs_0_), channel_id=1, source_target_pairs={{0,24},{1,7},{2,26},{3,1},{4,28},{5,3},{6,30},{7,5},{8,0},{9,15},{... | collective-permute-start | bytes 2359304 | tf_op jit(solution)/shard_map/ppermute | solution.py:474
  93.2 19.6 %collective-permute-start.15 = (bf16[4,3,32,1024]{3,2,1,0:T(8,128)(2,1)S(1)}, bf16[4,3,32,1024]{3,2,1,0:T(8,128)(2,1)S(1)}, u32[]{:S(2)}, u32[]{:S(2)}) collective-permute-start(bf16[4,3,32,1024]{3,2,1,0:T(8,128)(2,1)S(1)} %join.1.refs_0_), channel_id=1, source_target_pairs={{0,16},{1,5},{2,18},{3,7},{4,20},{5,1},{6,22},{7,3},{8,24},{9,13},... | collective-permute-start | bytes 2359304 | tf_op jit(solution)/shard_map/ppermute | solution.py:474
  116.2 3.5 %collective-permute-start.17 = (bf16[512,512]{1,0:T(8,128)(2,1)S(1)}, bf16[512,512]{1,0:T(8,128)(2,1)S(1)}, u32[]{:S(2)}, u32[]{:S(2)}) collective-permute-start(bf16[512,512]{1,0:T(8,128)(2,1)S(1)} %get-tuple-element.42), channel_id=1, source_target_pairs={{0,1},{1,0},{2,3},{3,2},{4,5},{5,4},{6,7},{7,6},{8,9},{9,8},{10,11... | collective-permute-start | bytes 1572872 | tf_op jit(solution)/shard_map/ppermute | solution.py:449
  119.9 9.3 %collective-permute-start.18 = (bf16[512,512]{1,0:T(8,128)(2,1)S(1)}, bf16[512,512]{1,0:T(8,128)(2,1)S(1)}, u32[]{:S(2)}, u32[]{:S(2)}) collective-permute-start(bf16[512,512]{1,0:T(8,128)(2,1)S(1)} %fusion.1), channel_id=1, source_target_pairs={{0,32},{1,97},{32,0},{33,65},{64,96},{65,33},{96,64},{97,1},{2,34}... | collective-permute-start | bytes 1572872 | tf_op jit(solution)/shard_map/ppermute | solution.py:458
  131.7 6.2 %collective-permute-start.19 = (bf16[3,512,1024]{2,1,0:T(8,128)(2,1)S(1)}, bf16[3,512,1024]{2,1,0:T(8,128)(2,1)S(1)}, u32[]{:S(2)}, u32[]{:S(2)}) collective-permute-start(bf16[3,512,1024]{2,1,0:T(8,128)(2,1)S(1)} %dec_sib.1), channel_id=1, source_target_pairs={{0,1},{1,0},{2,3},{3,2},{4,5},{5,4},{6,7},{7,6},{8,9},{9,8},{10,11... | collective-permute-start | bytes 9437192 | tf_op jit(solution)/shard_map/ppermute | solution.py:449
  132.6 11.3 %collective-permute-start.20 = (bf16[512,512]{1,0:T(8,128)(2,1)S(1)}, bf16[512,512]{1,0:T(8,128)(2,1)S(1)}, u32[]{:S(2)}, u32[]{:S(2)}) collective-permute-start(bf16[512,512]{1,0:T(8,128)(2,1)S(1)} %get-tuple-element.47), channel_id=1, source_target_pairs={{0,96},{1,33},{32,64},{33,1},{64,32},{65,97},{96,0},{97,65},{2,98}... | collective-permute-start | bytes 1572872 | tf_op jit(solution)/shard_map/ppermute | solution.py:458

commit v4 on v3

--- a/solution.py
+++ b/solution.py
@@ -19,7 +19,7 @@
     return lax.dot_general(a, b, (((ca,), (cb,)), ((), ())), preferred_element_type=F32)
 
 
-def call(body, name, grid, ins, outs, shapes, args, flops, moved, scratch=(), core=None, limit=VMEM_LIMIT):
+def call(body, name, grid, ins, outs, shapes, args, flops, moved, scratch=(), core=None, limit=VMEM_LIMIT, aliases=None):
     spec = dict(grid=grid, in_specs=ins, out_specs=outs, scratch_shapes=list(scratch))
     if core is not None:
         spec = dict(grid_spec=pltpu.PrefetchScalarGridSpec(num_scalar_prefetch=1, **spec))
@@ -34,66 +34,154 @@
             flops=int(flops), bytes_accessed=int(moved), transcendentals=0
         ),
         name=name,
+        input_output_aliases=aliases or {},
         **spec,
     )(*args)
 
 
-def pre_kernel(p_ref, x_ref, w_ref, dec_ref, tgt_ref, part_ref, dec_out, own_ref, sent_ref, acc):
-    k = pl.program_id(0)
-    dec_out[...] = dec_ref[...]
-    part = jnp.dot(x_ref[...], w_ref[...], preferred_element_type=F32)
-
-    @pl.when(k == 0)
-    def _():
-        acc[...] = part
-        half = own_ref.shape[2]
-        for ref, side in ((own_ref, p_ref[2]), (sent_ref, 1 - p_ref[2])):
-            ref[...] = tgt_ref[:, :, pl.ds(pl.multiple_of(side * half, half), half)]
-
-    @pl.when(k > 0)
-    def _():
-        acc[...] += part
-
-    @pl.when(k == pl.num_programs(0) - 1)
-    def _():
-        part_ref[...] = acc[...].astype(BF)
+STEPS = 4
+
+
+def pre_kernel(p_ref, x_ref, w_ref, dec_ref, tgt_ref, a_ref, b_ref, *refs):
+    outs, (x_buf, w_buf, acc, sems) = refs[:3], refs[3:]
+    depth = x_ref.shape[1]
+    step = depth // STEPS
+    half = outs[0].shape[2]
+    copies = []
+    for k in range(STEPS):
+        at = slice(k * step, (k + 1) * step)
+        copies.append(pltpu.make_async_copy(w_ref.at[at, :], w_buf.at[at, :], sems.at[2 * k]))
+        copies.append(pltpu.make_async_copy(x_ref.at[:, at], x_buf.at[:, at], sems.at[2 * k + 1]))
+    sides = ((dec_ref, 1 - p_ref[2]), (tgt_ref, p_ref[2]), (tgt_ref, 1 - p_ref[2]))
+    for i, ((src, side), to) in enumerate(zip(sides, outs)):
+        at = pl.ds(pl.multiple_of(side * half, half), half)
+        copies.append(pltpu.make_async_copy(src.at[:, :, at], to, sems.at[2 * STEPS + i]))
+    for copy in copies:
+        copy.start()
+    for k in range(STEPS):
+        copies[2 * k].wait()
+        copies[2 * k + 1].wait()
+        at = slice(k * step, (k + 1) * step)
+        part = jnp.dot(x_buf[:, at], w_buf[at, :], preferred_element_type=F32)
+        if k == 0:
+            acc[...] = part
+        else:
+            acc[...] += part
+    n = a_ref.shape[0]
+    a_ref[...] = acc[:n, :].astype(BF)
+    b_ref[...] = acc[n:, :].astype(BF)
+    for copy in copies[2 * STEPS :]:
+        copy.wait()
 
 
 def pre_call(place, x, w, dec, target):
     rows, depth = x.shape
     lats = w.shape[1]
     targets, few, wide = target.shape
-    half = wide // 2
-    step = 512
-    steps = depth // step
-    goal = pl.BlockSpec((targets, few, half), lambda k, p: (0, 0, 0))
+    outs = [jax.ShapeDtypeStruct((rows // 2, lats), BF)] * 2
+    outs += [jax.ShapeDtypeStruct((targets, lats, wide // 2), BF)]
+    outs += [jax.ShapeDtypeStruct((targets, few, wide // 2), BF)] * 2
     return call(
         pre_kernel,
         "pre",
-        (steps,),
-        [
-            pl.BlockSpec((rows, step), lambda k, p: (0, k)),
-            pl.BlockSpec((step, lats), lambda k, p: (k, 0)),
-            pl.BlockSpec((targets, lats // steps, half), lambda k, p: (0, k, 1 - p[2])),
-            pl.BlockSpec((targets, few, wide), lambda k, p: (0, 0, 0)),
-        ],
-        [
-            pl.BlockSpec((rows, lats), lambda k, p: (0, 0)),
-            pl.BlockSpec((targets, lats // steps, half), lambda k, p: (0, k, 0)),
-            goal,
-            goal,
-        ],
-        [
-            jax.ShapeDtypeStruct((rows, lats), BF),
-            jax.ShapeDtypeStruct((targets, lats, half), BF),
-        ]
-        + [jax.ShapeDtypeStruct((targets, few, half), BF)] * 2,
+        (1,),
+        [pl.BlockSpec(memory_space=pl.ANY)] * 4,
+        [pl.BlockSpec(o.shape, lambda i, p, n=len(o.shape): (0,) * n) for o in outs],
+        outs,
         (x, w, dec, target),
         2 * rows * depth * lats,
         2 * (rows + lats) * depth,
-        [pltpu.VMEM((rows, lats), F32)],
+        [
+            pltpu.VMEM((rows, depth), BF),
+            pltpu.VMEM((depth, lats), BF),
+            pltpu.VMEM((rows, lats), F32),
+            pltpu.SemaphoreType.DMA((2 * STEPS + 3,)),
+        ],
         core=place,
         limit=PRE_LIMIT,
+    )
+
+
+def total_kernel(own_ref, got_ref, err_ref, sum_ref, low_ref, same_ref):
+    total = own_ref[...] + got_ref[...].astype(F32)
+    sum_ref[...] = total
+    low_ref[...] = total.astype(BF)
+
+
+def total_call(own, got, err):
+    whole = pl.BlockSpec(own.shape, lambda i: (0, 0))
+    return call(
+        total_kernel,
+        "total",
+        (1,),
+        [whole, whole, pl.BlockSpec(memory_space=pl.ANY)],
+        [whole, whole, pl.BlockSpec(memory_space=pl.ANY)],
+        [
+            jax.ShapeDtypeStruct(own.shape, F32),
+            jax.ShapeDtypeStruct(own.shape, BF),
+            jax.ShapeDtypeStruct(err.shape, BF),
+        ],
+        (own, got, err),
+        own.size,
+        12 * own.size,
+        aliases={2: 2},
+    )
+
+
+def latent_kernel(near_a, far_a, near_b, far_b, active_ref, bias_ref, after_ref, out_ref):
+    rows = near_a.shape[0]
+    for r, (near, far) in enumerate(((near_a, far_a), (near_b, far_b))):
+        at = slice(r * rows, (r + 1) * rows)
+        total = near[...] + far[...].astype(F32) + bias_ref[...]
+        out_ref[at, :] = jnp.where(active_ref[at, :] > 0, total, 0.0).astype(BF)
+
+
+def latent_call(top, bottom, active, bias, after):
+    rows, lats = active.shape
+    part = pl.BlockSpec((rows // 2, lats), lambda i: (0, 0))
+    whole = pl.BlockSpec((rows, lats), lambda i: (0, 0))
+    return call(
+        latent_kernel,
+        "latents",
+        (1,),
+        [part] * 4
+        + [whole, pl.BlockSpec((1, lats), lambda i: (0, 0)), pl.BlockSpec(memory_space=pl.ANY)],
+        whole,
+        jax.ShapeDtypeStruct((rows, lats), BF),
+        (*top, *bottom, active, bias.reshape(1, lats), after),
+        4 * rows * lats,
+        4e6,
+    )
+
+
+def pick_kernel(p_ref, dec_ref, after_ref, out_ref, done_ref):
+    out_ref[...] = dec_ref[...]
+    done_ref[...] = jnp.zeros(done_ref.shape, F32)
+
+
+def pick_call(place, dec, after):
+    targets, lats, wide = dec.shape
+    half = wide // 2
+    return call(
+        pick_kernel,
+        "pick_half",
+        (targets,),
+        [
+            pl.BlockSpec((1, lats, half), lambda t, p: (t, 0, p[2])),
+            pl.BlockSpec(memory_space=pl.ANY),
+        ],
+        [
+            pl.BlockSpec((1, lats, half), lambda t, p: (t, 0, 0)),
+            pl.BlockSpec((8, 128), lambda t, p: (0, 0)),
+        ],
+        [
+            jax.ShapeDtypeStruct((targets, lats, half), BF),
+            jax.ShapeDtypeStruct((8, 128), F32),
+        ],
+        (dec, after),
+        0,
+        4 * targets * lats * half,
+        core=place,
     )
 
 
@@ -102,20 +190,27 @@
 
 
 def rebuild_kernel(p_ref, lat_ref, sib_ref, dec_ref, got_ref, *refs):
-    outs, held = refs[:SIDE], refs[SIDE]
+    outs, held = refs[:-1], refs[-1]
     total = jnp.dot(lat_ref[...], dec_ref[0], preferred_element_type=F32)
     total += jnp.dot(sib_ref[...], got_ref[0], preferred_element_type=F32)
     held[...] = total.reshape(held.shape)
-    for k in range(SIDE):
-        to = lax.rem(p_ref[3] + k, SIDE)
+    q = held.shape[2] // 2
+    for ref, (step, lo, hi) in zip(outs, CUTS):
+        to = lax.rem(p_ref[3] + step, SIDE)
         for i in range(SIDE):
-            outs[k][i, 0] = held[place_of(p_ref, to, i)].astype(outs[k].dtype)
+            block = held[place_of(p_ref, to, i)]
+            ref[i, 0] = block[:, lo * q : hi * q].astype(ref.dtype)
+
+
+CUTS = ((2, 0, 1), (2, 1, 2), (1, 0, 1), (1, 1, 2), (3, 0, 1), (3, 1, 2), (0, 0, 2))
+KINDS = (BF, BF, F32, BF, BF, F32, F32)
 
 
 def rebuild_call(place, lat, sib, dec, got):
     rows, lats = lat.shape
     targets, _, half = got.shape
     piece = rows // (SIDE * SIDE)
+    widths = [(hi - lo) * half // 2 for _, lo, hi in CUTS]
     whole = pl.BlockSpec((rows, lats), lambda t, p: (0, 0))
     return call(
         rebuild_kernel,
@@ -124,13 +219,13 @@
         [
             whole,
             whole,
-            pl.BlockSpec((1, lats, half), lambda t, p: (t, 0, p[2])),
             pl.BlockSpec((1, lats, half), lambda t, p: (t, 0, 0)),
-        ],
-        [pl.BlockSpec((SIDE, 1, piece, half), lambda t, p: (0, t, 0, 0))] * SIDE,
-        [
-            jax.ShapeDtypeStruct((SIDE, targets, piece, half), F32 if k == 0 else BF)
-            for k in range(SIDE)
+            pl.BlockSpec((1, lats, half), lambda t, p: (t, 0, 0)),
+        ],
+        [pl.BlockSpec((SIDE, 1, piece, w), lambda t, p: (0, t, 0, 0)) for w in widths],
+        [
+            jax.ShapeDtypeStruct((SIDE, targets, piece, w), kind)
+            for w, kind in zip(widths, KINDS)
         ],
         (lat, sib, dec, got),
         4 * rows * lats * half * targets,
@@ -140,28 +235,32 @@
     )
 
 
-def sum_kernel(p_ref, *refs):
-    parts, outs, held = refs[:SIDE], refs[SIDE : 2 * SIDE], refs[2 * SIDE]
-    total = parts[0][:, 0]
-    for part in parts[1:]:
-        total += part[:, 0].astype(F32)
-    held[...] = total
+def sum_kernel(p_ref, own_ref, *refs):
+    parts, outs, held = refs[:4], refs[4:-1], refs[-1]
+    q = held.shape[2] // 2
+    for h in range(2):
+        cols = slice(h * q, (h + 1) * q)
+        total = own_ref[:, 0, :, cols]
+        for part in parts[2 * h : 2 * h + 2]:
+            total += part[:, 0].astype(F32)
+        held[:, :, cols] = total
     for k in range(SIDE):
         outs[k][0] = held[lax.rem(p_ref[4] + k, SIDE)].astype(outs[k].dtype)
 
 
-def sum_call(place, parts):
-    _, targets, piece, half = parts[0].shape
+def sum_call(place, own, parts):
+    _, targets, piece, half = own.shape
+    block = pl.BlockSpec((SIDE, 1, piece, half // 2), lambda t, p: (0, t, 0, 0))
     return call(
         sum_kernel,
         "sum_first",
         (targets,),
-        [pl.BlockSpec((SIDE, 1, piece, half), lambda t, p: (0, t, 0, 0))] * SIDE,
+        [pl.BlockSpec((SIDE, 1, piece, half), lambda t, p: (0, t, 0, 0))] + [block] * 4,
         [pl.BlockSpec((1, piece, half), lambda t, p: (t, 0, 0))] * SIDE,
         [jax.ShapeDtypeStruct((targets, piece, half), F32 if k == 0 else BF) for k in range(SIDE)],
-        tuple(parts),
-        4 * parts[0].size,
-        12 * parts[0].size,
+        (own, *parts),
+        4 * own.size,
+        12 * own.size,
         [pltpu.VMEM((SIDE, piece, half), F32)],
         core=place,
     )
@@ -198,9 +297,12 @@
 
 
 def join_kernel(p_ref, *refs):
-    parts, out_ref = refs[:SIDE], refs[SIDE]
+    parts, outs = refs[:SIDE], refs[SIDE:]
+    q = outs[0].shape[3]
     for k in range(SIDE):
-        out_ref[lax.rem(p_ref[4] + SIDE - k, SIDE), 0] = parts[k][0]
+        at = lax.rem(p_ref[4] + SIDE - k, SIDE)
+        for h in range(2):
+            outs[h][at, 0] = parts[k][0, :, h * q : (h + 1) * q]
 
 
 def join_call(place, parts):
@@ -210,8 +312,8 @@
         "join",
         (targets,),
         [pl.BlockSpec((1, piece, half), lambda t, p: (t, 0, 0))] * SIDE,
-        pl.BlockSpec((SIDE, 1, piece, half), lambda t, p: (0, t, 0, 0)),
-        jax.ShapeDtypeStruct((SIDE, targets, piece, half), BF),
+        [pl.BlockSpec((SIDE, 1, piece, half // 2), lambda t, p: (0, t, 0, 0))] * 2,
+        [jax.ShapeDtypeStruct((SIDE, targets, piece, half // 2), BF)] * 2,
         tuple(parts),
         0,
         8 * parts[0].size,
@@ -237,19 +339,20 @@
 
 
 def back_sib_kernel(p_ref, dec_ref, after_ref, *refs):
-    parts, (err_ref, out_ref, acc) = refs[:SIDE], refs[SIDE:]
-    piece = parts[0].shape[2]
+    parts, (err_ref, out_ref, acc) = refs[: 2 * SIDE], refs[2 * SIDE :]
+    piece, q = parts[0].shape[2:]
     for k in range(SIDE):
         far = lax.rem(p_ref[3] + SIDE - k, SIDE)
         for i in range(SIDE):
             at = pl.ds(pl.multiple_of(place_of(p_ref, far, i) * piece, piece), piece)
-            err_ref[0, at, :] = parts[k][i, 0]
+            for h in range(2):
+                err_ref[0, at, h * q : (h + 1) * q] = parts[2 * k + h][i, 0]
     back_dot(err_ref[0], dec_ref, out_ref, acc)
 
 
 def back_sib_call(place, parts, dec, after):
-    _, targets, piece, half = parts[0].shape
-    lats = dec.shape[1]
+    _, targets, piece, q = parts[0].shape
+    lats, half = dec.shape[1:]
     rows = SIDE * SIDE * piece
     return call(
         back_sib_kernel,
@@ -259,7 +362,7 @@
             pl.BlockSpec((1, lats, half), lambda t, p: (t, 0, 0)),
             pl.BlockSpec(memory_space=pl.ANY),
         ]
-        + [pl.BlockSpec((SIDE, 1, piece, half), lambda t, p: (0, t, 0, 0))] * SIDE,
+        + [pl.BlockSpec((SIDE, 1, piece, q), lambda t, p: (0, t, 0, 0))] * (2 * SIDE),
         [
             pl.BlockSpec((1, rows, half), lambda t, p: (t, 0, 0)),
             pl.BlockSpec((rows, lats), lambda t, p: (0, 0)),
@@ -289,7 +392,7 @@
         (targets,),
         [
             pl.BlockSpec((1, rows, half), lambda t, p: (t, 0, 0)),
-            pl.BlockSpec((1, lats, half), lambda t, p: (t, 0, p[2])),
+            pl.BlockSpec((1, lats, half), lambda t, p: (t, 0, 0)),
         ],
         pl.BlockSpec((rows, lats), lambda t, p: (0, 0)),
         jax.ShapeDtypeStruct((rows, lats), F32),
@@ -301,17 +404,16 @@
     )
 
 
-def turn_kernel(x_ref, lat_ref, sib_ref, after_ref, x_out, lat_out, sib_out, done_ref):
+def turn_kernel(x_ref, lat_ref, after_ref, x_out, lat_out, done_ref):
     done_ref[...] = jnp.zeros(done_ref.shape, F32)
     x_out[...] = x_ref[...].T
 
     @pl.when(pl.program_id(0) == 0)
     def _():
         lat_out[...] = lat_ref[...].T
-        sib_out[...] = sib_ref[...].T
-
-
-def turn_call(x, lat, sib, after):
+
+
+def turn_call(x, lat, after):
     rows, depth = x.shape
     lats = lat.shape[1]
     step = 512
@@ -324,45 +426,19 @@
         [
             pl.BlockSpec((rows, step), lambda i: (0, i)),
             whole,
-            whole,
             pl.BlockSpec(memory_space=pl.ANY),
         ],
         [
             pl.BlockSpec((step, rows), lambda i: (i, 0)),
             turned,
-            turned,
             pl.BlockSpec((8, 128), lambda i: (0, 0)),
         ],
         [jax.ShapeDtypeStruct((depth, rows), BF)]
-        + [jax.ShapeDtypeStruct((lats, rows), BF)] * 2
+        + [jax.ShapeDtypeStruct((lats, rows), BF)]
         + [jax.ShapeDtypeStruct((8, 128), F32)],
-        (x, lat, sib, after),
+        (x, lat, after),
         0,
         6e6,
-    )
-
-
-def dec_sib_kernel(lat_ref, err_ref, after_ref, out_ref):
-    out_ref[0] = dot(lat_ref[...], err_ref[0], 1, 0).astype(BF)
-
-
-def dec_sib_call(lat, err, after):
-    targets, rows, half = err.shape
-    lats = lat.shape[0]
-    return call(
-        dec_sib_kernel,
-        "dec_sib",
-        (targets,),
-        [
-            pl.BlockSpec((lats, rows), lambda t: (0, 0)),
-            pl.BlockSpec((1, rows, half), lambda t: (t, 0, 0)),
-            pl.BlockSpec(memory_space=pl.ANY),
-        ],
-        pl.BlockSpec((1, lats, half), lambda t: (t, 0, 0)),
-        jax.ShapeDtypeStruct((targets, lats, half), BF),
-        (lat, err, after),
-        2 * rows * lats * half * targets,
-        7e6,
     )
 
 
@@ -376,7 +452,7 @@
 
     @pl.when(j == 1)
     def _():
-        out_ref[...] = got_ref[...]
+        out_ref[0] = dot(lat_ref[...], got_ref[0], 1, 0).astype(BF)
 
 
 def dec_call(place, lat, err, got):
@@ -389,7 +465,7 @@
         [
             pl.BlockSpec((lats, rows), lambda t, j, p: (0, 0)),
             pl.BlockSpec((1, rows, half), lambda t, j, p: (t, 0, 0)),
-            pl.BlockSpec((1, lats, half), lambda t, j, p: (t, 0, 0)),
+            pl.BlockSpec((1, rows, half), lambda t, j, p: (t, 0, 0)),
         ],
         [
             pl.BlockSpec((1, lats, half), lambda t, j, p: (t, 0, (j + p[2]) % 2)),
@@ -400,7 +476,7 @@
             jax.ShapeDtypeStruct((8, 128), F32),
         ],
         (lat, err, got),
-        2 * rows * lats * half * targets,
+        4 * rows * lats * half * targets,
         13e6,
         core=place,
     )
@@ -458,8 +534,8 @@
     return lax.ppermute(value, ("z", "c"), moves)
 
 
-def z_sum(part):
-    first = part.astype(F32) + pair(part.astype(BF), (EVEN, ODD)).astype(F32)
+def z_sum(part, low):
+    first = part.astype(F32) + pair(low, (EVEN, ODD)).astype(F32)
     return first, pair(first.astype(BF), (ODD, EVEN))
 
 
@@ -474,12 +550,32 @@
     return lax.ppermute(value, ("x", "y", "c"), moves)
 
 
-def scatter(parts, second):
-    return [parts[0]] + [shift(parts[k], second, k) for k in (1, 2, 3)]
-
-
-def spread(value, second):
-    return [value] + [shift(value, second, k) for k in (1, 2, 3)]
+def plus(a, b):
+    return (a + b.astype(F32)).astype(BF)
+
+
+def ring_sum(cuts):
+    far_a, far_b, up_a, up_b, down_a, down_b, own = cuts
+    met_a, met_b = shift(far_a, False, 1), shift(far_b, False, 3)
+    from_b, from_a = shift(up_b, False, 1), shift(down_a, False, 3)
+    ring_a = shift(plus(up_a, met_a), False, 1)
+    ring_b = shift(plus(down_b, met_b), False, 3)
+    return own, (ring_a, from_a, from_b, ring_b)
+
+
+def ring_gather(a, b):
+    below_a, above_b = shift(a, False, 1), shift(b, False, 3)
+    below_b, above_a = shift(b, False, 1), shift(a, False, 3)
+    far_a, far_b = shift(below_a, False, 1), shift(above_b, False, 3)
+    return a, b, below_a, below_b, far_a, far_b, above_a, above_b
+
+
+def scatter(parts):
+    return [parts[0]] + [shift(parts[k], True, k) for k in (1, 2, 3)]
+
+
+def spread(value):
+    return [value] + [shift(value, True, k) for k in (1, 2, 3)]
 
 
 def per_device(mlp_inputs, enc_weight, enc_bias, active, dec_weight, target):
@@ -489,26 +585,27 @@
     place = jnp.stack([x, y, c, first, second]).astype(jnp.int32)
     scale = 1.0 / math.sqrt(rows)
 
-    part, dec_sent, tgt_own, tgt_sent = pre_call(
+    top, bottom, dec_sent, tgt_own, tgt_sent = pre_call(
         place, mlp_inputs, enc_weight, dec_weight, target
     )
+    top, bottom = z_sum(top, top), z_sum(bottom, bottom)
     dec_got = swap(dec_sent)
     tgt_got = swap(tgt_sent)
-    near, far = z_sum(part)
-    lat = jnp.where(active > 0, near + far.astype(F32) + enc_bias, 0.0).astype(BF)
+    dec_own, done = pick_call(place, dec_weight, bottom[0])
+    lat = latent_call(top, bottom, active, enc_bias, done)
     lat_sib = swap(lat)
 
-    parts = scatter(rebuild_call(place, lat, lat_sib, dec_weight, dec_got), False)
-    parts = scatter(sum_call(place, parts), True)
+    own, parts = ring_sum(rebuild_call(place, lat, lat_sib, dec_own, dec_got))
+    parts = scatter(sum_call(place, own, parts))
     err = error_call(scale, place, tgt_own, tgt_got, parts)
-    parts = spread(join_call(place, spread(err, True)), False)
-    x_turned, lat_turned, sib_turned, done = turn_call(mlp_inputs, lat, lat_sib, parts[1])
+    parts = ring_gather(*join_call(place, spread(err)))
+    x_turned, lat_turned, done = turn_call(mlp_inputs, lat, parts[2])
 
     err, grad_got = back_sib_call(place, parts, dec_got, done)
     grad_got = swap(grad_got)
-    near, far = z_sum(back_own_call(place, err, dec_weight) + grad_got.astype(F32))
-    dec_part = swap(dec_sib_call(sib_turned, err, near))
-    dec_grad, done = dec_call(place, lat_turned, err, dec_part)
+    grad, low, err = total_call(back_own_call(place, err, dec_own), grad_got, err)
+    near, far = z_sum(grad, low)
+    dec_grad, done = dec_call(place, lat_turned, err, swap(err))
     enc_grad, bias_grad = enc_call(x_turned, active, done, near, far)
     return enc_grad, bias_grad.reshape(-1), dec_grad
 

time: 149 us -> 129 us (0.87); the launches traced: 147 us -> 129 us
  waiting for transfers between devices: 72.8 us -> 49.7 us
  starting transfers between devices: 32.1 us -> 39.9 us
  Pallas kernels: 34.9 us -> 32.5 us
    ppermute x12 -> x18, waiting for transfers between devices: 43.5 us -> 28.5 us  [shift(): return lax.ppermute(value, ('x', 'y', 'c'), moves)]
    ppermute x12 -> x18, starting transfers between devices: 21.6 us -> 29.1 us  [shift(): return lax.ppermute(value, ('x', 'y', 'c'), moves)]
    ppermute x4 -> x6, waiting for transfers between devices: 23.7 us -> 18 us  [pair(): return lax.ppermute(value, ('z', 'c'), moves)]
    pallas_call x11 -> x13, Pallas kernels: 34.9 us -> 32.5 us  [call(): pl.pallas_call(body, out_shape=shapes, compiler_params=pltpu.CompilerPara...]
    ppermute x5, waiting for transfers between devices: 5.54 us -> 3.2 us  [swap(): return lax.ppermute(value, 'c', [(0, 1), (1, 0)])]
    ppermute x4 -> x6, starting transfers between devices: 9.31 us -> 9.88 us  [pair(): return lax.ppermute(value, ('z', 'c'), moves)]
  transfers between devices with their start and end apart: 21 -> 29, of which waited for: 15 -> 17; matrix products, arithmetic and copies ran while one was open for 2% -> 2% of each run, Pallas kernels for 7% -> 9%
where the time goes in v4:
time: 129 us
  waiting for transfers between devices  49.7 us (39%)
  starting transfers between devices  39.9 us (31%)
  Pallas kernels  32.5 us (25%)
  local copies, waits for them, and re-layouts  3.48 us (3%)
  other arithmetic  2.53 us (2%)
    pallas_call x13, Pallas kernels, call(): pl.pallas_call(body, out_shape=shapes, compiler_params=pltpu.CompilerPara...  32.5 us
    ppermute x18, starting transfers between devices, shift(): return lax.ppermute(value, ('x', 'y', 'c'), moves)  29.1 us
    ppermute x18, waiting for transfers between devices, shift(): return lax.ppermute(value, ('x', 'y', 'c'), moves)  28.5 us
    ppermute x6, waiting for transfers between devices, pair(): return lax.ppermute(value, ('z', 'c'), moves)  18 us
    ppermute x6, starting transfers between devices, pair(): return lax.ppermute(value, ('z', 'c'), moves)  9.88 us
    ppermute x5, waiting for transfers between devices, swap(): return lax.ppermute(value, 'c', [(0, 1), (1, 0)])  3.2 us
    unnamed x14, local copies, waits for them, and re-layouts  2.81 us
  transfers between devices with their start and end apart: 29, of which 17 were waited for; matrix products, arithmetic and copies ran while one was open for 2% of the time, Pallas kernels for 9%

profile of v4, /device:TPU:0, one launch (start us, length us, event | category | flops | bytes accessed | tf_op | source)
XLA Modules:
  0.0 129.0 jit_solution(382107906613437777)
XLA Ops:
  0.6 0.7 stack.23.p_ref
  1.3 6.0 %pre.1 = (bf16[256,512]{1,0:T(8,128)(2,1)}, bf16[256,512]{1,0:T(8,128)(2,1)}, bf16[3,512,1024]{2,1,0:T(8,128)(2,1)}, bf16[3,16,1024]{2,1,0:T(8,128)(2,1)}, bf16[3,16,1024]{2,1,0:T(8,128)(2,1)}) custom-call(s32[5]{0:T(128)} %stack.23.p_ref, bf16[512,2048]{1,0:T(8,128)(2,1)} %x_ref.3, bf16[2048,512]{1,0:T(8,128)(2,1)} %w_ref.1, bf16[3,512,2048]{2,1,0:T(8,128)(2,1)} %dec_ref.3, ...), custom_call_target="tpu_custom_call" | custom-call | flops 1073741824 | bytes 4194304 | tf_op jit(solution)/shard_map/pre/pallas_call | solution.py:27
  7.4 2.1 %collective-permute-start = (bf16[256,512]{1,0:T(8,128)(2,1)}, bf16[256,512]{1,0:T(8,128)(2,1)S(1)}, u32[]{:S(2)}, u32[]{:S(2)}) collective-permute-start(bf16[256,512]{1,0:T(8,128)(2,1)} %get-tuple-element.35), channel_id=1, source_target_pairs={{0,32},{1,97},{32,0},{33,65},{64,96},{65,33},{96,64},{97,1},{2,34}... | collective-permute-start | bytes 786440 | tf_op jit(solution)/shard_map/ppermute | solution.py:534
  9.6 4.5 %collective-permute-done = bf16[256,512]{1,0:T(8,128)(2,1)S(1)} collective-permute-done((bf16[256,512]{1,0:T(8,128)(2,1)}, bf16[256,512]{1,0:T(8,128)(2,1)S(1)}, u32[]{:S(2)}, u32[]{:S(2)}) %collective-permute-start) | collective-permute-done | bytes 262176 | tf_op jit(solution)/shard_map/ppermute | solution.py:534
  14.1 1.0 fusion
  15.1 4.2 %collective-permute-start.1 = (bf16[256,512]{1,0:T(8,128)(2,1)S(1)}, bf16[256,512]{1,0:T(8,128)(2,1)S(1)}, u32[]{:S(2)}, u32[]{:S(2)}) collective-permute-start(bf16[256,512]{1,0:T(8,128)(2,1)S(1)} %get-tuple-element.71), channel_id=1, source_target_pairs={{0,96},{1,33},{32,64},{33,1},{64,32},{65,97},{96,0},{97,65},{2,98}... | collective-permute-start | bytes 786440 | tf_op jit(solution)/shard_map/ppermute | solution.py:534
  19.3 1.0 fusion.1
  20.4 1.8 %collective-permute-start.3 = (bf16[256,512]{1,0:T(8,128)(2,1)S(1)}, bf16[256,512]{1,0:T(8,128)(2,1)S(1)}, u32[]{:S(2)}, u32[]{:S(2)}) collective-permute-start(bf16[256,512]{1,0:T(8,128)(2,1)S(1)} %get-tuple-element.69), channel_id=1, source_target_pairs={{0,96},{1,33},{32,64},{33,1},{64,32},{65,97},{96,0},{97,65},{2,98}... | collective-permute-start | bytes 786440 | tf_op jit(solution)/shard_map/ppermute | solution.py:534
  22.1 2.8 %copy-done = bf16[3,512,2048]{2,1,0:T(8,128)(2,1)S(1)} copy-done((bf16[3,512,2048]{2,1,0:T(8,128)(2,1)S(1)}, bf16[3,512,2048]{2,1,0:T(8,128)(2,1)}, u32[]{:S(2)}) %copy-start) | copy-done | bytes 6291480
  24.9 1.0 pick_half.1
  26.0 2.1 %collective-permute-done.3.far_b = bf16[256,512]{1,0:T(8,128)(2,1)S(1)} collective-permute-done((bf16[256,512]{1,0:T(8,128)(2,1)S(1)}, bf16[256,512]{1,0:T(8,128)(2,1)S(1)}, u32[]{:S(2)}, u32[]{:S(2)}) %collective-permute-start.3) | collective-permute-done | bytes 262176 | tf_op jit(solution)/shard_map/ppermute | solution.py:534
  28.4 1.9 %collective-permute-done.5.sib_ref = bf16[512,512]{1,0:T(8,128)(2,1)S(1)} collective-permute-done((bf16[512,512]{1,0:T(8,128)(2,1)S(1)}, bf16[512,512]{1,0:T(8,128)(2,1)S(1)}, u32[]{:S(2)}, u32[]{:S(2)}) %collective-permute-start.5) | collective-permute-done | bytes 524320 | tf_op jit(solution)/shard_map/ppermute | solution.py:525
  30.3 5.1 %rebuild.1 = (bf16[4,3,32,512]{3,2,1,0:T(8,128)(2,1)S(1)}, bf16[4,3,32,512]{3,2,1,0:T(8,128)(2,1)S(1)}, f32[4,3,32,512]{3,2,1,0:T(8,128)S(1)}, bf16[4,3,32,512]{...) custom-call(s32[5]{0:T(128)S(1)} %copy-done.4, ...), custom_call_target="tpu_custom_call" | custom-call | flops 3221225472 | bytes 11000000 | tf_op jit(solution)/shard_map/rebuild/pallas_call | solution.py:27
  35.3 1.6 %collective-permute-start.7 = (bf16[4,3,32,512]{3,2,1,0:T(8,128)(2,1)S(1)}, bf16[4,3,32,512]{3,2,1,0:T(8,128)(2,1)S(1)}, u32[]{:S(2)}, u32[]{:S(2)}) collective-permute-start(bf16[4,3,32,512]{3,2,1,0:T(8,128)(2,1)S(1)} %get-tuple-element.44), channel_id=1, source_target_pairs={{0,8},{1,3},{2,10},{3,5},{4,12},{5,7},{6,14},{7,1},{8,16},{9,11},{... | collective-permute-start | bytes 1179656 | tf_op jit(solution)/shard_map/ppermute | solution.py:550
  36.9 1.7 %collective-permute-start.11 = (bf16[4,3,32,512]{3,2,1,0:T(8,128)(2,1)S(1)}, bf16[4,3,32,512]{3,2,1,0:T(8,128)(2,1)S(1)}, u32[]{:S(2)}, u32[]{:S(2)}) collective-permute-start(bf16[4,3,32,512]{3,2,1,0:T(8,128)(2,1)S(1)} %get-tuple-element.48), channel_id=1, source_target_pairs={{0,24},{1,7},{2,26},{3,1},{4,28},{5,3},{6,30},{7,5},{8,0},{9,15},{... | collective-permute-start | bytes 1179656 | tf_op jit(solution)/shard_map/ppermute | solution.py:550
  38.6 1.5 %collective-permute-start.9 = (bf16[4,3,32,512]{3,2,1,0:T(8,128)(2,1)S(1)}, bf16[4,3,32,512]{3,2,1,0:T(8,128)(2,1)S(1)}, u32[]{:S(2)}, u32[]{:S(2)}) collective-permute-start(bf16[4,3,32,512]{3,2,1,0:T(8,128)(2,1)S(1)} %get-tuple-element.45), channel_id=1, source_target_pairs={{0,24},{1,7},{2,26},{3,1},{4,28},{5,3},{6,30},{7,5},{8,0},{9,15},{... | collective-permute-start | bytes 1179656 | tf_op jit(solution)/shard_map/ppermute | solution.py:550
  40.7 3.7 %collective-permute-done.7 = bf16[4,3,32,512]{3,2,1,0:T(8,128)(2,1)S(1)} collective-permute-done((bf16[4,3,32,512]{3,2,1,0:T(8,128)(2,1)S(1)}, bf16[4,3,32,512]{3,2,1,0:T(8,128)(2,1)S(1)}, u32[]{:S(2)}, u32[]{:S(2)}) %collective-permute-start.7) | collective-permute-done | bytes 393248 | tf_op jit(solution)/shard_map/ppermute | solution.py:550
  45.0 3.0 %collective-permute-start.12 = (bf16[4,3,32,512]{3,2,1,0:T(8,128)(2,1)S(1)}, bf16[4,3,32,512]{3,2,1,0:T(8,128)(2,1)S(1)}, u32[]{:S(2)}, u32[]{:S(2)}) collective-permute-start(bf16[4,3,32,512]{3,2,1,0:T(8,128)(2,1)S(1)} %add_convert_fusion), channel_id=1, source_target_pairs={{0,24},{1,7},{2,26},{3,1},{4,28},{5,3},{6,30},{7,5},{8,0},{9,15},{... | collective-permute-start | bytes 1179656 | tf_op jit(solution)/shard_map/ppermute | solution.py:550
  48.0 0.8 collective-permute-done.9.refs_1_
  49.2 4.4 %collective-permute-done.8.refs_0_ = bf16[4,3,32,512]{3,2,1,0:T(8,128)(2,1)S(1)} collective-permute-done((bf16[4,3,32,512]{3,2,1,0:T(8,128)(2,1)S(1)}, bf16[4,3,32,512]{3,2,1,0:T(8,128)(2,1)S(1)}, u32[]{:S(2)}, u32[]{:S(2)}) %collective-permute-start.8) | collective-permute-done | bytes 393248 | tf_op jit(solution)/shard_map/ppermute | solution.py:550
  53.6 1.2 sum_first.1
  54.8 1.6 %collective-permute-start.13 = (bf16[3,32,1024]{2,1,0:T(8,128)(2,1)S(1)}, bf16[3,32,1024]{2,1,0:T(8,128)(2,1)S(1)}, u32[]{:S(2)}, u32[]{:S(2)}) collective-permute-start(bf16[3,32,1024]{2,1,0:T(8,128)(2,1)S(1)} %get-tuple-element.50), channel_id=1, source_target_pairs={{0,2},{1,9},{2,4},{3,11},{4,6},{5,13},{6,0},{7,15},{8,10},{9,17},{... | collective-permute-start | bytes 589832 | tf_op jit(solution)/shard_map/ppermute | solution.py:550
  56.5 2.9 %collective-permute-start.14 = (bf16[3,32,1024]{2,1,0:T(8,128)(2,1)S(1)}, bf16[3,32,1024]{2,1,0:T(8,128)(2,1)S(1)}, u32[]{:S(2)}, u32[]{:S(2)}) collective-permute-start(bf16[3,32,1024]{2,1,0:T(8,128)(2,1)S(1)} %get-tuple-element.51), channel_id=1, source_target_pairs={{0,4},{1,17},{2,6},{3,19},{4,0},{5,21},{6,2},{7,23},{8,12},{9,25},... | collective-permute-start | bytes 589832 | tf_op jit(solution)/shard_map/ppermute | solution.py:550
  59.4 1.3 %collective-permute-start.15 = (bf16[3,32,1024]{2,1,0:T(8,128)(2,1)S(1)}, bf16[3,32,1024]{2,1,0:T(8,128)(2,1)S(1)}, u32[]{:S(2)}, u32[]{:S(2)}) collective-permute-start(bf16[3,32,1024]{2,1,0:T(8,128)(2,1)S(1)} %get-tuple-element.52), channel_id=1, source_target_pairs={{0,6},{1,25},{2,0},{3,27},{4,2},{5,29},{6,4},{7,31},{8,14},{9,1},{... | collective-permute-start | bytes 589832 | tf_op jit(solution)/shard_map/ppermute | solution.py:550
  60.7 1.3 %collective-permute-done.4.got_ref = bf16[3,16,1024]{2,1,0:T(8,128)(2,1)S(1)} collective-permute-done((bf16[3,16,1024]{2,1,0:T(8,128)(2,1)S(1)}, bf16[3,16,1024]{2,1,0:T(8,128)(2,1)S(1)}, u32[]{:S(2)}, u32[]{:S(2)}) %collective-permute-start.4) | collective-permute-done | bytes 98336 | tf_op jit(solution)/shard_map/ppermute | solution.py:525
  62.0 3.1 %collective-permute-done.14.refs_2_ = bf16[3,32,1024]{2,1,0:T(8,128)(2,1)S(1)} collective-permute-done((bf16[3,32,1024]{2,1,0:T(8,128)(2,1)S(1)}, bf16[3,32,1024]{2,1,0:T(8,128)(2,1)S(1)}, u32[]{:S(2)}, u32[]{:S(2)}) %collective-permute-start.14) | collective-permute-done | bytes 196640 | tf_op jit(solution)/shard_map/ppermute | solution.py:550
  65.1 0.7 error.1.refs_0_
  65.9 2.5 %collective-permute-start.18 = (bf16[3,32,1024]{2,1,0:T(8,128)(2,1)S(1)}, bf16[3,32,1024]{2,1,0:T(8,128)(2,1)S(1)}, u32[]{:S(2)}, u32[]{:S(2)}) collective-permute-start(bf16[3,32,1024]{2,1,0:T(8,128)(2,1)S(1)} %error.1.refs_0_), channel_id=1, source_target_pairs={{0,6},{1,25},{2,0},{3,27},{4,2},{5,29},{6,4},{7,31},{8,14},{9,1},{... | collective-permute-start | bytes 589832 | tf_op jit(solution)/shard_map/ppermute | solution.py:550
  68.4 1.2 collective-permute-start.17
  70.2 3.5 %collective-permute-done.18.refs_3_ = bf16[3,32,1024]{2,1,0:T(8,128)(2,1)S(1)} collective-permute-done((bf16[3,32,1024]{2,1,0:T(8,128)(2,1)S(1)}, bf16[3,32,1024]{2,1,0:T(8,128)(2,1)S(1)}, u32[]{:S(2)}, u32[]{:S(2)}) %collective-permute-start.18) | collective-permute-done | bytes 196640 | tf_op jit(solution)/shard_map/ppermute | solution.py:550
  73.7 1.9 %collective-permute-done.17.refs_2_ = bf16[3,32,1024]{2,1,0:T(8,128)(2,1)S(1)} collective-permute-done((bf16[3,32,1024]{2,1,0:T(8,128)(2,1)S(1)}, bf16[3,32,1024]{2,1,0:T(8,128)(2,1)S(1)}, u32[]{:S(2)}, u32[]{:S(2)}) %collective-permute-start.17) | collective-permute-done | bytes 196640 | tf_op jit(solution)/shard_map/ppermute | solution.py:550
  75.7 2.0 %collective-permute-done.16.refs_1_ = bf16[3,32,1024]{2,1,0:T(8,128)(2,1)S(1)} collective-permute-done((bf16[3,32,1024]{2,1,0:T(8,128)(2,1)S(1)}, bf16[3,32,1024]{2,1,0:T(8,128)(2,1)S(1)}, u32[]{:S(2)}, u32[]{:S(2)}) %collective-permute-start.16) | collective-permute-done | bytes 196640 | tf_op jit(solution)/shard_map/ppermute | solution.py:550
  77.7 0.7 join.1
  78.4 1.5 %collective-permute-start.19 = (bf16[4,3,32,512]{3,2,1,0:T(8,128)(2,1)S(1)}, bf16[4,3,32,512]{3,2,1,0:T(8,128)(2,1)S(1)}, u32[]{:S(2)}, u32[]{:S(2)}) collective-permute-start(bf16[4,3,32,512]{3,2,1,0:T(8,128)(2,1)S(1)} %get-tuple-element.53.refs_0_), channel_id=1, source_target_pairs={{0,8},{1,3},{2,10},{3,5},{4,12},{5,7},{6,14},{7,1},{8,16},{9,11},{... | collective-permute-start | bytes 1179656 | tf_op jit(solution)/shard_map/ppermute | solution.py:550
  79.9 3.4 %collective-permute-start.22 = (bf16[4,3,32,512]{3,2,1,0:T(8,128)(2,1)S(1)}, bf16[4,3,32,512]{3,2,1,0:T(8,128)(2,1)S(1)}, u32[]{:S(2)}, u32[]{:S(2)}) collective-permute-start(bf16[4,3,32,512]{3,2,1,0:T(8,128)(2,1)S(1)} %get-tuple-element.57.refs_1_), channel_id=1, source_target_pairs={{0,24},{1,7},{2,26},{3,1},{4,28},{5,3},{6,30},{7,5},{8,0},{9,15},{... | collective-permute-start | bytes 1179656 | tf_op jit(solution)/shard_map/ppermute | solution.py:550
  83.3 1.9 %collective-permute-start.24 = (bf16[4,3,32,512]{3,2,1,0:T(8,128)(2,1)S(1)}, bf16[4,3,32,512]{3,2,1,0:T(8,128)(2,1)S(1)}, u32[]{:S(2)}, u32[]{:S(2)}) collective-permute-start(bf16[4,3,32,512]{3,2,1,0:T(8,128)(2,1)S(1)} %get-tuple-element.53.refs_0_), channel_id=1, source_target_pairs={{0,24},{1,7},{2,26},{3,1},{4,28},{5,3},{6,30},{7,5},{8,0},{9,15},{... | collective-permute-start | bytes 1179656 | tf_op jit(solution)/shard_map/ppermute | solution.py:550
  85.3 3.6 %collective-permute-done.19.after_ref.refs_2_ = bf16[4,3,32,512]{3,2,1,0:T(8,128)(2,1)S(1)} collective-permute-done((bf16[4,3,32,512]{3,2,1,0:T(8,128)(2,1)S(1)}, bf16[4,3,32,512]{3,2,1,0:T(8,128)(2,1)S(1)}, u32[]{:S(2)}, u32[]{:S(2)}) %collective-permute-start.19) | collective-permute-done | bytes 393248 | tf_op jit(solution)/shard_map/ppermute | solution.py:550
  89.0 3.3 %collective-permute-start.23 = (bf16[4,3,32,512]{3,2,1,0:T(8,128)(2,1)S(1)}, bf16[4,3,32,512]{3,2,1,0:T(8,128)(2,1)S(1)}, u32[]{:S(2)}, u32[]{:S(2)}) collective-permute-start(bf16[4,3,32,512]{3,2,1,0:T(8,128)(2,1)S(1)} %collective-permute-done.22.refs_7_), channel_id=1, source_target_pairs={{0,24},{1,7},{2,26},{3,1},{4,28},{5,3},{6,30},{7,5},{8,0},{9,15},{... | collective-permute-start | bytes 1179656 | tf_op jit(solution)/shard_map/ppermute | solution.py:550
  92.3 1.1 turn.1
  93.5 0.8 collective-permute-done.20.refs_3_
  94.2 4.2 %collective-permute-done.21.refs_4_ = bf16[4,3,32,512]{3,2,1,0:T(8,128)(2,1)S(1)} collective-permute-done((bf16[4,3,32,512]{3,2,1,0:T(8,128)(2,1)S(1)}, bf16[4,3,32,512]{3,2,1,0:T(8,128)(2,1)S(1)}, u32[]{:S(2)}, u32[]{:S(2)}) %collective-permute-start.21) | collective-permute-done | bytes 393248 | tf_op jit(solution)/shard_map/ppermute | solution.py:550
  98.5 3.5 %back_sib.1 = (bf16[3,512,1024]{2,1,0:T(8,128)(2,1)S(1)}, bf16[512,512]{1,0:T(8,128)(2,1)S(1)}) custom-call(s32[5]{0:T(128)S(1)} %copy-done.4, bf16[3,512,1024]{2,1,0:T(8,128)(2,1)S(1)} %collective-permute-done.6.got_ref.dec_ref, f32[8,128]{1,0:T(8,128)S(1)} %get-tuple-element.56.after_ref, bf16[4,3,32,512]{3,2,1,0:T(8,128)(2,1)S(1)} %get-tuple-element.53.refs_0_, ...), custom_call_target="tpu_custom_call" | custom-call | flops 1610612736 | bytes 10000000 | tf_op jit(solution)/shard_map/back_sib/pallas_call | solution.py:27
  102.1 3.1 %back_own.1.own_ref = f32[512,512]{1,0:T(8,128)S(1)} custom-call(s32[5]{0:T(128)S(1)} %copy-done.4, bf16[3,512,1024]{2,1,0:T(8,128)(2,1)S(1)} %get-tuple-element.58.err_ref, bf16[3,512,1024]{2,1,0:T(8,128)(2,1)S(1)} %get-tuple-element.40.dec_ref), custom_call_target="tpu_custom_call" | custom-call | flops 1610612736 | bytes 7000000 | tf_op jit(solution)/shard_map/back_own/pallas_call | solution.py:27
  105.9 9.2 %collective-permute-done.27 = bf16[512,512]{1,0:T(8,128)(2,1)S(1)} collective-permute-done((bf16[512,512]{1,0:T(8,128)(2,1)S(1)}, bf16[512,512]{1,0:T(8,128)(2,1)S(1)}, u32[]{:S(2)}, u32[]{:S(2)}) %collective-permute-start.27) | collective-permute-done | bytes 524320 | tf_op jit(solution)/shard_map/ppermute | solution.py:534
  115.3 1.8 %collective-permute-start.28 = (bf16[512,512]{1,0:T(8,128)(2,1)S(1)}, bf16[512,512]{1,0:T(8,128)(2,1)S(1)}, u32[]{:S(2)}, u32[]{:S(2)}) collective-permute-start(bf16[512,512]{1,0:T(8,128)(2,1)S(1)} %get-tuple-element.67), channel_id=1, source_target_pairs={{0,96},{1,33},{32,64},{33,1},{64,32},{65,97},{96,0},{97,65},{2,98}... | collective-permute-start | bytes 1572872 | tf_op jit(solution)/shard_map/ppermute | solution.py:534
  117.1 6.4 %dec_grad.1 = (bf16[3,512,2048]{2,1,0:T(8,128)(2,1)}, f32[8,128]{1,0:T(8,128)S(1)}) custom-call(s32[5]{0:T(128)S(1)} %copy-done.4, bf16[512,512]{1,0:T(8,128)(2,1)S(1)} %get-tuple-element.55.lat_ref, bf16[3,512,1024]{2,1,0:T(8,128)(2,1)S(1)} %get-tuple-element.60.err_ref, bf16[3,512,1024]{2,1,0:T(8,128)(2,1)S(1)} %collective-permute-done.26.got_ref), custom_call_target="tpu_custom_call" | custom-call | flops 3221225472 | bytes 13000000 | tf_op jit(solution)/shard_map/dec_grad/pallas_call | solution.py:27
  123.5 2.3 %collective-permute-done.28.got_ref = bf16[512,512]{1,0:T(8,128)(2,1)S(1)} collective-permute-done((bf16[512,512]{1,0:T(8,128)(2,1)S(1)}, bf16[512,512]{1,0:T(8,128)(2,1)S(1)}, u32[]{:S(2)}, u32[]{:S(2)}) %collective-permute-start.28) | collective-permute-done | bytes 524320 | tf_op jit(solution)/shard_map/ppermute | solution.py:534
  125.8 3.2 %enc_grad.1 = (bf16[2048,512]{1,0:T(8,128)(2,1)}, f32[1,512]{1,0:T(1,128)}) custom-call(bf16[2048,512]{1,0:T(8,128)(2,1)S(1)} %get-tuple-element.54.x_ref, s32[512,512]{1,0:T(8,128)S(1)} %copy-done.2, f32[8,128]{1,0:T(8,128)S(1)} %get-tuple-element.61.after_ref, f32[512,512]{1,0:T(8,128)S(1)} %get-tuple-element.68.sum_ref, ...), custom_call_target="tpu_custom_call" | custom-call | flops 1073741824 | bytes 7000000 | tf_op jit(solution)/shard_map/enc_grad/pallas_call | solution.py:27
  (43 shorter events, 3.6 us)
Async XLA Ops:
  1.3 20.8 %copy-start.4 = (s32[5]{0:T(128)S(1)}, s32[5]{0:T(128)}, u32[]{:S(2)}) copy-start(s32[5]{0:T(128)} %stack.23.p_ref) | copy-start | bytes 64
  7.3 23.0 %collective-permute-start.6 = (bf16[3,512,1024]{2,1,0:T(8,128)(2,1)}, bf16[3,512,1024]{2,1,0:T(8,128)(2,1)S(1)}, u32[]{:S(2)}, u32[]{:S(2)}) collective-permute-start(bf16[3,512,1024]{2,1,0:T(8,128)(2,1)} %get-tuple-element.41), channel_id=1, source_target_pairs={{0,1},{1,0},{2,3},{3,2},{4,5},{5,4},{6,7},{7,6},{8,9},{9,8},{10,11... | collective-permute-start | bytes 9437192 | tf_op jit(solution)/shard_map/ppermute | solution.py:525
  7.4 6.7 %collective-permute-start = (bf16[256,512]{1,0:T(8,128)(2,1)}, bf16[256,512]{1,0:T(8,128)(2,1)S(1)}, u32[]{:S(2)}, u32[]{:S(2)}) collective-permute-start(bf16[256,512]{1,0:T(8,128)(2,1)} %get-tuple-element.35), channel_id=1, source_target_pairs={{0,32},{1,97},{32,0},{33,65},{64,96},{65,33},{96,64},{97,1},{2,34}... | collective-permute-start | bytes 786440 | tf_op jit(solution)/shard_map/ppermute | solution.py:534
  9.5 9.8 %collective-permute-start.2 = (bf16[256,512]{1,0:T(8,128)(2,1)}, bf16[256,512]{1,0:T(8,128)(2,1)S(1)}, u32[]{:S(2)}, u32[]{:S(2)}) collective-permute-start(bf16[256,512]{1,0:T(8,128)(2,1)} %get-tuple-element.36), channel_id=1, source_target_pairs={{0,32},{1,97},{32,0},{33,65},{64,96},{65,33},{96,64},{97,1},{2,34}... | collective-permute-start | bytes 786440 | tf_op jit(solution)/shard_map/ppermute | solution.py:534
  15.1 10.9 %collective-permute-start.1 = (bf16[256,512]{1,0:T(8,128)(2,1)S(1)}, bf16[256,512]{1,0:T(8,128)(2,1)S(1)}, u32[]{:S(2)}, u32[]{:S(2)}) collective-permute-start(bf16[256,512]{1,0:T(8,128)(2,1)S(1)} %get-tuple-element.71), channel_id=1, source_target_pairs={{0,96},{1,33},{32,64},{33,1},{64,32},{65,97},{96,0},{97,65},{2,98}... | collective-permute-start | bytes 786440 | tf_op jit(solution)/shard_map/ppermute | solution.py:534
  20.4 7.7 %collective-permute-start.3 = (bf16[256,512]{1,0:T(8,128)(2,1)S(1)}, bf16[256,512]{1,0:T(8,128)(2,1)S(1)}, u32[]{:S(2)}, u32[]{:S(2)}) collective-permute-start(bf16[256,512]{1,0:T(8,128)(2,1)S(1)} %get-tuple-element.69), channel_id=1, source_target_pairs={{0,96},{1,33},{32,64},{33,1},{64,32},{65,97},{96,0},{97,65},{2,98}... | collective-permute-start | bytes 786440 | tf_op jit(solution)/shard_map/ppermute | solution.py:534
  22.1 2.8 %copy-start = (bf16[3,512,2048]{2,1,0:T(8,128)(2,1)S(1)}, bf16[3,512,2048]{2,1,0:T(8,128)(2,1)}, u32[]{:S(2)}) copy-start(bf16[3,512,2048]{2,1,0:T(8,128)(2,1)} %dec_ref.3) | copy-start | bytes 18874372
  24.9 3.1 %copy-start.2 = (s32[512,512]{1,0:T(8,128)S(1)}, s32[512,512]{1,0:T(8,128)}, u32[]{:S(2)}) copy-start(s32[512,512]{1,0:T(8,128)} %active_ref.3) | copy-start | bytes 3145732
  24.9 3.1 %copy-start.5 = (f32[512]{0:T(512)S(1)}, f32[512]{0:T(512)}, u32[]{:S(2)}) copy-start(f32[512]{0:T(512)} %param.8) | copy-start | bytes 6148
  28.3 2.0 %collective-permute-start.5 = (bf16[512,512]{1,0:T(8,128)(2,1)S(1)}, bf16[512,512]{1,0:T(8,128)(2,1)S(1)}, u32[]{:S(2)}, u32[]{:S(2)}) collective-permute-start(bf16[512,512]{1,0:T(8,128)(2,1)S(1)} %latents.1.lat_ref), channel_id=1, source_target_pairs={{0,1},{1,0},{2,3},{3,2},{4,5},{5,4},{6,7},{7,6},{8,9},{9,8},{10,11... | collective-permute-start | bytes 1572872 | tf_op jit(solution)/shard_map/ppermute | solution.py:525
  35.3 9.1 %collective-permute-start.7 = (bf16[4,3,32,512]{3,2,1,0:T(8,128)(2,1)S(1)}, bf16[4,3,32,512]{3,2,1,0:T(8,128)(2,1)S(1)}, u32[]{:S(2)}, u32[]{:S(2)}) collective-permute-start(bf16[4,3,32,512]{3,2,1,0:T(8,128)(2,1)S(1)} %get-tuple-element.44), channel_id=1, source_target_pairs={{0,8},{1,3},{2,10},{3,5},{4,12},{5,7},{6,14},{7,1},{8,16},{9,11},{... | collective-permute-start | bytes 1179656 | tf_op jit(solution)/shard_map/ppermute | solution.py:550
  36.9 8.0 %collective-permute-start.11 = (bf16[4,3,32,512]{3,2,1,0:T(8,128)(2,1)S(1)}, bf16[4,3,32,512]{3,2,1,0:T(8,128)(2,1)S(1)}, u32[]{:S(2)}, u32[]{:S(2)}) collective-permute-start(bf16[4,3,32,512]{3,2,1,0:T(8,128)(2,1)S(1)} %get-tuple-element.48), channel_id=1, source_target_pairs={{0,24},{1,7},{2,26},{3,1},{4,28},{5,3},{6,30},{7,5},{8,0},{9,15},{... | collective-permute-start | bytes 1179656 | tf_op jit(solution)/shard_map/ppermute | solution.py:550
  38.6 10.2 %collective-permute-start.9 = (bf16[4,3,32,512]{3,2,1,0:T(8,128)(2,1)S(1)}, bf16[4,3,32,512]{3,2,1,0:T(8,128)(2,1)S(1)}, u32[]{:S(2)}, u32[]{:S(2)}) collective-permute-start(bf16[4,3,32,512]{3,2,1,0:T(8,128)(2,1)S(1)} %get-tuple-element.45), channel_id=1, source_target_pairs={{0,24},{1,7},{2,26},{3,1},{4,28},{5,3},{6,30},{7,5},{8,0},{9,15},{... | collective-permute-start | bytes 1179656 | tf_op jit(solution)/shard_map/ppermute | solution.py:550
  40.2 9.0 %collective-permute-start.10 = (bf16[4,3,32,512]{3,2,1,0:T(8,128)(2,1)S(1)}, bf16[4,3,32,512]{3,2,1,0:T(8,128)(2,1)S(1)}, u32[]{:S(2)}, u32[]{:S(2)}) collective-permute-start(bf16[4,3,32,512]{3,2,1,0:T(8,128)(2,1)S(1)} %get-tuple-element.46), channel_id=1, source_target_pairs={{0,8},{1,3},{2,10},{3,5},{4,12},{5,7},{6,14},{7,1},{8,16},{9,11},{... | collective-permute-start | bytes 1179656 | tf_op jit(solution)/shard_map/ppermute | solution.py:550
  44.4 16.3 %copy-start.6 = (bf16[3,16,1024]{2,1,0:T(8,128)(2,1)S(1)}, bf16[3,16,1024]{2,1,0:T(8,128)(2,1)}, u32[]{:S(2)}) copy-start(bf16[3,16,1024]{2,1,0:T(8,128)(2,1)} %get-tuple-element.39) | copy-start | bytes 294916
  44.4 20.7 %copy-start.3 = (bf16[3,16,1024]{2,1,0:T(8,128)(2,1)S(1)}, bf16[3,16,1024]{2,1,0:T(8,128)(2,1)}, u32[]{:S(2)}) copy-start(bf16[3,16,1024]{2,1,0:T(8,128)(2,1)} %get-tuple-element.38.own_ref) | copy-start | bytes 294916
  44.5 9.1 %collective-permute-start.8 = (bf16[4,3,32,512]{3,2,1,0:T(8,128)(2,1)S(1)}, bf16[4,3,32,512]{3,2,1,0:T(8,128)(2,1)S(1)}, u32[]{:S(2)}, u32[]{:S(2)}) collective-permute-start(bf16[4,3,32,512]{3,2,1,0:T(8,128)(2,1)S(1)} %add_convert_fusion.1), channel_id=1, source_target_pairs={{0,8},{1,3},{2,10},{3,5},{4,12},{5,7},{6,14},{7,1},{8,16},{9,11},{... | collective-permute-start | bytes 1179656 | tf_op jit(solution)/shard_map/ppermute | solution.py:550
  44.9 47.4 %copy-start.1 = (bf16[512,2048]{1,0:T(8,128)(2,1)S(1)}, bf16[512,2048]{1,0:T(8,128)(2,1)}, u32[]{:S(2)}) copy-start(bf16[512,2048]{1,0:T(8,128)(2,1)} %x_ref.3) | copy-start | bytes 6291460
  45.0 8.6 %collective-permute-start.12 = (bf16[4,3,32,512]{3,2,1,0:T(8,128)(2,1)S(1)}, bf16[4,3,32,512]{3,2,1,0:T(8,128)(2,1)S(1)}, u32[]{:S(2)}, u32[]{:S(2)}) collective-permute-start(bf16[4,3,32,512]{3,2,1,0:T(8,128)(2,1)S(1)} %add_convert_fusion), channel_id=1, source_target_pairs={{0,24},{1,7},{2,26},{3,1},{4,28},{5,3},{6,30},{7,5},{8,0},{9,15},{... | collective-permute-start | bytes 1179656 | tf_op jit(solution)/shard_map/ppermute | solution.py:550
  54.8 7.2 %collective-permute-start.13 = (bf16[3,32,1024]{2,1,0:T(8,128)(2,1)S(1)}, bf16[3,32,1024]{2,1,0:T(8,128)(2,1)S(1)}, u32[]{:S(2)}, u32[]{:S(2)}) collective-permute-start(bf16[3,32,1024]{2,1,0:T(8,128)(2,1)S(1)} %get-tuple-element.50), channel_id=1, source_target_pairs={{0,2},{1,9},{2,4},{3,11},{4,6},{5,13},{6,0},{7,15},{8,10},{9,17},{... | collective-permute-start | bytes 589832 | tf_op jit(solution)/shard_map/ppermute | solution.py:550
  56.5 8.7 %collective-permute-start.14 = (bf16[3,32,1024]{2,1,0:T(8,128)(2,1)S(1)}, bf16[3,32,1024]{2,1,0:T(8,128)(2,1)S(1)}, u32[]{:S(2)}, u32[]{:S(2)}) collective-permute-start(bf16[3,32,1024]{2,1,0:T(8,128)(2,1)S(1)} %get-tuple-element.51), channel_id=1, source_target_pairs={{0,4},{1,17},{2,6},{3,19},{4,0},{5,21},{6,2},{7,23},{8,12},{9,25},... | collective-permute-start | bytes 589832 | tf_op jit(solution)/shard_map/ppermute | solution.py:550
  59.4 5.8 %collective-permute-start.15 = (bf16[3,32,1024]{2,1,0:T(8,128)(2,1)S(1)}, bf16[3,32,1024]{2,1,0:T(8,128)(2,1)S(1)}, u32[]{:S(2)}, u32[]{:S(2)}) collective-permute-start(bf16[3,32,1024]{2,1,0:T(8,128)(2,1)S(1)} %get-tuple-element.52), channel_id=1, source_target_pairs={{0,6},{1,25},{2,0},{3,27},{4,2},{5,29},{6,4},{7,31},{8,14},{9,1},{... | collective-permute-start | bytes 589832 | tf_op jit(solution)/shard_map/ppermute | solution.py:550
  60.7 1.3 %collective-permute-start.4 = (bf16[3,16,1024]{2,1,0:T(8,128)(2,1)S(1)}, bf16[3,16,1024]{2,1,0:T(8,128)(2,1)S(1)}, u32[]{:S(2)}, u32[]{:S(2)}) collective-permute-start(bf16[3,16,1024]{2,1,0:T(8,128)(2,1)S(1)} %copy-done.6), channel_id=1, source_target_pairs={{0,1},{1,0},{2,3},{3,2},{4,5},{5,4},{6,7},{7,6},{8,9},{9,8},{10,11... | collective-permute-start | bytes 294920 | tf_op jit(solution)/shard_map/ppermute | solution.py:525
  65.9 7.9 %collective-permute-start.18 = (bf16[3,32,1024]{2,1,0:T(8,128)(2,1)S(1)}, bf16[3,32,1024]{2,1,0:T(8,128)(2,1)S(1)}, u32[]{:S(2)}, u32[]{:S(2)}) collective-permute-start(bf16[3,32,1024]{2,1,0:T(8,128)(2,1)S(1)} %error.1.refs_0_), channel_id=1, source_target_pairs={{0,6},{1,25},{2,0},{3,27},{4,2},{5,29},{6,4},{7,31},{8,14},{9,1},{... | collective-permute-start | bytes 589832 | tf_op jit(solution)/shard_map/ppermute | solution.py:550
  68.4 7.3 %collective-permute-start.17 = (bf16[3,32,1024]{2,1,0:T(8,128)(2,1)S(1)}, bf16[3,32,1024]{2,1,0:T(8,128)(2,1)S(1)}, u32[]{:S(2)}, u32[]{:S(2)}) collective-permute-start(bf16[3,32,1024]{2,1,0:T(8,128)(2,1)S(1)} %error.1.refs_0_), channel_id=1, source_target_pairs={{0,4},{1,17},{2,6},{3,19},{4,0},{5,21},{6,2},{7,23},{8,12},{9,25},... | collective-permute-start | bytes 589832 | tf_op jit(solution)/shard_map/ppermute | solution.py:550
  69.6 8.0 %collective-permute-start.16 = (bf16[3,32,1024]{2,1,0:T(8,128)(2,1)S(1)}, bf16[3,32,1024]{2,1,0:T(8,128)(2,1)S(1)}, u32[]{:S(2)}, u32[]{:S(2)}) collective-permute-start(bf16[3,32,1024]{2,1,0:T(8,128)(2,1)S(1)} %error.1.refs_0_), channel_id=1, source_target_pairs={{0,2},{1,9},{2,4},{3,11},{4,6},{5,13},{6,0},{7,15},{8,10},{9,17},{... | collective-permute-start | bytes 589832 | tf_op jit(solution)/shard_map/ppermute | solution.py:550
  78.4 10.5 %collective-permute-start.19 = (bf16[4,3,32,512]{3,2,1,0:T(8,128)(2,1)S(1)}, bf16[4,3,32,512]{3,2,1,0:T(8,128)(2,1)S(1)}, u32[]{:S(2)}, u32[]{:S(2)}) collective-permute-start(bf16[4,3,32,512]{3,2,1,0:T(8,128)(2,1)S(1)} %get-tuple-element.53.refs_0_), channel_id=1, source_target_pairs={{0,8},{1,3},{2,10},{3,5},{4,12},{5,7},{6,14},{7,1},{8,16},{9,11},{... | collective-permute-start | bytes 1179656 | tf_op jit(solution)/shard_map/ppermute | solution.py:550
  79.9 9.0 %collective-permute-start.22 = (bf16[4,3,32,512]{3,2,1,0:T(8,128)(2,1)S(1)}, bf16[4,3,32,512]{3,2,1,0:T(8,128)(2,1)S(1)}, u32[]{:S(2)}, u32[]{:S(2)}) collective-permute-start(bf16[4,3,32,512]{3,2,1,0:T(8,128)(2,1)S(1)} %get-tuple-element.57.refs_1_), channel_id=1, source_target_pairs={{0,24},{1,7},{2,26},{3,1},{4,28},{5,3},{6,30},{7,5},{8,0},{9,15},{... | collective-permute-start | bytes 1179656 | tf_op jit(solution)/shard_map/ppermute | solution.py:550
  83.3 10.1 %collective-permute-start.24 = (bf16[4,3,32,512]{3,2,1,0:T(8,128)(2,1)S(1)}, bf16[4,3,32,512]{3,2,1,0:T(8,128)(2,1)S(1)}, u32[]{:S(2)}, u32[]{:S(2)}) collective-permute-start(bf16[4,3,32,512]{3,2,1,0:T(8,128)(2,1)S(1)} %get-tuple-element.53.refs_0_), channel_id=1, source_target_pairs={{0,24},{1,7},{2,26},{3,1},{4,28},{5,3},{6,30},{7,5},{8,0},{9,15},{... | collective-permute-start | bytes 1179656 | tf_op jit(solution)/shard_map/ppermute | solution.py:550
  85.2 9.0 %collective-permute-start.20 = (bf16[4,3,32,512]{3,2,1,0:T(8,128)(2,1)S(1)}, bf16[4,3,32,512]{3,2,1,0:T(8,128)(2,1)S(1)}, u32[]{:S(2)}, u32[]{:S(2)}) collective-permute-start(bf16[4,3,32,512]{3,2,1,0:T(8,128)(2,1)S(1)} %get-tuple-element.57.refs_1_), channel_id=1, source_target_pairs={{0,8},{1,3},{2,10},{3,5},{4,12},{5,7},{6,14},{7,1},{8,16},{9,11},{... | collective-permute-start | bytes 1179656 | tf_op jit(solution)/shard_map/ppermute | solution.py:550
  89.0 9.5 %collective-permute-start.21 = (bf16[4,3,32,512]{3,2,1,0:T(8,128)(2,1)S(1)}, bf16[4,3,32,512]{3,2,1,0:T(8,128)(2,1)S(1)}, u32[]{:S(2)}, u32[]{:S(2)}) collective-permute-start(bf16[4,3,32,512]{3,2,1,0:T(8,128)(2,1)S(1)} %collective-permute-done.19.after_ref.refs_2_), channel_id=1, source_target_pairs={{0,8},{1,3},{2,10},{3,5},{4,12},{5,7},{6,14},{7,1},{8,16},{9,11},{... | collective-permute-start | bytes 1179656 | tf_op jit(solution)/shard_map/ppermute | solution.py:550
  89.0 9.5 %collective-permute-start.23 = (bf16[4,3,32,512]{3,2,1,0:T(8,128)(2,1)S(1)}, bf16[4,3,32,512]{3,2,1,0:T(8,128)(2,1)S(1)}, u32[]{:S(2)}, u32[]{:S(2)}) collective-permute-start(bf16[4,3,32,512]{3,2,1,0:T(8,128)(2,1)S(1)} %collective-permute-done.22.refs_7_), channel_id=1, source_target_pairs={{0,24},{1,7},{2,26},{3,1},{4,28},{5,3},{6,30},{7,5},{8,0},{9,15},{... | collective-permute-start | bytes 1179656 | tf_op jit(solution)/shard_map/ppermute | solution.py:550
  102.0 3.2 %collective-permute-start.25 = (bf16[512,512]{1,0:T(8,128)(2,1)S(1)}, bf16[512,512]{1,0:T(8,128)(2,1)S(1)}, u32[]{:S(2)}, u32[]{:S(2)}) collective-permute-start(bf16[512,512]{1,0:T(8,128)(2,1)S(1)} %get-tuple-element.59), channel_id=1, source_target_pairs={{0,1},{1,0},{2,3},{3,2},{4,5},{5,4},{6,7},{7,6},{8,9},{9,8},{10,11... | collective-permute-start | bytes 1572872 | tf_op jit(solution)/shard_map/ppermute | solution.py:525
  105.3 11.7 %collective-permute-start.26 = (bf16[3,512,1024]{2,1,0:T(8,128)(2,1)S(1)}, bf16[3,512,1024]{2,1,0:T(8,128)(2,1)S(1)}, u32[]{:S(2)}, u32[]{:S(2)}) collective-permute-start(bf16[3,512,1024]{2,1,0:T(8,128)(2,1)S(1)} %get-tuple-element.60.err_ref), channel_id=1, source_target_pairs={{0,1},{1,0},{2,3},{3,2},{4,5},{5,4},{6,7},{7,6},{8,9},{9,8},{10,11... | collective-permute-start | bytes 9437192 | tf_op jit(solution)/shard_map/ppermute | solution.py:525
  105.9 9.2 %collective-permute-start.27 = (bf16[512,512]{1,0:T(8,128)(2,1)S(1)}, bf16[512,512]{1,0:T(8,128)(2,1)S(1)}, u32[]{:S(2)}, u32[]{:S(2)}) collective-permute-start(bf16[512,512]{1,0:T(8,128)(2,1)S(1)} %get-tuple-element.63), channel_id=1, source_target_pairs={{0,32},{1,97},{32,0},{33,65},{64,96},{65,33},{96,64},{97,1},{2,34}... | collective-permute-start | bytes 1572872 | tf_op jit(solution)/shard_map/ppermute | solution.py:534
  115.3 10.5 %collective-permute-start.28 = (bf16[512,512]{1,0:T(8,128)(2,1)S(1)}, bf16[512,512]{1,0:T(8,128)(2,1)S(1)}, u32[]{:S(2)}, u32[]{:S(2)}) collective-permute-start(bf16[512,512]{1,0:T(8,128)(2,1)S(1)} %get-tuple-element.67), channel_id=1, source_target_pairs={{0,96},{1,33},{32,64},{33,1},{64,32},{65,97},{96,0},{97,65},{2,98}... | collective-permute-start | bytes 1572872 | tf_op jit(solution)/shard_map/ppermute | solution.py:534

commit v5 on v4

--- a/solution.py
+++ b/solution.py
@@ -11,7 +11,7 @@
 BF = jnp.bfloat16
 F32 = jnp.float32
 VMEM_LIMIT = 16 * 1024 * 1024
-PRE_LIMIT = 60 * 1024 * 1024
+PRE_LIMIT = 52 * 1024 * 1024
 SIDE = 4
 
 
@@ -78,15 +78,16 @@
     rows, depth = x.shape
     lats = w.shape[1]
     targets, few, wide = target.shape
-    outs = [jax.ShapeDtypeStruct((rows // 2, lats), BF)] * 2
-    outs += [jax.ShapeDtypeStruct((targets, lats, wide // 2), BF)]
-    outs += [jax.ShapeDtypeStruct((targets, few, wide // 2), BF)] * 2
+    part = pl.BlockSpec((rows // 2, lats), lambda i, p: (0, 0))
+    outs = [pltpu.VMEM((rows // 2, lats), BF)] * 2
+    outs += [pltpu.VMEM((targets, lats, wide // 2), BF)]
+    outs += [pltpu.VMEM((targets, few, wide // 2), BF)] * 2
     return call(
         pre_kernel,
         "pre",
         (1,),
         [pl.BlockSpec(memory_space=pl.ANY)] * 4,
-        [pl.BlockSpec(o.shape, lambda i, p, n=len(o.shape): (0,) * n) for o in outs],
+        [part, part] + [pl.BlockSpec(memory_space=pl.ANY)] * 3,
         outs,
         (x, w, dec, target),
         2 * rows * depth * lats,

time: 129 us -> 125 us (0.969)
  local copies, waits for them, and re-layouts: 3.48 us -> 0.65 us
  other arithmetic: 2.53 us -> 0.62 us
  starting transfers between devices: 39.9 us -> 41.8 us
  Pallas kernels: 32.5 us -> 30.9 us
    unnamed x14 -> x12, local copies, waits for them, and re-layouts: 2.81 us -> 0.03 us
    convert_element_type x3, other arithmetic: 2.27 us -> 0.36 us  [z_sum(): return (first, pair(first.astype(BF), (ODD, EVEN)))]
    ppermute x6, starting transfers between devices: 9.88 us -> 11.8 us  [pair(): return lax.ppermute(value, ('z', 'c'), moves)]
    pallas_call x13, Pallas kernels: 32.5 us -> 30.9 us  [call(): pl.pallas_call(body, out_shape=shapes, compiler_params=pltpu.CompilerPara...]
  transfers between devices with their start and end apart: 29 -> 29, of which waited for: 17 -> 18; matrix products, arithmetic and copies ran while one was open for 2% -> 0% of each run, Pallas kernels for 9% -> 10%
where the time goes in v5:
time: 125 us
  waiting for transfers between devices  50.4 us (40%)
  starting transfers between devices  41.8 us (33%)
  Pallas kernels  30.9 us (25%)
    pallas_call x13, Pallas kernels, call(): pl.pallas_call(body, out_shape=shapes, compiler_params=pltpu.CompilerPara...  30.9 us
    ppermute x18, starting transfers between devices, shift(): return lax.ppermute(value, ('x', 'y', 'c'), moves)  29.1 us
    ppermute x18, waiting for transfers between devices, shift(): return lax.ppermute(value, ('x', 'y', 'c'), moves)  28.5 us
    ppermute x6, waiting for transfers between devices, pair(): return lax.ppermute(value, ('z', 'c'), moves)  18.7 us
    ppermute x6, starting transfers between devices, pair(): return lax.ppermute(value, ('z', 'c'), moves)  11.8 us
    ppermute x5, waiting for transfers between devices, swap(): return lax.ppermute(value, 'c', [(0, 1), (1, 0)])  3.2 us
  transfers between devices with their start and end apart: 29, of which 18 were waited for; matrix products, arithmetic and copies ran while one was open for 0% of the time, Pallas kernels for 10%

profile of v5, /device:TPU:0, one launch (start us, length us, event | category | flops | bytes accessed | tf_op | source)
XLA Modules:
  0.0 125.2 jit_solution(5791524486049843404)
XLA Ops:
  0.7 0.6 stack.23.p_ref
  1.3 4.4 %pre.1 = (bf16[256,512]{1,0:T(8,128)(2,1)S(1)}, bf16[256,512]{1,0:T(8,128)(2,1)S(1)}, bf16[3,512,1024]{2,1,0:T(8,128)(2,1)S(1)}, bf16[3,16,1024]{2,1,0:T(8,128)(2,1)S(1)}, bf16[3,16,1024]{2,1,0:T(8,128)(2,1)S(1)}) custom-call(s32[5]{0:T(128)} %stack.23.p_ref, bf16[512,2048]{1,0:T(8,128)(2,1)} %x_ref.3, bf16[2048,512]{1,0:T(8,128)(2,1)} %w_ref.1, ...), custom_call_target="tpu_custom_call" | custom-call | flops 1073741824 | bytes 4194304 | tf_op jit(solution)/shard_map/pre/pallas_call | solution.py:27
  5.8 2.1 %collective-permute-start = (bf16[256,512]{1,0:T(8,128)(2,1)S(1)}, bf16[256,512]{1,0:T(8,128)(2,1)S(1)}, u32[]{:S(2)}, u32[]{:S(2)}) collective-permute-start(bf16[256,512]{1,0:T(8,128)(2,1)S(1)} %get-tuple-element.35), channel_id=1, source_target_pairs={{0,32},{1,97},{32,0},{33,65},{64,96},{65,33},{96,64},{97,1},{2,34}... | collective-permute-start | bytes 786440 | tf_op jit(solution)/shard_map/ppermute | solution.py:535
  8.0 4.3 %collective-permute-done = bf16[256,512]{1,0:T(8,128)(2,1)S(1)} collective-permute-done((bf16[256,512]{1,0:T(8,128)(2,1)S(1)}, bf16[256,512]{1,0:T(8,128)(2,1)S(1)}, u32[]{:S(2)}, u32[]{:S(2)}) %collective-permute-start) | collective-permute-done | bytes 262176 | tf_op jit(solution)/shard_map/ppermute | solution.py:535
  12.3 4.2 %collective-permute-start.1 = (bf16[256,512]{1,0:T(8,128)(2,1)S(1)}, bf16[256,512]{1,0:T(8,128)(2,1)S(1)}, u32[]{:S(2)}, u32[]{:S(2)}) collective-permute-start(bf16[256,512]{1,0:T(8,128)(2,1)S(1)} %get-tuple-element.71), channel_id=1, source_target_pairs={{0,96},{1,33},{32,64},{33,1},{64,32},{65,97},{96,0},{97,65},{2,98}... | collective-permute-start | bytes 786440 | tf_op jit(solution)/shard_map/ppermute | solution.py:535
  16.6 2.7 %collective-permute-start.3 = (bf16[256,512]{1,0:T(8,128)(2,1)S(1)}, bf16[256,512]{1,0:T(8,128)(2,1)S(1)}, u32[]{:S(2)}, u32[]{:S(2)}) collective-permute-start(bf16[256,512]{1,0:T(8,128)(2,1)S(1)} %get-tuple-element.69), channel_id=1, source_target_pairs={{0,96},{1,33},{32,64},{33,1},{64,32},{65,97},{96,0},{97,65},{2,98}... | collective-permute-start | bytes 786440 | tf_op jit(solution)/shard_map/ppermute | solution.py:535
  19.4 1.0 pick_half.1
  20.9 3.4 %collective-permute-done.3.far_b = bf16[256,512]{1,0:T(8,128)(2,1)S(1)} collective-permute-done((bf16[256,512]{1,0:T(8,128)(2,1)S(1)}, bf16[256,512]{1,0:T(8,128)(2,1)S(1)}, u32[]{:S(2)}, u32[]{:S(2)}) %collective-permute-start.3) | collective-permute-done | bytes 262176 | tf_op jit(solution)/shard_map/ppermute | solution.py:535
  24.6 1.9 %collective-permute-done.5.sib_ref = bf16[512,512]{1,0:T(8,128)(2,1)S(1)} collective-permute-done((bf16[512,512]{1,0:T(8,128)(2,1)S(1)}, bf16[512,512]{1,0:T(8,128)(2,1)S(1)}, u32[]{:S(2)}, u32[]{:S(2)}) %collective-permute-start.5) | collective-permute-done | bytes 524320 | tf_op jit(solution)/shard_map/ppermute | solution.py:526
  26.5 5.1 %rebuild.1 = (bf16[4,3,32,512]{3,2,1,0:T(8,128)(2,1)S(1)}, bf16[4,3,32,512]{3,2,1,0:T(8,128)(2,1)S(1)}, f32[4,3,32,512]{3,2,1,0:T(8,128)S(1)}, bf16[4,3,32,512]{...) custom-call(s32[5]{0:T(128)S(1)} %copy-done.2, ...), custom_call_target="tpu_custom_call" | custom-call | flops 3221225472 | bytes 11000000 | tf_op jit(solution)/shard_map/rebuild/pallas_call | solution.py:27
  31.6 1.6 %collective-permute-start.7 = (bf16[4,3,32,512]{3,2,1,0:T(8,128)(2,1)S(1)}, bf16[4,3,32,512]{3,2,1,0:T(8,128)(2,1)S(1)}, u32[]{:S(2)}, u32[]{:S(2)}) collective-permute-start(bf16[4,3,32,512]{3,2,1,0:T(8,128)(2,1)S(1)} %get-tuple-element.44), channel_id=1, source_target_pairs={{0,8},{1,3},{2,10},{3,5},{4,12},{5,7},{6,14},{7,1},{8,16},{9,11},{... | collective-permute-start | bytes 1179656 | tf_op jit(solution)/shard_map/ppermute | solution.py:551
  33.2 1.8 %collective-permute-start.11 = (bf16[4,3,32,512]{3,2,1,0:T(8,128)(2,1)S(1)}, bf16[4,3,32,512]{3,2,1,0:T(8,128)(2,1)S(1)}, u32[]{:S(2)}, u32[]{:S(2)}) collective-permute-start(bf16[4,3,32,512]{3,2,1,0:T(8,128)(2,1)S(1)} %get-tuple-element.48), channel_id=1, source_target_pairs={{0,24},{1,7},{2,26},{3,1},{4,28},{5,3},{6,30},{7,5},{8,0},{9,15},{... | collective-permute-start | bytes 1179656 | tf_op jit(solution)/shard_map/ppermute | solution.py:551
  34.9 1.5 %collective-permute-start.9 = (bf16[4,3,32,512]{3,2,1,0:T(8,128)(2,1)S(1)}, bf16[4,3,32,512]{3,2,1,0:T(8,128)(2,1)S(1)}, u32[]{:S(2)}, u32[]{:S(2)}) collective-permute-start(bf16[4,3,32,512]{3,2,1,0:T(8,128)(2,1)S(1)} %get-tuple-element.45), channel_id=1, source_target_pairs={{0,24},{1,7},{2,26},{3,1},{4,28},{5,3},{6,30},{7,5},{8,0},{9,15},{... | collective-permute-start | bytes 1179656 | tf_op jit(solution)/shard_map/ppermute | solution.py:551
  36.5 0.5 collective-permute-start.10
  36.9 3.7 %collective-permute-done.7 = bf16[4,3,32,512]{3,2,1,0:T(8,128)(2,1)S(1)} collective-permute-done((bf16[4,3,32,512]{3,2,1,0:T(8,128)(2,1)S(1)}, bf16[4,3,32,512]{3,2,1,0:T(8,128)(2,1)S(1)}, u32[]{:S(2)}, u32[]{:S(2)}) %collective-permute-start.7) | collective-permute-done | bytes 393248 | tf_op jit(solution)/shard_map/ppermute | solution.py:551
  41.3 3.0 %collective-permute-start.12 = (bf16[4,3,32,512]{3,2,1,0:T(8,128)(2,1)S(1)}, bf16[4,3,32,512]{3,2,1,0:T(8,128)(2,1)S(1)}, u32[]{:S(2)}, u32[]{:S(2)}) collective-permute-start(bf16[4,3,32,512]{3,2,1,0:T(8,128)(2,1)S(1)} %add_convert_fusion), channel_id=1, source_target_pairs={{0,24},{1,7},{2,26},{3,1},{4,28},{5,3},{6,30},{7,5},{8,0},{9,15},{... | collective-permute-start | bytes 1179656 | tf_op jit(solution)/shard_map/ppermute | solution.py:551
  44.3 0.8 collective-permute-done.9.refs_1_
  45.5 4.4 %collective-permute-done.8.refs_0_ = bf16[4,3,32,512]{3,2,1,0:T(8,128)(2,1)S(1)} collective-permute-done((bf16[4,3,32,512]{3,2,1,0:T(8,128)(2,1)S(1)}, bf16[4,3,32,512]{3,2,1,0:T(8,128)(2,1)S(1)}, u32[]{:S(2)}, u32[]{:S(2)}) %collective-permute-start.8) | collective-permute-done | bytes 393248 | tf_op jit(solution)/shard_map/ppermute | solution.py:551
  49.9 1.2 sum_first.1
  51.1 1.6 %collective-permute-start.13 = (bf16[3,32,1024]{2,1,0:T(8,128)(2,1)S(1)}, bf16[3,32,1024]{2,1,0:T(8,128)(2,1)S(1)}, u32[]{:S(2)}, u32[]{:S(2)}) collective-permute-start(bf16[3,32,1024]{2,1,0:T(8,128)(2,1)S(1)} %get-tuple-element.50), channel_id=1, source_target_pairs={{0,2},{1,9},{2,4},{3,11},{4,6},{5,13},{6,0},{7,15},{8,10},{9,17},{... | collective-permute-start | bytes 589832 | tf_op jit(solution)/shard_map/ppermute | solution.py:551
  52.7 2.9 %collective-permute-start.14 = (bf16[3,32,1024]{2,1,0:T(8,128)(2,1)S(1)}, bf16[3,32,1024]{2,1,0:T(8,128)(2,1)S(1)}, u32[]{:S(2)}, u32[]{:S(2)}) collective-permute-start(bf16[3,32,1024]{2,1,0:T(8,128)(2,1)S(1)} %get-tuple-element.51), channel_id=1, source_target_pairs={{0,4},{1,17},{2,6},{3,19},{4,0},{5,21},{6,2},{7,23},{8,12},{9,25},... | collective-permute-start | bytes 589832 | tf_op jit(solution)/shard_map/ppermute | solution.py:551
  55.6 1.3 %collective-permute-start.15 = (bf16[3,32,1024]{2,1,0:T(8,128)(2,1)S(1)}, bf16[3,32,1024]{2,1,0:T(8,128)(2,1)S(1)}, u32[]{:S(2)}, u32[]{:S(2)}) collective-permute-start(bf16[3,32,1024]{2,1,0:T(8,128)(2,1)S(1)} %get-tuple-element.52), channel_id=1, source_target_pairs={{0,6},{1,25},{2,0},{3,27},{4,2},{5,29},{6,4},{7,31},{8,14},{9,1},{... | collective-permute-start | bytes 589832 | tf_op jit(solution)/shard_map/ppermute | solution.py:551
  57.0 1.3 %collective-permute-done.4.got_ref = bf16[3,16,1024]{2,1,0:T(8,128)(2,1)S(1)} collective-permute-done((bf16[3,16,1024]{2,1,0:T(8,128)(2,1)S(1)}, bf16[3,16,1024]{2,1,0:T(8,128)(2,1)S(1)}, u32[]{:S(2)}, u32[]{:S(2)}) %collective-permute-start.4) | collective-permute-done | bytes 98336 | tf_op jit(solution)/shard_map/ppermute | solution.py:526
  58.3 3.1 %collective-permute-done.14.refs_2_ = bf16[3,32,1024]{2,1,0:T(8,128)(2,1)S(1)} collective-permute-done((bf16[3,32,1024]{2,1,0:T(8,128)(2,1)S(1)}, bf16[3,32,1024]{2,1,0:T(8,128)(2,1)S(1)}, u32[]{:S(2)}, u32[]{:S(2)}) %collective-permute-start.14) | collective-permute-done | bytes 196640 | tf_op jit(solution)/shard_map/ppermute | solution.py:551
  61.4 0.7 error.1.refs_0_
  62.1 2.5 %collective-permute-start.18 = (bf16[3,32,1024]{2,1,0:T(8,128)(2,1)S(1)}, bf16[3,32,1024]{2,1,0:T(8,128)(2,1)S(1)}, u32[]{:S(2)}, u32[]{:S(2)}) collective-permute-start(bf16[3,32,1024]{2,1,0:T(8,128)(2,1)S(1)} %error.1.refs_0_), channel_id=1, source_target_pairs={{0,6},{1,25},{2,0},{3,27},{4,2},{5,29},{6,4},{7,31},{8,14},{9,1},{... | collective-permute-start | bytes 589832 | tf_op jit(solution)/shard_map/ppermute | solution.py:551
  64.7 1.2 collective-permute-start.17
  65.9 0.6 collective-permute-start.16
  66.5 3.5 %collective-permute-done.18.refs_3_ = bf16[3,32,1024]{2,1,0:T(8,128)(2,1)S(1)} collective-permute-done((bf16[3,32,1024]{2,1,0:T(8,128)(2,1)S(1)}, bf16[3,32,1024]{2,1,0:T(8,128)(2,1)S(1)}, u32[]{:S(2)}, u32[]{:S(2)}) %collective-permute-start.18) | collective-permute-done | bytes 196640 | tf_op jit(solution)/shard_map/ppermute | solution.py:551
  70.0 1.9 %collective-permute-done.17.refs_2_ = bf16[3,32,1024]{2,1,0:T(8,128)(2,1)S(1)} collective-permute-done((bf16[3,32,1024]{2,1,0:T(8,128)(2,1)S(1)}, bf16[3,32,1024]{2,1,0:T(8,128)(2,1)S(1)}, u32[]{:S(2)}, u32[]{:S(2)}) %collective-permute-start.17) | collective-permute-done | bytes 196640 | tf_op jit(solution)/shard_map/ppermute | solution.py:551
  71.9 2.0 %collective-permute-done.16.refs_1_ = bf16[3,32,1024]{2,1,0:T(8,128)(2,1)S(1)} collective-permute-done((bf16[3,32,1024]{2,1,0:T(8,128)(2,1)S(1)}, bf16[3,32,1024]{2,1,0:T(8,128)(2,1)S(1)}, u32[]{:S(2)}, u32[]{:S(2)}) %collective-permute-start.16) | collective-permute-done | bytes 196640 | tf_op jit(solution)/shard_map/ppermute | solution.py:551
  74.0 0.7 join.1
  74.7 1.5 %collective-permute-start.19 = (bf16[4,3,32,512]{3,2,1,0:T(8,128)(2,1)S(1)}, bf16[4,3,32,512]{3,2,1,0:T(8,128)(2,1)S(1)}, u32[]{:S(2)}, u32[]{:S(2)}) collective-permute-start(bf16[4,3,32,512]{3,2,1,0:T(8,128)(2,1)S(1)} %get-tuple-element.53.refs_0_), channel_id=1, source_target_pairs={{0,8},{1,3},{2,10},{3,5},{4,12},{5,7},{6,14},{7,1},{8,16},{9,11},{... | collective-permute-start | bytes 1179656 | tf_op jit(solution)/shard_map/ppermute | solution.py:551
  76.2 3.4 %collective-permute-start.22 = (bf16[4,3,32,512]{3,2,1,0:T(8,128)(2,1)S(1)}, bf16[4,3,32,512]{3,2,1,0:T(8,128)(2,1)S(1)}, u32[]{:S(2)}, u32[]{:S(2)}) collective-permute-start(bf16[4,3,32,512]{3,2,1,0:T(8,128)(2,1)S(1)} %get-tuple-element.57.refs_1_), channel_id=1, source_target_pairs={{0,24},{1,7},{2,26},{3,1},{4,28},{5,3},{6,30},{7,5},{8,0},{9,15},{... | collective-permute-start | bytes 1179656 | tf_op jit(solution)/shard_map/ppermute | solution.py:551
  79.6 1.9 %collective-permute-start.24 = (bf16[4,3,32,512]{3,2,1,0:T(8,128)(2,1)S(1)}, bf16[4,3,32,512]{3,2,1,0:T(8,128)(2,1)S(1)}, u32[]{:S(2)}, u32[]{:S(2)}) collective-permute-start(bf16[4,3,32,512]{3,2,1,0:T(8,128)(2,1)S(1)} %get-tuple-element.53.refs_0_), channel_id=1, source_target_pairs={{0,24},{1,7},{2,26},{3,1},{4,28},{5,3},{6,30},{7,5},{8,0},{9,15},{... | collective-permute-start | bytes 1179656 | tf_op jit(solution)/shard_map/ppermute | solution.py:551
  81.6 3.6 %collective-permute-done.19.after_ref.refs_2_ = bf16[4,3,32,512]{3,2,1,0:T(8,128)(2,1)S(1)} collective-permute-done((bf16[4,3,32,512]{3,2,1,0:T(8,128)(2,1)S(1)}, bf16[4,3,32,512]{3,2,1,0:T(8,128)(2,1)S(1)}, u32[]{:S(2)}, u32[]{:S(2)}) %collective-permute-start.19) | collective-permute-done | bytes 393248 | tf_op jit(solution)/shard_map/ppermute | solution.py:551
  85.3 3.3 %collective-permute-start.23 = (bf16[4,3,32,512]{3,2,1,0:T(8,128)(2,1)S(1)}, bf16[4,3,32,512]{3,2,1,0:T(8,128)(2,1)S(1)}, u32[]{:S(2)}, u32[]{:S(2)}) collective-permute-start(bf16[4,3,32,512]{3,2,1,0:T(8,128)(2,1)S(1)} %collective-permute-done.22.refs_7_), channel_id=1, source_target_pairs={{0,24},{1,7},{2,26},{3,1},{4,28},{5,3},{6,30},{7,5},{8,0},{9,15},{... | collective-permute-start | bytes 1179656 | tf_op jit(solution)/shard_map/ppermute | solution.py:551
  88.6 1.1 turn.1
  89.7 0.8 collective-permute-done.20.refs_3_
  90.5 4.2 %collective-permute-done.21.refs_4_ = bf16[4,3,32,512]{3,2,1,0:T(8,128)(2,1)S(1)} collective-permute-done((bf16[4,3,32,512]{3,2,1,0:T(8,128)(2,1)S(1)}, bf16[4,3,32,512]{3,2,1,0:T(8,128)(2,1)S(1)}, u32[]{:S(2)}, u32[]{:S(2)}) %collective-permute-start.21) | collective-permute-done | bytes 393248 | tf_op jit(solution)/shard_map/ppermute | solution.py:551
  94.7 3.5 %back_sib.1 = (bf16[3,512,1024]{2,1,0:T(8,128)(2,1)S(1)}, bf16[512,512]{1,0:T(8,128)(2,1)S(1)}) custom-call(s32[5]{0:T(128)S(1)} %copy-done.2, bf16[3,512,1024]{2,1,0:T(8,128)(2,1)S(1)} %collective-permute-done.6.got_ref.dec_ref, f32[8,128]{1,0:T(8,128)S(1)} %get-tuple-element.56.after_ref, bf16[4,3,32,512]{3,2,1,0:T(8,128)(2,1)S(1)} %get-tuple-element.53.refs_0_, ...), custom_call_target="tpu_custom_call" | custom-call | flops 1610612736 | bytes 10000000 | tf_op jit(solution)/shard_map/back_sib/pallas_call | solution.py:27
  98.3 3.1 %back_own.1.own_ref = f32[512,512]{1,0:T(8,128)S(1)} custom-call(s32[5]{0:T(128)S(1)} %copy-done.2, bf16[3,512,1024]{2,1,0:T(8,128)(2,1)S(1)} %get-tuple-element.58.err_ref, bf16[3,512,1024]{2,1,0:T(8,128)(2,1)S(1)} %get-tuple-element.40.dec_ref), custom_call_target="tpu_custom_call" | custom-call | flops 1610612736 | bytes 7000000 | tf_op jit(solution)/shard_map/back_own/pallas_call | solution.py:27
  101.6 0.6 collective-permute-start.26
  102.2 9.2 %collective-permute-done.27 = bf16[512,512]{1,0:T(8,128)(2,1)S(1)} collective-permute-done((bf16[512,512]{1,0:T(8,128)(2,1)S(1)}, bf16[512,512]{1,0:T(8,128)(2,1)S(1)}, u32[]{:S(2)}, u32[]{:S(2)}) %collective-permute-start.27) | collective-permute-done | bytes 524320 | tf_op jit(solution)/shard_map/ppermute | solution.py:535
  111.6 2.7 %collective-permute-start.28 = (bf16[512,512]{1,0:T(8,128)(2,1)S(1)}, bf16[512,512]{1,0:T(8,128)(2,1)S(1)}, u32[]{:S(2)}, u32[]{:S(2)}) collective-permute-start(bf16[512,512]{1,0:T(8,128)(2,1)S(1)} %get-tuple-element.67), channel_id=1, source_target_pairs={{0,96},{1,33},{32,64},{33,1},{64,32},{65,97},{96,0},{97,65},{2,98}... | collective-permute-start | bytes 1572872 | tf_op jit(solution)/shard_map/ppermute | solution.py:535
  114.3 6.4 %dec_grad.1 = (bf16[3,512,2048]{2,1,0:T(8,128)(2,1)}, f32[8,128]{1,0:T(8,128)S(1)}) custom-call(s32[5]{0:T(128)S(1)} %copy-done.2, bf16[512,512]{1,0:T(8,128)(2,1)S(1)} %get-tuple-element.55.lat_ref, bf16[3,512,1024]{2,1,0:T(8,128)(2,1)S(1)} %get-tuple-element.60.err_ref, bf16[3,512,1024]{2,1,0:T(8,128)(2,1)S(1)} %collective-permute-done.26.got_ref), custom_call_target="tpu_custom_call" | custom-call | flops 3221225472 | bytes 13000000 | tf_op jit(solution)/shard_map/dec_grad/pallas_call | solution.py:27
  120.7 1.4 %collective-permute-done.28.got_ref = bf16[512,512]{1,0:T(8,128)(2,1)S(1)} collective-permute-done((bf16[512,512]{1,0:T(8,128)(2,1)S(1)}, bf16[512,512]{1,0:T(8,128)(2,1)S(1)}, u32[]{:S(2)}, u32[]{:S(2)}) %collective-permute-start.28) | collective-permute-done | bytes 524320 | tf_op jit(solution)/shard_map/ppermute | solution.py:535
  122.0 3.2 %enc_grad.1 = (bf16[2048,512]{1,0:T(8,128)(2,1)}, f32[1,512]{1,0:T(1,128)}) custom-call(bf16[2048,512]{1,0:T(8,128)(2,1)S(1)} %get-tuple-element.54.x_ref, s32[512,512]{1,0:T(8,128)S(1)} %copy-done.1, f32[8,128]{1,0:T(8,128)S(1)} %get-tuple-element.61.after_ref, f32[512,512]{1,0:T(8,128)S(1)} %get-tuple-element.68.sum_ref, ...), custom_call_target="tpu_custom_call" | custom-call | flops 1073741824 | bytes 7000000 | tf_op jit(solution)/shard_map/enc_grad/pallas_call | solution.py:27
  (42 shorter events, 2.6 us)
Async XLA Ops:
  0.6 18.7 %slice-start = ((s8[6291456]{0:T(1024)(128)(4,1)}), s8[2097152]{0:T(1024)(128)(4,1)S(1)}, s32[]{:S(2)}) async-start(s8[6291456]{0:T(1024)(128)(4,1)} %bitcast.7), calls=%async_computation | async-start | bytes 4194304
  1.3 18.1 %slice-start.1 = ((s8[6291456]{0:T(1024)(128)(4,1)}), s8[4194304]{0:T(1024)(128)(4,1)S(1)}, s32[]{:S(2)}) async-start(s8[6291456]{0:T(1024)(128)(4,1)} %bitcast.7), calls=%async_computation.1 | async-start | bytes 8388608
  1.3 18.1 %copy-start.2 = (s32[5]{0:T(128)S(1)}, s32[5]{0:T(128)}, u32[]{:S(2)}) copy-start(s32[5]{0:T(128)} %stack.23.p_ref) | copy-start | bytes 64
  5.7 20.8 %collective-permute-start.6 = (bf16[3,512,1024]{2,1,0:T(8,128)(2,1)S(1)}, bf16[3,512,1024]{2,1,0:T(8,128)(2,1)S(1)}, u32[]{:S(2)}, u32[]{:S(2)}) collective-permute-start(bf16[3,512,1024]{2,1,0:T(8,128)(2,1)S(1)} %get-tuple-element.41), channel_id=1, source_target_pairs={{0,1},{1,0},{2,3},{3,2},{4,5},{5,4},{6,7},{7,6},{8,9},{9,8},{10,11... | collective-permute-start | bytes 9437192 | tf_op jit(solution)/shard_map/ppermute | solution.py:526
  5.8 6.5 %collective-permute-start = (bf16[256,512]{1,0:T(8,128)(2,1)S(1)}, bf16[256,512]{1,0:T(8,128)(2,1)S(1)}, u32[]{:S(2)}, u32[]{:S(2)}) collective-permute-start(bf16[256,512]{1,0:T(8,128)(2,1)S(1)} %get-tuple-element.35), channel_id=1, source_target_pairs={{0,32},{1,97},{32,0},{33,65},{64,96},{65,33},{96,64},{97,1},{2,34}... | collective-permute-start | bytes 786440 | tf_op jit(solution)/shard_map/ppermute | solution.py:535
  7.9 8.7 %collective-permute-start.2 = (bf16[256,512]{1,0:T(8,128)(2,1)S(1)}, bf16[256,512]{1,0:T(8,128)(2,1)S(1)}, u32[]{:S(2)}, u32[]{:S(2)}) collective-permute-start(bf16[256,512]{1,0:T(8,128)(2,1)S(1)} %get-tuple-element.36), channel_id=1, source_target_pairs={{0,32},{1,97},{32,0},{33,65},{64,96},{65,33},{96,64},{97,1},{2,34}... | collective-permute-start | bytes 786440 | tf_op jit(solution)/shard_map/ppermute | solution.py:535
  12.3 8.6 %collective-permute-start.1 = (bf16[256,512]{1,0:T(8,128)(2,1)S(1)}, bf16[256,512]{1,0:T(8,128)(2,1)S(1)}, u32[]{:S(2)}, u32[]{:S(2)}) collective-permute-start(bf16[256,512]{1,0:T(8,128)(2,1)S(1)} %get-tuple-element.71), channel_id=1, source_target_pairs={{0,96},{1,33},{32,64},{33,1},{64,32},{65,97},{96,0},{97,65},{2,98}... | collective-permute-start | bytes 786440 | tf_op jit(solution)/shard_map/ppermute | solution.py:535
  16.6 7.7 %collective-permute-start.3 = (bf16[256,512]{1,0:T(8,128)(2,1)S(1)}, bf16[256,512]{1,0:T(8,128)(2,1)S(1)}, u32[]{:S(2)}, u32[]{:S(2)}) collective-permute-start(bf16[256,512]{1,0:T(8,128)(2,1)S(1)} %get-tuple-element.69), channel_id=1, source_target_pairs={{0,96},{1,33},{32,64},{33,1},{64,32},{65,97},{96,0},{97,65},{2,98}... | collective-permute-start | bytes 786440 | tf_op jit(solution)/shard_map/ppermute | solution.py:535
  19.4 4.9 %copy-start.1 = (s32[512,512]{1,0:T(8,128)S(1)}, s32[512,512]{1,0:T(8,128)}, u32[]{:S(2)}) copy-start(s32[512,512]{1,0:T(8,128)} %active_ref.3) | copy-start | bytes 3145732
  19.4 4.9 %copy-start.3 = (f32[512]{0:T(512)S(1)}, f32[512]{0:T(512)}, u32[]{:S(2)}) copy-start(f32[512]{0:T(512)} %param.8) | copy-start | bytes 6148
  24.5 2.0 %collective-permute-start.5 = (bf16[512,512]{1,0:T(8,128)(2,1)S(1)}, bf16[512,512]{1,0:T(8,128)(2,1)S(1)}, u32[]{:S(2)}, u32[]{:S(2)}) collective-permute-start(bf16[512,512]{1,0:T(8,128)(2,1)S(1)} %latents.1.lat_ref), channel_id=1, source_target_pairs={{0,1},{1,0},{2,3},{3,2},{4,5},{5,4},{6,7},{7,6},{8,9},{9,8},{10,11... | collective-permute-start | bytes 1572872 | tf_op jit(solution)/shard_map/ppermute | solution.py:526
  31.6 9.1 %collective-permute-start.7 = (bf16[4,3,32,512]{3,2,1,0:T(8,128)(2,1)S(1)}, bf16[4,3,32,512]{3,2,1,0:T(8,128)(2,1)S(1)}, u32[]{:S(2)}, u32[]{:S(2)}) collective-permute-start(bf16[4,3,32,512]{3,2,1,0:T(8,128)(2,1)S(1)} %get-tuple-element.44), channel_id=1, source_target_pairs={{0,8},{1,3},{2,10},{3,5},{4,12},{5,7},{6,14},{7,1},{8,16},{9,11},{... | collective-permute-start | bytes 1179656 | tf_op jit(solution)/shard_map/ppermute | solution.py:551
  33.2 8.0 %collective-permute-start.11 = (bf16[4,3,32,512]{3,2,1,0:T(8,128)(2,1)S(1)}, bf16[4,3,32,512]{3,2,1,0:T(8,128)(2,1)S(1)}, u32[]{:S(2)}, u32[]{:S(2)}) collective-permute-start(bf16[4,3,32,512]{3,2,1,0:T(8,128)(2,1)S(1)} %get-tuple-element.48), channel_id=1, source_target_pairs={{0,24},{1,7},{2,26},{3,1},{4,28},{5,3},{6,30},{7,5},{8,0},{9,15},{... | collective-permute-start | bytes 1179656 | tf_op jit(solution)/shard_map/ppermute | solution.py:551
  34.9 10.2 %collective-permute-start.9 = (bf16[4,3,32,512]{3,2,1,0:T(8,128)(2,1)S(1)}, bf16[4,3,32,512]{3,2,1,0:T(8,128)(2,1)S(1)}, u32[]{:S(2)}, u32[]{:S(2)}) collective-permute-start(bf16[4,3,32,512]{3,2,1,0:T(8,128)(2,1)S(1)} %get-tuple-element.45), channel_id=1, source_target_pairs={{0,24},{1,7},{2,26},{3,1},{4,28},{5,3},{6,30},{7,5},{8,0},{9,15},{... | collective-permute-start | bytes 1179656 | tf_op jit(solution)/shard_map/ppermute | solution.py:551
  36.5 9.0 %collective-permute-start.10 = (bf16[4,3,32,512]{3,2,1,0:T(8,128)(2,1)S(1)}, bf16[4,3,32,512]{3,2,1,0:T(8,128)(2,1)S(1)}, u32[]{:S(2)}, u32[]{:S(2)}) collective-permute-start(bf16[4,3,32,512]{3,2,1,0:T(8,128)(2,1)S(1)} %get-tuple-element.46), channel_id=1, source_target_pairs={{0,8},{1,3},{2,10},{3,5},{4,12},{5,7},{6,14},{7,1},{8,16},{9,11},{... | collective-permute-start | bytes 1179656 | tf_op jit(solution)/shard_map/ppermute | solution.py:551
  40.8 9.1 %collective-permute-start.8 = (bf16[4,3,32,512]{3,2,1,0:T(8,128)(2,1)S(1)}, bf16[4,3,32,512]{3,2,1,0:T(8,128)(2,1)S(1)}, u32[]{:S(2)}, u32[]{:S(2)}) collective-permute-start(bf16[4,3,32,512]{3,2,1,0:T(8,128)(2,1)S(1)} %add_convert_fusion.1), channel_id=1, source_target_pairs={{0,8},{1,3},{2,10},{3,5},{4,12},{5,7},{6,14},{7,1},{8,16},{9,11},{... | collective-permute-start | bytes 1179656 | tf_op jit(solution)/shard_map/ppermute | solution.py:551
  41.1 47.4 %copy-start = (bf16[512,2048]{1,0:T(8,128)(2,1)S(1)}, bf16[512,2048]{1,0:T(8,128)(2,1)}, u32[]{:S(2)}) copy-start(bf16[512,2048]{1,0:T(8,128)(2,1)} %x_ref.3) | copy-start | bytes 6291460
  41.3 8.6 %collective-permute-start.12 = (bf16[4,3,32,512]{3,2,1,0:T(8,128)(2,1)S(1)}, bf16[4,3,32,512]{3,2,1,0:T(8,128)(2,1)S(1)}, u32[]{:S(2)}, u32[]{:S(2)}) collective-permute-start(bf16[4,3,32,512]{3,2,1,0:T(8,128)(2,1)S(1)} %add_convert_fusion), channel_id=1, source_target_pairs={{0,24},{1,7},{2,26},{3,1},{4,28},{5,3},{6,30},{7,5},{8,0},{9,15},{... | collective-permute-start | bytes 1179656 | tf_op jit(solution)/shard_map/ppermute | solution.py:551
  51.1 7.2 %collective-permute-start.13 = (bf16[3,32,1024]{2,1,0:T(8,128)(2,1)S(1)}, bf16[3,32,1024]{2,1,0:T(8,128)(2,1)S(1)}, u32[]{:S(2)}, u32[]{:S(2)}) collective-permute-start(bf16[3,32,1024]{2,1,0:T(8,128)(2,1)S(1)} %get-tuple-element.50), channel_id=1, source_target_pairs={{0,2},{1,9},{2,4},{3,11},{4,6},{5,13},{6,0},{7,15},{8,10},{9,17},{... | collective-permute-start | bytes 589832 | tf_op jit(solution)/shard_map/ppermute | solution.py:551
  52.7 8.7 %collective-permute-start.14 = (bf16[3,32,1024]{2,1,0:T(8,128)(2,1)S(1)}, bf16[3,32,1024]{2,1,0:T(8,128)(2,1)S(1)}, u32[]{:S(2)}, u32[]{:S(2)}) collective-permute-start(bf16[3,32,1024]{2,1,0:T(8,128)(2,1)S(1)} %get-tuple-element.51), channel_id=1, source_target_pairs={{0,4},{1,17},{2,6},{3,19},{4,0},{5,21},{6,2},{7,23},{8,12},{9,25},... | collective-permute-start | bytes 589832 | tf_op jit(solution)/shard_map/ppermute | solution.py:551
  55.6 5.8 %collective-permute-start.15 = (bf16[3,32,1024]{2,1,0:T(8,128)(2,1)S(1)}, bf16[3,32,1024]{2,1,0:T(8,128)(2,1)S(1)}, u32[]{:S(2)}, u32[]{:S(2)}) collective-permute-start(bf16[3,32,1024]{2,1,0:T(8,128)(2,1)S(1)} %get-tuple-element.52), channel_id=1, source_target_pairs={{0,6},{1,25},{2,0},{3,27},{4,2},{5,29},{6,4},{7,31},{8,14},{9,1},{... | collective-permute-start | bytes 589832 | tf_op jit(solution)/shard_map/ppermute | solution.py:551
  57.0 1.3 %collective-permute-start.4 = (bf16[3,16,1024]{2,1,0:T(8,128)(2,1)S(1)}, bf16[3,16,1024]{2,1,0:T(8,128)(2,1)S(1)}, u32[]{:S(2)}, u32[]{:S(2)}) collective-permute-start(bf16[3,16,1024]{2,1,0:T(8,128)(2,1)S(1)} %get-tuple-element.39), channel_id=1, source_target_pairs={{0,1},{1,0},{2,3},{3,2},{4,5},{5,4},{6,7},{7,6},{8,9},{9,8},{10,11... | collective-permute-start | bytes 294920 | tf_op jit(solution)/shard_map/ppermute | solution.py:526
  62.1 7.9 %collective-permute-start.18 = (bf16[3,32,1024]{2,1,0:T(8,128)(2,1)S(1)}, bf16[3,32,1024]{2,1,0:T(8,128)(2,1)S(1)}, u32[]{:S(2)}, u32[]{:S(2)}) collective-permute-start(bf16[3,32,1024]{2,1,0:T(8,128)(2,1)S(1)} %error.1.refs_0_), channel_id=1, source_target_pairs={{0,6},{1,25},{2,0},{3,27},{4,2},{5,29},{6,4},{7,31},{8,14},{9,1},{... | collective-permute-start | bytes 589832 | tf_op jit(solution)/shard_map/ppermute | solution.py:551
  64.7 7.3 %collective-permute-start.17 = (bf16[3,32,1024]{2,1,0:T(8,128)(2,1)S(1)}, bf16[3,32,1024]{2,1,0:T(8,128)(2,1)S(1)}, u32[]{:S(2)}, u32[]{:S(2)}) collective-permute-start(bf16[3,32,1024]{2,1,0:T(8,128)(2,1)S(1)} %error.1.refs_0_), channel_id=1, source_target_pairs={{0,4},{1,17},{2,6},{3,19},{4,0},{5,21},{6,2},{7,23},{8,12},{9,25},... | collective-permute-start | bytes 589832 | tf_op jit(solution)/shard_map/ppermute | solution.py:551
  65.9 8.0 %collective-permute-start.16 = (bf16[3,32,1024]{2,1,0:T(8,128)(2,1)S(1)}, bf16[3,32,1024]{2,1,0:T(8,128)(2,1)S(1)}, u32[]{:S(2)}, u32[]{:S(2)}) collective-permute-start(bf16[3,32,1024]{2,1,0:T(8,128)(2,1)S(1)} %error.1.refs_0_), channel_id=1, source_target_pairs={{0,2},{1,9},{2,4},{3,11},{4,6},{5,13},{6,0},{7,15},{8,10},{9,17},{... | collective-permute-start | bytes 589832 | tf_op jit(solution)/shard_map/ppermute | solution.py:551
  74.7 10.5 %collective-permute-start.19 = (bf16[4,3,32,512]{3,2,1,0:T(8,128)(2,1)S(1)}, bf16[4,3,32,512]{3,2,1,0:T(8,128)(2,1)S(1)}, u32[]{:S(2)}, u32[]{:S(2)}) collective-permute-start(bf16[4,3,32,512]{3,2,1,0:T(8,128)(2,1)S(1)} %get-tuple-element.53.refs_0_), channel_id=1, source_target_pairs={{0,8},{1,3},{2,10},{3,5},{4,12},{5,7},{6,14},{7,1},{8,16},{9,11},{... | collective-permute-start | bytes 1179656 | tf_op jit(solution)/shard_map/ppermute | solution.py:551
  76.2 9.0 %collective-permute-start.22 = (bf16[4,3,32,512]{3,2,1,0:T(8,128)(2,1)S(1)}, bf16[4,3,32,512]{3,2,1,0:T(8,128)(2,1)S(1)}, u32[]{:S(2)}, u32[]{:S(2)}) collective-permute-start(bf16[4,3,32,512]{3,2,1,0:T(8,128)(2,1)S(1)} %get-tuple-element.57.refs_1_), channel_id=1, source_target_pairs={{0,24},{1,7},{2,26},{3,1},{4,28},{5,3},{6,30},{7,5},{8,0},{9,15},{... | collective-permute-start | bytes 1179656 | tf_op jit(solution)/shard_map/ppermute | solution.py:551
  79.6 10.1 %collective-permute-start.24 = (bf16[4,3,32,512]{3,2,1,0:T(8,128)(2,1)S(1)}, bf16[4,3,32,512]{3,2,1,0:T(8,128)(2,1)S(1)}, u32[]{:S(2)}, u32[]{:S(2)}) collective-permute-start(bf16[4,3,32,512]{3,2,1,0:T(8,128)(2,1)S(1)} %get-tuple-element.53.refs_0_), channel_id=1, source_target_pairs={{0,24},{1,7},{2,26},{3,1},{4,28},{5,3},{6,30},{7,5},{8,0},{9,15},{... | collective-permute-start | bytes 1179656 | tf_op jit(solution)/shard_map/ppermute | solution.py:551
  81.5 9.0 %collective-permute-start.20 = (bf16[4,3,32,512]{3,2,1,0:T(8,128)(2,1)S(1)}, bf16[4,3,32,512]{3,2,1,0:T(8,128)(2,1)S(1)}, u32[]{:S(2)}, u32[]{:S(2)}) collective-permute-start(bf16[4,3,32,512]{3,2,1,0:T(8,128)(2,1)S(1)} %get-tuple-element.57.refs_1_), channel_id=1, source_target_pairs={{0,8},{1,3},{2,10},{3,5},{4,12},{5,7},{6,14},{7,1},{8,16},{9,11},{... | collective-permute-start | bytes 1179656 | tf_op jit(solution)/shard_map/ppermute | solution.py:551
  85.2 9.5 %collective-permute-start.21 = (bf16[4,3,32,512]{3,2,1,0:T(8,128)(2,1)S(1)}, bf16[4,3,32,512]{3,2,1,0:T(8,128)(2,1)S(1)}, u32[]{:S(2)}, u32[]{:S(2)}) collective-permute-start(bf16[4,3,32,512]{3,2,1,0:T(8,128)(2,1)S(1)} %collective-permute-done.19.after_ref.refs_2_), channel_id=1, source_target_pairs={{0,8},{1,3},{2,10},{3,5},{4,12},{5,7},{6,14},{7,1},{8,16},{9,11},{... | collective-permute-start | bytes 1179656 | tf_op jit(solution)/shard_map/ppermute | solution.py:551
  85.3 9.5 %collective-permute-start.23 = (bf16[4,3,32,512]{3,2,1,0:T(8,128)(2,1)S(1)}, bf16[4,3,32,512]{3,2,1,0:T(8,128)(2,1)S(1)}, u32[]{:S(2)}, u32[]{:S(2)}) collective-permute-start(bf16[4,3,32,512]{3,2,1,0:T(8,128)(2,1)S(1)} %collective-permute-done.22.refs_7_), channel_id=1, source_target_pairs={{0,24},{1,7},{2,26},{3,1},{4,28},{5,3},{6,30},{7,5},{8,0},{9,15},{... | collective-permute-start | bytes 1179656 | tf_op jit(solution)/shard_map/ppermute | solution.py:551
  98.2 3.2 %collective-permute-start.25 = (bf16[512,512]{1,0:T(8,128)(2,1)S(1)}, bf16[512,512]{1,0:T(8,128)(2,1)S(1)}, u32[]{:S(2)}, u32[]{:S(2)}) collective-permute-start(bf16[512,512]{1,0:T(8,128)(2,1)S(1)} %get-tuple-element.59), channel_id=1, source_target_pairs={{0,1},{1,0},{2,3},{3,2},{4,5},{5,4},{6,7},{7,6},{8,9},{9,8},{10,11... | collective-permute-start | bytes 1572872 | tf_op jit(solution)/shard_map/ppermute | solution.py:526
  101.6 12.6 %collective-permute-start.26 = (bf16[3,512,1024]{2,1,0:T(8,128)(2,1)S(1)}, bf16[3,512,1024]{2,1,0:T(8,128)(2,1)S(1)}, u32[]{:S(2)}, u32[]{:S(2)}) collective-permute-start(bf16[3,512,1024]{2,1,0:T(8,128)(2,1)S(1)} %get-tuple-element.60.err_ref), channel_id=1, source_target_pairs={{0,1},{1,0},{2,3},{3,2},{4,5},{5,4},{6,7},{7,6},{8,9},{9,8},{10,11... | collective-permute-start | bytes 9437192 | tf_op jit(solution)/shard_map/ppermute | solution.py:526
  102.2 9.2 %collective-permute-start.27 = (bf16[512,512]{1,0:T(8,128)(2,1)S(1)}, bf16[512,512]{1,0:T(8,128)(2,1)S(1)}, u32[]{:S(2)}, u32[]{:S(2)}) collective-permute-start(bf16[512,512]{1,0:T(8,128)(2,1)S(1)} %get-tuple-element.63), channel_id=1, source_target_pairs={{0,32},{1,97},{32,0},{33,65},{64,96},{65,33},{96,64},{97,1},{2,34}... | collective-permute-start | bytes 1572872 | tf_op jit(solution)/shard_map/ppermute | solution.py:535
  111.6 10.5 %collective-permute-start.28 = (bf16[512,512]{1,0:T(8,128)(2,1)S(1)}, bf16[512,512]{1,0:T(8,128)(2,1)S(1)}, u32[]{:S(2)}, u32[]{:S(2)}) collective-permute-start(bf16[512,512]{1,0:T(8,128)(2,1)S(1)} %get-tuple-element.67), channel_id=1, source_target_pairs={{0,96},{1,33},{32,64},{33,1},{64,32},{65,97},{96,0},{97,65},{2,98}... | collective-permute-start | bytes 1572872 | tf_op jit(solution)/shard_map/ppermute | solution.py:535

commit v6 on v5

--- a/solution.py
+++ b/solution.py
@@ -103,29 +103,31 @@
     )
 
 
-def total_kernel(own_ref, got_ref, err_ref, sum_ref, low_ref, same_ref):
-    total = own_ref[...] + got_ref[...].astype(F32)
-    sum_ref[...] = total
-    low_ref[...] = total.astype(BF)
+def total_kernel(own_ref, got_ref, err_ref, *refs):
+    rows = own_ref.shape[0] // 2
+    for r in range(2):
+        at = slice(r * rows, (r + 1) * rows)
+        total = own_ref[at, :] + got_ref[at, :].astype(F32)
+        refs[2 * r][...] = total
+        refs[2 * r + 1][...] = total.astype(BF)
 
 
 def total_call(own, got, err):
+    rows, lats = own.shape
     whole = pl.BlockSpec(own.shape, lambda i: (0, 0))
+    part = pl.BlockSpec((rows // 2, lats), lambda i: (0, 0))
+    kept = [jax.ShapeDtypeStruct((rows // 2, lats), kind) for kind in (F32, BF)]
     return call(
         total_kernel,
         "total",
         (1,),
         [whole, whole, pl.BlockSpec(memory_space=pl.ANY)],
-        [whole, whole, pl.BlockSpec(memory_space=pl.ANY)],
-        [
-            jax.ShapeDtypeStruct(own.shape, F32),
-            jax.ShapeDtypeStruct(own.shape, BF),
-            jax.ShapeDtypeStruct(err.shape, BF),
-        ],
+        [part] * 4 + [pl.BlockSpec(memory_space=pl.ANY)],
+        kept * 2 + [jax.ShapeDtypeStruct(err.shape, BF)],
         (own, got, err),
         own.size,
         12 * own.size,
-        aliases={2: 2},
+        aliases={2: 4},
     )
 
 
@@ -297,7 +299,7 @@
     )
 
 
-def join_kernel(p_ref, *refs):
+def join_kernel(p_ref, after_ref, *refs):
     parts, outs = refs[:SIDE], refs[SIDE:]
     q = outs[0].shape[3]
     for k in range(SIDE):
@@ -306,16 +308,17 @@
             outs[h][at, 0] = parts[k][0, :, h * q : (h + 1) * q]
 
 
-def join_call(place, parts):
+def join_call(place, parts, after):
     targets, piece, half = parts[0].shape
     return call(
         join_kernel,
         "join",
         (targets,),
-        [pl.BlockSpec((1, piece, half), lambda t, p: (t, 0, 0))] * SIDE,
+        [pl.BlockSpec(memory_space=pl.ANY)]
+        + [pl.BlockSpec((1, piece, half), lambda t, p: (t, 0, 0))] * SIDE,
         [pl.BlockSpec((SIDE, 1, piece, half // 2), lambda t, p: (0, t, 0, 0))] * 2,
         [jax.ShapeDtypeStruct((SIDE, targets, piece, half // 2), BF)] * 2,
-        tuple(parts),
+        (after, *parts),
         0,
         8 * parts[0].size,
         core=place,
@@ -324,7 +327,7 @@
 
 def back_dot(err, dec_ref, out_ref, acc):
     t = pl.program_id(0)
-    part = dot(err, dec_ref[0], 1, 1)
+    part = dot(err, dec_ref[0], 1, 0)
 
     @pl.when(t == 0)
     def _():
@@ -339,7 +342,7 @@
         out_ref[...] = acc[...].astype(out_ref.dtype)
 
 
-def back_sib_kernel(p_ref, dec_ref, after_ref, *refs):
+def back_sib_kernel(p_ref, dec_ref, *refs):
     parts, (err_ref, out_ref, acc) = refs[: 2 * SIDE], refs[2 * SIDE :]
     piece, q = parts[0].shape[2:]
     for k in range(SIDE):
@@ -351,17 +354,16 @@
     back_dot(err_ref[0], dec_ref, out_ref, acc)
 
 
-def back_sib_call(place, parts, dec, after):
+def back_sib_call(place, parts, dec):
     _, targets, piece, q = parts[0].shape
-    lats, half = dec.shape[1:]
+    half, lats = dec.shape[1:]
     rows = SIDE * SIDE * piece
     return call(
         back_sib_kernel,
         "back_sib",
         (targets,),
         [
-            pl.BlockSpec((1, lats, half), lambda t, p: (t, 0, 0)),
-            pl.BlockSpec(memory_space=pl.ANY),
+            pl.BlockSpec((1, half, lats), lambda t, p: (t, 0, 0)),
         ]
         + [pl.BlockSpec((SIDE, 1, piece, q), lambda t, p: (0, t, 0, 0))] * (2 * SIDE),
         [
@@ -372,7 +374,7 @@
             jax.ShapeDtypeStruct((targets, rows, half), BF),
             jax.ShapeDtypeStruct((rows, lats), BF),
         ],
-        (dec, after, *parts),
+        (dec, *parts),
         2 * rows * lats * half * targets,
         10e6,
         [pltpu.VMEM((rows, lats), F32)],
@@ -386,14 +388,14 @@
 
 def back_own_call(place, err, dec):
     targets, rows, half = err.shape
-    lats = dec.shape[1]
+    lats = dec.shape[2]
     return call(
         back_own_kernel,
         "back_own",
         (targets,),
         [
             pl.BlockSpec((1, rows, half), lambda t, p: (t, 0, 0)),
-            pl.BlockSpec((1, lats, half), lambda t, p: (t, 0, 0)),
+            pl.BlockSpec((1, half, lats), lambda t, p: (t, 0, 0)),
         ],
         pl.BlockSpec((rows, lats), lambda t, p: (0, 0)),
         jax.ShapeDtypeStruct((rows, lats), F32),
@@ -443,79 +445,101 @@
     )
 
 
-def dec_kernel(p_ref, lat_ref, err_ref, got_ref, out_ref, done_ref):
-    j = pl.program_id(1)
+def turn_dec_kernel(own_ref, got_ref, after_ref, own_out, got_out, done_ref):
     done_ref[...] = jnp.zeros(done_ref.shape, F32)
-
-    @pl.when(j == 0)
-    def _():
-        out_ref[0] = dot(lat_ref[...], err_ref[0], 1, 0).astype(BF)
-
-    @pl.when(j == 1)
-    def _():
-        out_ref[0] = dot(lat_ref[...], got_ref[0], 1, 0).astype(BF)
-
-
-def dec_call(place, lat, err, got):
+    own_out[0] = own_ref[0].T
+    got_out[0] = got_ref[0].T
+
+
+def turn_dec_call(own, got, after):
+    targets, lats, half = own.shape
+    plain = pl.BlockSpec((1, lats, half), lambda t: (t, 0, 0))
+    turned = pl.BlockSpec((1, half, lats), lambda t: (t, 0, 0))
+    return call(
+        turn_dec_kernel,
+        "turn_dec",
+        (targets,),
+        [plain, plain, pl.BlockSpec(memory_space=pl.ANY)],
+        [turned, turned, pl.BlockSpec((8, 128), lambda t: (0, 0))],
+        [jax.ShapeDtypeStruct((targets, half, lats), BF)] * 2
+        + [jax.ShapeDtypeStruct((8, 128), F32)],
+        (own, got, after),
+        0,
+        12e6,
+    )
+
+
+def dec_kernel(p_ref, lat_ref, err_ref, *refs):
+    out_ref, done_ref = refs[-2:]
+    done_ref[...] = jnp.zeros(done_ref.shape, F32)
+    out_ref[0] = dot(lat_ref[...], err_ref[0], 1, 0).astype(BF)
+
+
+def dec_call(place, lat, err, grad=None):
     targets, rows, half = err.shape
     lats = lat.shape[0]
+    own = grad is None
     return call(
         dec_kernel,
-        "dec_grad",
-        (targets, 2),
-        [
-            pl.BlockSpec((lats, rows), lambda t, j, p: (0, 0)),
-            pl.BlockSpec((1, rows, half), lambda t, j, p: (t, 0, 0)),
-            pl.BlockSpec((1, rows, half), lambda t, j, p: (t, 0, 0)),
-        ],
-        [
-            pl.BlockSpec((1, lats, half), lambda t, j, p: (t, 0, (j + p[2]) % 2)),
-            pl.BlockSpec((8, 128), lambda t, j, p: (0, 0)),
+        "dec_grad_own" if own else "dec_grad_sib",
+        (targets,),
+        [
+            pl.BlockSpec((lats, rows), lambda t, p: (0, 0)),
+            pl.BlockSpec((1, rows, half), lambda t, p: (t, 0, 0)),
+        ]
+        + ([] if own else [pl.BlockSpec(memory_space=pl.ANY)]),
+        [
+            pl.BlockSpec((1, lats, half), lambda t, p: (t, 0, p[2] if own else 1 - p[2])),
+            pl.BlockSpec((8, 128), lambda t, p: (0, 0)),
         ],
         [
             jax.ShapeDtypeStruct((targets, lats, 2 * half), BF),
             jax.ShapeDtypeStruct((8, 128), F32),
         ],
-        (lat, err, got),
-        4 * rows * lats * half * targets,
-        13e6,
-        core=place,
-    )
-
-
-def enc_kernel(x_ref, active_ref, after_ref, sum_ref, got_ref, enc_ref, bias_ref, grad):
+        (lat, err) if own else (lat, err, grad),
+        2 * rows * lats * half * targets,
+        7e6,
+        core=place,
+        aliases=None if own else {3: 0},
+    )
+
+
+def enc_kernel(x_ref, active_ref, after_ref, near_a, far_a, near_b, far_b, enc_ref, bias_ref, grad):
     @pl.when(pl.program_id(0) == 0)
     def _():
-        total = sum_ref[...] + got_ref[...].astype(F32)
-        kept = jnp.where(active_ref[...] > 0, total, 0.0).astype(BF)
-        grad[...] = kept
-        bias_ref[...] = jnp.sum(kept.astype(F32), axis=0, keepdims=True)
+        rows = near_a.shape[0]
+        sums = jnp.zeros(bias_ref.shape, F32)
+        for r, (near, far) in enumerate(((near_a, far_a), (near_b, far_b))):
+            at = slice(r * rows, (r + 1) * rows)
+            total = near[...] + far[...].astype(F32)
+            kept = jnp.where(active_ref[at, :] > 0, total, 0.0).astype(BF)
+            grad[at, :] = kept
+            sums += jnp.sum(kept.astype(F32), axis=0, keepdims=True)
+        bias_ref[...] = sums
 
     enc_ref[...] = dot(x_ref[...], grad[...], 1, 0).astype(BF)
 
 
-def enc_call(x, active, after, sums, got):
+def enc_call(x, active, after, top, bottom):
     depth, rows = x.shape
     lats = active.shape[1]
     step = 512
-    whole = pl.BlockSpec((rows, lats), lambda i: (0, 0))
     return call(
         enc_kernel,
         "enc_grad",
         (depth // step,),
         [
             pl.BlockSpec((step, rows), lambda i: (i, 0)),
-            whole,
+            pl.BlockSpec((rows, lats), lambda i: (0, 0)),
             pl.BlockSpec(memory_space=pl.ANY),
-            whole,
-            whole,
-        ],
+        ]
+        + [pl.BlockSpec((rows // 2, lats), lambda i: (0, 0))] * 4,
         [
             pl.BlockSpec((step, lats), lambda i: (i, 0)),
             pl.BlockSpec((1, lats), lambda i: (0, 0)),
         ],
         [jax.ShapeDtypeStruct((depth, lats), BF), jax.ShapeDtypeStruct((1, lats), F32)],
-        (x, active, after, sums, got),
+        (x, active, after, *top, *bottom),
         2 * rows * depth * lats,
         7e6,
         [pltpu.VMEM((rows, lats), BF)],
@@ -526,6 +550,27 @@
     return lax.ppermute(value, "c", [(0, 1), (1, 0)])
 
 
+def pair_kernel(own_ref, got_ref, after_ref, sum_ref, low_ref):
+    total = own_ref[...] + got_ref[...].astype(F32)
+    sum_ref[...] = total
+    low_ref[...] = total.astype(BF)
+
+
+def pair_call(own, got, after):
+    whole = pl.BlockSpec(own.shape, lambda i: (0, 0))
+    return call(
+        pair_kernel,
+        "pair_sum",
+        (1,),
+        [whole, whole, pl.BlockSpec(memory_space=pl.ANY)],
+        [whole, whole],
+        [jax.ShapeDtypeStruct(own.shape, kind) for kind in (F32, BF)],
+        (own, got, after),
+        own.size,
+        12 * own.size,
+    )
+
+
 EVEN = (1, 0, 3, 2)
 ODD = (3, 2, 1, 0)
 
@@ -535,9 +580,13 @@
     return lax.ppermute(value, ("z", "c"), moves)
 
 
-def z_sum(part, low):
-    first = part.astype(F32) + pair(low, (EVEN, ODD)).astype(F32)
-    return first, pair(first.astype(BF), (ODD, EVEN))
+def z_sum(part, low, after=None):
+    got = pair(low, (EVEN, ODD))
+    if after is None:
+        first = part.astype(F32) + got.astype(F32)
+        return first, pair(first.astype(BF), (ODD, EVEN))
+    first, low = pair_call(part, got, after)
+    return first, pair(low, (ODD, EVEN))
 
 
 def shift(value, second, step):
@@ -599,15 +648,19 @@
     own, parts = ring_sum(rebuild_call(place, lat, lat_sib, dec_own, dec_got))
     parts = scatter(sum_call(place, own, parts))
     err = error_call(scale, place, tgt_own, tgt_got, parts)
-    parts = ring_gather(*join_call(place, spread(err)))
-    x_turned, lat_turned, done = turn_call(mlp_inputs, lat, parts[2])
-
-    err, grad_got = back_sib_call(place, parts, dec_got, done)
+    x_turned, lat_turned, done = turn_call(mlp_inputs, lat, err)
+    own_turned, got_turned, done = turn_dec_call(dec_own, dec_got, done)
+    parts = ring_gather(*join_call(place, spread(err), done))
+
+    err, grad_got = back_sib_call(place, parts, got_turned)
     grad_got = swap(grad_got)
-    grad, low, err = total_call(back_own_call(place, err, dec_own), grad_got, err)
-    near, far = z_sum(grad, low)
-    dec_grad, done = dec_call(place, lat_turned, err, swap(err))
-    enc_grad, bias_grad = enc_call(x_turned, active, done, near, far)
+    top, low_top, bottom, low_bottom, err = total_call(
+        back_own_call(place, err, own_turned), grad_got, err
+    )
+    dec_grad, done = dec_call(place, lat_turned, err)
+    top, bottom = z_sum(top, low_top, done), z_sum(bottom, low_bottom, done)
+    dec_grad, done = dec_call(place, lat_turned, swap(err), dec_grad)
+    enc_grad, bias_grad = enc_call(x_turned, active, done, top, bottom)
     return enc_grad, bias_grad.reshape(-1), dec_grad
 
 

time: 125 us -> 124 us (level); the launches traced: 125 us -> 123 us
  waiting for transfers between devices: 50.4 us -> 37.3 us
  starting transfers between devices: 41.8 us -> 49.1 us
  Pallas kernels: 30.9 us -> 34.3 us
    ppermute x6 -> x8, waiting for transfers between devices: 18.7 us -> 9.61 us  [pair(): return lax.ppermute(value, ('z', 'c'), moves)]
    ppermute x6 -> x8, starting transfers between devices: 11.8 us -> 16.5 us  [pair(): return lax.ppermute(value, ('z', 'c'), moves)]
    ppermute x18, waiting for transfers between devices: 28.5 us -> 24.5 us  [shift(): return lax.ppermute(value, ('x', 'y', 'c'), moves)]
    pallas_call x13 -> x17, Pallas kernels: 30.9 us -> 34.3 us  [call(): pl.pallas_call(body, out_shape=shapes, compiler_params=pltpu.CompilerPara...]
    ppermute x18, starting transfers between devices: 29.1 us -> 31.8 us  [shift(): return lax.ppermute(value, ('x', 'y', 'c'), moves)]
  transfers between devices with their start and end apart: 29 -> 31, of which waited for: 18 -> 16; matrix products, arithmetic and copies ran while one was open for 0% -> 0% of each run, Pallas kernels for 10% -> 12%
where the time goes in v6:
time: 124 us; the launch traced here: 123 us
  starting transfers between devices  49.1 us (40%)
  waiting for transfers between devices  37.3 us (30%)
  Pallas kernels  34.3 us (28%)
    pallas_call x17, Pallas kernels, call(): pl.pallas_call(body, out_shape=shapes, compiler_params=pltpu.CompilerPara...  34.3 us
    ppermute x18, starting transfers between devices, shift(): return lax.ppermute(value, ('x', 'y', 'c'), moves)  31.8 us
    ppermute x18, waiting for transfers between devices, shift(): return lax.ppermute(value, ('x', 'y', 'c'), moves)  24.5 us
    ppermute x8, starting transfers between devices, pair(): return lax.ppermute(value, ('z', 'c'), moves)  16.5 us
    ppermute x8, waiting for transfers between devices, pair(): return lax.ppermute(value, ('z', 'c'), moves)  9.61 us
    ppermute x5, waiting for transfers between devices, swap(): return lax.ppermute(value, 'c', [(0, 1), (1, 0)])  3.2 us
  transfers between devices with their start and end apart: 31, of which 16 were waited for; matrix products, arithmetic and copies ran while one was open for 0% of the time, Pallas kernels for 12%

profile of v6, /device:TPU:0, one launch (start us, length us, event | category | flops | bytes accessed | tf_op | source)
XLA Modules:
  0.0 122.8 jit_solution(5442883745628642854)
XLA Ops:
  0.7 0.7 stack.23.p_ref
  1.3 4.4 %pre.1 = (bf16[256,512]{1,0:T(8,128)(2,1)S(1)}, bf16[256,512]{1,0:T(8,128)(2,1)S(1)}, bf16[3,512,1024]{2,1,0:T(8,128)(2,1)S(1)}, bf16[3,16,1024]{2,1,0:T(8,128)(2,1)S(1)}, bf16[3,16,1024]{2,1,0:T(8,128)(2,1)S(1)}) custom-call(s32[5]{0:T(128)} %stack.23.p_ref, bf16[512,2048]{1,0:T(8,128)(2,1)} %x_ref.3, bf16[2048,512]{1,0:T(8,128)(2,1)} %w_ref.1, ...), custom_call_target="tpu_custom_call" | custom-call | flops 1073741824 | bytes 4194304 | tf_op jit(solution)/shard_map/pre/pallas_call | solution.py:27
  5.8 2.1 %collective-permute-start.2 = (bf16[256,512]{1,0:T(8,128)(2,1)S(1)}, bf16[256,512]{1,0:T(8,128)(2,1)S(1)}, u32[]{:S(2)}, u32[]{:S(2)}) collective-permute-start(bf16[256,512]{1,0:T(8,128)(2,1)S(1)} %get-tuple-element.47), channel_id=1, source_target_pairs={{0,32},{1,97},{32,0},{33,65},{64,96},{65,33},{96,64},{97,1},{2,34}... | collective-permute-start | bytes 786440 | tf_op jit(solution)/shard_map/ppermute | solution.py:580
  8.0 4.3 %collective-permute-done.2 = bf16[256,512]{1,0:T(8,128)(2,1)S(1)} collective-permute-done((bf16[256,512]{1,0:T(8,128)(2,1)S(1)}, bf16[256,512]{1,0:T(8,128)(2,1)S(1)}, u32[]{:S(2)}, u32[]{:S(2)}) %collective-permute-start.2) | collective-permute-done | bytes 262176 | tf_op jit(solution)/shard_map/ppermute | solution.py:580
  12.4 4.2 %collective-permute-start.3 = (bf16[256,512]{1,0:T(8,128)(2,1)S(1)}, bf16[256,512]{1,0:T(8,128)(2,1)S(1)}, u32[]{:S(2)}, u32[]{:S(2)}) collective-permute-start(bf16[256,512]{1,0:T(8,128)(2,1)S(1)} %get-tuple-element.89), channel_id=1, source_target_pairs={{0,96},{1,33},{32,64},{33,1},{64,32},{65,97},{96,0},{97,65},{2,98}... | collective-permute-start | bytes 786440 | tf_op jit(solution)/shard_map/ppermute | solution.py:580
  16.7 2.7 %collective-permute-start.1 = (bf16[256,512]{1,0:T(8,128)(2,1)S(1)}, bf16[256,512]{1,0:T(8,128)(2,1)S(1)}, u32[]{:S(2)}, u32[]{:S(2)}) collective-permute-start(bf16[256,512]{1,0:T(8,128)(2,1)S(1)} %get-tuple-element.91), channel_id=1, source_target_pairs={{0,96},{1,33},{32,64},{33,1},{64,32},{65,97},{96,0},{97,65},{2,98}... | collective-permute-start | bytes 786440 | tf_op jit(solution)/shard_map/ppermute | solution.py:580
  19.4 1.0 pick_half.1
  20.9 3.4 %collective-permute-done.1.far_a = bf16[256,512]{1,0:T(8,128)(2,1)S(1)} collective-permute-done((bf16[256,512]{1,0:T(8,128)(2,1)S(1)}, bf16[256,512]{1,0:T(8,128)(2,1)S(1)}, u32[]{:S(2)}, u32[]{:S(2)}) %collective-permute-start.1) | collective-permute-done | bytes 262176 | tf_op jit(solution)/shard_map/ppermute | solution.py:580
  24.7 1.9 %collective-permute-done.5.sib_ref = bf16[512,512]{1,0:T(8,128)(2,1)S(1)} collective-permute-done((bf16[512,512]{1,0:T(8,128)(2,1)S(1)}, bf16[512,512]{1,0:T(8,128)(2,1)S(1)}, u32[]{:S(2)}, u32[]{:S(2)}) %collective-permute-start.5) | collective-permute-done | bytes 524320 | tf_op jit(solution)/shard_map/ppermute | solution.py:550
  26.6 5.0 %rebuild.1 = (bf16[4,3,32,512]{3,2,1,0:T(8,128)(2,1)S(1)}, bf16[4,3,32,512]{3,2,1,0:T(8,128)(2,1)S(1)}, f32[4,3,32,512]{3,2,1,0:T(8,128)S(1)}, bf16[4,3,32,512]{...) custom-call(s32[5]{0:T(128)S(1)} %copy-done.2, ...), custom_call_target="tpu_custom_call" | custom-call | flops 3221225472 | bytes 11000000 | tf_op jit(solution)/shard_map/rebuild/pallas_call | solution.py:27
  31.6 2.8 %collective-permute-start.11 = (bf16[4,3,32,512]{3,2,1,0:T(8,128)(2,1)S(1)}, bf16[4,3,32,512]{3,2,1,0:T(8,128)(2,1)S(1)}, u32[]{:S(2)}, u32[]{:S(2)}) collective-permute-start(bf16[4,3,32,512]{3,2,1,0:T(8,128)(2,1)S(1)} %get-tuple-element.59), channel_id=1, source_target_pairs={{0,24},{1,7},{2,26},{3,1},{4,28},{5,3},{6,30},{7,5},{8,0},{9,15},{... | collective-permute-start | bytes 1179656 | tf_op jit(solution)/shard_map/ppermute | solution.py:600
  34.4 0.8 collective-permute-start.10
  35.2 2.5 %collective-permute-start.9 = (bf16[4,3,32,512]{3,2,1,0:T(8,128)(2,1)S(1)}, bf16[4,3,32,512]{3,2,1,0:T(8,128)(2,1)S(1)}, u32[]{:S(2)}, u32[]{:S(2)}) collective-permute-start(bf16[4,3,32,512]{3,2,1,0:T(8,128)(2,1)S(1)} %get-tuple-element.56), channel_id=1, source_target_pairs={{0,24},{1,7},{2,26},{3,1},{4,28},{5,3},{6,30},{7,5},{8,0},{9,15},{... | collective-permute-start | bytes 1179656 | tf_op jit(solution)/shard_map/ppermute | solution.py:600
  37.7 2.0 %collective-permute-done.11 = bf16[4,3,32,512]{3,2,1,0:T(8,128)(2,1)S(1)} collective-permute-done((bf16[4,3,32,512]{3,2,1,0:T(8,128)(2,1)S(1)}, bf16[4,3,32,512]{3,2,1,0:T(8,128)(2,1)S(1)}, u32[]{:S(2)}, u32[]{:S(2)}) %collective-permute-start.11) | collective-permute-done | bytes 393248 | tf_op jit(solution)/shard_map/ppermute | solution.py:600
  39.9 3.8 %collective-permute-start.12 = (bf16[4,3,32,512]{3,2,1,0:T(8,128)(2,1)S(1)}, bf16[4,3,32,512]{3,2,1,0:T(8,128)(2,1)S(1)}, u32[]{:S(2)}, u32[]{:S(2)}) collective-permute-start(bf16[4,3,32,512]{3,2,1,0:T(8,128)(2,1)S(1)} %add_convert_fusion), channel_id=1, source_target_pairs={{0,24},{1,7},{2,26},{3,1},{4,28},{5,3},{6,30},{7,5},{8,0},{9,15},{... | collective-permute-start | bytes 1179656 | tf_op jit(solution)/shard_map/ppermute | solution.py:600
  43.9 3.8 %collective-permute-done.10.refs_2_ = bf16[4,3,32,512]{3,2,1,0:T(8,128)(2,1)S(1)} collective-permute-done((bf16[4,3,32,512]{3,2,1,0:T(8,128)(2,1)S(1)}, bf16[4,3,32,512]{3,2,1,0:T(8,128)(2,1)S(1)}, u32[]{:S(2)}, u32[]{:S(2)}) %collective-permute-start.10) | collective-permute-done | bytes 393248 | tf_op jit(solution)/shard_map/ppermute | solution.py:600
  47.6 1.3 %collective-permute-done.12.refs_3_ = bf16[4,3,32,512]{3,2,1,0:T(8,128)(2,1)S(1)} collective-permute-done((bf16[4,3,32,512]{3,2,1,0:T(8,128)(2,1)S(1)}, bf16[4,3,32,512]{3,2,1,0:T(8,128)(2,1)S(1)}, u32[]{:S(2)}, u32[]{:S(2)}) %collective-permute-start.12) | collective-permute-done | bytes 393248 | tf_op jit(solution)/shard_map/ppermute | solution.py:600
  48.9 3.9 %collective-permute-done.8.refs_0_ = bf16[4,3,32,512]{3,2,1,0:T(8,128)(2,1)S(1)} collective-permute-done((bf16[4,3,32,512]{3,2,1,0:T(8,128)(2,1)S(1)}, bf16[4,3,32,512]{3,2,1,0:T(8,128)(2,1)S(1)}, u32[]{:S(2)}, u32[]{:S(2)}) %collective-permute-start.8) | collective-permute-done | bytes 393248 | tf_op jit(solution)/shard_map/ppermute | solution.py:600
  52.8 1.2 sum_first.1
  54.1 1.6 %collective-permute-start.13 = (bf16[3,32,1024]{2,1,0:T(8,128)(2,1)S(1)}, bf16[3,32,1024]{2,1,0:T(8,128)(2,1)S(1)}, u32[]{:S(2)}, u32[]{:S(2)}) collective-permute-start(bf16[3,32,1024]{2,1,0:T(8,128)(2,1)S(1)} %get-tuple-element.61), channel_id=1, source_target_pairs={{0,2},{1,9},{2,4},{3,11},{4,6},{5,13},{6,0},{7,15},{8,10},{9,17},{... | collective-permute-start | bytes 589832 | tf_op jit(solution)/shard_map/ppermute | solution.py:600
  55.7 2.9 %collective-permute-start.14 = (bf16[3,32,1024]{2,1,0:T(8,128)(2,1)S(1)}, bf16[3,32,1024]{2,1,0:T(8,128)(2,1)S(1)}, u32[]{:S(2)}, u32[]{:S(2)}) collective-permute-start(bf16[3,32,1024]{2,1,0:T(8,128)(2,1)S(1)} %get-tuple-element.62), channel_id=1, source_target_pairs={{0,4},{1,17},{2,6},{3,19},{4,0},{5,21},{6,2},{7,23},{8,12},{9,25},... | collective-permute-start | bytes 589832 | tf_op jit(solution)/shard_map/ppermute | solution.py:600
  58.6 1.7 %collective-permute-start.15 = (bf16[3,32,1024]{2,1,0:T(8,128)(2,1)S(1)}, bf16[3,32,1024]{2,1,0:T(8,128)(2,1)S(1)}, u32[]{:S(2)}, u32[]{:S(2)}) collective-permute-start(bf16[3,32,1024]{2,1,0:T(8,128)(2,1)S(1)} %get-tuple-element.63), channel_id=1, source_target_pairs={{0,6},{1,25},{2,0},{3,27},{4,2},{5,29},{6,4},{7,31},{8,14},{9,1},{... | collective-permute-start | bytes 589832 | tf_op jit(solution)/shard_map/ppermute | solution.py:600
  60.3 1.3 %collective-permute-done.4.got_ref = bf16[3,16,1024]{2,1,0:T(8,128)(2,1)S(1)} collective-permute-done((bf16[3,16,1024]{2,1,0:T(8,128)(2,1)S(1)}, bf16[3,16,1024]{2,1,0:T(8,128)(2,1)S(1)}, u32[]{:S(2)}, u32[]{:S(2)}) %collective-permute-start.4) | collective-permute-done | bytes 98336 | tf_op jit(solution)/shard_map/ppermute | solution.py:550
  61.6 2.8 %collective-permute-done.14.refs_2_ = bf16[3,32,1024]{2,1,0:T(8,128)(2,1)S(1)} collective-permute-done((bf16[3,32,1024]{2,1,0:T(8,128)(2,1)S(1)}, bf16[3,32,1024]{2,1,0:T(8,128)(2,1)S(1)}, u32[]{:S(2)}, u32[]{:S(2)}) %collective-permute-start.14) | collective-permute-done | bytes 196640 | tf_op jit(solution)/shard_map/ppermute | solution.py:600
  64.4 0.7 error.1.after_ref.refs_0_
  65.1 1.7 %collective-permute-start.16 = (bf16[3,32,1024]{2,1,0:T(8,128)(2,1)S(1)}, bf16[3,32,1024]{2,1,0:T(8,128)(2,1)S(1)}, u32[]{:S(2)}, u32[]{:S(2)}) collective-permute-start(bf16[3,32,1024]{2,1,0:T(8,128)(2,1)S(1)} %error.1.after_ref.refs_0_), channel_id=1, source_target_pairs={{0,2},{1,9},{2,4},{3,11},{4,6},{5,13},{6,0},{7,15},{8,10},{9,17},{... | collective-permute-start | bytes 589832 | tf_op jit(solution)/shard_map/ppermute | solution.py:600
  66.8 2.6 %collective-permute-start.17 = (bf16[3,32,1024]{2,1,0:T(8,128)(2,1)S(1)}, bf16[3,32,1024]{2,1,0:T(8,128)(2,1)S(1)}, u32[]{:S(2)}, u32[]{:S(2)}) collective-permute-start(bf16[3,32,1024]{2,1,0:T(8,128)(2,1)S(1)} %error.1.after_ref.refs_0_), channel_id=1, source_target_pairs={{0,4},{1,17},{2,6},{3,19},{4,0},{5,21},{6,2},{7,23},{8,12},{9,25},... | collective-permute-start | bytes 589832 | tf_op jit(solution)/shard_map/ppermute | solution.py:600
  69.4 1.5 %collective-permute-start.18 = (bf16[3,32,1024]{2,1,0:T(8,128)(2,1)S(1)}, bf16[3,32,1024]{2,1,0:T(8,128)(2,1)S(1)}, u32[]{:S(2)}, u32[]{:S(2)}) collective-permute-start(bf16[3,32,1024]{2,1,0:T(8,128)(2,1)S(1)} %error.1.after_ref.refs_0_), channel_id=1, source_target_pairs={{0,6},{1,25},{2,0},{3,27},{4,2},{5,29},{6,4},{7,31},{8,14},{9,1},{... | collective-permute-start | bytes 589832 | tf_op jit(solution)/shard_map/ppermute | solution.py:600
  71.0 1.1 turn.1
  72.1 1.8 %turn_dec.1 = (bf16[3,1024,512]{2,1,0:T(8,128)(2,1)S(1)}, bf16[3,1024,512]{2,1,0:T(8,128)(2,1)S(1)}, f32[8,128]{1,0:T(8,128)S(1)}) custom-call(bf16[3,512,1024]{2,1,0:T(8,128)(2,1)S(1)} %get-tuple-element.51.dec_ref.own_ref, bf16[3,512,1024]{2,1,0:T(8,128)(2,1)S(1)} %collective-permute-done.6.got_ref, f32[8,128]{1,0:T(8,128)S(1)} %get-tuple-element.66.after_ref), custom_call_target="tpu_custom_call" | custom-call | bytes 12000000 | tf_op jit(solution)/shard_map/turn_dec/pallas_call | solution.py:27
  74.0 2.5 %collective-permute-done.17.refs_2_ = bf16[3,32,1024]{2,1,0:T(8,128)(2,1)S(1)} collective-permute-done((bf16[3,32,1024]{2,1,0:T(8,128)(2,1)S(1)}, bf16[3,32,1024]{2,1,0:T(8,128)(2,1)S(1)}, u32[]{:S(2)}, u32[]{:S(2)}) %collective-permute-start.17) | collective-permute-done | bytes 196640 | tf_op jit(solution)/shard_map/ppermute | solution.py:600
  76.5 0.7 join.1
  77.3 3.2 %collective-permute-start.22 = (bf16[4,3,32,512]{3,2,1,0:T(8,128)(2,1)S(1)}, bf16[4,3,32,512]{3,2,1,0:T(8,128)(2,1)S(1)}, u32[]{:S(2)}, u32[]{:S(2)}) collective-permute-start(bf16[4,3,32,512]{3,2,1,0:T(8,128)(2,1)S(1)} %get-tuple-element.70.refs_1_), channel_id=1, source_target_pairs={{0,24},{1,7},{2,26},{3,1},{4,28},{5,3},{6,30},{7,5},{8,0},{9,15},{... | collective-permute-start | bytes 1179656 | tf_op jit(solution)/shard_map/ppermute | solution.py:600
  80.5 3.2 %collective-permute-start.24 = (bf16[4,3,32,512]{3,2,1,0:T(8,128)(2,1)S(1)}, bf16[4,3,32,512]{3,2,1,0:T(8,128)(2,1)S(1)}, u32[]{:S(2)}, u32[]{:S(2)}) collective-permute-start(bf16[4,3,32,512]{3,2,1,0:T(8,128)(2,1)S(1)} %get-tuple-element.69.refs_0_), channel_id=1, source_target_pairs={{0,24},{1,7},{2,26},{3,1},{4,28},{5,3},{6,30},{7,5},{8,0},{9,15},{... | collective-permute-start | bytes 1179656 | tf_op jit(solution)/shard_map/ppermute | solution.py:600
  83.8 2.5 %collective-permute-done.19.refs_2_ = bf16[4,3,32,512]{3,2,1,0:T(8,128)(2,1)S(1)} collective-permute-done((bf16[4,3,32,512]{3,2,1,0:T(8,128)(2,1)S(1)}, bf16[4,3,32,512]{3,2,1,0:T(8,128)(2,1)S(1)}, u32[]{:S(2)}, u32[]{:S(2)}) %collective-permute-start.19) | collective-permute-done | bytes 393248 | tf_op jit(solution)/shard_map/ppermute | solution.py:600
  86.3 3.2 %collective-permute-start.23 = (bf16[4,3,32,512]{3,2,1,0:T(8,128)(2,1)S(1)}, bf16[4,3,32,512]{3,2,1,0:T(8,128)(2,1)S(1)}, u32[]{:S(2)}, u32[]{:S(2)}) collective-permute-start(bf16[4,3,32,512]{3,2,1,0:T(8,128)(2,1)S(1)} %collective-permute-done.22.refs_7_), channel_id=1, source_target_pairs={{0,24},{1,7},{2,26},{3,1},{4,28},{5,3},{6,30},{7,5},{8,0},{9,15},{... | collective-permute-start | bytes 1179656 | tf_op jit(solution)/shard_map/ppermute | solution.py:600
  89.5 1.0 collective-permute-done.20.refs_3_
  90.5 4.8 %collective-permute-done.21.refs_4_ = bf16[4,3,32,512]{3,2,1,0:T(8,128)(2,1)S(1)} collective-permute-done((bf16[4,3,32,512]{3,2,1,0:T(8,128)(2,1)S(1)}, bf16[4,3,32,512]{3,2,1,0:T(8,128)(2,1)S(1)}, u32[]{:S(2)}, u32[]{:S(2)}) %collective-permute-start.21) | collective-permute-done | bytes 393248 | tf_op jit(solution)/shard_map/ppermute | solution.py:600
  95.3 3.5 %back_sib.1 = (bf16[3,512,1024]{2,1,0:T(8,128)(2,1)S(1)}, bf16[512,512]{1,0:T(8,128)(2,1)S(1)}) custom-call(s32[5]{0:T(128)S(1)} %copy-done.2, bf16[3,1024,512]{2,1,0:T(8,128)(2,1)S(1)} %get-tuple-element.67.dec_ref, bf16[4,3,32,512]{3,2,1,0:T(8,128)(2,1)S(1)} %get-tuple-element.69.refs_0_, bf16[4,3,32,512]{3,2,1,0:T(8,128)(2,1)S(1)} %get-tuple-element.70.refs_1_, ...), custom_call_target="tpu_custom_call" | custom-call | flops 1610612736 | bytes 10000000 | tf_op jit(solution)/shard_map/back_sib/pallas_call | solution.py:27
  98.9 3.0 %back_own.1.own_ref = f32[512,512]{1,0:T(8,128)S(1)} custom-call(s32[5]{0:T(128)S(1)} %copy-done.2, bf16[3,512,1024]{2,1,0:T(8,128)(2,1)S(1)} %get-tuple-element.71.err_ref, bf16[3,1024,512]{2,1,0:T(8,128)(2,1)S(1)} %get-tuple-element.72.dec_ref), custom_call_target="tpu_custom_call" | custom-call | flops 1610612736 | bytes 7000000 | tf_op jit(solution)/shard_map/back_own/pallas_call | solution.py:27
  102.1 0.6 collective-permute-start.26
  102.6 2.0 %collective-permute-start.27 = (bf16[256,512]{1,0:T(8,128)(2,1)S(1)}, bf16[256,512]{1,0:T(8,128)(2,1)S(1)}, u32[]{:S(2)}, u32[]{:S(2)}) collective-permute-start(bf16[256,512]{1,0:T(8,128)(2,1)S(1)} %get-tuple-element.78), channel_id=1, source_target_pairs={{0,32},{1,97},{32,0},{33,65},{64,96},{65,33},{96,64},{97,1},{2,34}... | collective-permute-start | bytes 786440 | tf_op jit(solution)/shard_map/ppermute | solution.py:580
  104.7 3.9 %dec_grad_own.1 = (bf16[3,512,2048]{2,1,0:T(8,128)(2,1)}, f32[8,128]{1,0:T(8,128)S(1)}) custom-call(s32[5]{0:T(128)S(1)} %copy-done.2, bf16[512,512]{1,0:T(8,128)(2,1)S(1)} %get-tuple-element.65.lat_ref, bf16[3,512,1024]{2,1,0:T(8,128)(2,1)S(1)} %get-tuple-element.74.err_ref), custom_call_target="tpu_custom_call" | custom-call | flops 1610612736 | bytes 7000000 | tf_op jit(solution)/shard_map/dec_grad_own/pallas_call | solution.py:27
  109.1 2.7 %collective-permute-start.30 = (bf16[256,512]{1,0:T(8,128)(2,1)S(1)}, bf16[256,512]{1,0:T(8,128)(2,1)S(1)}, u32[]{:S(2)}, u32[]{:S(2)}) collective-permute-start(bf16[256,512]{1,0:T(8,128)(2,1)S(1)} %get-tuple-element.85), channel_id=1, source_target_pairs={{0,96},{1,33},{32,64},{33,1},{64,32},{65,97},{96,0},{97,65},{2,98}... | collective-permute-start | bytes 786440 | tf_op jit(solution)/shard_map/ppermute | solution.py:580
  111.9 2.7 %collective-permute-start.28 = (bf16[256,512]{1,0:T(8,128)(2,1)S(1)}, bf16[256,512]{1,0:T(8,128)(2,1)S(1)}, u32[]{:S(2)}, u32[]{:S(2)}) collective-permute-start(bf16[256,512]{1,0:T(8,128)(2,1)S(1)} %get-tuple-element.81), channel_id=1, source_target_pairs={{0,96},{1,33},{32,64},{33,1},{64,32},{65,97},{96,0},{97,65},{2,98}... | collective-permute-start | bytes 786440 | tf_op jit(solution)/shard_map/ppermute | solution.py:580
  114.6 3.9 %dec_grad_sib.1 = (bf16[3,512,2048]{2,1,0:T(8,128)(2,1)}, f32[8,128]{1,0:T(8,128)S(1)}) custom-call(s32[5]{0:T(128)S(1)} %copy-done.2, bf16[512,512]{1,0:T(8,128)(2,1)S(1)} %get-tuple-element.65.lat_ref, bf16[3,512,1024]{2,1,0:T(8,128)(2,1)S(1)} %collective-permute-done.26.err_ref, ...), custom_call_target="tpu_custom_call", output_to_operand_aliasing={{0}: (3, {})} | custom-call | flops 1610612736 | bytes 7000000 | tf_op jit(solution)/shard_map/dec_grad_sib/pallas_call | solution.py:27
  118.6 1.0 collective-permute-done.28.far_a
  119.6 3.2 %enc_grad.1 = (bf16[2048,512]{1,0:T(8,128)(2,1)}, f32[1,512]{1,0:T(1,128)}) custom-call(bf16[2048,512]{1,0:T(8,128)(2,1)S(1)} %get-tuple-element.64.x_ref, s32[512,512]{1,0:T(8,128)S(1)} %copy-done.1, f32[8,128]{1,0:T(8,128)S(1)} %get-tuple-element.76.after_ref, f32[256,512]{1,0:T(8,128)S(1)} %get-tuple-element.80.near_a, ...), custom_call_target="tpu_custom_call" | custom-call | flops 1073741824 | bytes 7000000 | tf_op jit(solution)/shard_map/enc_grad/pallas_call | solution.py:27
  (49 shorter events, 2.5 us)
Async XLA Ops:
  0.6 18.7 %slice-start = ((s8[6291456]{0:T(1024)(128)(4,1)}), s8[2097152]{0:T(1024)(128)(4,1)S(1)}, s32[]{:S(2)}) async-start(s8[6291456]{0:T(1024)(128)(4,1)} %bitcast.7), calls=%async_computation | async-start | bytes 4194304
  1.3 18.1 %slice-start.1 = ((s8[6291456]{0:T(1024)(128)(4,1)}), s8[4194304]{0:T(1024)(128)(4,1)S(1)}, s32[]{:S(2)}) async-start(s8[6291456]{0:T(1024)(128)(4,1)} %bitcast.7), calls=%async_computation.1 | async-start | bytes 8388608
  1.3 18.1 %copy-start.2 = (s32[5]{0:T(128)S(1)}, s32[5]{0:T(128)}, u32[]{:S(2)}) copy-start(s32[5]{0:T(128)} %stack.23.p_ref) | copy-start | bytes 64
  5.7 20.8 %collective-permute-start.6 = (bf16[3,512,1024]{2,1,0:T(8,128)(2,1)S(1)}, bf16[3,512,1024]{2,1,0:T(8,128)(2,1)S(1)}, u32[]{:S(2)}, u32[]{:S(2)}) collective-permute-start(bf16[3,512,1024]{2,1,0:T(8,128)(2,1)S(1)} %get-tuple-element.52), channel_id=1, source_target_pairs={{0,1},{1,0},{2,3},{3,2},{4,5},{5,4},{6,7},{7,6},{8,9},{9,8},{10,11... | collective-permute-start | bytes 9437192 | tf_op jit(solution)/shard_map/ppermute | solution.py:550
  5.8 6.5 %collective-permute-start.2 = (bf16[256,512]{1,0:T(8,128)(2,1)S(1)}, bf16[256,512]{1,0:T(8,128)(2,1)S(1)}, u32[]{:S(2)}, u32[]{:S(2)}) collective-permute-start(bf16[256,512]{1,0:T(8,128)(2,1)S(1)} %get-tuple-element.47), channel_id=1, source_target_pairs={{0,32},{1,97},{32,0},{33,65},{64,96},{65,33},{96,64},{97,1},{2,34}... | collective-permute-start | bytes 786440 | tf_op jit(solution)/shard_map/ppermute | solution.py:580
  7.9 8.7 %collective-permute-start = (bf16[256,512]{1,0:T(8,128)(2,1)S(1)}, bf16[256,512]{1,0:T(8,128)(2,1)S(1)}, u32[]{:S(2)}, u32[]{:S(2)}) collective-permute-start(bf16[256,512]{1,0:T(8,128)(2,1)S(1)} %get-tuple-element.46), channel_id=1, source_target_pairs={{0,32},{1,97},{32,0},{33,65},{64,96},{65,33},{96,64},{97,1},{2,34}... | collective-permute-start | bytes 786440 | tf_op jit(solution)/shard_map/ppermute | solution.py:580
  12.4 8.6 %collective-permute-start.3 = (bf16[256,512]{1,0:T(8,128)(2,1)S(1)}, bf16[256,512]{1,0:T(8,128)(2,1)S(1)}, u32[]{:S(2)}, u32[]{:S(2)}) collective-permute-start(bf16[256,512]{1,0:T(8,128)(2,1)S(1)} %get-tuple-element.89), channel_id=1, source_target_pairs={{0,96},{1,33},{32,64},{33,1},{64,32},{65,97},{96,0},{97,65},{2,98}... | collective-permute-start | bytes 786440 | tf_op jit(solution)/shard_map/ppermute | solution.py:580
  16.7 7.7 %collective-permute-start.1 = (bf16[256,512]{1,0:T(8,128)(2,1)S(1)}, bf16[256,512]{1,0:T(8,128)(2,1)S(1)}, u32[]{:S(2)}, u32[]{:S(2)}) collective-permute-start(bf16[256,512]{1,0:T(8,128)(2,1)S(1)} %get-tuple-element.91), channel_id=1, source_target_pairs={{0,96},{1,33},{32,64},{33,1},{64,32},{65,97},{96,0},{97,65},{2,98}... | collective-permute-start | bytes 786440 | tf_op jit(solution)/shard_map/ppermute | solution.py:580
  19.4 4.9 %copy-start.1 = (s32[512,512]{1,0:T(8,128)S(1)}, s32[512,512]{1,0:T(8,128)}, u32[]{:S(2)}) copy-start(s32[512,512]{1,0:T(8,128)} %active_ref.3) | copy-start | bytes 3145732
  19.4 4.9 %copy-start.3 = (f32[512]{0:T(512)S(1)}, f32[512]{0:T(512)}, u32[]{:S(2)}) copy-start(f32[512]{0:T(512)} %param.8) | copy-start | bytes 6148
  24.6 2.0 %collective-permute-start.5 = (bf16[512,512]{1,0:T(8,128)(2,1)S(1)}, bf16[512,512]{1,0:T(8,128)(2,1)S(1)}, u32[]{:S(2)}, u32[]{:S(2)}) collective-permute-start(bf16[512,512]{1,0:T(8,128)(2,1)S(1)} %latents.1.lat_ref), channel_id=1, source_target_pairs={{0,1},{1,0},{2,3},{3,2},{4,5},{5,4},{6,7},{7,6},{8,9},{9,8},{10,11... | collective-permute-start | bytes 1572872 | tf_op jit(solution)/shard_map/ppermute | solution.py:550
  31.6 8.1 %collective-permute-start.11 = (bf16[4,3,32,512]{3,2,1,0:T(8,128)(2,1)S(1)}, bf16[4,3,32,512]{3,2,1,0:T(8,128)(2,1)S(1)}, u32[]{:S(2)}, u32[]{:S(2)}) collective-permute-start(bf16[4,3,32,512]{3,2,1,0:T(8,128)(2,1)S(1)} %get-tuple-element.59), channel_id=1, source_target_pairs={{0,24},{1,7},{2,26},{3,1},{4,28},{5,3},{6,30},{7,5},{8,0},{9,15},{... | collective-permute-start | bytes 1179656 | tf_op jit(solution)/shard_map/ppermute | solution.py:600
  34.4 9.2 %collective-permute-start.7 = (bf16[4,3,32,512]{3,2,1,0:T(8,128)(2,1)S(1)}, bf16[4,3,32,512]{3,2,1,0:T(8,128)(2,1)S(1)}, u32[]{:S(2)}, u32[]{:S(2)}) collective-permute-start(bf16[4,3,32,512]{3,2,1,0:T(8,128)(2,1)S(1)} %get-tuple-element.55), channel_id=1, source_target_pairs={{0,8},{1,3},{2,10},{3,5},{4,12},{5,7},{6,14},{7,1},{8,16},{9,11},{... | collective-permute-start | bytes 1179656 | tf_op jit(solution)/shard_map/ppermute | solution.py:600
  34.4 13.2 %collective-permute-start.10 = (bf16[4,3,32,512]{3,2,1,0:T(8,128)(2,1)S(1)}, bf16[4,3,32,512]{3,2,1,0:T(8,128)(2,1)S(1)}, u32[]{:S(2)}, u32[]{:S(2)}) collective-permute-start(bf16[4,3,32,512]{3,2,1,0:T(8,128)(2,1)S(1)} %get-tuple-element.57), channel_id=1, source_target_pairs={{0,8},{1,3},{2,10},{3,5},{4,12},{5,7},{6,14},{7,1},{8,16},{9,11},{... | collective-permute-start | bytes 1179656 | tf_op jit(solution)/shard_map/ppermute | solution.py:600
  35.2 12.4 %collective-permute-start.9 = (bf16[4,3,32,512]{3,2,1,0:T(8,128)(2,1)S(1)}, bf16[4,3,32,512]{3,2,1,0:T(8,128)(2,1)S(1)}, u32[]{:S(2)}, u32[]{:S(2)}) collective-permute-start(bf16[4,3,32,512]{3,2,1,0:T(8,128)(2,1)S(1)} %get-tuple-element.56), channel_id=1, source_target_pairs={{0,24},{1,7},{2,26},{3,1},{4,28},{5,3},{6,30},{7,5},{8,0},{9,15},{... | collective-permute-start | bytes 1179656 | tf_op jit(solution)/shard_map/ppermute | solution.py:600
  39.9 31.1 %copy-start = (bf16[512,2048]{1,0:T(8,128)(2,1)S(1)}, bf16[512,2048]{1,0:T(8,128)(2,1)}, u32[]{:S(2)}) copy-start(bf16[512,2048]{1,0:T(8,128)(2,1)} %x_ref.3) | copy-start | bytes 6291460
  39.9 9.1 %collective-permute-start.12 = (bf16[4,3,32,512]{3,2,1,0:T(8,128)(2,1)S(1)}, bf16[4,3,32,512]{3,2,1,0:T(8,128)(2,1)S(1)}, u32[]{:S(2)}, u32[]{:S(2)}) collective-permute-start(bf16[4,3,32,512]{3,2,1,0:T(8,128)(2,1)S(1)} %add_convert_fusion), channel_id=1, source_target_pairs={{0,24},{1,7},{2,26},{3,1},{4,28},{5,3},{6,30},{7,5},{8,0},{9,15},{... | collective-permute-start | bytes 1179656 | tf_op jit(solution)/shard_map/ppermute | solution.py:600
  43.8 9.1 %collective-permute-start.8 = (bf16[4,3,32,512]{3,2,1,0:T(8,128)(2,1)S(1)}, bf16[4,3,32,512]{3,2,1,0:T(8,128)(2,1)S(1)}, u32[]{:S(2)}, u32[]{:S(2)}) collective-permute-start(bf16[4,3,32,512]{3,2,1,0:T(8,128)(2,1)S(1)} %add_convert_fusion.1), channel_id=1, source_target_pairs={{0,8},{1,3},{2,10},{3,5},{4,12},{5,7},{6,14},{7,1},{8,16},{9,11},{... | collective-permute-start | bytes 1179656 | tf_op jit(solution)/shard_map/ppermute | solution.py:600
  54.1 7.5 %collective-permute-start.13 = (bf16[3,32,1024]{2,1,0:T(8,128)(2,1)S(1)}, bf16[3,32,1024]{2,1,0:T(8,128)(2,1)S(1)}, u32[]{:S(2)}, u32[]{:S(2)}) collective-permute-start(bf16[3,32,1024]{2,1,0:T(8,128)(2,1)S(1)} %get-tuple-element.61), channel_id=1, source_target_pairs={{0,2},{1,9},{2,4},{3,11},{4,6},{5,13},{6,0},{7,15},{8,10},{9,17},{... | collective-permute-start | bytes 589832 | tf_op jit(solution)/shard_map/ppermute | solution.py:600
  55.7 8.7 %collective-permute-start.14 = (bf16[3,32,1024]{2,1,0:T(8,128)(2,1)S(1)}, bf16[3,32,1024]{2,1,0:T(8,128)(2,1)S(1)}, u32[]{:S(2)}, u32[]{:S(2)}) collective-permute-start(bf16[3,32,1024]{2,1,0:T(8,128)(2,1)S(1)} %get-tuple-element.62), channel_id=1, source_target_pairs={{0,4},{1,17},{2,6},{3,19},{4,0},{5,21},{6,2},{7,23},{8,12},{9,25},... | collective-permute-start | bytes 589832 | tf_op jit(solution)/shard_map/ppermute | solution.py:600
  58.6 5.8 %collective-permute-start.15 = (bf16[3,32,1024]{2,1,0:T(8,128)(2,1)S(1)}, bf16[3,32,1024]{2,1,0:T(8,128)(2,1)S(1)}, u32[]{:S(2)}, u32[]{:S(2)}) collective-permute-start(bf16[3,32,1024]{2,1,0:T(8,128)(2,1)S(1)} %get-tuple-element.63), channel_id=1, source_target_pairs={{0,6},{1,25},{2,0},{3,27},{4,2},{5,29},{6,4},{7,31},{8,14},{9,1},{... | collective-permute-start | bytes 589832 | tf_op jit(solution)/shard_map/ppermute | solution.py:600
  60.3 1.3 %collective-permute-start.4 = (bf16[3,16,1024]{2,1,0:T(8,128)(2,1)S(1)}, bf16[3,16,1024]{2,1,0:T(8,128)(2,1)S(1)}, u32[]{:S(2)}, u32[]{:S(2)}) collective-permute-start(bf16[3,16,1024]{2,1,0:T(8,128)(2,1)S(1)} %get-tuple-element.50), channel_id=1, source_target_pairs={{0,1},{1,0},{2,3},{3,2},{4,5},{5,4},{6,7},{7,6},{8,9},{9,8},{10,11... | collective-permute-start | bytes 294920 | tf_op jit(solution)/shard_map/ppermute | solution.py:550
  65.1 8.9 %collective-permute-start.16 = (bf16[3,32,1024]{2,1,0:T(8,128)(2,1)S(1)}, bf16[3,32,1024]{2,1,0:T(8,128)(2,1)S(1)}, u32[]{:S(2)}, u32[]{:S(2)}) collective-permute-start(bf16[3,32,1024]{2,1,0:T(8,128)(2,1)S(1)} %error.1.after_ref.refs_0_), channel_id=1, source_target_pairs={{0,2},{1,9},{2,4},{3,11},{4,6},{5,13},{6,0},{7,15},{8,10},{9,17},{... | collective-permute-start | bytes 589832 | tf_op jit(solution)/shard_map/ppermute | solution.py:600
  66.8 9.7 %collective-permute-start.17 = (bf16[3,32,1024]{2,1,0:T(8,128)(2,1)S(1)}, bf16[3,32,1024]{2,1,0:T(8,128)(2,1)S(1)}, u32[]{:S(2)}, u32[]{:S(2)}) collective-permute-start(bf16[3,32,1024]{2,1,0:T(8,128)(2,1)S(1)} %error.1.after_ref.refs_0_), channel_id=1, source_target_pairs={{0,4},{1,17},{2,6},{3,19},{4,0},{5,21},{6,2},{7,23},{8,12},{9,25},... | collective-permute-start | bytes 589832 | tf_op jit(solution)/shard_map/ppermute | solution.py:600
  69.4 7.0 %collective-permute-start.18 = (bf16[3,32,1024]{2,1,0:T(8,128)(2,1)S(1)}, bf16[3,32,1024]{2,1,0:T(8,128)(2,1)S(1)}, u32[]{:S(2)}, u32[]{:S(2)}) collective-permute-start(bf16[3,32,1024]{2,1,0:T(8,128)(2,1)S(1)} %error.1.after_ref.refs_0_), channel_id=1, source_target_pairs={{0,6},{1,25},{2,0},{3,27},{4,2},{5,29},{6,4},{7,31},{8,14},{9,1},{... | collective-permute-start | bytes 589832 | tf_op jit(solution)/shard_map/ppermute | solution.py:600
  77.2 9.1 %collective-permute-start.19 = (bf16[4,3,32,512]{3,2,1,0:T(8,128)(2,1)S(1)}, bf16[4,3,32,512]{3,2,1,0:T(8,128)(2,1)S(1)}, u32[]{:S(2)}, u32[]{:S(2)}) collective-permute-start(bf16[4,3,32,512]{3,2,1,0:T(8,128)(2,1)S(1)} %get-tuple-element.69.refs_0_), channel_id=1, source_target_pairs={{0,8},{1,3},{2,10},{3,5},{4,12},{5,7},{6,14},{7,1},{8,16},{9,11},{... | collective-permute-start | bytes 1179656 | tf_op jit(solution)/shard_map/ppermute | solution.py:600
  77.3 9.0 %collective-permute-start.22 = (bf16[4,3,32,512]{3,2,1,0:T(8,128)(2,1)S(1)}, bf16[4,3,32,512]{3,2,1,0:T(8,128)(2,1)S(1)}, u32[]{:S(2)}, u32[]{:S(2)}) collective-permute-start(bf16[4,3,32,512]{3,2,1,0:T(8,128)(2,1)S(1)} %get-tuple-element.70.refs_1_), channel_id=1, source_target_pairs={{0,24},{1,7},{2,26},{3,1},{4,28},{5,3},{6,30},{7,5},{8,0},{9,15},{... | collective-permute-start | bytes 1179656 | tf_op jit(solution)/shard_map/ppermute | solution.py:600
  80.5 10.0 %collective-permute-start.20 = (bf16[4,3,32,512]{3,2,1,0:T(8,128)(2,1)S(1)}, bf16[4,3,32,512]{3,2,1,0:T(8,128)(2,1)S(1)}, u32[]{:S(2)}, u32[]{:S(2)}) collective-permute-start(bf16[4,3,32,512]{3,2,1,0:T(8,128)(2,1)S(1)} %get-tuple-element.70.refs_1_), channel_id=1, source_target_pairs={{0,8},{1,3},{2,10},{3,5},{4,12},{5,7},{6,14},{7,1},{8,16},{9,11},{... | collective-permute-start | bytes 1179656 | tf_op jit(solution)/shard_map/ppermute | solution.py:600
  80.5 10.0 %collective-permute-start.24 = (bf16[4,3,32,512]{3,2,1,0:T(8,128)(2,1)S(1)}, bf16[4,3,32,512]{3,2,1,0:T(8,128)(2,1)S(1)}, u32[]{:S(2)}, u32[]{:S(2)}) collective-permute-start(bf16[4,3,32,512]{3,2,1,0:T(8,128)(2,1)S(1)} %get-tuple-element.69.refs_0_), channel_id=1, source_target_pairs={{0,24},{1,7},{2,26},{3,1},{4,28},{5,3},{6,30},{7,5},{8,0},{9,15},{... | collective-permute-start | bytes 1179656 | tf_op jit(solution)/shard_map/ppermute | solution.py:600
  86.3 9.0 %collective-permute-start.21 = (bf16[4,3,32,512]{3,2,1,0:T(8,128)(2,1)S(1)}, bf16[4,3,32,512]{3,2,1,0:T(8,128)(2,1)S(1)}, u32[]{:S(2)}, u32[]{:S(2)}) collective-permute-start(bf16[4,3,32,512]{3,2,1,0:T(8,128)(2,1)S(1)} %collective-permute-done.19.refs_2_), channel_id=1, source_target_pairs={{0,8},{1,3},{2,10},{3,5},{4,12},{5,7},{6,14},{7,1},{8,16},{9,11},{... | collective-permute-start | bytes 1179656 | tf_op jit(solution)/shard_map/ppermute | solution.py:600
  86.3 9.0 %collective-permute-start.23 = (bf16[4,3,32,512]{3,2,1,0:T(8,128)(2,1)S(1)}, bf16[4,3,32,512]{3,2,1,0:T(8,128)(2,1)S(1)}, u32[]{:S(2)}, u32[]{:S(2)}) collective-permute-start(bf16[4,3,32,512]{3,2,1,0:T(8,128)(2,1)S(1)} %collective-permute-done.22.refs_7_), channel_id=1, source_target_pairs={{0,24},{1,7},{2,26},{3,1},{4,28},{5,3},{6,30},{7,5},{8,0},{9,15},{... | collective-permute-start | bytes 1179656 | tf_op jit(solution)/shard_map/ppermute | solution.py:600
  98.8 3.1 %collective-permute-start.25 = (bf16[512,512]{1,0:T(8,128)(2,1)S(1)}, bf16[512,512]{1,0:T(8,128)(2,1)S(1)}, u32[]{:S(2)}, u32[]{:S(2)}) collective-permute-start(bf16[512,512]{1,0:T(8,128)(2,1)S(1)} %get-tuple-element.73), channel_id=1, source_target_pairs={{0,1},{1,0},{2,3},{3,2},{4,5},{5,4},{6,7},{7,6},{8,9},{9,8},{10,11... | collective-permute-start | bytes 1572872 | tf_op jit(solution)/shard_map/ppermute | solution.py:550
  102.1 12.6 %collective-permute-start.26 = (bf16[3,512,1024]{2,1,0:T(8,128)(2,1)S(1)}, bf16[3,512,1024]{2,1,0:T(8,128)(2,1)S(1)}, u32[]{:S(2)}, u32[]{:S(2)}) collective-permute-start(bf16[3,512,1024]{2,1,0:T(8,128)(2,1)S(1)} %get-tuple-element.74.err_ref), channel_id=1, source_target_pairs={{0,1},{1,0},{2,3},{3,2},{4,5},{5,4},{6,7},{7,6},{8,9},{9,8},{10,11... | collective-permute-start | bytes 9437192 | tf_op jit(solution)/shard_map/ppermute | solution.py:550
  102.6 6.4 %collective-permute-start.29 = (bf16[256,512]{1,0:T(8,128)(2,1)S(1)}, bf16[256,512]{1,0:T(8,128)(2,1)S(1)}, u32[]{:S(2)}, u32[]{:S(2)}) collective-permute-start(bf16[256,512]{1,0:T(8,128)(2,1)S(1)} %get-tuple-element.83), channel_id=1, source_target_pairs={{0,32},{1,97},{32,0},{33,65},{64,96},{65,33},{96,64},{97,1},{2,34}... | collective-permute-start | bytes 786440 | tf_op jit(solution)/shard_map/ppermute | solution.py:580
  102.6 9.2 %collective-permute-start.27 = (bf16[256,512]{1,0:T(8,128)(2,1)S(1)}, bf16[256,512]{1,0:T(8,128)(2,1)S(1)}, u32[]{:S(2)}, u32[]{:S(2)}) collective-permute-start(bf16[256,512]{1,0:T(8,128)(2,1)S(1)} %get-tuple-element.78), channel_id=1, source_target_pairs={{0,32},{1,97},{32,0},{33,65},{64,96},{65,33},{96,64},{97,1},{2,34}... | collective-permute-start | bytes 786440 | tf_op jit(solution)/shard_map/ppermute | solution.py:580
  109.1 9.5 %collective-permute-start.30 = (bf16[256,512]{1,0:T(8,128)(2,1)S(1)}, bf16[256,512]{1,0:T(8,128)(2,1)S(1)}, u32[]{:S(2)}, u32[]{:S(2)}) collective-permute-start(bf16[256,512]{1,0:T(8,128)(2,1)S(1)} %get-tuple-element.85), channel_id=1, source_target_pairs={{0,96},{1,33},{32,64},{33,1},{64,32},{65,97},{96,0},{97,65},{2,98}... | collective-permute-start | bytes 786440 | tf_op jit(solution)/shard_map/ppermute | solution.py:580
  111.9 7.7 %collective-permute-start.28 = (bf16[256,512]{1,0:T(8,128)(2,1)S(1)}, bf16[256,512]{1,0:T(8,128)(2,1)S(1)}, u32[]{:S(2)}, u32[]{:S(2)}) collective-permute-start(bf16[256,512]{1,0:T(8,128)(2,1)S(1)} %get-tuple-element.81), channel_id=1, source_target_pairs={{0,96},{1,33},{32,64},{33,1},{64,32},{65,97},{96,0},{97,65},{2,98}... | collective-permute-start | bytes 786440 | tf_op jit(solution)/shard_map/ppermute | solution.py:580

commit v7 on v6

--- a/solution.py
+++ b/solution.py
@@ -193,16 +193,25 @@
 
 
 def rebuild_kernel(p_ref, lat_ref, sib_ref, dec_ref, got_ref, *refs):
-    outs, held = refs[:-1], refs[-1]
-    total = jnp.dot(lat_ref[...], dec_ref[0], preferred_element_type=F32)
-    total += jnp.dot(sib_ref[...], got_ref[0], preferred_element_type=F32)
-    held[...] = total.reshape(held.shape)
-    q = held.shape[2] // 2
+    outs, (lat, sib) = refs[:-2], refs[-2:]
+    piece, half = outs[-1].shape[2:]
+    strip, q = SIDE * piece, half // 2
+
+    @pl.when(pl.program_id(0) == 0)
+    def _():
+        for step in range(SIDE):
+            to = lax.rem(p_ref[3] + step, SIDE)
+            for i in range(SIDE):
+                src = pl.ds(pl.multiple_of(place_of(p_ref, to, i) * piece, piece), piece)
+                at = step * strip + i * piece
+                lat[at : at + piece, :] = lat_ref[src, :]
+                sib[at : at + piece, :] = sib_ref[src, :]
+
+    total = jnp.dot(lat[...], dec_ref[0], preferred_element_type=F32)
+    total += jnp.dot(sib[...], got_ref[0], preferred_element_type=F32)
     for ref, (step, lo, hi) in zip(outs, CUTS):
-        to = lax.rem(p_ref[3] + step, SIDE)
-        for i in range(SIDE):
-            block = held[place_of(p_ref, to, i)]
-            ref[i, 0] = block[:, lo * q : hi * q].astype(ref.dtype)
+        block = total[step * strip : (step + 1) * strip, lo * q : hi * q]
+        ref[:, 0] = block.astype(ref.dtype).reshape(SIDE, piece, (hi - lo) * q)
 
 
 CUTS = ((2, 0, 1), (2, 1, 2), (1, 0, 1), (1, 1, 2), (3, 0, 1), (3, 1, 2), (0, 0, 2))
@@ -233,7 +242,7 @@
         (lat, sib, dec, got),
         4 * rows * lats * half * targets,
         11e6,
-        [pltpu.VMEM((SIDE * SIDE, piece, half), F32)],
+        [pltpu.VMEM((rows, lats), BF)] * 2,
         core=place,
     )
 
@@ -273,28 +282,28 @@
     parts, out, goal = refs[:SIDE], refs[SIDE], refs[SIDE + 1]
     few = own_ref.shape[1]
     for ref, side in ((own_ref, p_ref[2]), (got_ref, 1 - p_ref[2])):
-        goal[pl.ds(pl.multiple_of(side * few, few), few), :] = ref[0].astype(F32)
-    total = parts[0][0]
+        goal[:, pl.ds(pl.multiple_of(side * few, few), few), :] = ref[...].astype(F32)
+    total = parts[0][...]
     for part in parts[1:]:
-        total += part[0].astype(F32)
-    out[0] = ((total - goal[...]) * scale).astype(BF)
+        total += part[...].astype(F32)
+    out[...] = ((total - goal[...]) * scale).astype(BF)
 
 
 def error_call(scale, place, own, got, parts):
-    targets, piece, half = parts[0].shape
-    one = pl.BlockSpec((1, piece, half), lambda t, p: (t, 0, 0))
-    goal = pl.BlockSpec((1,) + own.shape[1:], lambda t, p: (t, 0, 0))
+    shape = parts[0].shape
+    one = pl.BlockSpec(shape, lambda t, p: (0, 0, 0))
+    goal = pl.BlockSpec(own.shape, lambda t, p: (0, 0, 0))
     return call(
         functools.partial(error_kernel, scale),
         "error",
-        (targets,),
+        (1,),
         [goal, goal] + [one] * SIDE,
         one,
-        jax.ShapeDtypeStruct((targets, piece, half), BF),
+        jax.ShapeDtypeStruct(shape, BF),
         (own, got, *parts),
-        8 * targets * piece * half,
+        8 * parts[0].size,
         2e6,
-        [pltpu.VMEM((piece, half), F32)],
+        [pltpu.VMEM(shape, F32)],
         core=place,
     )
 
@@ -305,19 +314,20 @@
     for k in range(SIDE):
         at = lax.rem(p_ref[4] + SIDE - k, SIDE)
         for h in range(2):
-            outs[h][at, 0] = parts[k][0, :, h * q : (h + 1) * q]
+            outs[h][at] = parts[k][:, :, h * q : (h + 1) * q]
 
 
 def join_call(place, parts, after):
     targets, piece, half = parts[0].shape
+    shape = (SIDE, targets, piece, half // 2)
     return call(
         join_kernel,
         "join",
-        (targets,),
+        (1,),
         [pl.BlockSpec(memory_space=pl.ANY)]
-        + [pl.BlockSpec((1, piece, half), lambda t, p: (t, 0, 0))] * SIDE,
-        [pl.BlockSpec((SIDE, 1, piece, half // 2), lambda t, p: (0, t, 0, 0))] * 2,
-        [jax.ShapeDtypeStruct((SIDE, targets, piece, half // 2), BF)] * 2,
+        + [pl.BlockSpec(parts[0].shape, lambda t, p: (0, 0, 0))] * SIDE,
+        [pl.BlockSpec(shape, lambda t, p: (0, 0, 0, 0))] * 2,
+        [jax.ShapeDtypeStruct(shape, BF)] * 2,
         (after, *parts),
         0,
         8 * parts[0].size,
@@ -523,7 +533,7 @@
 def enc_call(x, active, after, top, bottom):
     depth, rows = x.shape
     lats = active.shape[1]
-    step = 512
+    step = 1024
     return call(
         enc_kernel,
         "enc_grad",

time: 124 us -> 123 us (level)
  transfers between devices with their start and end apart: 31 -> 31, of which waited for: 16 -> 16; matrix products, arithmetic and copies ran while one was open for 0% -> 0% of each run, Pallas kernels for 12% -> 13%
where the time goes in v7:
time: 123 us; the launch traced here: 122 us
  starting transfers between devices  49.2 us (40%)
  waiting for transfers between devices  37.5 us (30%)
  Pallas kernels  33.4 us (27%)
    pallas_call x17, Pallas kernels, call(): pl.pallas_call(body, out_shape=shapes, compiler_params=pltpu.CompilerPara...  33.4 us
    ppermute x18, starting transfers between devices, shift(): return lax.ppermute(value, ('x', 'y', 'c'), moves)  31.8 us
    ppermute x18, waiting for transfers between devices, shift(): return lax.ppermute(value, ('x', 'y', 'c'), moves)  24.7 us
    ppermute x8, starting transfers between devices, pair(): return lax.ppermute(value, ('z', 'c'), moves)  16.5 us
    ppermute x8, waiting for transfers between devices, pair(): return lax.ppermute(value, ('z', 'c'), moves)  9.6 us
    ppermute x5, waiting for transfers between devices, swap(): return lax.ppermute(value, 'c', [(0, 1), (1, 0)])  3.2 us
  transfers between devices with their start and end apart: 31, of which 16 were waited for; matrix products, arithmetic and copies ran while one was open for 0% of the time, Pallas kernels for 13%

profile of v7, /device:TPU:0, one launch (start us, length us, event | category | flops | bytes accessed | tf_op | source)
XLA Modules:
  0.0 122.1 jit_solution(15227781845026745413)
XLA Ops:
  0.7 0.7 stack.23.p_ref
  1.3 4.4 %pre.1 = (bf16[256,512]{1,0:T(8,128)(2,1)S(1)}, bf16[256,512]{1,0:T(8,128)(2,1)S(1)}, bf16[3,512,1024]{2,1,0:T(8,128)(2,1)S(1)}, bf16[3,16,1024]{2,1,0:T(8,128)(2,1)S(1)}, bf16[3,16,1024]{2,1,0:T(8,128)(2,1)S(1)}) custom-call(s32[5]{0:T(128)} %stack.23.p_ref, bf16[512,2048]{1,0:T(8,128)(2,1)} %x_ref.3, bf16[2048,512]{1,0:T(8,128)(2,1)} %w_ref.1, ...), custom_call_target="tpu_custom_call" | custom-call | flops 1073741824 | bytes 4194304 | tf_op jit(solution)/shard_map/pre/pallas_call | solution.py:27
  5.8 2.1 %collective-permute-start.2 = (bf16[256,512]{1,0:T(8,128)(2,1)S(1)}, bf16[256,512]{1,0:T(8,128)(2,1)S(1)}, u32[]{:S(2)}, u32[]{:S(2)}) collective-permute-start(bf16[256,512]{1,0:T(8,128)(2,1)S(1)} %get-tuple-element.47), channel_id=1, source_target_pairs={{0,32},{1,97},{32,0},{33,65},{64,96},{65,33},{96,64},{97,1},{2,34}... | collective-permute-start | bytes 786440 | tf_op jit(solution)/shard_map/ppermute | solution.py:590
  8.0 4.3 %collective-permute-done.2 = bf16[256,512]{1,0:T(8,128)(2,1)S(1)} collective-permute-done((bf16[256,512]{1,0:T(8,128)(2,1)S(1)}, bf16[256,512]{1,0:T(8,128)(2,1)S(1)}, u32[]{:S(2)}, u32[]{:S(2)}) %collective-permute-start.2) | collective-permute-done | bytes 262176 | tf_op jit(solution)/shard_map/ppermute | solution.py:590
  12.4 4.2 %collective-permute-start.3 = (bf16[256,512]{1,0:T(8,128)(2,1)S(1)}, bf16[256,512]{1,0:T(8,128)(2,1)S(1)}, u32[]{:S(2)}, u32[]{:S(2)}) collective-permute-start(bf16[256,512]{1,0:T(8,128)(2,1)S(1)} %get-tuple-element.89), channel_id=1, source_target_pairs={{0,96},{1,33},{32,64},{33,1},{64,32},{65,97},{96,0},{97,65},{2,98}... | collective-permute-start | bytes 786440 | tf_op jit(solution)/shard_map/ppermute | solution.py:590
  16.7 2.7 %collective-permute-start.1 = (bf16[256,512]{1,0:T(8,128)(2,1)S(1)}, bf16[256,512]{1,0:T(8,128)(2,1)S(1)}, u32[]{:S(2)}, u32[]{:S(2)}) collective-permute-start(bf16[256,512]{1,0:T(8,128)(2,1)S(1)} %get-tuple-element.91), channel_id=1, source_target_pairs={{0,96},{1,33},{32,64},{33,1},{64,32},{65,97},{96,0},{97,65},{2,98}... | collective-permute-start | bytes 786440 | tf_op jit(solution)/shard_map/ppermute | solution.py:590
  19.4 1.0 pick_half.1
  20.9 3.4 %collective-permute-done.1.far_a = bf16[256,512]{1,0:T(8,128)(2,1)S(1)} collective-permute-done((bf16[256,512]{1,0:T(8,128)(2,1)S(1)}, bf16[256,512]{1,0:T(8,128)(2,1)S(1)}, u32[]{:S(2)}, u32[]{:S(2)}) %collective-permute-start.1) | collective-permute-done | bytes 262176 | tf_op jit(solution)/shard_map/ppermute | solution.py:590
  24.7 1.9 %collective-permute-done.5.sib_ref = bf16[512,512]{1,0:T(8,128)(2,1)S(1)} collective-permute-done((bf16[512,512]{1,0:T(8,128)(2,1)S(1)}, bf16[512,512]{1,0:T(8,128)(2,1)S(1)}, u32[]{:S(2)}, u32[]{:S(2)}) %collective-permute-start.5) | collective-permute-done | bytes 524320 | tf_op jit(solution)/shard_map/ppermute | solution.py:560
  26.6 4.8 %rebuild.1 = (bf16[4,3,32,512]{3,2,1,0:T(8,128)(2,1)S(1)}, bf16[4,3,32,512]{3,2,1,0:T(8,128)(2,1)S(1)}, f32[4,3,32,512]{3,2,1,0:T(8,128)S(1)}, bf16[4,3,32,512]{...) custom-call(s32[5]{0:T(128)S(1)} %copy-done.2, ...), custom_call_target="tpu_custom_call" | custom-call | flops 3221225472 | bytes 11000000 | tf_op jit(solution)/shard_map/rebuild/pallas_call | solution.py:27
  31.4 2.8 %collective-permute-start.11 = (bf16[4,3,32,512]{3,2,1,0:T(8,128)(2,1)S(1)}, bf16[4,3,32,512]{3,2,1,0:T(8,128)(2,1)S(1)}, u32[]{:S(2)}, u32[]{:S(2)}) collective-permute-start(bf16[4,3,32,512]{3,2,1,0:T(8,128)(2,1)S(1)} %get-tuple-element.59), channel_id=1, source_target_pairs={{0,24},{1,7},{2,26},{3,1},{4,28},{5,3},{6,30},{7,5},{8,0},{9,15},{... | collective-permute-start | bytes 1179656 | tf_op jit(solution)/shard_map/ppermute | solution.py:610
  34.3 0.8 collective-permute-start.10
  35.0 2.5 %collective-permute-start.9 = (bf16[4,3,32,512]{3,2,1,0:T(8,128)(2,1)S(1)}, bf16[4,3,32,512]{3,2,1,0:T(8,128)(2,1)S(1)}, u32[]{:S(2)}, u32[]{:S(2)}) collective-permute-start(bf16[4,3,32,512]{3,2,1,0:T(8,128)(2,1)S(1)} %get-tuple-element.56), channel_id=1, source_target_pairs={{0,24},{1,7},{2,26},{3,1},{4,28},{5,3},{6,30},{7,5},{8,0},{9,15},{... | collective-permute-start | bytes 1179656 | tf_op jit(solution)/shard_map/ppermute | solution.py:610
  37.5 2.0 %collective-permute-done.11 = bf16[4,3,32,512]{3,2,1,0:T(8,128)(2,1)S(1)} collective-permute-done((bf16[4,3,32,512]{3,2,1,0:T(8,128)(2,1)S(1)}, bf16[4,3,32,512]{3,2,1,0:T(8,128)(2,1)S(1)}, u32[]{:S(2)}, u32[]{:S(2)}) %collective-permute-start.11) | collective-permute-done | bytes 393248 | tf_op jit(solution)/shard_map/ppermute | solution.py:610
  39.7 3.8 %collective-permute-start.12 = (bf16[4,3,32,512]{3,2,1,0:T(8,128)(2,1)S(1)}, bf16[4,3,32,512]{3,2,1,0:T(8,128)(2,1)S(1)}, u32[]{:S(2)}, u32[]{:S(2)}) collective-permute-start(bf16[4,3,32,512]{3,2,1,0:T(8,128)(2,1)S(1)} %add_convert_fusion), channel_id=1, source_target_pairs={{0,24},{1,7},{2,26},{3,1},{4,28},{5,3},{6,30},{7,5},{8,0},{9,15},{... | collective-permute-start | bytes 1179656 | tf_op jit(solution)/shard_map/ppermute | solution.py:610
  43.7 3.8 %collective-permute-done.10.refs_2_ = bf16[4,3,32,512]{3,2,1,0:T(8,128)(2,1)S(1)} collective-permute-done((bf16[4,3,32,512]{3,2,1,0:T(8,128)(2,1)S(1)}, bf16[4,3,32,512]{3,2,1,0:T(8,128)(2,1)S(1)}, u32[]{:S(2)}, u32[]{:S(2)}) %collective-permute-start.10) | collective-permute-done | bytes 393248 | tf_op jit(solution)/shard_map/ppermute | solution.py:610
  47.5 1.3 %collective-permute-done.12.refs_3_ = bf16[4,3,32,512]{3,2,1,0:T(8,128)(2,1)S(1)} collective-permute-done((bf16[4,3,32,512]{3,2,1,0:T(8,128)(2,1)S(1)}, bf16[4,3,32,512]{3,2,1,0:T(8,128)(2,1)S(1)}, u32[]{:S(2)}, u32[]{:S(2)}) %collective-permute-start.12) | collective-permute-done | bytes 393248 | tf_op jit(solution)/shard_map/ppermute | solution.py:610
  48.7 3.9 %collective-permute-done.8.refs_0_ = bf16[4,3,32,512]{3,2,1,0:T(8,128)(2,1)S(1)} collective-permute-done((bf16[4,3,32,512]{3,2,1,0:T(8,128)(2,1)S(1)}, bf16[4,3,32,512]{3,2,1,0:T(8,128)(2,1)S(1)}, u32[]{:S(2)}, u32[]{:S(2)}) %collective-permute-start.8) | collective-permute-done | bytes 393248 | tf_op jit(solution)/shard_map/ppermute | solution.py:610
  52.6 1.2 %sum_first.1 = (f32[3,32,1024]{2,1,0:T(8,128)S(1)}, bf16[3,32,1024]{2,1,0:T(8,128)(2,1)S(1)}, bf16[3,32,1024]{2,1,0:T(8,128)(2,1)S(1)}, bf16[3,32,1024]{2,1,0:T(8,128)(2,1)S(1)}) custom-call(s32[5]{0:T(128)S(1)} %copy-done.2, f32[4,3,32,1024]{3,2,1,0:T(8,128)S(1)} %get-tuple-element.53.own_ref, bf16[4,3,32,512]{3,2,1,0:T(8,128)(2,1)S(1)} %collective-permute-done.8.refs_0_, ...), custom_call_target="tpu_custom_call" | custom-call | flops 1572864 | bytes 4718592 | tf_op jit(solution)/shard_map/sum_first/pallas_call | solution.py:27
  53.9 1.6 %collective-permute-start.13 = (bf16[3,32,1024]{2,1,0:T(8,128)(2,1)S(1)}, bf16[3,32,1024]{2,1,0:T(8,128)(2,1)S(1)}, u32[]{:S(2)}, u32[]{:S(2)}) collective-permute-start(bf16[3,32,1024]{2,1,0:T(8,128)(2,1)S(1)} %get-tuple-element.61), channel_id=1, source_target_pairs={{0,2},{1,9},{2,4},{3,11},{4,6},{5,13},{6,0},{7,15},{8,10},{9,17},{... | collective-permute-start | bytes 589832 | tf_op jit(solution)/shard_map/ppermute | solution.py:610
  55.5 2.9 %collective-permute-start.14 = (bf16[3,32,1024]{2,1,0:T(8,128)(2,1)S(1)}, bf16[3,32,1024]{2,1,0:T(8,128)(2,1)S(1)}, u32[]{:S(2)}, u32[]{:S(2)}) collective-permute-start(bf16[3,32,1024]{2,1,0:T(8,128)(2,1)S(1)} %get-tuple-element.62), channel_id=1, source_target_pairs={{0,4},{1,17},{2,6},{3,19},{4,0},{5,21},{6,2},{7,23},{8,12},{9,25},... | collective-permute-start | bytes 589832 | tf_op jit(solution)/shard_map/ppermute | solution.py:610
  58.4 1.7 %collective-permute-start.15 = (bf16[3,32,1024]{2,1,0:T(8,128)(2,1)S(1)}, bf16[3,32,1024]{2,1,0:T(8,128)(2,1)S(1)}, u32[]{:S(2)}, u32[]{:S(2)}) collective-permute-start(bf16[3,32,1024]{2,1,0:T(8,128)(2,1)S(1)} %get-tuple-element.63), channel_id=1, source_target_pairs={{0,6},{1,25},{2,0},{3,27},{4,2},{5,29},{6,4},{7,31},{8,14},{9,1},{... | collective-permute-start | bytes 589832 | tf_op jit(solution)/shard_map/ppermute | solution.py:610
  60.1 1.3 %collective-permute-done.4.got_ref = bf16[3,16,1024]{2,1,0:T(8,128)(2,1)S(1)} collective-permute-done((bf16[3,16,1024]{2,1,0:T(8,128)(2,1)S(1)}, bf16[3,16,1024]{2,1,0:T(8,128)(2,1)S(1)}, u32[]{:S(2)}, u32[]{:S(2)}) %collective-permute-start.4) | collective-permute-done | bytes 98336 | tf_op jit(solution)/shard_map/ppermute | solution.py:560
  61.4 2.8 %collective-permute-done.14.refs_2_ = bf16[3,32,1024]{2,1,0:T(8,128)(2,1)S(1)} collective-permute-done((bf16[3,32,1024]{2,1,0:T(8,128)(2,1)S(1)}, bf16[3,32,1024]{2,1,0:T(8,128)(2,1)S(1)}, u32[]{:S(2)}, u32[]{:S(2)}) %collective-permute-start.14) | collective-permute-done | bytes 196640 | tf_op jit(solution)/shard_map/ppermute | solution.py:610
  64.2 0.7 error.1.after_ref.refs_0_
  64.9 1.7 %collective-permute-start.16 = (bf16[3,32,1024]{2,1,0:T(8,128)(2,1)S(1)}, bf16[3,32,1024]{2,1,0:T(8,128)(2,1)S(1)}, u32[]{:S(2)}, u32[]{:S(2)}) collective-permute-start(bf16[3,32,1024]{2,1,0:T(8,128)(2,1)S(1)} %error.1.after_ref.refs_0_), channel_id=1, source_target_pairs={{0,2},{1,9},{2,4},{3,11},{4,6},{5,13},{6,0},{7,15},{8,10},{9,17},{... | collective-permute-start | bytes 589832 | tf_op jit(solution)/shard_map/ppermute | solution.py:610
  66.6 2.6 %collective-permute-start.17 = (bf16[3,32,1024]{2,1,0:T(8,128)(2,1)S(1)}, bf16[3,32,1024]{2,1,0:T(8,128)(2,1)S(1)}, u32[]{:S(2)}, u32[]{:S(2)}) collective-permute-start(bf16[3,32,1024]{2,1,0:T(8,128)(2,1)S(1)} %error.1.after_ref.refs_0_), channel_id=1, source_target_pairs={{0,4},{1,17},{2,6},{3,19},{4,0},{5,21},{6,2},{7,23},{8,12},{9,25},... | collective-permute-start | bytes 589832 | tf_op jit(solution)/shard_map/ppermute | solution.py:610
  69.3 1.5 %collective-permute-start.18 = (bf16[3,32,1024]{2,1,0:T(8,128)(2,1)S(1)}, bf16[3,32,1024]{2,1,0:T(8,128)(2,1)S(1)}, u32[]{:S(2)}, u32[]{:S(2)}) collective-permute-start(bf16[3,32,1024]{2,1,0:T(8,128)(2,1)S(1)} %error.1.after_ref.refs_0_), channel_id=1, source_target_pairs={{0,6},{1,25},{2,0},{3,27},{4,2},{5,29},{6,4},{7,31},{8,14},{9,1},{... | collective-permute-start | bytes 589832 | tf_op jit(solution)/shard_map/ppermute | solution.py:610
  70.8 1.1 turn.1
  72.0 1.8 %turn_dec.1 = (bf16[3,1024,512]{2,1,0:T(8,128)(2,1)S(1)}, bf16[3,1024,512]{2,1,0:T(8,128)(2,1)S(1)}, f32[8,128]{1,0:T(8,128)S(1)}) custom-call(bf16[3,512,1024]{2,1,0:T(8,128)(2,1)S(1)} %get-tuple-element.51.dec_ref.own_ref, bf16[3,512,1024]{2,1,0:T(8,128)(2,1)S(1)} %collective-permute-done.6.got_ref, f32[8,128]{1,0:T(8,128)S(1)} %get-tuple-element.66.after_ref), custom_call_target="tpu_custom_call" | custom-call | bytes 12000000 | tf_op jit(solution)/shard_map/turn_dec/pallas_call | solution.py:27
  73.8 2.6 %collective-permute-done.17.refs_2_ = bf16[3,32,1024]{2,1,0:T(8,128)(2,1)S(1)} collective-permute-done((bf16[3,32,1024]{2,1,0:T(8,128)(2,1)S(1)}, bf16[3,32,1024]{2,1,0:T(8,128)(2,1)S(1)}, u32[]{:S(2)}, u32[]{:S(2)}) %collective-permute-start.17) | collective-permute-done | bytes 196640 | tf_op jit(solution)/shard_map/ppermute | solution.py:610
  76.4 0.6 join.1
  77.1 3.2 %collective-permute-start.22 = (bf16[4,3,32,512]{3,2,1,0:T(8,128)(2,1)S(1)}, bf16[4,3,32,512]{3,2,1,0:T(8,128)(2,1)S(1)}, u32[]{:S(2)}, u32[]{:S(2)}) collective-permute-start(bf16[4,3,32,512]{3,2,1,0:T(8,128)(2,1)S(1)} %get-tuple-element.70.refs_1_), channel_id=1, source_target_pairs={{0,24},{1,7},{2,26},{3,1},{4,28},{5,3},{6,30},{7,5},{8,0},{9,15},{... | collective-permute-start | bytes 1179656 | tf_op jit(solution)/shard_map/ppermute | solution.py:610
  80.4 3.2 %collective-permute-start.24 = (bf16[4,3,32,512]{3,2,1,0:T(8,128)(2,1)S(1)}, bf16[4,3,32,512]{3,2,1,0:T(8,128)(2,1)S(1)}, u32[]{:S(2)}, u32[]{:S(2)}) collective-permute-start(bf16[4,3,32,512]{3,2,1,0:T(8,128)(2,1)S(1)} %get-tuple-element.69.refs_0_), channel_id=1, source_target_pairs={{0,24},{1,7},{2,26},{3,1},{4,28},{5,3},{6,30},{7,5},{8,0},{9,15},{... | collective-permute-start | bytes 1179656 | tf_op jit(solution)/shard_map/ppermute | solution.py:610
  83.6 2.5 %collective-permute-done.19.refs_2_ = bf16[4,3,32,512]{3,2,1,0:T(8,128)(2,1)S(1)} collective-permute-done((bf16[4,3,32,512]{3,2,1,0:T(8,128)(2,1)S(1)}, bf16[4,3,32,512]{3,2,1,0:T(8,128)(2,1)S(1)}, u32[]{:S(2)}, u32[]{:S(2)}) %collective-permute-start.19) | collective-permute-done | bytes 393248 | tf_op jit(solution)/shard_map/ppermute | solution.py:610
  86.1 3.2 %collective-permute-start.23 = (bf16[4,3,32,512]{3,2,1,0:T(8,128)(2,1)S(1)}, bf16[4,3,32,512]{3,2,1,0:T(8,128)(2,1)S(1)}, u32[]{:S(2)}, u32[]{:S(2)}) collective-permute-start(bf16[4,3,32,512]{3,2,1,0:T(8,128)(2,1)S(1)} %collective-permute-done.22.refs_7_), channel_id=1, source_target_pairs={{0,24},{1,7},{2,26},{3,1},{4,28},{5,3},{6,30},{7,5},{8,0},{9,15},{... | collective-permute-start | bytes 1179656 | tf_op jit(solution)/shard_map/ppermute | solution.py:610
  89.4 1.0 collective-permute-done.20.refs_3_
  90.3 4.8 %collective-permute-done.21.refs_4_ = bf16[4,3,32,512]{3,2,1,0:T(8,128)(2,1)S(1)} collective-permute-done((bf16[4,3,32,512]{3,2,1,0:T(8,128)(2,1)S(1)}, bf16[4,3,32,512]{3,2,1,0:T(8,128)(2,1)S(1)}, u32[]{:S(2)}, u32[]{:S(2)}) %collective-permute-start.21) | collective-permute-done | bytes 393248 | tf_op jit(solution)/shard_map/ppermute | solution.py:610
  95.1 3.5 %back_sib.1 = (bf16[3,512,1024]{2,1,0:T(8,128)(2,1)S(1)}, bf16[512,512]{1,0:T(8,128)(2,1)S(1)}) custom-call(s32[5]{0:T(128)S(1)} %copy-done.2, bf16[3,1024,512]{2,1,0:T(8,128)(2,1)S(1)} %get-tuple-element.67.dec_ref, bf16[4,3,32,512]{3,2,1,0:T(8,128)(2,1)S(1)} %get-tuple-element.69.refs_0_, bf16[4,3,32,512]{3,2,1,0:T(8,128)(2,1)S(1)} %get-tuple-element.70.refs_1_, ...), custom_call_target="tpu_custom_call" | custom-call | flops 1610612736 | bytes 10000000 | tf_op jit(solution)/shard_map/back_sib/pallas_call | solution.py:27
  98.7 3.0 %back_own.1.own_ref = f32[512,512]{1,0:T(8,128)S(1)} custom-call(s32[5]{0:T(128)S(1)} %copy-done.2, bf16[3,512,1024]{2,1,0:T(8,128)(2,1)S(1)} %get-tuple-element.71.err_ref, bf16[3,1024,512]{2,1,0:T(8,128)(2,1)S(1)} %get-tuple-element.72.dec_ref), custom_call_target="tpu_custom_call" | custom-call | flops 1610612736 | bytes 7000000 | tf_op jit(solution)/shard_map/back_own/pallas_call | solution.py:27
  101.9 0.6 collective-permute-start.26
  102.5 2.0 %collective-permute-start.27 = (bf16[256,512]{1,0:T(8,128)(2,1)S(1)}, bf16[256,512]{1,0:T(8,128)(2,1)S(1)}, u32[]{:S(2)}, u32[]{:S(2)}) collective-permute-start(bf16[256,512]{1,0:T(8,128)(2,1)S(1)} %get-tuple-element.78), channel_id=1, source_target_pairs={{0,32},{1,97},{32,0},{33,65},{64,96},{65,33},{96,64},{97,1},{2,34}... | collective-permute-start | bytes 786440 | tf_op jit(solution)/shard_map/ppermute | solution.py:590
  104.5 3.9 %dec_grad_own.1 = (bf16[3,512,2048]{2,1,0:T(8,128)(2,1)}, f32[8,128]{1,0:T(8,128)S(1)}) custom-call(s32[5]{0:T(128)S(1)} %copy-done.2, bf16[512,512]{1,0:T(8,128)(2,1)S(1)} %get-tuple-element.65.lat_ref, bf16[3,512,1024]{2,1,0:T(8,128)(2,1)S(1)} %get-tuple-element.74.err_ref), custom_call_target="tpu_custom_call" | custom-call | flops 1610612736 | bytes 7000000 | tf_op jit(solution)/shard_map/dec_grad_own/pallas_call | solution.py:27
  108.9 2.7 %collective-permute-start.30 = (bf16[256,512]{1,0:T(8,128)(2,1)S(1)}, bf16[256,512]{1,0:T(8,128)(2,1)S(1)}, u32[]{:S(2)}, u32[]{:S(2)}) collective-permute-start(bf16[256,512]{1,0:T(8,128)(2,1)S(1)} %get-tuple-element.85), channel_id=1, source_target_pairs={{0,96},{1,33},{32,64},{33,1},{64,32},{65,97},{96,0},{97,65},{2,98}... | collective-permute-start | bytes 786440 | tf_op jit(solution)/shard_map/ppermute | solution.py:590
  111.7 2.7 %collective-permute-start.28 = (bf16[256,512]{1,0:T(8,128)(2,1)S(1)}, bf16[256,512]{1,0:T(8,128)(2,1)S(1)}, u32[]{:S(2)}, u32[]{:S(2)}) collective-permute-start(bf16[256,512]{1,0:T(8,128)(2,1)S(1)} %get-tuple-element.81), channel_id=1, source_target_pairs={{0,96},{1,33},{32,64},{33,1},{64,32},{65,97},{96,0},{97,65},{2,98}... | collective-permute-start | bytes 786440 | tf_op jit(solution)/shard_map/ppermute | solution.py:590
  114.5 3.9 %dec_grad_sib.1 = (bf16[3,512,2048]{2,1,0:T(8,128)(2,1)}, f32[8,128]{1,0:T(8,128)S(1)}) custom-call(s32[5]{0:T(128)S(1)} %copy-done.2, bf16[512,512]{1,0:T(8,128)(2,1)S(1)} %get-tuple-element.65.lat_ref, bf16[3,512,1024]{2,1,0:T(8,128)(2,1)S(1)} %collective-permute-done.26.err_ref, ...), custom_call_target="tpu_custom_call", output_to_operand_aliasing={{0}: (3, {})} | custom-call | flops 1610612736 | bytes 7000000 | tf_op jit(solution)/shard_map/dec_grad_sib/pallas_call | solution.py:27
  118.4 1.0 collective-permute-done.28.far_a
  119.4 2.7 %enc_grad.1 = (bf16[2048,512]{1,0:T(8,128)(2,1)}, f32[1,512]{1,0:T(1,128)}) custom-call(bf16[2048,512]{1,0:T(8,128)(2,1)S(1)} %get-tuple-element.64.x_ref, s32[512,512]{1,0:T(8,128)S(1)} %copy-done.1, f32[8,128]{1,0:T(8,128)S(1)} %get-tuple-element.76.after_ref, f32[256,512]{1,0:T(8,128)S(1)} %get-tuple-element.80.near_a, ...), custom_call_target="tpu_custom_call" | custom-call | flops 1073741824 | bytes 7000000 | tf_op jit(solution)/shard_map/enc_grad/pallas_call | solution.py:27
  (49 shorter events, 2.4 us)
Async XLA Ops:
  0.6 18.7 %slice-start = ((s8[6291456]{0:T(1024)(128)(4,1)}), s8[2097152]{0:T(1024)(128)(4,1)S(1)}, s32[]{:S(2)}) async-start(s8[6291456]{0:T(1024)(128)(4,1)} %bitcast.7), calls=%async_computation | async-start | bytes 4194304
  1.3 18.1 %slice-start.1 = ((s8[6291456]{0:T(1024)(128)(4,1)}), s8[4194304]{0:T(1024)(128)(4,1)S(1)}, s32[]{:S(2)}) async-start(s8[6291456]{0:T(1024)(128)(4,1)} %bitcast.7), calls=%async_computation.1 | async-start | bytes 8388608
  1.3 18.1 %copy-start.2 = (s32[5]{0:T(128)S(1)}, s32[5]{0:T(128)}, u32[]{:S(2)}) copy-start(s32[5]{0:T(128)} %stack.23.p_ref) | copy-start | bytes 64
  5.7 20.8 %collective-permute-start.6 = (bf16[3,512,1024]{2,1,0:T(8,128)(2,1)S(1)}, bf16[3,512,1024]{2,1,0:T(8,128)(2,1)S(1)}, u32[]{:S(2)}, u32[]{:S(2)}) collective-permute-start(bf16[3,512,1024]{2,1,0:T(8,128)(2,1)S(1)} %get-tuple-element.52), channel_id=1, source_target_pairs={{0,1},{1,0},{2,3},{3,2},{4,5},{5,4},{6,7},{7,6},{8,9},{9,8},{10,11... | collective-permute-start | bytes 9437192 | tf_op jit(solution)/shard_map/ppermute | solution.py:560
  5.8 6.5 %collective-permute-start.2 = (bf16[256,512]{1,0:T(8,128)(2,1)S(1)}, bf16[256,512]{1,0:T(8,128)(2,1)S(1)}, u32[]{:S(2)}, u32[]{:S(2)}) collective-permute-start(bf16[256,512]{1,0:T(8,128)(2,1)S(1)} %get-tuple-element.47), channel_id=1, source_target_pairs={{0,32},{1,97},{32,0},{33,65},{64,96},{65,33},{96,64},{97,1},{2,34}... | collective-permute-start | bytes 786440 | tf_op jit(solution)/shard_map/ppermute | solution.py:590
  7.9 8.7 %collective-permute-start = (bf16[256,512]{1,0:T(8,128)(2,1)S(1)}, bf16[256,512]{1,0:T(8,128)(2,1)S(1)}, u32[]{:S(2)}, u32[]{:S(2)}) collective-permute-start(bf16[256,512]{1,0:T(8,128)(2,1)S(1)} %get-tuple-element.46), channel_id=1, source_target_pairs={{0,32},{1,97},{32,0},{33,65},{64,96},{65,33},{96,64},{97,1},{2,34}... | collective-permute-start | bytes 786440 | tf_op jit(solution)/shard_map/ppermute | solution.py:590
  12.4 8.6 %collective-permute-start.3 = (bf16[256,512]{1,0:T(8,128)(2,1)S(1)}, bf16[256,512]{1,0:T(8,128)(2,1)S(1)}, u32[]{:S(2)}, u32[]{:S(2)}) collective-permute-start(bf16[256,512]{1,0:T(8,128)(2,1)S(1)} %get-tuple-element.89), channel_id=1, source_target_pairs={{0,96},{1,33},{32,64},{33,1},{64,32},{65,97},{96,0},{97,65},{2,98}... | collective-permute-start | bytes 786440 | tf_op jit(solution)/shard_map/ppermute | solution.py:590
  16.7 7.7 %collective-permute-start.1 = (bf16[256,512]{1,0:T(8,128)(2,1)S(1)}, bf16[256,512]{1,0:T(8,128)(2,1)S(1)}, u32[]{:S(2)}, u32[]{:S(2)}) collective-permute-start(bf16[256,512]{1,0:T(8,128)(2,1)S(1)} %get-tuple-element.91), channel_id=1, source_target_pairs={{0,96},{1,33},{32,64},{33,1},{64,32},{65,97},{96,0},{97,65},{2,98}... | collective-permute-start | bytes 786440 | tf_op jit(solution)/shard_map/ppermute | solution.py:590
  19.4 4.9 %copy-start.1 = (s32[512,512]{1,0:T(8,128)S(1)}, s32[512,512]{1,0:T(8,128)}, u32[]{:S(2)}) copy-start(s32[512,512]{1,0:T(8,128)} %active_ref.3) | copy-start | bytes 3145732
  19.4 4.9 %copy-start.3 = (f32[512]{0:T(512)S(1)}, f32[512]{0:T(512)}, u32[]{:S(2)}) copy-start(f32[512]{0:T(512)} %param.8) | copy-start | bytes 6148
  24.6 2.0 %collective-permute-start.5 = (bf16[512,512]{1,0:T(8,128)(2,1)S(1)}, bf16[512,512]{1,0:T(8,128)(2,1)S(1)}, u32[]{:S(2)}, u32[]{:S(2)}) collective-permute-start(bf16[512,512]{1,0:T(8,128)(2,1)S(1)} %latents.1.lat_ref), channel_id=1, source_target_pairs={{0,1},{1,0},{2,3},{3,2},{4,5},{5,4},{6,7},{7,6},{8,9},{9,8},{10,11... | collective-permute-start | bytes 1572872 | tf_op jit(solution)/shard_map/ppermute | solution.py:560
  31.4 8.1 %collective-permute-start.11 = (bf16[4,3,32,512]{3,2,1,0:T(8,128)(2,1)S(1)}, bf16[4,3,32,512]{3,2,1,0:T(8,128)(2,1)S(1)}, u32[]{:S(2)}, u32[]{:S(2)}) collective-permute-start(bf16[4,3,32,512]{3,2,1,0:T(8,128)(2,1)S(1)} %get-tuple-element.59), channel_id=1, source_target_pairs={{0,24},{1,7},{2,26},{3,1},{4,28},{5,3},{6,30},{7,5},{8,0},{9,15},{... | collective-permute-start | bytes 1179656 | tf_op jit(solution)/shard_map/ppermute | solution.py:610
  34.3 9.2 %collective-permute-start.7 = (bf16[4,3,32,512]{3,2,1,0:T(8,128)(2,1)S(1)}, bf16[4,3,32,512]{3,2,1,0:T(8,128)(2,1)S(1)}, u32[]{:S(2)}, u32[]{:S(2)}) collective-permute-start(bf16[4,3,32,512]{3,2,1,0:T(8,128)(2,1)S(1)} %get-tuple-element.55), channel_id=1, source_target_pairs={{0,8},{1,3},{2,10},{3,5},{4,12},{5,7},{6,14},{7,1},{8,16},{9,11},{... | collective-permute-start | bytes 1179656 | tf_op jit(solution)/shard_map/ppermute | solution.py:610
  34.3 13.2 %collective-permute-start.10 = (bf16[4,3,32,512]{3,2,1,0:T(8,128)(2,1)S(1)}, bf16[4,3,32,512]{3,2,1,0:T(8,128)(2,1)S(1)}, u32[]{:S(2)}, u32[]{:S(2)}) collective-permute-start(bf16[4,3,32,512]{3,2,1,0:T(8,128)(2,1)S(1)} %get-tuple-element.57), channel_id=1, source_target_pairs={{0,8},{1,3},{2,10},{3,5},{4,12},{5,7},{6,14},{7,1},{8,16},{9,11},{... | collective-permute-start | bytes 1179656 | tf_op jit(solution)/shard_map/ppermute | solution.py:610
  35.0 12.4 %collective-permute-start.9 = (bf16[4,3,32,512]{3,2,1,0:T(8,128)(2,1)S(1)}, bf16[4,3,32,512]{3,2,1,0:T(8,128)(2,1)S(1)}, u32[]{:S(2)}, u32[]{:S(2)}) collective-permute-start(bf16[4,3,32,512]{3,2,1,0:T(8,128)(2,1)S(1)} %get-tuple-element.56), channel_id=1, source_target_pairs={{0,24},{1,7},{2,26},{3,1},{4,28},{5,3},{6,30},{7,5},{8,0},{9,15},{... | collective-permute-start | bytes 1179656 | tf_op jit(solution)/shard_map/ppermute | solution.py:610
  39.7 31.1 %copy-start = (bf16[512,2048]{1,0:T(8,128)(2,1)S(1)}, bf16[512,2048]{1,0:T(8,128)(2,1)}, u32[]{:S(2)}) copy-start(bf16[512,2048]{1,0:T(8,128)(2,1)} %x_ref.3) | copy-start | bytes 6291460
  39.7 9.1 %collective-permute-start.12 = (bf16[4,3,32,512]{3,2,1,0:T(8,128)(2,1)S(1)}, bf16[4,3,32,512]{3,2,1,0:T(8,128)(2,1)S(1)}, u32[]{:S(2)}, u32[]{:S(2)}) collective-permute-start(bf16[4,3,32,512]{3,2,1,0:T(8,128)(2,1)S(1)} %add_convert_fusion), channel_id=1, source_target_pairs={{0,24},{1,7},{2,26},{3,1},{4,28},{5,3},{6,30},{7,5},{8,0},{9,15},{... | collective-permute-start | bytes 1179656 | tf_op jit(solution)/shard_map/ppermute | solution.py:610
  43.6 9.1 %collective-permute-start.8 = (bf16[4,3,32,512]{3,2,1,0:T(8,128)(2,1)S(1)}, bf16[4,3,32,512]{3,2,1,0:T(8,128)(2,1)S(1)}, u32[]{:S(2)}, u32[]{:S(2)}) collective-permute-start(bf16[4,3,32,512]{3,2,1,0:T(8,128)(2,1)S(1)} %add_convert_fusion.1), channel_id=1, source_target_pairs={{0,8},{1,3},{2,10},{3,5},{4,12},{5,7},{6,14},{7,1},{8,16},{9,11},{... | collective-permute-start | bytes 1179656 | tf_op jit(solution)/shard_map/ppermute | solution.py:610
  53.9 7.5 %collective-permute-start.13 = (bf16[3,32,1024]{2,1,0:T(8,128)(2,1)S(1)}, bf16[3,32,1024]{2,1,0:T(8,128)(2,1)S(1)}, u32[]{:S(2)}, u32[]{:S(2)}) collective-permute-start(bf16[3,32,1024]{2,1,0:T(8,128)(2,1)S(1)} %get-tuple-element.61), channel_id=1, source_target_pairs={{0,2},{1,9},{2,4},{3,11},{4,6},{5,13},{6,0},{7,15},{8,10},{9,17},{... | collective-permute-start | bytes 589832 | tf_op jit(solution)/shard_map/ppermute | solution.py:610
  55.5 8.7 %collective-permute-start.14 = (bf16[3,32,1024]{2,1,0:T(8,128)(2,1)S(1)}, bf16[3,32,1024]{2,1,0:T(8,128)(2,1)S(1)}, u32[]{:S(2)}, u32[]{:S(2)}) collective-permute-start(bf16[3,32,1024]{2,1,0:T(8,128)(2,1)S(1)} %get-tuple-element.62), channel_id=1, source_target_pairs={{0,4},{1,17},{2,6},{3,19},{4,0},{5,21},{6,2},{7,23},{8,12},{9,25},... | collective-permute-start | bytes 589832 | tf_op jit(solution)/shard_map/ppermute | solution.py:610
  58.4 5.8 %collective-permute-start.15 = (bf16[3,32,1024]{2,1,0:T(8,128)(2,1)S(1)}, bf16[3,32,1024]{2,1,0:T(8,128)(2,1)S(1)}, u32[]{:S(2)}, u32[]{:S(2)}) collective-permute-start(bf16[3,32,1024]{2,1,0:T(8,128)(2,1)S(1)} %get-tuple-element.63), channel_id=1, source_target_pairs={{0,6},{1,25},{2,0},{3,27},{4,2},{5,29},{6,4},{7,31},{8,14},{9,1},{... | collective-permute-start | bytes 589832 | tf_op jit(solution)/shard_map/ppermute | solution.py:610
  60.1 1.3 %collective-permute-start.4 = (bf16[3,16,1024]{2,1,0:T(8,128)(2,1)S(1)}, bf16[3,16,1024]{2,1,0:T(8,128)(2,1)S(1)}, u32[]{:S(2)}, u32[]{:S(2)}) collective-permute-start(bf16[3,16,1024]{2,1,0:T(8,128)(2,1)S(1)} %get-tuple-element.50), channel_id=1, source_target_pairs={{0,1},{1,0},{2,3},{3,2},{4,5},{5,4},{6,7},{7,6},{8,9},{9,8},{10,11... | collective-permute-start | bytes 294920 | tf_op jit(solution)/shard_map/ppermute | solution.py:560
  64.9 8.9 %collective-permute-start.16 = (bf16[3,32,1024]{2,1,0:T(8,128)(2,1)S(1)}, bf16[3,32,1024]{2,1,0:T(8,128)(2,1)S(1)}, u32[]{:S(2)}, u32[]{:S(2)}) collective-permute-start(bf16[3,32,1024]{2,1,0:T(8,128)(2,1)S(1)} %error.1.after_ref.refs_0_), channel_id=1, source_target_pairs={{0,2},{1,9},{2,4},{3,11},{4,6},{5,13},{6,0},{7,15},{8,10},{9,17},{... | collective-permute-start | bytes 589832 | tf_op jit(solution)/shard_map/ppermute | solution.py:610
  66.6 9.8 %collective-permute-start.17 = (bf16[3,32,1024]{2,1,0:T(8,128)(2,1)S(1)}, bf16[3,32,1024]{2,1,0:T(8,128)(2,1)S(1)}, u32[]{:S(2)}, u32[]{:S(2)}) collective-permute-start(bf16[3,32,1024]{2,1,0:T(8,128)(2,1)S(1)} %error.1.after_ref.refs_0_), channel_id=1, source_target_pairs={{0,4},{1,17},{2,6},{3,19},{4,0},{5,21},{6,2},{7,23},{8,12},{9,25},... | collective-permute-start | bytes 589832 | tf_op jit(solution)/shard_map/ppermute | solution.py:610
  69.3 7.2 %collective-permute-start.18 = (bf16[3,32,1024]{2,1,0:T(8,128)(2,1)S(1)}, bf16[3,32,1024]{2,1,0:T(8,128)(2,1)S(1)}, u32[]{:S(2)}, u32[]{:S(2)}) collective-permute-start(bf16[3,32,1024]{2,1,0:T(8,128)(2,1)S(1)} %error.1.after_ref.refs_0_), channel_id=1, source_target_pairs={{0,6},{1,25},{2,0},{3,27},{4,2},{5,29},{6,4},{7,31},{8,14},{9,1},{... | collective-permute-start | bytes 589832 | tf_op jit(solution)/shard_map/ppermute | solution.py:610
  77.1 9.1 %collective-permute-start.19 = (bf16[4,3,32,512]{3,2,1,0:T(8,128)(2,1)S(1)}, bf16[4,3,32,512]{3,2,1,0:T(8,128)(2,1)S(1)}, u32[]{:S(2)}, u32[]{:S(2)}) collective-permute-start(bf16[4,3,32,512]{3,2,1,0:T(8,128)(2,1)S(1)} %get-tuple-element.69.refs_0_), channel_id=1, source_target_pairs={{0,8},{1,3},{2,10},{3,5},{4,12},{5,7},{6,14},{7,1},{8,16},{9,11},{... | collective-permute-start | bytes 1179656 | tf_op jit(solution)/shard_map/ppermute | solution.py:610
  77.1 9.0 %collective-permute-start.22 = (bf16[4,3,32,512]{3,2,1,0:T(8,128)(2,1)S(1)}, bf16[4,3,32,512]{3,2,1,0:T(8,128)(2,1)S(1)}, u32[]{:S(2)}, u32[]{:S(2)}) collective-permute-start(bf16[4,3,32,512]{3,2,1,0:T(8,128)(2,1)S(1)} %get-tuple-element.70.refs_1_), channel_id=1, source_target_pairs={{0,24},{1,7},{2,26},{3,1},{4,28},{5,3},{6,30},{7,5},{8,0},{9,15},{... | collective-permute-start | bytes 1179656 | tf_op jit(solution)/shard_map/ppermute | solution.py:610
  80.4 10.0 %collective-permute-start.20 = (bf16[4,3,32,512]{3,2,1,0:T(8,128)(2,1)S(1)}, bf16[4,3,32,512]{3,2,1,0:T(8,128)(2,1)S(1)}, u32[]{:S(2)}, u32[]{:S(2)}) collective-permute-start(bf16[4,3,32,512]{3,2,1,0:T(8,128)(2,1)S(1)} %get-tuple-element.70.refs_1_), channel_id=1, source_target_pairs={{0,8},{1,3},{2,10},{3,5},{4,12},{5,7},{6,14},{7,1},{8,16},{9,11},{... | collective-permute-start | bytes 1179656 | tf_op jit(solution)/shard_map/ppermute | solution.py:610
  80.4 10.0 %collective-permute-start.24 = (bf16[4,3,32,512]{3,2,1,0:T(8,128)(2,1)S(1)}, bf16[4,3,32,512]{3,2,1,0:T(8,128)(2,1)S(1)}, u32[]{:S(2)}, u32[]{:S(2)}) collective-permute-start(bf16[4,3,32,512]{3,2,1,0:T(8,128)(2,1)S(1)} %get-tuple-element.69.refs_0_), channel_id=1, source_target_pairs={{0,24},{1,7},{2,26},{3,1},{4,28},{5,3},{6,30},{7,5},{8,0},{9,15},{... | collective-permute-start | bytes 1179656 | tf_op jit(solution)/shard_map/ppermute | solution.py:610
  86.1 9.0 %collective-permute-start.21 = (bf16[4,3,32,512]{3,2,1,0:T(8,128)(2,1)S(1)}, bf16[4,3,32,512]{3,2,1,0:T(8,128)(2,1)S(1)}, u32[]{:S(2)}, u32[]{:S(2)}) collective-permute-start(bf16[4,3,32,512]{3,2,1,0:T(8,128)(2,1)S(1)} %collective-permute-done.19.refs_2_), channel_id=1, source_target_pairs={{0,8},{1,3},{2,10},{3,5},{4,12},{5,7},{6,14},{7,1},{8,16},{9,11},{... | collective-permute-start | bytes 1179656 | tf_op jit(solution)/shard_map/ppermute | solution.py:610
  86.1 9.0 %collective-permute-start.23 = (bf16[4,3,32,512]{3,2,1,0:T(8,128)(2,1)S(1)}, bf16[4,3,32,512]{3,2,1,0:T(8,128)(2,1)S(1)}, u32[]{:S(2)}, u32[]{:S(2)}) collective-permute-start(bf16[4,3,32,512]{3,2,1,0:T(8,128)(2,1)S(1)} %collective-permute-done.22.refs_7_), channel_id=1, source_target_pairs={{0,24},{1,7},{2,26},{3,1},{4,28},{5,3},{6,30},{7,5},{8,0},{9,15},{... | collective-permute-start | bytes 1179656 | tf_op jit(solution)/shard_map/ppermute | solution.py:610
  98.6 3.1 %collective-permute-start.25 = (bf16[512,512]{1,0:T(8,128)(2,1)S(1)}, bf16[512,512]{1,0:T(8,128)(2,1)S(1)}, u32[]{:S(2)}, u32[]{:S(2)}) collective-permute-start(bf16[512,512]{1,0:T(8,128)(2,1)S(1)} %get-tuple-element.73), channel_id=1, source_target_pairs={{0,1},{1,0},{2,3},{3,2},{4,5},{5,4},{6,7},{7,6},{8,9},{9,8},{10,11... | collective-permute-start | bytes 1572872 | tf_op jit(solution)/shard_map/ppermute | solution.py:560
  101.9 12.6 %collective-permute-start.26 = (bf16[3,512,1024]{2,1,0:T(8,128)(2,1)S(1)}, bf16[3,512,1024]{2,1,0:T(8,128)(2,1)S(1)}, u32[]{:S(2)}, u32[]{:S(2)}) collective-permute-start(bf16[3,512,1024]{2,1,0:T(8,128)(2,1)S(1)} %get-tuple-element.74.err_ref), channel_id=1, source_target_pairs={{0,1},{1,0},{2,3},{3,2},{4,5},{5,4},{6,7},{7,6},{8,9},{9,8},{10,11... | collective-permute-start | bytes 9437192 | tf_op jit(solution)/shard_map/ppermute | solution.py:560
  102.5 6.4 %collective-permute-start.29 = (bf16[256,512]{1,0:T(8,128)(2,1)S(1)}, bf16[256,512]{1,0:T(8,128)(2,1)S(1)}, u32[]{:S(2)}, u32[]{:S(2)}) collective-permute-start(bf16[256,512]{1,0:T(8,128)(2,1)S(1)} %get-tuple-element.83), channel_id=1, source_target_pairs={{0,32},{1,97},{32,0},{33,65},{64,96},{65,33},{96,64},{97,1},{2,34}... | collective-permute-start | bytes 786440 | tf_op jit(solution)/shard_map/ppermute | solution.py:590
  102.5 9.2 %collective-permute-start.27 = (bf16[256,512]{1,0:T(8,128)(2,1)S(1)}, bf16[256,512]{1,0:T(8,128)(2,1)S(1)}, u32[]{:S(2)}, u32[]{:S(2)}) collective-permute-start(bf16[256,512]{1,0:T(8,128)(2,1)S(1)} %get-tuple-element.78), channel_id=1, source_target_pairs={{0,32},{1,97},{32,0},{33,65},{64,96},{65,33},{96,64},{97,1},{2,34}... | collective-permute-start | bytes 786440 | tf_op jit(solution)/shard_map/ppermute | solution.py:590
  108.9 9.5 %collective-permute-start.30 = (bf16[256,512]{1,0:T(8,128)(2,1)S(1)}, bf16[256,512]{1,0:T(8,128)(2,1)S(1)}, u32[]{:S(2)}, u32[]{:S(2)}) collective-permute-start(bf16[256,512]{1,0:T(8,128)(2,1)S(1)} %get-tuple-element.85), channel_id=1, source_target_pairs={{0,96},{1,33},{32,64},{33,1},{64,32},{65,97},{96,0},{97,65},{2,98}... | collective-permute-start | bytes 786440 | tf_op jit(solution)/shard_map/ppermute | solution.py:590
  111.7 7.7 %collective-permute-start.28 = (bf16[256,512]{1,0:T(8,128)(2,1)S(1)}, bf16[256,512]{1,0:T(8,128)(2,1)S(1)}, u32[]{:S(2)}, u32[]{:S(2)}) collective-permute-start(bf16[256,512]{1,0:T(8,128)(2,1)S(1)} %get-tuple-element.81), channel_id=1, source_target_pairs={{0,96},{1,33},{32,64},{33,1},{64,32},{65,97},{96,0},{97,65},{2,98}... | collective-permute-start | bytes 786440 | tf_op jit(solution)/shard_map/ppermute | solution.py:590

commit v8 on v7

--- a/solution.py
+++ b/solution.py
@@ -39,7 +39,7 @@
     )(*args)
 
 
-STEPS = 4
+STEPS = 2
 
 
 def pre_kernel(p_ref, x_ref, w_ref, dec_ref, tgt_ref, a_ref, b_ref, *refs):
@@ -131,29 +131,30 @@
     )
 
 
-def latent_kernel(near_a, far_a, near_b, far_b, active_ref, bias_ref, after_ref, out_ref):
-    rows = near_a.shape[0]
-    for r, (near, far) in enumerate(((near_a, far_a), (near_b, far_b))):
-        at = slice(r * rows, (r + 1) * rows)
-        total = near[...] + far[...].astype(F32) + bias_ref[...]
-        out_ref[at, :] = jnp.where(active_ref[at, :] > 0, total, 0.0).astype(BF)
-
-
-def latent_call(top, bottom, active, bias, after):
-    rows, lats = active.shape
-    part = pl.BlockSpec((rows // 2, lats), lambda i: (0, 0))
-    whole = pl.BlockSpec((rows, lats), lambda i: (0, 0))
+def latent_kernel(near_ref, far_ref, active_ref, bias_ref, after_ref, out_ref):
+    total = near_ref[...] + far_ref[...].astype(F32) + bias_ref[...]
+    out_ref[...] = jnp.where(active_ref[...] > 0, total, 0.0).astype(BF)
+
+
+def latent_call(r, terms, active, bias, after):
+    rows, lats = terms[0].shape
+    part = pl.BlockSpec((rows, lats), lambda i: (0, 0))
     return call(
         latent_kernel,
-        "latents",
+        f"latents_{r}",
         (1,),
-        [part] * 4
-        + [whole, pl.BlockSpec((1, lats), lambda i: (0, 0)), pl.BlockSpec(memory_space=pl.ANY)],
-        whole,
+        [
+            part,
+            part,
+            pl.BlockSpec((rows, lats), lambda i: (r, 0)),
+            pl.BlockSpec((1, lats), lambda i: (0, 0)),
+            pl.BlockSpec(memory_space=pl.ANY),
+        ],
+        part,
         jax.ShapeDtypeStruct((rows, lats), BF),
-        (*top, *bottom, active, bias.reshape(1, lats), after),
+        (*terms, active, bias.reshape(1, lats), after),
         4 * rows * lats,
-        4e6,
+        2e6,
     )
 
 
@@ -192,20 +193,21 @@
     return jnp.where(p_ref[2] == 0, far * SIDE + near, near * SIDE + far)
 
 
-def rebuild_kernel(p_ref, lat_ref, sib_ref, dec_ref, got_ref, *refs):
-    outs, (lat, sib) = refs[:-2], refs[-2:]
+def rebuild_kernel(p_ref, *refs):
+    halves, (dec_ref, got_ref), outs, (lat, sib) = refs[:4], refs[4:6], refs[6:-2], refs[-2:]
     piece, half = outs[-1].shape[2:]
     strip, q = SIDE * piece, half // 2
 
     @pl.when(pl.program_id(0) == 0)
     def _():
-        for step in range(SIDE):
-            to = lax.rem(p_ref[3] + step, SIDE)
-            for i in range(SIDE):
-                src = pl.ds(pl.multiple_of(place_of(p_ref, to, i) * piece, piece), piece)
-                at = step * strip + i * piece
-                lat[at : at + piece, :] = lat_ref[src, :]
-                sib[at : at + piece, :] = sib_ref[src, :]
+        for x in range(SIDE):
+            for y in range(SIDE):
+                first, other = (jnp.where(p_ref[2] == 0, a, b) for a, b in ((x, y), (y, x)))
+                spot = lax.rem(first - p_ref[3] + SIDE, SIDE) * SIDE + other
+                to = pl.ds(pl.multiple_of(spot * piece, piece), piece)
+                r, src = divmod((x * SIDE + y) * piece, halves[0].shape[0])
+                lat[to, :] = halves[r][src : src + piece, :]
+                sib[to, :] = halves[2 + r][src : src + piece, :]
 
     total = jnp.dot(lat[...], dec_ref[0], preferred_element_type=F32)
     total += jnp.dot(sib[...], got_ref[0], preferred_element_type=F32)
@@ -219,18 +221,21 @@
 
 
 def rebuild_call(place, lat, sib, dec, got):
-    rows, lats = lat.shape
+    rows, lats = lat[0].shape
+    rows *= 2
     targets, _, half = got.shape
     piece = rows // (SIDE * SIDE)
     widths = [(hi - lo) * half // 2 for _, lo, hi in CUTS]
-    whole = pl.BlockSpec((rows, lats), lambda t, p: (0, 0))
+    part = pl.BlockSpec((rows // 2, lats), lambda t, p: (0, 0))
     return call(
         rebuild_kernel,
         "rebuild",
         (targets,),
         [
-            whole,
-            whole,
+            part,
+            part,
+            part,
+            part,
             pl.BlockSpec((1, lats, half), lambda t, p: (t, 0, 0)),
             pl.BlockSpec((1, lats, half), lambda t, p: (t, 0, 0)),
         ],
@@ -239,7 +244,7 @@
             jax.ShapeDtypeStruct((SIDE, targets, piece, w), kind)
             for w, kind in zip(widths, KINDS)
         ],
-        (lat, sib, dec, got),
+        (*lat, *sib, dec, got),
         4 * rows * lats * half * targets,
         11e6,
         [pltpu.VMEM((rows, lats), BF)] * 2,
@@ -417,20 +422,22 @@
     )
 
 
-def turn_kernel(x_ref, lat_ref, after_ref, x_out, lat_out, done_ref):
+def turn_kernel(x_ref, top_ref, bottom_ref, after_ref, x_out, lat_out, done_ref):
     done_ref[...] = jnp.zeros(done_ref.shape, F32)
     x_out[...] = x_ref[...].T
 
     @pl.when(pl.program_id(0) == 0)
     def _():
-        lat_out[...] = lat_ref[...].T
+        n = top_ref.shape[0]
+        lat_out[:, :n] = top_ref[...].T
+        lat_out[:, n:] = bottom_ref[...].T
 
 
 def turn_call(x, lat, after):
     rows, depth = x.shape
-    lats = lat.shape[1]
+    lats = lat[0].shape[1]
     step = 512
-    whole = pl.BlockSpec((rows, lats), lambda i: (0, 0))
+    part = pl.BlockSpec((rows // 2, lats), lambda i: (0, 0))
     turned = pl.BlockSpec((lats, rows), lambda i: (0, 0))
     return call(
         turn_kernel,
@@ -438,7 +445,8 @@
         (depth // step,),
         [
             pl.BlockSpec((rows, step), lambda i: (0, i)),
-            whole,
+            part,
+            part,
             pl.BlockSpec(memory_space=pl.ANY),
         ],
         [
@@ -449,7 +457,7 @@
         [jax.ShapeDtypeStruct((depth, rows), BF)]
         + [jax.ShapeDtypeStruct((lats, rows), BF)]
         + [jax.ShapeDtypeStruct((8, 128), F32)],
-        (x, lat, after),
+        (x, *lat, after),
         0,
         6e6,
     )
@@ -652,8 +660,11 @@
     dec_got = swap(dec_sent)
     tgt_got = swap(tgt_sent)
     dec_own, done = pick_call(place, dec_weight, bottom[0])
-    lat = latent_call(top, bottom, active, enc_bias, done)
-    lat_sib = swap(lat)
+    lat = [
+        latent_call(0, top, active, enc_bias, top[0]),
+        latent_call(1, bottom, active, enc_bias, done),
+    ]
+    lat_sib = [swap(half) for half in lat]
 
     own, parts = ring_sum(rebuild_call(place, lat, lat_sib, dec_own, dec_got))
     parts = scatter(sum_call(place, own, parts))

time: 123 us -> 122 us (level)
    ppermute x5 -> x6, waiting for transfers between devices: 3.2 us -> 2.82 us  [swap(): return lax.ppermute(value, 'c', [(0, 1), (1, 0)])]
    pallas_call x17 -> x18, Pallas kernels: 33.4 us -> 33.4 us  [call(): pl.pallas_call(body, out_shape=shapes, compiler_params=pltpu.CompilerPara...]
  transfers between devices with their start and end apart: 31 -> 32, of which waited for: 16 -> 17; matrix products, arithmetic and copies ran while one was open for 0% -> 0% of each run, Pallas kernels for 13% -> 13%
where the time goes in v8:
time: 122 us
  starting transfers between devices  49.2 us (40%)
  waiting for transfers between devices  36.9 us (30%)
  Pallas kernels  33.4 us (27%)
    pallas_call x18, Pallas kernels, call(): pl.pallas_call(body, out_shape=shapes, compiler_params=pltpu.CompilerPara...  33.4 us
    ppermute x18, starting transfers between devices, shift(): return lax.ppermute(value, ('x', 'y', 'c'), moves)  31.8 us
    ppermute x18, waiting for transfers between devices, shift(): return lax.ppermute(value, ('x', 'y', 'c'), moves)  24.7 us
    ppermute x8, starting transfers between devices, pair(): return lax.ppermute(value, ('z', 'c'), moves)  16.5 us
    ppermute x8, waiting for transfers between devices, pair(): return lax.ppermute(value, ('z', 'c'), moves)  9.36 us
    ppermute x6, waiting for transfers between devices, swap(): return lax.ppermute(value, 'c', [(0, 1), (1, 0)])  2.82 us
  transfers between devices with their start and end apart: 32, of which 17 were waited for; matrix products, arithmetic and copies ran while one was open for 0% of the time, Pallas kernels for 13%

profile of v8, /device:TPU:0, one launch (start us, length us, event | category | flops | bytes accessed | tf_op | source)
XLA Modules:
  0.0 121.6 jit_solution(7842762634784524836)
XLA Ops:
  0.7 0.7 stack.23.p_ref
  1.3 4.3 %pre.1 = (bf16[256,512]{1,0:T(8,128)(2,1)S(1)}, bf16[256,512]{1,0:T(8,128)(2,1)S(1)}, bf16[3,512,1024]{2,1,0:T(8,128)(2,1)S(1)}, bf16[3,16,1024]{2,1,0:T(8,128)(2,1)S(1)}, bf16[3,16,1024]{2,1,0:T(8,128)(2,1)S(1)}) custom-call(s32[5]{0:T(128)} %stack.23.p_ref, bf16[512,2048]{1,0:T(8,128)(2,1)} %x_ref.3, bf16[2048,512]{1,0:T(8,128)(2,1)} %w_ref.1, ...), custom_call_target="tpu_custom_call" | custom-call | flops 1073741824 | bytes 4194304 | tf_op jit(solution)/shard_map/pre/pallas_call | solution.py:27
  5.8 2.1 %collective-permute-start.2 = (bf16[256,512]{1,0:T(8,128)(2,1)S(1)}, bf16[256,512]{1,0:T(8,128)(2,1)S(1)}, u32[]{:S(2)}, u32[]{:S(2)}) collective-permute-start(bf16[256,512]{1,0:T(8,128)(2,1)S(1)} %get-tuple-element.47), channel_id=1, source_target_pairs={{0,32},{1,97},{32,0},{33,65},{64,96},{65,33},{96,64},{97,1},{2,34}... | collective-permute-start | bytes 786440 | tf_op jit(solution)/shard_map/ppermute | solution.py:598
  7.9 4.3 %collective-permute-done.2 = bf16[256,512]{1,0:T(8,128)(2,1)S(1)} collective-permute-done((bf16[256,512]{1,0:T(8,128)(2,1)S(1)}, bf16[256,512]{1,0:T(8,128)(2,1)S(1)}, u32[]{:S(2)}, u32[]{:S(2)}) %collective-permute-start.2) | collective-permute-done | bytes 262176 | tf_op jit(solution)/shard_map/ppermute | solution.py:598
  12.3 4.2 %collective-permute-start.3 = (bf16[256,512]{1,0:T(8,128)(2,1)S(1)}, bf16[256,512]{1,0:T(8,128)(2,1)S(1)}, u32[]{:S(2)}, u32[]{:S(2)}) collective-permute-start(bf16[256,512]{1,0:T(8,128)(2,1)S(1)} %get-tuple-element.89), channel_id=1, source_target_pairs={{0,96},{1,33},{32,64},{33,1},{64,32},{65,97},{96,0},{97,65},{2,98}... | collective-permute-start | bytes 786440 | tf_op jit(solution)/shard_map/ppermute | solution.py:598
  16.6 2.7 %collective-permute-start.1 = (bf16[256,512]{1,0:T(8,128)(2,1)S(1)}, bf16[256,512]{1,0:T(8,128)(2,1)S(1)}, u32[]{:S(2)}, u32[]{:S(2)}) collective-permute-start(bf16[256,512]{1,0:T(8,128)(2,1)S(1)} %get-tuple-element.91), channel_id=1, source_target_pairs={{0,96},{1,33},{32,64},{33,1},{64,32},{65,97},{96,0},{97,65},{2,98}... | collective-permute-start | bytes 786440 | tf_op jit(solution)/shard_map/ppermute | solution.py:598
  19.4 1.0 pick_half.1
  20.4 0.5 collective-permute-done.3.far_ref
  21.1 3.2 %collective-permute-done.1.far_ref = bf16[256,512]{1,0:T(8,128)(2,1)S(1)} collective-permute-done((bf16[256,512]{1,0:T(8,128)(2,1)S(1)}, bf16[256,512]{1,0:T(8,128)(2,1)S(1)}, u32[]{:S(2)}, u32[]{:S(2)}) %collective-permute-start.1) | collective-permute-done | bytes 262176 | tf_op jit(solution)/shard_map/ppermute | solution.py:598
  24.5 1.5 %collective-permute-done.5.refs_2_ = bf16[256,512]{1,0:T(8,128)(2,1)S(1)} collective-permute-done((bf16[256,512]{1,0:T(8,128)(2,1)S(1)}, bf16[256,512]{1,0:T(8,128)(2,1)S(1)}, u32[]{:S(2)}, u32[]{:S(2)}) %collective-permute-start.5) | collective-permute-done | bytes 262176 | tf_op jit(solution)/shard_map/ppermute | solution.py:568
  26.0 4.9 %rebuild.1 = (bf16[4,3,32,512]{3,2,1,0:T(8,128)(2,1)S(1)}, bf16[4,3,32,512]{3,2,1,0:T(8,128)(2,1)S(1)}, f32[4,3,32,512]{3,2,1,0:T(8,128)S(1)}, bf16[4,3,32,512]{...) custom-call(s32[5]{0:T(128)S(1)} %copy-done.2, ...), custom_call_target="tpu_custom_call" | custom-call | flops 3221225472 | bytes 11000000 | tf_op jit(solution)/shard_map/rebuild/pallas_call | solution.py:27
  30.9 2.8 %collective-permute-start.12 = (bf16[4,3,32,512]{3,2,1,0:T(8,128)(2,1)S(1)}, bf16[4,3,32,512]{3,2,1,0:T(8,128)(2,1)S(1)}, u32[]{:S(2)}, u32[]{:S(2)}) collective-permute-start(bf16[4,3,32,512]{3,2,1,0:T(8,128)(2,1)S(1)} %get-tuple-element.59), channel_id=1, source_target_pairs={{0,24},{1,7},{2,26},{3,1},{4,28},{5,3},{6,30},{7,5},{8,0},{9,15},{... | collective-permute-start | bytes 1179656 | tf_op jit(solution)/shard_map/ppermute | solution.py:618
  33.7 3.2 %collective-permute-start.10 = (bf16[4,3,32,512]{3,2,1,0:T(8,128)(2,1)S(1)}, bf16[4,3,32,512]{3,2,1,0:T(8,128)(2,1)S(1)}, u32[]{:S(2)}, u32[]{:S(2)}) collective-permute-start(bf16[4,3,32,512]{3,2,1,0:T(8,128)(2,1)S(1)} %get-tuple-element.56), channel_id=1, source_target_pairs={{0,24},{1,7},{2,26},{3,1},{4,28},{5,3},{6,30},{7,5},{8,0},{9,15},{... | collective-permute-start | bytes 1179656 | tf_op jit(solution)/shard_map/ppermute | solution.py:618
  37.0 2.1 %collective-permute-done.12 = bf16[4,3,32,512]{3,2,1,0:T(8,128)(2,1)S(1)} collective-permute-done((bf16[4,3,32,512]{3,2,1,0:T(8,128)(2,1)S(1)}, bf16[4,3,32,512]{3,2,1,0:T(8,128)(2,1)S(1)}, u32[]{:S(2)}, u32[]{:S(2)}) %collective-permute-start.12) | collective-permute-done | bytes 393248 | tf_op jit(solution)/shard_map/ppermute | solution.py:618
  39.2 3.8 %collective-permute-start.13 = (bf16[4,3,32,512]{3,2,1,0:T(8,128)(2,1)S(1)}, bf16[4,3,32,512]{3,2,1,0:T(8,128)(2,1)S(1)}, u32[]{:S(2)}, u32[]{:S(2)}) collective-permute-start(bf16[4,3,32,512]{3,2,1,0:T(8,128)(2,1)S(1)} %add_convert_fusion), channel_id=1, source_target_pairs={{0,24},{1,7},{2,26},{3,1},{4,28},{5,3},{6,30},{7,5},{8,0},{9,15},{... | collective-permute-start | bytes 1179656 | tf_op jit(solution)/shard_map/ppermute | solution.py:618
  43.2 3.7 %collective-permute-done.11.refs_2_ = bf16[4,3,32,512]{3,2,1,0:T(8,128)(2,1)S(1)} collective-permute-done((bf16[4,3,32,512]{3,2,1,0:T(8,128)(2,1)S(1)}, bf16[4,3,32,512]{3,2,1,0:T(8,128)(2,1)S(1)}, u32[]{:S(2)}, u32[]{:S(2)}) %collective-permute-start.11) | collective-permute-done | bytes 393248 | tf_op jit(solution)/shard_map/ppermute | solution.py:618
  46.9 1.3 %collective-permute-done.13.refs_3_ = bf16[4,3,32,512]{3,2,1,0:T(8,128)(2,1)S(1)} collective-permute-done((bf16[4,3,32,512]{3,2,1,0:T(8,128)(2,1)S(1)}, bf16[4,3,32,512]{3,2,1,0:T(8,128)(2,1)S(1)}, u32[]{:S(2)}, u32[]{:S(2)}) %collective-permute-start.13) | collective-permute-done | bytes 393248 | tf_op jit(solution)/shard_map/ppermute | solution.py:618
  48.2 3.9 %collective-permute-done.9.refs_0_ = bf16[4,3,32,512]{3,2,1,0:T(8,128)(2,1)S(1)} collective-permute-done((bf16[4,3,32,512]{3,2,1,0:T(8,128)(2,1)S(1)}, bf16[4,3,32,512]{3,2,1,0:T(8,128)(2,1)S(1)}, u32[]{:S(2)}, u32[]{:S(2)}) %collective-permute-start.9) | collective-permute-done | bytes 393248 | tf_op jit(solution)/shard_map/ppermute | solution.py:618
  52.1 1.2 %sum_first.1 = (f32[3,32,1024]{2,1,0:T(8,128)S(1)}, bf16[3,32,1024]{2,1,0:T(8,128)(2,1)S(1)}, bf16[3,32,1024]{2,1,0:T(8,128)(2,1)S(1)}, bf16[3,32,1024]{2,1,0:T(8,128)(2,1)S(1)}) custom-call(s32[5]{0:T(128)S(1)} %copy-done.2, f32[4,3,32,1024]{3,2,1,0:T(8,128)S(1)} %get-tuple-element.53.own_ref, bf16[4,3,32,512]{3,2,1,0:T(8,128)(2,1)S(1)} %collective-permute-done.9.refs_0_, ...), custom_call_target="tpu_custom_call" | custom-call | flops 1572864 | bytes 4718592 | tf_op jit(solution)/shard_map/sum_first/pallas_call | solution.py:27
  53.4 1.6 %collective-permute-start.14 = (bf16[3,32,1024]{2,1,0:T(8,128)(2,1)S(1)}, bf16[3,32,1024]{2,1,0:T(8,128)(2,1)S(1)}, u32[]{:S(2)}, u32[]{:S(2)}) collective-permute-start(bf16[3,32,1024]{2,1,0:T(8,128)(2,1)S(1)} %get-tuple-element.61), channel_id=1, source_target_pairs={{0,2},{1,9},{2,4},{3,11},{4,6},{5,13},{6,0},{7,15},{8,10},{9,17},{... | collective-permute-start | bytes 589832 | tf_op jit(solution)/shard_map/ppermute | solution.py:618
  55.0 2.9 %collective-permute-start.15 = (bf16[3,32,1024]{2,1,0:T(8,128)(2,1)S(1)}, bf16[3,32,1024]{2,1,0:T(8,128)(2,1)S(1)}, u32[]{:S(2)}, u32[]{:S(2)}) collective-permute-start(bf16[3,32,1024]{2,1,0:T(8,128)(2,1)S(1)} %get-tuple-element.62), channel_id=1, source_target_pairs={{0,4},{1,17},{2,6},{3,19},{4,0},{5,21},{6,2},{7,23},{8,12},{9,25},... | collective-permute-start | bytes 589832 | tf_op jit(solution)/shard_map/ppermute | solution.py:618
  57.9 1.7 %collective-permute-start.16 = (bf16[3,32,1024]{2,1,0:T(8,128)(2,1)S(1)}, bf16[3,32,1024]{2,1,0:T(8,128)(2,1)S(1)}, u32[]{:S(2)}, u32[]{:S(2)}) collective-permute-start(bf16[3,32,1024]{2,1,0:T(8,128)(2,1)S(1)} %get-tuple-element.63), channel_id=1, source_target_pairs={{0,6},{1,25},{2,0},{3,27},{4,2},{5,29},{6,4},{7,31},{8,14},{9,1},{... | collective-permute-start | bytes 589832 | tf_op jit(solution)/shard_map/ppermute | solution.py:618
  59.6 1.3 %collective-permute-done.4.got_ref = bf16[3,16,1024]{2,1,0:T(8,128)(2,1)S(1)} collective-permute-done((bf16[3,16,1024]{2,1,0:T(8,128)(2,1)S(1)}, bf16[3,16,1024]{2,1,0:T(8,128)(2,1)S(1)}, u32[]{:S(2)}, u32[]{:S(2)}) %collective-permute-start.4) | collective-permute-done | bytes 98336 | tf_op jit(solution)/shard_map/ppermute | solution.py:568
  60.9 2.8 %collective-permute-done.15.refs_2_ = bf16[3,32,1024]{2,1,0:T(8,128)(2,1)S(1)} collective-permute-done((bf16[3,32,1024]{2,1,0:T(8,128)(2,1)S(1)}, bf16[3,32,1024]{2,1,0:T(8,128)(2,1)S(1)}, u32[]{:S(2)}, u32[]{:S(2)}) %collective-permute-start.15) | collective-permute-done | bytes 196640 | tf_op jit(solution)/shard_map/ppermute | solution.py:618
  63.7 0.7 error.1.after_ref.refs_0_
  64.4 1.7 %collective-permute-start.17 = (bf16[3,32,1024]{2,1,0:T(8,128)(2,1)S(1)}, bf16[3,32,1024]{2,1,0:T(8,128)(2,1)S(1)}, u32[]{:S(2)}, u32[]{:S(2)}) collective-permute-start(bf16[3,32,1024]{2,1,0:T(8,128)(2,1)S(1)} %error.1.after_ref.refs_0_), channel_id=1, source_target_pairs={{0,2},{1,9},{2,4},{3,11},{4,6},{5,13},{6,0},{7,15},{8,10},{9,17},{... | collective-permute-start | bytes 589832 | tf_op jit(solution)/shard_map/ppermute | solution.py:618
  66.1 2.6 %collective-permute-start.18 = (bf16[3,32,1024]{2,1,0:T(8,128)(2,1)S(1)}, bf16[3,32,1024]{2,1,0:T(8,128)(2,1)S(1)}, u32[]{:S(2)}, u32[]{:S(2)}) collective-permute-start(bf16[3,32,1024]{2,1,0:T(8,128)(2,1)S(1)} %error.1.after_ref.refs_0_), channel_id=1, source_target_pairs={{0,4},{1,17},{2,6},{3,19},{4,0},{5,21},{6,2},{7,23},{8,12},{9,25},... | collective-permute-start | bytes 589832 | tf_op jit(solution)/shard_map/ppermute | solution.py:618
  68.7 1.5 %collective-permute-start.19 = (bf16[3,32,1024]{2,1,0:T(8,128)(2,1)S(1)}, bf16[3,32,1024]{2,1,0:T(8,128)(2,1)S(1)}, u32[]{:S(2)}, u32[]{:S(2)}) collective-permute-start(bf16[3,32,1024]{2,1,0:T(8,128)(2,1)S(1)} %error.1.after_ref.refs_0_), channel_id=1, source_target_pairs={{0,6},{1,25},{2,0},{3,27},{4,2},{5,29},{6,4},{7,31},{8,14},{9,1},{... | collective-permute-start | bytes 589832 | tf_op jit(solution)/shard_map/ppermute | solution.py:618
  70.3 1.1 turn.1
  71.4 1.8 %turn_dec.1 = (bf16[3,1024,512]{2,1,0:T(8,128)(2,1)S(1)}, bf16[3,1024,512]{2,1,0:T(8,128)(2,1)S(1)}, f32[8,128]{1,0:T(8,128)S(1)}) custom-call(bf16[3,512,1024]{2,1,0:T(8,128)(2,1)S(1)} %get-tuple-element.51.refs_4_.own_ref, bf16[3,512,1024]{2,1,0:T(8,128)(2,1)S(1)} %collective-permute-done.7.refs_5_.got_ref, f32[8,128]{1,0:T(8,128)S(1)} %get-tuple-element.66.after_ref), custom_call_target="tpu_custom_call" | custom-call | bytes 12000000 | tf_op jit(solution)/shard_map/turn_dec/pallas_call | solution.py:27
  73.3 2.6 %collective-permute-done.18.refs_2_ = bf16[3,32,1024]{2,1,0:T(8,128)(2,1)S(1)} collective-permute-done((bf16[3,32,1024]{2,1,0:T(8,128)(2,1)S(1)}, bf16[3,32,1024]{2,1,0:T(8,128)(2,1)S(1)}, u32[]{:S(2)}, u32[]{:S(2)}) %collective-permute-start.18) | collective-permute-done | bytes 196640 | tf_op jit(solution)/shard_map/ppermute | solution.py:618
  75.9 0.6 join.1
  76.6 3.2 %collective-permute-start.23 = (bf16[4,3,32,512]{3,2,1,0:T(8,128)(2,1)S(1)}, bf16[4,3,32,512]{3,2,1,0:T(8,128)(2,1)S(1)}, u32[]{:S(2)}, u32[]{:S(2)}) collective-permute-start(bf16[4,3,32,512]{3,2,1,0:T(8,128)(2,1)S(1)} %get-tuple-element.70.refs_1_), channel_id=1, source_target_pairs={{0,24},{1,7},{2,26},{3,1},{4,28},{5,3},{6,30},{7,5},{8,0},{9,15},{... | collective-permute-start | bytes 1179656 | tf_op jit(solution)/shard_map/ppermute | solution.py:618
  79.8 3.2 %collective-permute-start.25 = (bf16[4,3,32,512]{3,2,1,0:T(8,128)(2,1)S(1)}, bf16[4,3,32,512]{3,2,1,0:T(8,128)(2,1)S(1)}, u32[]{:S(2)}, u32[]{:S(2)}) collective-permute-start(bf16[4,3,32,512]{3,2,1,0:T(8,128)(2,1)S(1)} %get-tuple-element.69.refs_0_), channel_id=1, source_target_pairs={{0,24},{1,7},{2,26},{3,1},{4,28},{5,3},{6,30},{7,5},{8,0},{9,15},{... | collective-permute-start | bytes 1179656 | tf_op jit(solution)/shard_map/ppermute | solution.py:618
  83.1 2.5 %collective-permute-done.20.refs_2_ = bf16[4,3,32,512]{3,2,1,0:T(8,128)(2,1)S(1)} collective-permute-done((bf16[4,3,32,512]{3,2,1,0:T(8,128)(2,1)S(1)}, bf16[4,3,32,512]{3,2,1,0:T(8,128)(2,1)S(1)}, u32[]{:S(2)}, u32[]{:S(2)}) %collective-permute-start.20) | collective-permute-done | bytes 393248 | tf_op jit(solution)/shard_map/ppermute | solution.py:618
  85.6 3.2 %collective-permute-start.24 = (bf16[4,3,32,512]{3,2,1,0:T(8,128)(2,1)S(1)}, bf16[4,3,32,512]{3,2,1,0:T(8,128)(2,1)S(1)}, u32[]{:S(2)}, u32[]{:S(2)}) collective-permute-start(bf16[4,3,32,512]{3,2,1,0:T(8,128)(2,1)S(1)} %collective-permute-done.23.refs_7_), channel_id=1, source_target_pairs={{0,24},{1,7},{2,26},{3,1},{4,28},{5,3},{6,30},{7,5},{8,0},{9,15},{... | collective-permute-start | bytes 1179656 | tf_op jit(solution)/shard_map/ppermute | solution.py:618
  88.8 1.0 collective-permute-done.21.refs_3_
  89.8 4.8 %collective-permute-done.22.refs_4_ = bf16[4,3,32,512]{3,2,1,0:T(8,128)(2,1)S(1)} collective-permute-done((bf16[4,3,32,512]{3,2,1,0:T(8,128)(2,1)S(1)}, bf16[4,3,32,512]{3,2,1,0:T(8,128)(2,1)S(1)}, u32[]{:S(2)}, u32[]{:S(2)}) %collective-permute-start.22) | collective-permute-done | bytes 393248 | tf_op jit(solution)/shard_map/ppermute | solution.py:618
  94.6 3.5 %back_sib.1 = (bf16[3,512,1024]{2,1,0:T(8,128)(2,1)S(1)}, bf16[512,512]{1,0:T(8,128)(2,1)S(1)}) custom-call(s32[5]{0:T(128)S(1)} %copy-done.2, bf16[3,1024,512]{2,1,0:T(8,128)(2,1)S(1)} %get-tuple-element.67.dec_ref, bf16[4,3,32,512]{3,2,1,0:T(8,128)(2,1)S(1)} %get-tuple-element.69.refs_0_, bf16[4,3,32,512]{3,2,1,0:T(8,128)(2,1)S(1)} %get-tuple-element.70.refs_1_, ...), custom_call_target="tpu_custom_call" | custom-call | flops 1610612736 | bytes 10000000 | tf_op jit(solution)/shard_map/back_sib/pallas_call | solution.py:27
  98.2 3.0 %back_own.1.own_ref = f32[512,512]{1,0:T(8,128)S(1)} custom-call(s32[5]{0:T(128)S(1)} %copy-done.2, bf16[3,512,1024]{2,1,0:T(8,128)(2,1)S(1)} %get-tuple-element.71.err_ref, bf16[3,1024,512]{2,1,0:T(8,128)(2,1)S(1)} %get-tuple-element.72.dec_ref), custom_call_target="tpu_custom_call" | custom-call | flops 1610612736 | bytes 7000000 | tf_op jit(solution)/shard_map/back_own/pallas_call | solution.py:27
  101.4 0.6 collective-permute-start.27
  102.0 2.0 %collective-permute-start.28 = (bf16[256,512]{1,0:T(8,128)(2,1)S(1)}, bf16[256,512]{1,0:T(8,128)(2,1)S(1)}, u32[]{:S(2)}, u32[]{:S(2)}) collective-permute-start(bf16[256,512]{1,0:T(8,128)(2,1)S(1)} %get-tuple-element.78), channel_id=1, source_target_pairs={{0,32},{1,97},{32,0},{33,65},{64,96},{65,33},{96,64},{97,1},{2,34}... | collective-permute-start | bytes 786440 | tf_op jit(solution)/shard_map/ppermute | solution.py:598
  104.0 3.9 %dec_grad_own.1 = (bf16[3,512,2048]{2,1,0:T(8,128)(2,1)}, f32[8,128]{1,0:T(8,128)S(1)}) custom-call(s32[5]{0:T(128)S(1)} %copy-done.2, bf16[512,512]{1,0:T(8,128)(2,1)S(1)} %get-tuple-element.65.lat_ref, bf16[3,512,1024]{2,1,0:T(8,128)(2,1)S(1)} %get-tuple-element.74.err_ref), custom_call_target="tpu_custom_call" | custom-call | flops 1610612736 | bytes 7000000 | tf_op jit(solution)/shard_map/dec_grad_own/pallas_call | solution.py:27
  108.4 2.7 %collective-permute-start.31 = (bf16[256,512]{1,0:T(8,128)(2,1)S(1)}, bf16[256,512]{1,0:T(8,128)(2,1)S(1)}, u32[]{:S(2)}, u32[]{:S(2)}) collective-permute-start(bf16[256,512]{1,0:T(8,128)(2,1)S(1)} %get-tuple-element.85), channel_id=1, source_target_pairs={{0,96},{1,33},{32,64},{33,1},{64,32},{65,97},{96,0},{97,65},{2,98}... | collective-permute-start | bytes 786440 | tf_op jit(solution)/shard_map/ppermute | solution.py:598
  111.2 2.7 %collective-permute-start.29 = (bf16[256,512]{1,0:T(8,128)(2,1)S(1)}, bf16[256,512]{1,0:T(8,128)(2,1)S(1)}, u32[]{:S(2)}, u32[]{:S(2)}) collective-permute-start(bf16[256,512]{1,0:T(8,128)(2,1)S(1)} %get-tuple-element.81), channel_id=1, source_target_pairs={{0,96},{1,33},{32,64},{33,1},{64,32},{65,97},{96,0},{97,65},{2,98}... | collective-permute-start | bytes 786440 | tf_op jit(solution)/shard_map/ppermute | solution.py:598
  113.9 3.9 %dec_grad_sib.1 = (bf16[3,512,2048]{2,1,0:T(8,128)(2,1)}, f32[8,128]{1,0:T(8,128)S(1)}) custom-call(s32[5]{0:T(128)S(1)} %copy-done.2, bf16[512,512]{1,0:T(8,128)(2,1)S(1)} %get-tuple-element.65.lat_ref, bf16[3,512,1024]{2,1,0:T(8,128)(2,1)S(1)} %collective-permute-done.27.err_ref, ...), custom_call_target="tpu_custom_call", output_to_operand_aliasing={{0}: (3, {})} | custom-call | flops 1610612736 | bytes 7000000 | tf_op jit(solution)/shard_map/dec_grad_sib/pallas_call | solution.py:27
  117.9 1.0 collective-permute-done.29.far_a
  118.9 2.7 %enc_grad.1 = (bf16[2048,512]{1,0:T(8,128)(2,1)}, f32[1,512]{1,0:T(1,128)}) custom-call(bf16[2048,512]{1,0:T(8,128)(2,1)S(1)} %get-tuple-element.64.x_ref, s32[512,512]{1,0:T(8,128)S(1)} %copy-done, f32[8,128]{1,0:T(8,128)S(1)} %get-tuple-element.76.after_ref, f32[256,512]{1,0:T(8,128)S(1)} %get-tuple-element.80.near_a, ...), custom_call_target="tpu_custom_call" | custom-call | flops 1073741824 | bytes 7000000 | tf_op jit(solution)/shard_map/enc_grad/pallas_call | solution.py:27
  (52 shorter events, 2.2 us)
Async XLA Ops:
  0.6 18.7 %slice-start = ((s8[6291456]{0:T(1024)(128)(4,1)}), s8[2097152]{0:T(1024)(128)(4,1)S(1)}, s32[]{:S(2)}) async-start(s8[6291456]{0:T(1024)(128)(4,1)} %bitcast.7), calls=%async_computation | async-start | bytes 4194304
  1.3 18.0 %slice-start.1 = ((s8[6291456]{0:T(1024)(128)(4,1)}), s8[4194304]{0:T(1024)(128)(4,1)S(1)}, s32[]{:S(2)}) async-start(s8[6291456]{0:T(1024)(128)(4,1)} %bitcast.7), calls=%async_computation.1 | async-start | bytes 8388608
  1.3 18.0 %copy-start.2 = (s32[5]{0:T(128)S(1)}, s32[5]{0:T(128)}, u32[]{:S(2)}) copy-start(s32[5]{0:T(128)} %stack.23.p_ref) | copy-start | bytes 64
  5.7 20.3 %collective-permute-start.7 = (bf16[3,512,1024]{2,1,0:T(8,128)(2,1)S(1)}, bf16[3,512,1024]{2,1,0:T(8,128)(2,1)S(1)}, u32[]{:S(2)}, u32[]{:S(2)}) collective-permute-start(bf16[3,512,1024]{2,1,0:T(8,128)(2,1)S(1)} %get-tuple-element.52), channel_id=1, source_target_pairs={{0,1},{1,0},{2,3},{3,2},{4,5},{5,4},{6,7},{7,6},{8,9},{9,8},{10,11... | collective-permute-start | bytes 9437192 | tf_op jit(solution)/shard_map/ppermute | solution.py:568
  5.8 6.5 %collective-permute-start.2 = (bf16[256,512]{1,0:T(8,128)(2,1)S(1)}, bf16[256,512]{1,0:T(8,128)(2,1)S(1)}, u32[]{:S(2)}, u32[]{:S(2)}) collective-permute-start(bf16[256,512]{1,0:T(8,128)(2,1)S(1)} %get-tuple-element.47), channel_id=1, source_target_pairs={{0,32},{1,97},{32,0},{33,65},{64,96},{65,33},{96,64},{97,1},{2,34}... | collective-permute-start | bytes 786440 | tf_op jit(solution)/shard_map/ppermute | solution.py:598
  7.8 8.7 %collective-permute-start = (bf16[256,512]{1,0:T(8,128)(2,1)S(1)}, bf16[256,512]{1,0:T(8,128)(2,1)S(1)}, u32[]{:S(2)}, u32[]{:S(2)}) collective-permute-start(bf16[256,512]{1,0:T(8,128)(2,1)S(1)} %get-tuple-element.46), channel_id=1, source_target_pairs={{0,32},{1,97},{32,0},{33,65},{64,96},{65,33},{96,64},{97,1},{2,34}... | collective-permute-start | bytes 786440 | tf_op jit(solution)/shard_map/ppermute | solution.py:598
  12.3 8.6 %collective-permute-start.3 = (bf16[256,512]{1,0:T(8,128)(2,1)S(1)}, bf16[256,512]{1,0:T(8,128)(2,1)S(1)}, u32[]{:S(2)}, u32[]{:S(2)}) collective-permute-start(bf16[256,512]{1,0:T(8,128)(2,1)S(1)} %get-tuple-element.89), channel_id=1, source_target_pairs={{0,96},{1,33},{32,64},{33,1},{64,32},{65,97},{96,0},{97,65},{2,98}... | collective-permute-start | bytes 786440 | tf_op jit(solution)/shard_map/ppermute | solution.py:598
  16.6 7.7 %collective-permute-start.1 = (bf16[256,512]{1,0:T(8,128)(2,1)S(1)}, bf16[256,512]{1,0:T(8,128)(2,1)S(1)}, u32[]{:S(2)}, u32[]{:S(2)}) collective-permute-start(bf16[256,512]{1,0:T(8,128)(2,1)S(1)} %get-tuple-element.91), channel_id=1, source_target_pairs={{0,96},{1,33},{32,64},{33,1},{64,32},{65,97},{96,0},{97,65},{2,98}... | collective-permute-start | bytes 786440 | tf_op jit(solution)/shard_map/ppermute | solution.py:598
  19.3 1.5 %copy-start = (s32[512,512]{1,0:T(8,128)S(1)}, s32[512,512]{1,0:T(8,128)}, u32[]{:S(2)}) copy-start(s32[512,512]{1,0:T(8,128)} %active_ref.5) | copy-start | bytes 3145732
  19.4 1.5 %copy-start.3 = (f32[512]{0:T(512)S(1)}, f32[512]{0:T(512)}, u32[]{:S(2)}) copy-start(f32[512]{0:T(512)} %param.8) | copy-start | bytes 6148
  21.0 3.5 %collective-permute-start.6 = (bf16[256,512]{1,0:T(8,128)(2,1)S(1)}, bf16[256,512]{1,0:T(8,128)(2,1)S(1)}, u32[]{:S(2)}, u32[]{:S(2)}) collective-permute-start(bf16[256,512]{1,0:T(8,128)(2,1)S(1)} %latents_1.1.refs_1_.bottom_ref), channel_id=1, source_target_pairs={{0,1},{1,0},{2,3},{3,2},{4,5},{5,4},{6,7},{7,6},{8,9},{9,8},{10,11... | collective-permute-start | bytes 786440 | tf_op jit(solution)/shard_map/ppermute | solution.py:568
  24.4 1.6 %collective-permute-start.5 = (bf16[256,512]{1,0:T(8,128)(2,1)S(1)}, bf16[256,512]{1,0:T(8,128)(2,1)S(1)}, u32[]{:S(2)}, u32[]{:S(2)}) collective-permute-start(bf16[256,512]{1,0:T(8,128)(2,1)S(1)} %latents_0.1.refs_0_.top_ref), channel_id=1, source_target_pairs={{0,1},{1,0},{2,3},{3,2},{4,5},{5,4},{6,7},{7,6},{8,9},{9,8},{10,11... | collective-permute-start | bytes 786440 | tf_op jit(solution)/shard_map/ppermute | solution.py:568
  30.9 8.1 %collective-permute-start.12 = (bf16[4,3,32,512]{3,2,1,0:T(8,128)(2,1)S(1)}, bf16[4,3,32,512]{3,2,1,0:T(8,128)(2,1)S(1)}, u32[]{:S(2)}, u32[]{:S(2)}) collective-permute-start(bf16[4,3,32,512]{3,2,1,0:T(8,128)(2,1)S(1)} %get-tuple-element.59), channel_id=1, source_target_pairs={{0,24},{1,7},{2,26},{3,1},{4,28},{5,3},{6,30},{7,5},{8,0},{9,15},{... | collective-permute-start | bytes 1179656 | tf_op jit(solution)/shard_map/ppermute | solution.py:618
  33.7 9.2 %collective-permute-start.8 = (bf16[4,3,32,512]{3,2,1,0:T(8,128)(2,1)S(1)}, bf16[4,3,32,512]{3,2,1,0:T(8,128)(2,1)S(1)}, u32[]{:S(2)}, u32[]{:S(2)}) collective-permute-start(bf16[4,3,32,512]{3,2,1,0:T(8,128)(2,1)S(1)} %get-tuple-element.55), channel_id=1, source_target_pairs={{0,8},{1,3},{2,10},{3,5},{4,12},{5,7},{6,14},{7,1},{8,16},{9,11},{... | collective-permute-start | bytes 1179656 | tf_op jit(solution)/shard_map/ppermute | solution.py:618
  33.7 9.5 %collective-permute-start.10 = (bf16[4,3,32,512]{3,2,1,0:T(8,128)(2,1)S(1)}, bf16[4,3,32,512]{3,2,1,0:T(8,128)(2,1)S(1)}, u32[]{:S(2)}, u32[]{:S(2)}) collective-permute-start(bf16[4,3,32,512]{3,2,1,0:T(8,128)(2,1)S(1)} %get-tuple-element.56), channel_id=1, source_target_pairs={{0,24},{1,7},{2,26},{3,1},{4,28},{5,3},{6,30},{7,5},{8,0},{9,15},{... | collective-permute-start | bytes 1179656 | tf_op jit(solution)/shard_map/ppermute | solution.py:618
  37.0 10.0 %collective-permute-start.11 = (bf16[4,3,32,512]{3,2,1,0:T(8,128)(2,1)S(1)}, bf16[4,3,32,512]{3,2,1,0:T(8,128)(2,1)S(1)}, u32[]{:S(2)}, u32[]{:S(2)}) collective-permute-start(bf16[4,3,32,512]{3,2,1,0:T(8,128)(2,1)S(1)} %get-tuple-element.57), channel_id=1, source_target_pairs={{0,8},{1,3},{2,10},{3,5},{4,12},{5,7},{6,14},{7,1},{8,16},{9,11},{... | collective-permute-start | bytes 1179656 | tf_op jit(solution)/shard_map/ppermute | solution.py:618
  39.2 31.1 %copy-start.1 = (bf16[512,2048]{1,0:T(8,128)(2,1)S(1)}, bf16[512,2048]{1,0:T(8,128)(2,1)}, u32[]{:S(2)}) copy-start(bf16[512,2048]{1,0:T(8,128)(2,1)} %x_ref.3) | copy-start | bytes 6291460
  39.2 9.1 %collective-permute-start.13 = (bf16[4,3,32,512]{3,2,1,0:T(8,128)(2,1)S(1)}, bf16[4,3,32,512]{3,2,1,0:T(8,128)(2,1)S(1)}, u32[]{:S(2)}, u32[]{:S(2)}) collective-permute-start(bf16[4,3,32,512]{3,2,1,0:T(8,128)(2,1)S(1)} %add_convert_fusion), channel_id=1, source_target_pairs={{0,24},{1,7},{2,26},{3,1},{4,28},{5,3},{6,30},{7,5},{8,0},{9,15},{... | collective-permute-start | bytes 1179656 | tf_op jit(solution)/shard_map/ppermute | solution.py:618
  43.1 9.1 %collective-permute-start.9 = (bf16[4,3,32,512]{3,2,1,0:T(8,128)(2,1)S(1)}, bf16[4,3,32,512]{3,2,1,0:T(8,128)(2,1)S(1)}, u32[]{:S(2)}, u32[]{:S(2)}) collective-permute-start(bf16[4,3,32,512]{3,2,1,0:T(8,128)(2,1)S(1)} %add_convert_fusion.1), channel_id=1, source_target_pairs={{0,8},{1,3},{2,10},{3,5},{4,12},{5,7},{6,14},{7,1},{8,16},{9,11},{... | collective-permute-start | bytes 1179656 | tf_op jit(solution)/shard_map/ppermute | solution.py:618
  53.4 7.5 %collective-permute-start.14 = (bf16[3,32,1024]{2,1,0:T(8,128)(2,1)S(1)}, bf16[3,32,1024]{2,1,0:T(8,128)(2,1)S(1)}, u32[]{:S(2)}, u32[]{:S(2)}) collective-permute-start(bf16[3,32,1024]{2,1,0:T(8,128)(2,1)S(1)} %get-tuple-element.61), channel_id=1, source_target_pairs={{0,2},{1,9},{2,4},{3,11},{4,6},{5,13},{6,0},{7,15},{8,10},{9,17},{... | collective-permute-start | bytes 589832 | tf_op jit(solution)/shard_map/ppermute | solution.py:618
  55.0 8.7 %collective-permute-start.15 = (bf16[3,32,1024]{2,1,0:T(8,128)(2,1)S(1)}, bf16[3,32,1024]{2,1,0:T(8,128)(2,1)S(1)}, u32[]{:S(2)}, u32[]{:S(2)}) collective-permute-start(bf16[3,32,1024]{2,1,0:T(8,128)(2,1)S(1)} %get-tuple-element.62), channel_id=1, source_target_pairs={{0,4},{1,17},{2,6},{3,19},{4,0},{5,21},{6,2},{7,23},{8,12},{9,25},... | collective-permute-start | bytes 589832 | tf_op jit(solution)/shard_map/ppermute | solution.py:618
  57.9 5.8 %collective-permute-start.16 = (bf16[3,32,1024]{2,1,0:T(8,128)(2,1)S(1)}, bf16[3,32,1024]{2,1,0:T(8,128)(2,1)S(1)}, u32[]{:S(2)}, u32[]{:S(2)}) collective-permute-start(bf16[3,32,1024]{2,1,0:T(8,128)(2,1)S(1)} %get-tuple-element.63), channel_id=1, source_target_pairs={{0,6},{1,25},{2,0},{3,27},{4,2},{5,29},{6,4},{7,31},{8,14},{9,1},{... | collective-permute-start | bytes 589832 | tf_op jit(solution)/shard_map/ppermute | solution.py:618
  59.6 1.3 %collective-permute-start.4 = (bf16[3,16,1024]{2,1,0:T(8,128)(2,1)S(1)}, bf16[3,16,1024]{2,1,0:T(8,128)(2,1)S(1)}, u32[]{:S(2)}, u32[]{:S(2)}) collective-permute-start(bf16[3,16,1024]{2,1,0:T(8,128)(2,1)S(1)} %get-tuple-element.50), channel_id=1, source_target_pairs={{0,1},{1,0},{2,3},{3,2},{4,5},{5,4},{6,7},{7,6},{8,9},{9,8},{10,11... | collective-permute-start | bytes 294920 | tf_op jit(solution)/shard_map/ppermute | solution.py:568
  64.4 8.9 %collective-permute-start.17 = (bf16[3,32,1024]{2,1,0:T(8,128)(2,1)S(1)}, bf16[3,32,1024]{2,1,0:T(8,128)(2,1)S(1)}, u32[]{:S(2)}, u32[]{:S(2)}) collective-permute-start(bf16[3,32,1024]{2,1,0:T(8,128)(2,1)S(1)} %error.1.after_ref.refs_0_), channel_id=1, source_target_pairs={{0,2},{1,9},{2,4},{3,11},{4,6},{5,13},{6,0},{7,15},{8,10},{9,17},{... | collective-permute-start | bytes 589832 | tf_op jit(solution)/shard_map/ppermute | solution.py:618
  66.1 9.8 %collective-permute-start.18 = (bf16[3,32,1024]{2,1,0:T(8,128)(2,1)S(1)}, bf16[3,32,1024]{2,1,0:T(8,128)(2,1)S(1)}, u32[]{:S(2)}, u32[]{:S(2)}) collective-permute-start(bf16[3,32,1024]{2,1,0:T(8,128)(2,1)S(1)} %error.1.after_ref.refs_0_), channel_id=1, source_target_pairs={{0,4},{1,17},{2,6},{3,19},{4,0},{5,21},{6,2},{7,23},{8,12},{9,25},... | collective-permute-start | bytes 589832 | tf_op jit(solution)/shard_map/ppermute | solution.py:618
  68.7 7.2 %collective-permute-start.19 = (bf16[3,32,1024]{2,1,0:T(8,128)(2,1)S(1)}, bf16[3,32,1024]{2,1,0:T(8,128)(2,1)S(1)}, u32[]{:S(2)}, u32[]{:S(2)}) collective-permute-start(bf16[3,32,1024]{2,1,0:T(8,128)(2,1)S(1)} %error.1.after_ref.refs_0_), channel_id=1, source_target_pairs={{0,6},{1,25},{2,0},{3,27},{4,2},{5,29},{6,4},{7,31},{8,14},{9,1},{... | collective-permute-start | bytes 589832 | tf_op jit(solution)/shard_map/ppermute | solution.py:618
  76.5 9.1 %collective-permute-start.20 = (bf16[4,3,32,512]{3,2,1,0:T(8,128)(2,1)S(1)}, bf16[4,3,32,512]{3,2,1,0:T(8,128)(2,1)S(1)}, u32[]{:S(2)}, u32[]{:S(2)}) collective-permute-start(bf16[4,3,32,512]{3,2,1,0:T(8,128)(2,1)S(1)} %get-tuple-element.69.refs_0_), channel_id=1, source_target_pairs={{0,8},{1,3},{2,10},{3,5},{4,12},{5,7},{6,14},{7,1},{8,16},{9,11},{... | collective-permute-start | bytes 1179656 | tf_op jit(solution)/shard_map/ppermute | solution.py:618
  76.6 9.0 %collective-permute-start.23 = (bf16[4,3,32,512]{3,2,1,0:T(8,128)(2,1)S(1)}, bf16[4,3,32,512]{3,2,1,0:T(8,128)(2,1)S(1)}, u32[]{:S(2)}, u32[]{:S(2)}) collective-permute-start(bf16[4,3,32,512]{3,2,1,0:T(8,128)(2,1)S(1)} %get-tuple-element.70.refs_1_), channel_id=1, source_target_pairs={{0,24},{1,7},{2,26},{3,1},{4,28},{5,3},{6,30},{7,5},{8,0},{9,15},{... | collective-permute-start | bytes 1179656 | tf_op jit(solution)/shard_map/ppermute | solution.py:618
  79.8 10.0 %collective-permute-start.21 = (bf16[4,3,32,512]{3,2,1,0:T(8,128)(2,1)S(1)}, bf16[4,3,32,512]{3,2,1,0:T(8,128)(2,1)S(1)}, u32[]{:S(2)}, u32[]{:S(2)}) collective-permute-start(bf16[4,3,32,512]{3,2,1,0:T(8,128)(2,1)S(1)} %get-tuple-element.70.refs_1_), channel_id=1, source_target_pairs={{0,8},{1,3},{2,10},{3,5},{4,12},{5,7},{6,14},{7,1},{8,16},{9,11},{... | collective-permute-start | bytes 1179656 | tf_op jit(solution)/shard_map/ppermute | solution.py:618
  79.8 10.0 %collective-permute-start.25 = (bf16[4,3,32,512]{3,2,1,0:T(8,128)(2,1)S(1)}, bf16[4,3,32,512]{3,2,1,0:T(8,128)(2,1)S(1)}, u32[]{:S(2)}, u32[]{:S(2)}) collective-permute-start(bf16[4,3,32,512]{3,2,1,0:T(8,128)(2,1)S(1)} %get-tuple-element.69.refs_0_), channel_id=1, source_target_pairs={{0,24},{1,7},{2,26},{3,1},{4,28},{5,3},{6,30},{7,5},{8,0},{9,15},{... | collective-permute-start | bytes 1179656 | tf_op jit(solution)/shard_map/ppermute | solution.py:618
  85.6 9.0 %collective-permute-start.22 = (bf16[4,3,32,512]{3,2,1,0:T(8,128)(2,1)S(1)}, bf16[4,3,32,512]{3,2,1,0:T(8,128)(2,1)S(1)}, u32[]{:S(2)}, u32[]{:S(2)}) collective-permute-start(bf16[4,3,32,512]{3,2,1,0:T(8,128)(2,1)S(1)} %collective-permute-done.20.refs_2_), channel_id=1, source_target_pairs={{0,8},{1,3},{2,10},{3,5},{4,12},{5,7},{6,14},{7,1},{8,16},{9,11},{... | collective-permute-start | bytes 1179656 | tf_op jit(solution)/shard_map/ppermute | solution.py:618
  85.6 9.0 %collective-permute-start.24 = (bf16[4,3,32,512]{3,2,1,0:T(8,128)(2,1)S(1)}, bf16[4,3,32,512]{3,2,1,0:T(8,128)(2,1)S(1)}, u32[]{:S(2)}, u32[]{:S(2)}) collective-permute-start(bf16[4,3,32,512]{3,2,1,0:T(8,128)(2,1)S(1)} %collective-permute-done.23.refs_7_), channel_id=1, source_target_pairs={{0,24},{1,7},{2,26},{3,1},{4,28},{5,3},{6,30},{7,5},{8,0},{9,15},{... | collective-permute-start | bytes 1179656 | tf_op jit(solution)/shard_map/ppermute | solution.py:618
  98.1 3.1 %collective-permute-start.26 = (bf16[512,512]{1,0:T(8,128)(2,1)S(1)}, bf16[512,512]{1,0:T(8,128)(2,1)S(1)}, u32[]{:S(2)}, u32[]{:S(2)}) collective-permute-start(bf16[512,512]{1,0:T(8,128)(2,1)S(1)} %get-tuple-element.73), channel_id=1, source_target_pairs={{0,1},{1,0},{2,3},{3,2},{4,5},{5,4},{6,7},{7,6},{8,9},{9,8},{10,11... | collective-permute-start | bytes 1572872 | tf_op jit(solution)/shard_map/ppermute | solution.py:568
  101.4 12.5 %collective-permute-start.27 = (bf16[3,512,1024]{2,1,0:T(8,128)(2,1)S(1)}, bf16[3,512,1024]{2,1,0:T(8,128)(2,1)S(1)}, u32[]{:S(2)}, u32[]{:S(2)}) collective-permute-start(bf16[3,512,1024]{2,1,0:T(8,128)(2,1)S(1)} %get-tuple-element.74.err_ref), channel_id=1, source_target_pairs={{0,1},{1,0},{2,3},{3,2},{4,5},{5,4},{6,7},{7,6},{8,9},{9,8},{10,11... | collective-permute-start | bytes 9437192 | tf_op jit(solution)/shard_map/ppermute | solution.py:568
  102.0 6.4 %collective-permute-start.30 = (bf16[256,512]{1,0:T(8,128)(2,1)S(1)}, bf16[256,512]{1,0:T(8,128)(2,1)S(1)}, u32[]{:S(2)}, u32[]{:S(2)}) collective-permute-start(bf16[256,512]{1,0:T(8,128)(2,1)S(1)} %get-tuple-element.83), channel_id=1, source_target_pairs={{0,32},{1,97},{32,0},{33,65},{64,96},{65,33},{96,64},{97,1},{2,34}... | collective-permute-start | bytes 786440 | tf_op jit(solution)/shard_map/ppermute | solution.py:598
  102.0 9.2 %collective-permute-start.28 = (bf16[256,512]{1,0:T(8,128)(2,1)S(1)}, bf16[256,512]{1,0:T(8,128)(2,1)S(1)}, u32[]{:S(2)}, u32[]{:S(2)}) collective-permute-start(bf16[256,512]{1,0:T(8,128)(2,1)S(1)} %get-tuple-element.78), channel_id=1, source_target_pairs={{0,32},{1,97},{32,0},{33,65},{64,96},{65,33},{96,64},{97,1},{2,34}... | collective-permute-start | bytes 786440 | tf_op jit(solution)/shard_map/ppermute | solution.py:598
  108.4 9.4 %collective-permute-start.31 = (bf16[256,512]{1,0:T(8,128)(2,1)S(1)}, bf16[256,512]{1,0:T(8,128)(2,1)S(1)}, u32[]{:S(2)}, u32[]{:S(2)}) collective-permute-start(bf16[256,512]{1,0:T(8,128)(2,1)S(1)} %get-tuple-element.85), channel_id=1, source_target_pairs={{0,96},{1,33},{32,64},{33,1},{64,32},{65,97},{96,0},{97,65},{2,98}... | collective-permute-start | bytes 786440 | tf_op jit(solution)/shard_map/ppermute | solution.py:598
  111.2 7.7 %collective-permute-start.29 = (bf16[256,512]{1,0:T(8,128)(2,1)S(1)}, bf16[256,512]{1,0:T(8,128)(2,1)S(1)}, u32[]{:S(2)}, u32[]{:S(2)}) collective-permute-start(bf16[256,512]{1,0:T(8,128)(2,1)S(1)} %get-tuple-element.81), channel_id=1, source_target_pairs={{0,96},{1,33},{32,64},{33,1},{64,32},{65,97},{96,0},{97,65},{2,98}... | collective-permute-start | bytes 786440 | tf_op jit(solution)/shard_map/ppermute | solution.py:598

commit v9 on v8

--- a/solution.py
+++ b/solution.py
@@ -190,7 +190,7 @@
 
 
 def place_of(p_ref, far, near):
-    return jnp.where(p_ref[2] == 0, far * SIDE + near, near * SIDE + far)
+    return jnp.where(p_ref[2] == 1, far * SIDE + near, near * SIDE + far)
 
 
 def rebuild_kernel(p_ref, *refs):
@@ -202,7 +202,7 @@
     def _():
         for x in range(SIDE):
             for y in range(SIDE):
-                first, other = (jnp.where(p_ref[2] == 0, a, b) for a, b in ((x, y), (y, x)))
+                first, other = (jnp.where(p_ref[2] == 1, a, b) for a, b in ((x, y), (y, x)))
                 spot = lax.rem(first - p_ref[3] + SIDE, SIDE) * SIDE + other
                 to = pl.ds(pl.multiple_of(spot * piece, piece), piece)
                 r, src = divmod((x * SIDE + y) * piece, halves[0].shape[0])
@@ -612,7 +612,7 @@
     for x in range(SIDE):
         for y in range(SIDE):
             for c in range(2):
-                along_x = (c == 0) != second
+                along_x = (c == 1) != second
                 to = ((x + step) % SIDE, y) if along_x else (x, (y + step) % SIDE)
                 moves.append(((x * SIDE + y) * 2 + c, (to[0] * SIDE + to[1]) * 2 + c))
     return lax.ppermute(value, ("x", "y", "c"), moves)
@@ -649,7 +649,7 @@
 def per_device(mlp_inputs, enc_weight, enc_bias, active, dec_weight, target):
     rows = mlp_inputs.shape[0]
     x, y, c = (lax.axis_index(a) for a in "xyc")
-    first, second = jnp.where(c == 0, x, y), jnp.where(c == 0, y, x)
+    first, second = jnp.where(c == 1, x, y), jnp.where(c == 1, y, x)
     place = jnp.stack([x, y, c, first, second]).astype(jnp.int32)
     scale = 1.0 / math.sqrt(rows)
 

time: 122 us -> 122 us (level)
  no operation moved by 1% of the time
where the time goes in v9:
time: 122 us
  starting transfers between devices  49.6 us (41%)
  waiting for transfers between devices  36.7 us (30%)
  Pallas kernels  33.4 us (27%)
    pallas_call x18, Pallas kernels, call(): pl.pallas_call(body, out_shape=shapes, compiler_params=pltpu.CompilerPara...  33.4 us
    ppermute x18, starting transfers between devices, shift(): return lax.ppermute(value, ('x', 'y', 'c'), moves)  32.1 us
    ppermute x18, waiting for transfers between devices, shift(): return lax.ppermute(value, ('x', 'y', 'c'), moves)  24.5 us
    ppermute x8, starting transfers between devices, pair(): return lax.ppermute(value, ('z', 'c'), moves)  16.5 us
    ppermute x8, waiting for transfers between devices, pair(): return lax.ppermute(value, ('z', 'c'), moves)  9.38 us
    ppermute x6, waiting for transfers between devices, swap(): return lax.ppermute(value, 'c', [(0, 1), (1, 0)])  2.82 us
  transfers between devices with their start and end apart: 32, of which 17 were waited for; matrix products, arithmetic and copies ran while one was open for 0% of the time, Pallas kernels for 13%

profile of v9, /device:TPU:0, one launch (start us, length us, event | category | flops | bytes accessed | tf_op | source)
XLA Modules:
  0.0 121.8 jit_solution(7307634677118909248)
XLA Ops:
  0.7 0.7 stack.23.p_ref
  1.3 4.3 %pre.1 = (bf16[256,512]{1,0:T(8,128)(2,1)S(1)}, bf16[256,512]{1,0:T(8,128)(2,1)S(1)}, bf16[3,512,1024]{2,1,0:T(8,128)(2,1)S(1)}, bf16[3,16,1024]{2,1,0:T(8,128)(2,1)S(1)}, bf16[3,16,1024]{2,1,0:T(8,128)(2,1)S(1)}) custom-call(s32[5]{0:T(128)} %stack.23.p_ref, bf16[512,2048]{1,0:T(8,128)(2,1)} %x_ref.3, bf16[2048,512]{1,0:T(8,128)(2,1)} %w_ref.1, ...), custom_call_target="tpu_custom_call" | custom-call | flops 1073741824 | bytes 4194304 | tf_op jit(solution)/shard_map/pre/pallas_call | solution.py:27
  5.8 2.1 %collective-permute-start.2 = (bf16[256,512]{1,0:T(8,128)(2,1)S(1)}, bf16[256,512]{1,0:T(8,128)(2,1)S(1)}, u32[]{:S(2)}, u32[]{:S(2)}) collective-permute-start(bf16[256,512]{1,0:T(8,128)(2,1)S(1)} %get-tuple-element.47), channel_id=1, source_target_pairs={{0,32},{1,97},{32,0},{33,65},{64,96},{65,33},{96,64},{97,1},{2,34}... | collective-permute-start | bytes 786440 | tf_op jit(solution)/shard_map/ppermute | solution.py:598
  7.9 4.3 %collective-permute-done.2 = bf16[256,512]{1,0:T(8,128)(2,1)S(1)} collective-permute-done((bf16[256,512]{1,0:T(8,128)(2,1)S(1)}, bf16[256,512]{1,0:T(8,128)(2,1)S(1)}, u32[]{:S(2)}, u32[]{:S(2)}) %collective-permute-start.2) | collective-permute-done | bytes 262176 | tf_op jit(solution)/shard_map/ppermute | solution.py:598
  12.3 4.2 %collective-permute-start.3 = (bf16[256,512]{1,0:T(8,128)(2,1)S(1)}, bf16[256,512]{1,0:T(8,128)(2,1)S(1)}, u32[]{:S(2)}, u32[]{:S(2)}) collective-permute-start(bf16[256,512]{1,0:T(8,128)(2,1)S(1)} %get-tuple-element.89), channel_id=1, source_target_pairs={{0,96},{1,33},{32,64},{33,1},{64,32},{65,97},{96,0},{97,65},{2,98}... | collective-permute-start | bytes 786440 | tf_op jit(solution)/shard_map/ppermute | solution.py:598
  16.6 2.7 %collective-permute-start.1 = (bf16[256,512]{1,0:T(8,128)(2,1)S(1)}, bf16[256,512]{1,0:T(8,128)(2,1)S(1)}, u32[]{:S(2)}, u32[]{:S(2)}) collective-permute-start(bf16[256,512]{1,0:T(8,128)(2,1)S(1)} %get-tuple-element.91), channel_id=1, source_target_pairs={{0,96},{1,33},{32,64},{33,1},{64,32},{65,97},{96,0},{97,65},{2,98}... | collective-permute-start | bytes 786440 | tf_op jit(solution)/shard_map/ppermute | solution.py:598
  19.4 1.0 pick_half.1
  20.4 0.5 collective-permute-done.3.far_ref
  21.1 3.2 %collective-permute-done.1.far_ref = bf16[256,512]{1,0:T(8,128)(2,1)S(1)} collective-permute-done((bf16[256,512]{1,0:T(8,128)(2,1)S(1)}, bf16[256,512]{1,0:T(8,128)(2,1)S(1)}, u32[]{:S(2)}, u32[]{:S(2)}) %collective-permute-start.1) | collective-permute-done | bytes 262176 | tf_op jit(solution)/shard_map/ppermute | solution.py:598
  24.5 1.5 %collective-permute-done.5.refs_2_ = bf16[256,512]{1,0:T(8,128)(2,1)S(1)} collective-permute-done((bf16[256,512]{1,0:T(8,128)(2,1)S(1)}, bf16[256,512]{1,0:T(8,128)(2,1)S(1)}, u32[]{:S(2)}, u32[]{:S(2)}) %collective-permute-start.5) | collective-permute-done | bytes 262176 | tf_op jit(solution)/shard_map/ppermute | solution.py:568
  26.0 4.9 %rebuild.1 = (bf16[4,3,32,512]{3,2,1,0:T(8,128)(2,1)S(1)}, bf16[4,3,32,512]{3,2,1,0:T(8,128)(2,1)S(1)}, f32[4,3,32,512]{3,2,1,0:T(8,128)S(1)}, bf16[4,3,32,512]{...) custom-call(s32[5]{0:T(128)S(1)} %copy-done.2, ...), custom_call_target="tpu_custom_call" | custom-call | flops 3221225472 | bytes 11000000 | tf_op jit(solution)/shard_map/rebuild/pallas_call | solution.py:27
  30.9 3.1 %collective-permute-start.12 = (bf16[4,3,32,512]{3,2,1,0:T(8,128)(2,1)S(1)}, bf16[4,3,32,512]{3,2,1,0:T(8,128)(2,1)S(1)}, u32[]{:S(2)}, u32[]{:S(2)}) collective-permute-start(bf16[4,3,32,512]{3,2,1,0:T(8,128)(2,1)S(1)} %get-tuple-element.59), channel_id=1, source_target_pairs={{0,6},{1,25},{2,0},{3,27},{4,2},{5,29},{6,4},{7,31},{8,14},{9,1},{... | collective-permute-start | bytes 1179656 | tf_op jit(solution)/shard_map/ppermute | solution.py:618
  34.0 3.2 %collective-permute-start.10 = (bf16[4,3,32,512]{3,2,1,0:T(8,128)(2,1)S(1)}, bf16[4,3,32,512]{3,2,1,0:T(8,128)(2,1)S(1)}, u32[]{:S(2)}, u32[]{:S(2)}) collective-permute-start(bf16[4,3,32,512]{3,2,1,0:T(8,128)(2,1)S(1)} %get-tuple-element.56), channel_id=1, source_target_pairs={{0,6},{1,25},{2,0},{3,27},{4,2},{5,29},{6,4},{7,31},{8,14},{9,1},{... | collective-permute-start | bytes 1179656 | tf_op jit(solution)/shard_map/ppermute | solution.py:618
  37.2 2.1 %collective-permute-done.12 = bf16[4,3,32,512]{3,2,1,0:T(8,128)(2,1)S(1)} collective-permute-done((bf16[4,3,32,512]{3,2,1,0:T(8,128)(2,1)S(1)}, bf16[4,3,32,512]{3,2,1,0:T(8,128)(2,1)S(1)}, u32[]{:S(2)}, u32[]{:S(2)}) %collective-permute-start.12) | collective-permute-done | bytes 393248 | tf_op jit(solution)/shard_map/ppermute | solution.py:618
  39.4 3.8 %collective-permute-start.13 = (bf16[4,3,32,512]{3,2,1,0:T(8,128)(2,1)S(1)}, bf16[4,3,32,512]{3,2,1,0:T(8,128)(2,1)S(1)}, u32[]{:S(2)}, u32[]{:S(2)}) collective-permute-start(bf16[4,3,32,512]{3,2,1,0:T(8,128)(2,1)S(1)} %add_convert_fusion), channel_id=1, source_target_pairs={{0,6},{1,25},{2,0},{3,27},{4,2},{5,29},{6,4},{7,31},{8,14},{9,1},{... | collective-permute-start | bytes 1179656 | tf_op jit(solution)/shard_map/ppermute | solution.py:618
  43.5 3.7 %collective-permute-done.11.refs_2_ = bf16[4,3,32,512]{3,2,1,0:T(8,128)(2,1)S(1)} collective-permute-done((bf16[4,3,32,512]{3,2,1,0:T(8,128)(2,1)S(1)}, bf16[4,3,32,512]{3,2,1,0:T(8,128)(2,1)S(1)}, u32[]{:S(2)}, u32[]{:S(2)}) %collective-permute-start.11) | collective-permute-done | bytes 393248 | tf_op jit(solution)/shard_map/ppermute | solution.py:618
  47.2 1.3 %collective-permute-done.13.refs_3_ = bf16[4,3,32,512]{3,2,1,0:T(8,128)(2,1)S(1)} collective-permute-done((bf16[4,3,32,512]{3,2,1,0:T(8,128)(2,1)S(1)}, bf16[4,3,32,512]{3,2,1,0:T(8,128)(2,1)S(1)}, u32[]{:S(2)}, u32[]{:S(2)}) %collective-permute-start.13) | collective-permute-done | bytes 393248 | tf_op jit(solution)/shard_map/ppermute | solution.py:618
  48.5 3.9 %collective-permute-done.9.refs_0_ = bf16[4,3,32,512]{3,2,1,0:T(8,128)(2,1)S(1)} collective-permute-done((bf16[4,3,32,512]{3,2,1,0:T(8,128)(2,1)S(1)}, bf16[4,3,32,512]{3,2,1,0:T(8,128)(2,1)S(1)}, u32[]{:S(2)}, u32[]{:S(2)}) %collective-permute-start.9) | collective-permute-done | bytes 393248 | tf_op jit(solution)/shard_map/ppermute | solution.py:618
  52.4 1.2 %sum_first.1 = (f32[3,32,1024]{2,1,0:T(8,128)S(1)}, bf16[3,32,1024]{2,1,0:T(8,128)(2,1)S(1)}, bf16[3,32,1024]{2,1,0:T(8,128)(2,1)S(1)}, bf16[3,32,1024]{2,1,0:T(8,128)(2,1)S(1)}) custom-call(s32[5]{0:T(128)S(1)} %copy-done.2, f32[4,3,32,1024]{3,2,1,0:T(8,128)S(1)} %get-tuple-element.53.own_ref, bf16[4,3,32,512]{3,2,1,0:T(8,128)(2,1)S(1)} %collective-permute-done.9.refs_0_, ...), custom_call_target="tpu_custom_call" | custom-call | flops 1572864 | bytes 4718592 | tf_op jit(solution)/shard_map/sum_first/pallas_call | solution.py:27
  53.6 1.5 %collective-permute-start.14 = (bf16[3,32,1024]{2,1,0:T(8,128)(2,1)S(1)}, bf16[3,32,1024]{2,1,0:T(8,128)(2,1)S(1)}, u32[]{:S(2)}, u32[]{:S(2)}) collective-permute-start(bf16[3,32,1024]{2,1,0:T(8,128)(2,1)S(1)} %get-tuple-element.61), channel_id=1, source_target_pairs={{0,8},{1,3},{2,10},{3,5},{4,12},{5,7},{6,14},{7,1},{8,16},{9,11},{... | collective-permute-start | bytes 589832 | tf_op jit(solution)/shard_map/ppermute | solution.py:618
  55.2 2.7 %collective-permute-start.15 = (bf16[3,32,1024]{2,1,0:T(8,128)(2,1)S(1)}, bf16[3,32,1024]{2,1,0:T(8,128)(2,1)S(1)}, u32[]{:S(2)}, u32[]{:S(2)}) collective-permute-start(bf16[3,32,1024]{2,1,0:T(8,128)(2,1)S(1)} %get-tuple-element.62), channel_id=1, source_target_pairs={{0,16},{1,5},{2,18},{3,7},{4,20},{5,1},{6,22},{7,3},{8,24},{9,13},... | collective-permute-start | bytes 589832 | tf_op jit(solution)/shard_map/ppermute | solution.py:618
  57.9 1.9 %collective-permute-start.16 = (bf16[3,32,1024]{2,1,0:T(8,128)(2,1)S(1)}, bf16[3,32,1024]{2,1,0:T(8,128)(2,1)S(1)}, u32[]{:S(2)}, u32[]{:S(2)}) collective-permute-start(bf16[3,32,1024]{2,1,0:T(8,128)(2,1)S(1)} %get-tuple-element.63), channel_id=1, source_target_pairs={{0,24},{1,7},{2,26},{3,1},{4,28},{5,3},{6,30},{7,5},{8,0},{9,15},{... | collective-permute-start | bytes 589832 | tf_op jit(solution)/shard_map/ppermute | solution.py:618
  59.8 1.3 %collective-permute-done.4.got_ref = bf16[3,16,1024]{2,1,0:T(8,128)(2,1)S(1)} collective-permute-done((bf16[3,16,1024]{2,1,0:T(8,128)(2,1)S(1)}, bf16[3,16,1024]{2,1,0:T(8,128)(2,1)S(1)}, u32[]{:S(2)}, u32[]{:S(2)}) %collective-permute-start.4) | collective-permute-done | bytes 98336 | tf_op jit(solution)/shard_map/ppermute | solution.py:568
  61.1 2.6 %collective-permute-done.15.refs_2_ = bf16[3,32,1024]{2,1,0:T(8,128)(2,1)S(1)} collective-permute-done((bf16[3,32,1024]{2,1,0:T(8,128)(2,1)S(1)}, bf16[3,32,1024]{2,1,0:T(8,128)(2,1)S(1)}, u32[]{:S(2)}, u32[]{:S(2)}) %collective-permute-start.15) | collective-permute-done | bytes 196640 | tf_op jit(solution)/shard_map/ppermute | solution.py:618
  63.7 0.7 error.1.after_ref.refs_0_
  64.4 2.0 %collective-permute-start.17 = (bf16[3,32,1024]{2,1,0:T(8,128)(2,1)S(1)}, bf16[3,32,1024]{2,1,0:T(8,128)(2,1)S(1)}, u32[]{:S(2)}, u32[]{:S(2)}) collective-permute-start(bf16[3,32,1024]{2,1,0:T(8,128)(2,1)S(1)} %error.1.after_ref.refs_0_), channel_id=1, source_target_pairs={{0,8},{1,3},{2,10},{3,5},{4,12},{5,7},{6,14},{7,1},{8,16},{9,11},{... | collective-permute-start | bytes 589832 | tf_op jit(solution)/shard_map/ppermute | solution.py:618
  66.4 2.6 %collective-permute-start.18 = (bf16[3,32,1024]{2,1,0:T(8,128)(2,1)S(1)}, bf16[3,32,1024]{2,1,0:T(8,128)(2,1)S(1)}, u32[]{:S(2)}, u32[]{:S(2)}) collective-permute-start(bf16[3,32,1024]{2,1,0:T(8,128)(2,1)S(1)} %error.1.after_ref.refs_0_), channel_id=1, source_target_pairs={{0,16},{1,5},{2,18},{3,7},{4,20},{5,1},{6,22},{7,3},{8,24},{9,13},... | collective-permute-start | bytes 589832 | tf_op jit(solution)/shard_map/ppermute | solution.py:618
  68.9 1.5 %collective-permute-start.19 = (bf16[3,32,1024]{2,1,0:T(8,128)(2,1)S(1)}, bf16[3,32,1024]{2,1,0:T(8,128)(2,1)S(1)}, u32[]{:S(2)}, u32[]{:S(2)}) collective-permute-start(bf16[3,32,1024]{2,1,0:T(8,128)(2,1)S(1)} %error.1.after_ref.refs_0_), channel_id=1, source_target_pairs={{0,24},{1,7},{2,26},{3,1},{4,28},{5,3},{6,30},{7,5},{8,0},{9,15},{... | collective-permute-start | bytes 589832 | tf_op jit(solution)/shard_map/ppermute | solution.py:618
  70.5 1.1 turn.1
  71.6 1.8 %turn_dec.1 = (bf16[3,1024,512]{2,1,0:T(8,128)(2,1)S(1)}, bf16[3,1024,512]{2,1,0:T(8,128)(2,1)S(1)}, f32[8,128]{1,0:T(8,128)S(1)}) custom-call(bf16[3,512,1024]{2,1,0:T(8,128)(2,1)S(1)} %get-tuple-element.51.refs_4_.own_ref, bf16[3,512,1024]{2,1,0:T(8,128)(2,1)S(1)} %collective-permute-done.7.refs_5_.got_ref, f32[8,128]{1,0:T(8,128)S(1)} %get-tuple-element.66.after_ref), custom_call_target="tpu_custom_call" | custom-call | bytes 12000000 | tf_op jit(solution)/shard_map/turn_dec/pallas_call | solution.py:27
  73.5 2.6 %collective-permute-done.18.refs_2_ = bf16[3,32,1024]{2,1,0:T(8,128)(2,1)S(1)} collective-permute-done((bf16[3,32,1024]{2,1,0:T(8,128)(2,1)S(1)}, bf16[3,32,1024]{2,1,0:T(8,128)(2,1)S(1)}, u32[]{:S(2)}, u32[]{:S(2)}) %collective-permute-start.18) | collective-permute-done | bytes 196640 | tf_op jit(solution)/shard_map/ppermute | solution.py:618
  76.1 0.6 join.1
  76.8 3.2 %collective-permute-start.23 = (bf16[4,3,32,512]{3,2,1,0:T(8,128)(2,1)S(1)}, bf16[4,3,32,512]{3,2,1,0:T(8,128)(2,1)S(1)}, u32[]{:S(2)}, u32[]{:S(2)}) collective-permute-start(bf16[4,3,32,512]{3,2,1,0:T(8,128)(2,1)S(1)} %get-tuple-element.70.refs_1_), channel_id=1, source_target_pairs={{0,6},{1,25},{2,0},{3,27},{4,2},{5,29},{6,4},{7,31},{8,14},{9,1},{... | collective-permute-start | bytes 1179656 | tf_op jit(solution)/shard_map/ppermute | solution.py:618
  80.0 3.2 %collective-permute-start.25 = (bf16[4,3,32,512]{3,2,1,0:T(8,128)(2,1)S(1)}, bf16[4,3,32,512]{3,2,1,0:T(8,128)(2,1)S(1)}, u32[]{:S(2)}, u32[]{:S(2)}) collective-permute-start(bf16[4,3,32,512]{3,2,1,0:T(8,128)(2,1)S(1)} %get-tuple-element.69.refs_0_), channel_id=1, source_target_pairs={{0,6},{1,25},{2,0},{3,27},{4,2},{5,29},{6,4},{7,31},{8,14},{9,1},{... | collective-permute-start | bytes 1179656 | tf_op jit(solution)/shard_map/ppermute | solution.py:618
  83.3 2.5 %collective-permute-done.20.refs_2_ = bf16[4,3,32,512]{3,2,1,0:T(8,128)(2,1)S(1)} collective-permute-done((bf16[4,3,32,512]{3,2,1,0:T(8,128)(2,1)S(1)}, bf16[4,3,32,512]{3,2,1,0:T(8,128)(2,1)S(1)}, u32[]{:S(2)}, u32[]{:S(2)}) %collective-permute-start.20) | collective-permute-done | bytes 393248 | tf_op jit(solution)/shard_map/ppermute | solution.py:618
  85.8 3.2 %collective-permute-start.24 = (bf16[4,3,32,512]{3,2,1,0:T(8,128)(2,1)S(1)}, bf16[4,3,32,512]{3,2,1,0:T(8,128)(2,1)S(1)}, u32[]{:S(2)}, u32[]{:S(2)}) collective-permute-start(bf16[4,3,32,512]{3,2,1,0:T(8,128)(2,1)S(1)} %collective-permute-done.23.refs_7_), channel_id=1, source_target_pairs={{0,6},{1,25},{2,0},{3,27},{4,2},{5,29},{6,4},{7,31},{8,14},{9,1},{... | collective-permute-start | bytes 1179656 | tf_op jit(solution)/shard_map/ppermute | solution.py:618
  89.0 1.0 collective-permute-done.21.refs_3_
  90.0 4.8 %collective-permute-done.22.refs_4_ = bf16[4,3,32,512]{3,2,1,0:T(8,128)(2,1)S(1)} collective-permute-done((bf16[4,3,32,512]{3,2,1,0:T(8,128)(2,1)S(1)}, bf16[4,3,32,512]{3,2,1,0:T(8,128)(2,1)S(1)}, u32[]{:S(2)}, u32[]{:S(2)}) %collective-permute-start.22) | collective-permute-done | bytes 393248 | tf_op jit(solution)/shard_map/ppermute | solution.py:618
  94.8 3.5 %back_sib.1 = (bf16[3,512,1024]{2,1,0:T(8,128)(2,1)S(1)}, bf16[512,512]{1,0:T(8,128)(2,1)S(1)}) custom-call(s32[5]{0:T(128)S(1)} %copy-done.2, bf16[3,1024,512]{2,1,0:T(8,128)(2,1)S(1)} %get-tuple-element.67.dec_ref, bf16[4,3,32,512]{3,2,1,0:T(8,128)(2,1)S(1)} %get-tuple-element.69.refs_0_, bf16[4,3,32,512]{3,2,1,0:T(8,128)(2,1)S(1)} %get-tuple-element.70.refs_1_, ...), custom_call_target="tpu_custom_call" | custom-call | flops 1610612736 | bytes 10000000 | tf_op jit(solution)/shard_map/back_sib/pallas_call | solution.py:27
  98.4 3.0 %back_own.1.own_ref = f32[512,512]{1,0:T(8,128)S(1)} custom-call(s32[5]{0:T(128)S(1)} %copy-done.2, bf16[3,512,1024]{2,1,0:T(8,128)(2,1)S(1)} %get-tuple-element.71.err_ref, bf16[3,1024,512]{2,1,0:T(8,128)(2,1)S(1)} %get-tuple-element.72.dec_ref), custom_call_target="tpu_custom_call" | custom-call | flops 1610612736 | bytes 7000000 | tf_op jit(solution)/shard_map/back_own/pallas_call | solution.py:27
  101.6 0.6 collective-permute-start.27
  102.2 2.0 %collective-permute-start.28 = (bf16[256,512]{1,0:T(8,128)(2,1)S(1)}, bf16[256,512]{1,0:T(8,128)(2,1)S(1)}, u32[]{:S(2)}, u32[]{:S(2)}) collective-permute-start(bf16[256,512]{1,0:T(8,128)(2,1)S(1)} %get-tuple-element.78), channel_id=1, source_target_pairs={{0,32},{1,97},{32,0},{33,65},{64,96},{65,33},{96,64},{97,1},{2,34}... | collective-permute-start | bytes 786440 | tf_op jit(solution)/shard_map/ppermute | solution.py:598
  104.2 3.9 %dec_grad_own.1 = (bf16[3,512,2048]{2,1,0:T(8,128)(2,1)}, f32[8,128]{1,0:T(8,128)S(1)}) custom-call(s32[5]{0:T(128)S(1)} %copy-done.2, bf16[512,512]{1,0:T(8,128)(2,1)S(1)} %get-tuple-element.65.lat_ref, bf16[3,512,1024]{2,1,0:T(8,128)(2,1)S(1)} %get-tuple-element.74.err_ref), custom_call_target="tpu_custom_call" | custom-call | flops 1610612736 | bytes 7000000 | tf_op jit(solution)/shard_map/dec_grad_own/pallas_call | solution.py:27
  108.6 2.7 %collective-permute-start.31 = (bf16[256,512]{1,0:T(8,128)(2,1)S(1)}, bf16[256,512]{1,0:T(8,128)(2,1)S(1)}, u32[]{:S(2)}, u32[]{:S(2)}) collective-permute-start(bf16[256,512]{1,0:T(8,128)(2,1)S(1)} %get-tuple-element.85), channel_id=1, source_target_pairs={{0,96},{1,33},{32,64},{33,1},{64,32},{65,97},{96,0},{97,65},{2,98}... | collective-permute-start | bytes 786440 | tf_op jit(solution)/shard_map/ppermute | solution.py:598
  111.4 2.7 %collective-permute-start.29 = (bf16[256,512]{1,0:T(8,128)(2,1)S(1)}, bf16[256,512]{1,0:T(8,128)(2,1)S(1)}, u32[]{:S(2)}, u32[]{:S(2)}) collective-permute-start(bf16[256,512]{1,0:T(8,128)(2,1)S(1)} %get-tuple-element.81), channel_id=1, source_target_pairs={{0,96},{1,33},{32,64},{33,1},{64,32},{65,97},{96,0},{97,65},{2,98}... | collective-permute-start | bytes 786440 | tf_op jit(solution)/shard_map/ppermute | solution.py:598
  114.1 3.9 %dec_grad_sib.1 = (bf16[3,512,2048]{2,1,0:T(8,128)(2,1)}, f32[8,128]{1,0:T(8,128)S(1)}) custom-call(s32[5]{0:T(128)S(1)} %copy-done.2, bf16[512,512]{1,0:T(8,128)(2,1)S(1)} %get-tuple-element.65.lat_ref, bf16[3,512,1024]{2,1,0:T(8,128)(2,1)S(1)} %collective-permute-done.27.err_ref, ...), custom_call_target="tpu_custom_call", output_to_operand_aliasing={{0}: (3, {})} | custom-call | flops 1610612736 | bytes 7000000 | tf_op jit(solution)/shard_map/dec_grad_sib/pallas_call | solution.py:27
  118.1 1.0 collective-permute-done.29.far_a
  119.1 2.7 %enc_grad.1 = (bf16[2048,512]{1,0:T(8,128)(2,1)}, f32[1,512]{1,0:T(1,128)}) custom-call(bf16[2048,512]{1,0:T(8,128)(2,1)S(1)} %get-tuple-element.64.x_ref, s32[512,512]{1,0:T(8,128)S(1)} %copy-done, f32[8,128]{1,0:T(8,128)S(1)} %get-tuple-element.76.after_ref, f32[256,512]{1,0:T(8,128)S(1)} %get-tuple-element.80.near_a, ...), custom_call_target="tpu_custom_call" | custom-call | flops 1073741824 | bytes 7000000 | tf_op jit(solution)/shard_map/enc_grad/pallas_call | solution.py:27
  (52 shorter events, 2.2 us)
Async XLA Ops:
  0.6 18.7 %slice-start = ((s8[6291456]{0:T(1024)(128)(4,1)}), s8[2097152]{0:T(1024)(128)(4,1)S(1)}, s32[]{:S(2)}) async-start(s8[6291456]{0:T(1024)(128)(4,1)} %bitcast.7), calls=%async_computation | async-start | bytes 4194304
  1.3 18.0 %slice-start.1 = ((s8[6291456]{0:T(1024)(128)(4,1)}), s8[4194304]{0:T(1024)(128)(4,1)S(1)}, s32[]{:S(2)}) async-start(s8[6291456]{0:T(1024)(128)(4,1)} %bitcast.7), calls=%async_computation.1 | async-start | bytes 8388608
  1.3 18.0 %copy-start.2 = (s32[5]{0:T(128)S(1)}, s32[5]{0:T(128)}, u32[]{:S(2)}) copy-start(s32[5]{0:T(128)} %stack.23.p_ref) | copy-start | bytes 64
  5.7 20.3 %collective-permute-start.7 = (bf16[3,512,1024]{2,1,0:T(8,128)(2,1)S(1)}, bf16[3,512,1024]{2,1,0:T(8,128)(2,1)S(1)}, u32[]{:S(2)}, u32[]{:S(2)}) collective-permute-start(bf16[3,512,1024]{2,1,0:T(8,128)(2,1)S(1)} %get-tuple-element.52), channel_id=1, source_target_pairs={{0,1},{1,0},{2,3},{3,2},{4,5},{5,4},{6,7},{7,6},{8,9},{9,8},{10,11... | collective-permute-start | bytes 9437192 | tf_op jit(solution)/shard_map/ppermute | solution.py:568
  5.8 6.5 %collective-permute-start.2 = (bf16[256,512]{1,0:T(8,128)(2,1)S(1)}, bf16[256,512]{1,0:T(8,128)(2,1)S(1)}, u32[]{:S(2)}, u32[]{:S(2)}) collective-permute-start(bf16[256,512]{1,0:T(8,128)(2,1)S(1)} %get-tuple-element.47), channel_id=1, source_target_pairs={{0,32},{1,97},{32,0},{33,65},{64,96},{65,33},{96,64},{97,1},{2,34}... | collective-permute-start | bytes 786440 | tf_op jit(solution)/shard_map/ppermute | solution.py:598
  7.8 8.7 %collective-permute-start = (bf16[256,512]{1,0:T(8,128)(2,1)S(1)}, bf16[256,512]{1,0:T(8,128)(2,1)S(1)}, u32[]{:S(2)}, u32[]{:S(2)}) collective-permute-start(bf16[256,512]{1,0:T(8,128)(2,1)S(1)} %get-tuple-element.46), channel_id=1, source_target_pairs={{0,32},{1,97},{32,0},{33,65},{64,96},{65,33},{96,64},{97,1},{2,34}... | collective-permute-start | bytes 786440 | tf_op jit(solution)/shard_map/ppermute | solution.py:598
  12.3 8.6 %collective-permute-start.3 = (bf16[256,512]{1,0:T(8,128)(2,1)S(1)}, bf16[256,512]{1,0:T(8,128)(2,1)S(1)}, u32[]{:S(2)}, u32[]{:S(2)}) collective-permute-start(bf16[256,512]{1,0:T(8,128)(2,1)S(1)} %get-tuple-element.89), channel_id=1, source_target_pairs={{0,96},{1,33},{32,64},{33,1},{64,32},{65,97},{96,0},{97,65},{2,98}... | collective-permute-start | bytes 786440 | tf_op jit(solution)/shard_map/ppermute | solution.py:598
  16.6 7.7 %collective-permute-start.1 = (bf16[256,512]{1,0:T(8,128)(2,1)S(1)}, bf16[256,512]{1,0:T(8,128)(2,1)S(1)}, u32[]{:S(2)}, u32[]{:S(2)}) collective-permute-start(bf16[256,512]{1,0:T(8,128)(2,1)S(1)} %get-tuple-element.91), channel_id=1, source_target_pairs={{0,96},{1,33},{32,64},{33,1},{64,32},{65,97},{96,0},{97,65},{2,98}... | collective-permute-start | bytes 786440 | tf_op jit(solution)/shard_map/ppermute | solution.py:598
  19.3 1.5 %copy-start = (s32[512,512]{1,0:T(8,128)S(1)}, s32[512,512]{1,0:T(8,128)}, u32[]{:S(2)}) copy-start(s32[512,512]{1,0:T(8,128)} %active_ref.5) | copy-start | bytes 3145732
  19.4 1.5 %copy-start.3 = (f32[512]{0:T(512)S(1)}, f32[512]{0:T(512)}, u32[]{:S(2)}) copy-start(f32[512]{0:T(512)} %param.8) | copy-start | bytes 6148
  21.0 3.5 %collective-permute-start.6 = (bf16[256,512]{1,0:T(8,128)(2,1)S(1)}, bf16[256,512]{1,0:T(8,128)(2,1)S(1)}, u32[]{:S(2)}, u32[]{:S(2)}) collective-permute-start(bf16[256,512]{1,0:T(8,128)(2,1)S(1)} %latents_1.1.refs_1_.bottom_ref), channel_id=1, source_target_pairs={{0,1},{1,0},{2,3},{3,2},{4,5},{5,4},{6,7},{7,6},{8,9},{9,8},{10,11... | collective-permute-start | bytes 786440 | tf_op jit(solution)/shard_map/ppermute | solution.py:568
  24.4 1.6 %collective-permute-start.5 = (bf16[256,512]{1,0:T(8,128)(2,1)S(1)}, bf16[256,512]{1,0:T(8,128)(2,1)S(1)}, u32[]{:S(2)}, u32[]{:S(2)}) collective-permute-start(bf16[256,512]{1,0:T(8,128)(2,1)S(1)} %latents_0.1.refs_0_.top_ref), channel_id=1, source_target_pairs={{0,1},{1,0},{2,3},{3,2},{4,5},{5,4},{6,7},{7,6},{8,9},{9,8},{10,11... | collective-permute-start | bytes 786440 | tf_op jit(solution)/shard_map/ppermute | solution.py:568
  30.9 8.4 %collective-permute-start.12 = (bf16[4,3,32,512]{3,2,1,0:T(8,128)(2,1)S(1)}, bf16[4,3,32,512]{3,2,1,0:T(8,128)(2,1)S(1)}, u32[]{:S(2)}, u32[]{:S(2)}) collective-permute-start(bf16[4,3,32,512]{3,2,1,0:T(8,128)(2,1)S(1)} %get-tuple-element.59), channel_id=1, source_target_pairs={{0,6},{1,25},{2,0},{3,27},{4,2},{5,29},{6,4},{7,31},{8,14},{9,1},{... | collective-permute-start | bytes 1179656 | tf_op jit(solution)/shard_map/ppermute | solution.py:618
  34.0 9.2 %collective-permute-start.8 = (bf16[4,3,32,512]{3,2,1,0:T(8,128)(2,1)S(1)}, bf16[4,3,32,512]{3,2,1,0:T(8,128)(2,1)S(1)}, u32[]{:S(2)}, u32[]{:S(2)}) collective-permute-start(bf16[4,3,32,512]{3,2,1,0:T(8,128)(2,1)S(1)} %get-tuple-element.55), channel_id=1, source_target_pairs={{0,2},{1,9},{2,4},{3,11},{4,6},{5,13},{6,0},{7,15},{8,10},{9,17},{... | collective-permute-start | bytes 1179656 | tf_op jit(solution)/shard_map/ppermute | solution.py:618
  34.0 9.5 %collective-permute-start.10 = (bf16[4,3,32,512]{3,2,1,0:T(8,128)(2,1)S(1)}, bf16[4,3,32,512]{3,2,1,0:T(8,128)(2,1)S(1)}, u32[]{:S(2)}, u32[]{:S(2)}) collective-permute-start(bf16[4,3,32,512]{3,2,1,0:T(8,128)(2,1)S(1)} %get-tuple-element.56), channel_id=1, source_target_pairs={{0,6},{1,25},{2,0},{3,27},{4,2},{5,29},{6,4},{7,31},{8,14},{9,1},{... | collective-permute-start | bytes 1179656 | tf_op jit(solution)/shard_map/ppermute | solution.py:618
  37.2 10.0 %collective-permute-start.11 = (bf16[4,3,32,512]{3,2,1,0:T(8,128)(2,1)S(1)}, bf16[4,3,32,512]{3,2,1,0:T(8,128)(2,1)S(1)}, u32[]{:S(2)}, u32[]{:S(2)}) collective-permute-start(bf16[4,3,32,512]{3,2,1,0:T(8,128)(2,1)S(1)} %get-tuple-element.57), channel_id=1, source_target_pairs={{0,2},{1,9},{2,4},{3,11},{4,6},{5,13},{6,0},{7,15},{8,10},{9,17},{... | collective-permute-start | bytes 1179656 | tf_op jit(solution)/shard_map/ppermute | solution.py:618
  39.4 31.1 %copy-start.1 = (bf16[512,2048]{1,0:T(8,128)(2,1)S(1)}, bf16[512,2048]{1,0:T(8,128)(2,1)}, u32[]{:S(2)}) copy-start(bf16[512,2048]{1,0:T(8,128)(2,1)} %x_ref.3) | copy-start | bytes 6291460
  39.4 9.1 %collective-permute-start.13 = (bf16[4,3,32,512]{3,2,1,0:T(8,128)(2,1)S(1)}, bf16[4,3,32,512]{3,2,1,0:T(8,128)(2,1)S(1)}, u32[]{:S(2)}, u32[]{:S(2)}) collective-permute-start(bf16[4,3,32,512]{3,2,1,0:T(8,128)(2,1)S(1)} %add_convert_fusion), channel_id=1, source_target_pairs={{0,6},{1,25},{2,0},{3,27},{4,2},{5,29},{6,4},{7,31},{8,14},{9,1},{... | collective-permute-start | bytes 1179656 | tf_op jit(solution)/shard_map/ppermute | solution.py:618
  43.3 9.1 %collective-permute-start.9 = (bf16[4,3,32,512]{3,2,1,0:T(8,128)(2,1)S(1)}, bf16[4,3,32,512]{3,2,1,0:T(8,128)(2,1)S(1)}, u32[]{:S(2)}, u32[]{:S(2)}) collective-permute-start(bf16[4,3,32,512]{3,2,1,0:T(8,128)(2,1)S(1)} %add_convert_fusion.1), channel_id=1, source_target_pairs={{0,2},{1,9},{2,4},{3,11},{4,6},{5,13},{6,0},{7,15},{8,10},{9,17},{... | collective-permute-start | bytes 1179656 | tf_op jit(solution)/shard_map/ppermute | solution.py:618
  53.6 7.5 %collective-permute-start.14 = (bf16[3,32,1024]{2,1,0:T(8,128)(2,1)S(1)}, bf16[3,32,1024]{2,1,0:T(8,128)(2,1)S(1)}, u32[]{:S(2)}, u32[]{:S(2)}) collective-permute-start(bf16[3,32,1024]{2,1,0:T(8,128)(2,1)S(1)} %get-tuple-element.61), channel_id=1, source_target_pairs={{0,8},{1,3},{2,10},{3,5},{4,12},{5,7},{6,14},{7,1},{8,16},{9,11},{... | collective-permute-start | bytes 589832 | tf_op jit(solution)/shard_map/ppermute | solution.py:618
  55.2 8.5 %collective-permute-start.15 = (bf16[3,32,1024]{2,1,0:T(8,128)(2,1)S(1)}, bf16[3,32,1024]{2,1,0:T(8,128)(2,1)S(1)}, u32[]{:S(2)}, u32[]{:S(2)}) collective-permute-start(bf16[3,32,1024]{2,1,0:T(8,128)(2,1)S(1)} %get-tuple-element.62), channel_id=1, source_target_pairs={{0,16},{1,5},{2,18},{3,7},{4,20},{5,1},{6,22},{7,3},{8,24},{9,13},... | collective-permute-start | bytes 589832 | tf_op jit(solution)/shard_map/ppermute | solution.py:618
  57.9 5.8 %collective-permute-start.16 = (bf16[3,32,1024]{2,1,0:T(8,128)(2,1)S(1)}, bf16[3,32,1024]{2,1,0:T(8,128)(2,1)S(1)}, u32[]{:S(2)}, u32[]{:S(2)}) collective-permute-start(bf16[3,32,1024]{2,1,0:T(8,128)(2,1)S(1)} %get-tuple-element.63), channel_id=1, source_target_pairs={{0,24},{1,7},{2,26},{3,1},{4,28},{5,3},{6,30},{7,5},{8,0},{9,15},{... | collective-permute-start | bytes 589832 | tf_op jit(solution)/shard_map/ppermute | solution.py:618
  59.8 1.3 %collective-permute-start.4 = (bf16[3,16,1024]{2,1,0:T(8,128)(2,1)S(1)}, bf16[3,16,1024]{2,1,0:T(8,128)(2,1)S(1)}, u32[]{:S(2)}, u32[]{:S(2)}) collective-permute-start(bf16[3,16,1024]{2,1,0:T(8,128)(2,1)S(1)} %get-tuple-element.50), channel_id=1, source_target_pairs={{0,1},{1,0},{2,3},{3,2},{4,5},{5,4},{6,7},{7,6},{8,9},{9,8},{10,11... | collective-permute-start | bytes 294920 | tf_op jit(solution)/shard_map/ppermute | solution.py:568
  64.4 9.1 %collective-permute-start.17 = (bf16[3,32,1024]{2,1,0:T(8,128)(2,1)S(1)}, bf16[3,32,1024]{2,1,0:T(8,128)(2,1)S(1)}, u32[]{:S(2)}, u32[]{:S(2)}) collective-permute-start(bf16[3,32,1024]{2,1,0:T(8,128)(2,1)S(1)} %error.1.after_ref.refs_0_), channel_id=1, source_target_pairs={{0,8},{1,3},{2,10},{3,5},{4,12},{5,7},{6,14},{7,1},{8,16},{9,11},{... | collective-permute-start | bytes 589832 | tf_op jit(solution)/shard_map/ppermute | solution.py:618
  66.4 9.7 %collective-permute-start.18 = (bf16[3,32,1024]{2,1,0:T(8,128)(2,1)S(1)}, bf16[3,32,1024]{2,1,0:T(8,128)(2,1)S(1)}, u32[]{:S(2)}, u32[]{:S(2)}) collective-permute-start(bf16[3,32,1024]{2,1,0:T(8,128)(2,1)S(1)} %error.1.after_ref.refs_0_), channel_id=1, source_target_pairs={{0,16},{1,5},{2,18},{3,7},{4,20},{5,1},{6,22},{7,3},{8,24},{9,13},... | collective-permute-start | bytes 589832 | tf_op jit(solution)/shard_map/ppermute | solution.py:618
  68.9 7.2 %collective-permute-start.19 = (bf16[3,32,1024]{2,1,0:T(8,128)(2,1)S(1)}, bf16[3,32,1024]{2,1,0:T(8,128)(2,1)S(1)}, u32[]{:S(2)}, u32[]{:S(2)}) collective-permute-start(bf16[3,32,1024]{2,1,0:T(8,128)(2,1)S(1)} %error.1.after_ref.refs_0_), channel_id=1, source_target_pairs={{0,24},{1,7},{2,26},{3,1},{4,28},{5,3},{6,30},{7,5},{8,0},{9,15},{... | collective-permute-start | bytes 589832 | tf_op jit(solution)/shard_map/ppermute | solution.py:618
  76.7 9.1 %collective-permute-start.20 = (bf16[4,3,32,512]{3,2,1,0:T(8,128)(2,1)S(1)}, bf16[4,3,32,512]{3,2,1,0:T(8,128)(2,1)S(1)}, u32[]{:S(2)}, u32[]{:S(2)}) collective-permute-start(bf16[4,3,32,512]{3,2,1,0:T(8,128)(2,1)S(1)} %get-tuple-element.69.refs_0_), channel_id=1, source_target_pairs={{0,2},{1,9},{2,4},{3,11},{4,6},{5,13},{6,0},{7,15},{8,10},{9,17},{... | collective-permute-start | bytes 1179656 | tf_op jit(solution)/shard_map/ppermute | solution.py:618
  76.8 9.0 %collective-permute-start.23 = (bf16[4,3,32,512]{3,2,1,0:T(8,128)(2,1)S(1)}, bf16[4,3,32,512]{3,2,1,0:T(8,128)(2,1)S(1)}, u32[]{:S(2)}, u32[]{:S(2)}) collective-permute-start(bf16[4,3,32,512]{3,2,1,0:T(8,128)(2,1)S(1)} %get-tuple-element.70.refs_1_), channel_id=1, source_target_pairs={{0,6},{1,25},{2,0},{3,27},{4,2},{5,29},{6,4},{7,31},{8,14},{9,1},{... | collective-permute-start | bytes 1179656 | tf_op jit(solution)/shard_map/ppermute | solution.py:618
  80.0 10.0 %collective-permute-start.21 = (bf16[4,3,32,512]{3,2,1,0:T(8,128)(2,1)S(1)}, bf16[4,3,32,512]{3,2,1,0:T(8,128)(2,1)S(1)}, u32[]{:S(2)}, u32[]{:S(2)}) collective-permute-start(bf16[4,3,32,512]{3,2,1,0:T(8,128)(2,1)S(1)} %get-tuple-element.70.refs_1_), channel_id=1, source_target_pairs={{0,2},{1,9},{2,4},{3,11},{4,6},{5,13},{6,0},{7,15},{8,10},{9,17},{... | collective-permute-start | bytes 1179656 | tf_op jit(solution)/shard_map/ppermute | solution.py:618
  80.0 10.0 %collective-permute-start.25 = (bf16[4,3,32,512]{3,2,1,0:T(8,128)(2,1)S(1)}, bf16[4,3,32,512]{3,2,1,0:T(8,128)(2,1)S(1)}, u32[]{:S(2)}, u32[]{:S(2)}) collective-permute-start(bf16[4,3,32,512]{3,2,1,0:T(8,128)(2,1)S(1)} %get-tuple-element.69.refs_0_), channel_id=1, source_target_pairs={{0,6},{1,25},{2,0},{3,27},{4,2},{5,29},{6,4},{7,31},{8,14},{9,1},{... | collective-permute-start | bytes 1179656 | tf_op jit(solution)/shard_map/ppermute | solution.py:618
  85.8 9.0 %collective-permute-start.22 = (bf16[4,3,32,512]{3,2,1,0:T(8,128)(2,1)S(1)}, bf16[4,3,32,512]{3,2,1,0:T(8,128)(2,1)S(1)}, u32[]{:S(2)}, u32[]{:S(2)}) collective-permute-start(bf16[4,3,32,512]{3,2,1,0:T(8,128)(2,1)S(1)} %collective-permute-done.20.refs_2_), channel_id=1, source_target_pairs={{0,2},{1,9},{2,4},{3,11},{4,6},{5,13},{6,0},{7,15},{8,10},{9,17},{... | collective-permute-start | bytes 1179656 | tf_op jit(solution)/shard_map/ppermute | solution.py:618
  85.8 9.0 %collective-permute-start.24 = (bf16[4,3,32,512]{3,2,1,0:T(8,128)(2,1)S(1)}, bf16[4,3,32,512]{3,2,1,0:T(8,128)(2,1)S(1)}, u32[]{:S(2)}, u32[]{:S(2)}) collective-permute-start(bf16[4,3,32,512]{3,2,1,0:T(8,128)(2,1)S(1)} %collective-permute-done.23.refs_7_), channel_id=1, source_target_pairs={{0,6},{1,25},{2,0},{3,27},{4,2},{5,29},{6,4},{7,31},{8,14},{9,1},{... | collective-permute-start | bytes 1179656 | tf_op jit(solution)/shard_map/ppermute | solution.py:618
  98.3 3.1 %collective-permute-start.26 = (bf16[512,512]{1,0:T(8,128)(2,1)S(1)}, bf16[512,512]{1,0:T(8,128)(2,1)S(1)}, u32[]{:S(2)}, u32[]{:S(2)}) collective-permute-start(bf16[512,512]{1,0:T(8,128)(2,1)S(1)} %get-tuple-element.73), channel_id=1, source_target_pairs={{0,1},{1,0},{2,3},{3,2},{4,5},{5,4},{6,7},{7,6},{8,9},{9,8},{10,11... | collective-permute-start | bytes 1572872 | tf_op jit(solution)/shard_map/ppermute | solution.py:568
  101.6 12.5 %collective-permute-start.27 = (bf16[3,512,1024]{2,1,0:T(8,128)(2,1)S(1)}, bf16[3,512,1024]{2,1,0:T(8,128)(2,1)S(1)}, u32[]{:S(2)}, u32[]{:S(2)}) collective-permute-start(bf16[3,512,1024]{2,1,0:T(8,128)(2,1)S(1)} %get-tuple-element.74.err_ref), channel_id=1, source_target_pairs={{0,1},{1,0},{2,3},{3,2},{4,5},{5,4},{6,7},{7,6},{8,9},{9,8},{10,11... | collective-permute-start | bytes 9437192 | tf_op jit(solution)/shard_map/ppermute | solution.py:568
  102.1 6.4 %collective-permute-start.30 = (bf16[256,512]{1,0:T(8,128)(2,1)S(1)}, bf16[256,512]{1,0:T(8,128)(2,1)S(1)}, u32[]{:S(2)}, u32[]{:S(2)}) collective-permute-start(bf16[256,512]{1,0:T(8,128)(2,1)S(1)} %get-tuple-element.83), channel_id=1, source_target_pairs={{0,32},{1,97},{32,0},{33,65},{64,96},{65,33},{96,64},{97,1},{2,34}... | collective-permute-start | bytes 786440 | tf_op jit(solution)/shard_map/ppermute | solution.py:598
  102.2 9.2 %collective-permute-start.28 = (bf16[256,512]{1,0:T(8,128)(2,1)S(1)}, bf16[256,512]{1,0:T(8,128)(2,1)S(1)}, u32[]{:S(2)}, u32[]{:S(2)}) collective-permute-start(bf16[256,512]{1,0:T(8,128)(2,1)S(1)} %get-tuple-element.78), channel_id=1, source_target_pairs={{0,32},{1,97},{32,0},{33,65},{64,96},{65,33},{96,64},{97,1},{2,34}... | collective-permute-start | bytes 786440 | tf_op jit(solution)/shard_map/ppermute | solution.py:598
  108.6 9.4 %collective-permute-start.31 = (bf16[256,512]{1,0:T(8,128)(2,1)S(1)}, bf16[256,512]{1,0:T(8,128)(2,1)S(1)}, u32[]{:S(2)}, u32[]{:S(2)}) collective-permute-start(bf16[256,512]{1,0:T(8,128)(2,1)S(1)} %get-tuple-element.85), channel_id=1, source_target_pairs={{0,96},{1,33},{32,64},{33,1},{64,32},{65,97},{96,0},{97,65},{2,98}... | collective-permute-start | bytes 786440 | tf_op jit(solution)/shard_map/ppermute | solution.py:598
  111.4 7.7 %collective-permute-start.29 = (bf16[256,512]{1,0:T(8,128)(2,1)S(1)}, bf16[256,512]{1,0:T(8,128)(2,1)S(1)}, u32[]{:S(2)}, u32[]{:S(2)}) collective-permute-start(bf16[256,512]{1,0:T(8,128)(2,1)S(1)} %get-tuple-element.81), channel_id=1, source_target_pairs={{0,96},{1,33},{32,64},{33,1},{64,32},{65,97},{96,0},{97,65},{2,98}... | collective-permute-start | bytes 786440 | tf_op jit(solution)/shard_map/ppermute | solution.py:598
